TPU v7x, 32 devices: a whole 2x2x4 slice. The times are simulated.
32 devices in a mesh: groups: 2 (over x), seq: 8 (over z, y), tp: 2 (over core).
Axes of the slice: x: 2, y: 2, z: 4, core: 2. Of those that a mesh axis runs over, the one named last changes fastest.
Arguments:
- tokens: bfloat16 [8192, 4096], P(('groups', 'seq')), parts along dimension 0, may hold values from -6 to 6
- gain: float32 [4096], replicated, may hold values from 0.1 to 1.9
- segments: int32 [8192], P(('groups', 'seq')), parts along dimension 0, may hold values from 0 to 3, never falling along the last dimension, each value on 1 to 2048 neighbouring positions
- w_query: bfloat16 [4096, 512], P(None, 'tp')
- w_keyval: bfloat16 [4096, 512], P(None, 'tp')
- w_out: bfloat16 [512, 4096], P('tp'), may hold values from -2.109375 to 2.109375
- sum_exps: int32 [8192, 32], P(('groups', 'seq')), parts along dimension 0, may hold values from -9 to -5
- out_exps: int32 [8192, 32], P(('groups', 'seq')), parts along dimension 0, may hold values from -9 to -5
Outputs:
- mixed: bfloat16 [8192, 4096], P(('groups', 'seq')), parts along dimension 0
There are 2 independent parts, one for each index of `groups`. A program takes and returns all parts, laid end to end along the dimension named above; an argument that names none is the same for every part. Nothing has to cross between parts.
All inputs are finite; a program needn't handle non-finite values.
Results may differ from a plain program's by a relative error of at most 0.007.
The roundings to bfloat16 on the way count: a program that leaves them out, or rounds other values in their place, can miss the bound.
Values may be sent and summed in bfloat16 or wider, within the bound.
No kernel may reach another device: no remote copies, remote signals or barrier semaphores. Data moves between devices by JAX's collectives and lax.ppermute only.
A program may use at most 128 MiB of HBM per device.

v0:
```python
import jax
import jax.numpy as jnp
from jax import lax
from jax.sharding import PartitionSpec as P

HD = 256


def on_device(tokens, gain, segments, w_query, w_keyval, w_out, sum_exps, out_exps):
    row_count = tokens.shape[0]
    wide_tokens = tokens.astype(jnp.float32)
    center = wide_tokens - jnp.mean(wide_tokens, axis=1, keepdims=True)
    spread = jnp.mean(center * center, axis=1, keepdims=True)
    normed = (center * lax.rsqrt(spread + 1e-05) * gain).astype(jnp.bfloat16)
    heads_here = w_query.shape[1] // HD
    query = jnp.dot(normed, w_query, preferred_element_type=jnp.float32).astype(jnp.bfloat16)
    query = query.reshape(row_count, heads_here, HD)
    kv_local = jnp.dot(normed, w_keyval, preferred_element_type=jnp.float32).astype(jnp.bfloat16)
    seq_index = lax.axis_index("seq")
    query_pos = seq_index * row_count + jnp.arange(row_count, dtype=jnp.int32)
    factor = HD ** (-0.5)
    keyval = lax.all_gather(kv_local, "tp", axis=1, tiled=True)
    running = jnp.full((heads_here, row_count), -1e30, jnp.float32)
    absorb_keyval = lax.all_gather(keyval, "seq", axis=0, tiled=True)
    seg_ids = lax.all_gather(segments, "seq", axis=0, tiled=True)
    key_rows = absorb_keyval[:, :HD]
    value_rows = absorb_keyval[:, HD:]
    scores = jnp.einsum("qhd,kd->hqk", query, key_rows, preferred_element_type=jnp.float32) * factor
    key_pos = jnp.arange(absorb_keyval.shape[0], dtype=jnp.int32)
    allowed = ((segments[:, None] == seg_ids[None, :]) & (key_pos[None, :] <= query_pos[:, None]))[
        None
    ]
    fresh = jnp.maximum(running, jnp.max(jnp.where(allowed, scores, -1e30), axis=2))
    weights = jnp.where(allowed, jnp.exp(scores - fresh[:, :, None]), 0.0)
    total = jnp.sum(weights, axis=2)
    weighted = jnp.einsum(
        "hqk,kd->hqd", weights.astype(jnp.bfloat16), value_rows, preferred_element_type=jnp.float32
    )
    running, total, weighted = (fresh, total, weighted)
    attended = (weighted / total[:, :, None]).astype(jnp.bfloat16)
    attended = jnp.transpose(attended, (1, 0, 2)).reshape(row_count, heads_here * HD)
    term = jnp.dot(attended, w_out, preferred_element_type=jnp.float32)
    sum_scale = jnp.repeat(jnp.exp2(sum_exps.astype(jnp.float32)), 128, axis=1)
    out_scale = jnp.repeat(jnp.exp2(out_exps.astype(jnp.float32)), 128, axis=1)
    quant = jnp.clip(term / sum_scale, -448.0, 448.0)
    summed = lax.psum(quant.astype(jnp.bfloat16), "tp").astype(jnp.float32)
    combined = wide_tokens + sum_scale * summed
    coded = lax.optimization_barrier(
        jnp.clip(combined / out_scale, -448.0, 448.0).astype(jnp.bfloat16)
    )
    return (coded.astype(jnp.float32) * out_scale).astype(jnp.bfloat16)


def solution(mesh):
    in_specs = (
        P(("groups", "seq"), None),
        P(),
        P(("groups", "seq")),
        P(None, "tp"),
        P(None, "tp"),
        P("tp", None),
        P(("groups", "seq"), None),
        P(("groups", "seq"), None),
    )
    out_specs = P(("groups", "seq"), None)
    return jax.shard_map(
        on_device, mesh=mesh, in_specs=in_specs, out_specs=out_specs, check_vma=False
    )
```

profile of v0, /device:TPU:11, one launch (start us, length us, event | category | flops | bytes accessed | tf_op | source)
XLA Modules:
  0.0 195.0 jit_solution(10168462754625231819)
XLA Ops:
  6.5 0.0 copy-start
  6.5 0.0 all-gather.3.cloned.1.call-start
  6.5 0.0 copy-start.6
  6.6 3.0 %convert_reduce_fusion = f32[512]{0:T(512)S(1)} fusion(bf16[512,4096]{1,0:T(8,128)(2,1)} %param.8), kind=kLoop, calls=%fused_computation.2 | loop fusion | flops 4193792 | bytes 4196352 | tf_op jit(solution)/shard_map/reduce_sum | solution.py:12
  9.5 3.7 %fusion.2 = f32[512]{0:T(512)S(1)} fusion(bf16[512,4096]{1,0:T(8,128)(2,1)} %param.8, f32[512]{0:T(512)S(1)} %broadcast_multiply_fusion), kind=kLoop, calls=%fused_computation.5 | loop fusion | flops 8388096 | bytes 4198400 | tf_op jit(solution)/shard_map/reduce_sum | solution.py:13
  13.2 0.0 copy-start.3
  13.3 0.0 copy-start.5
  13.3 1.5 convolution_convert_fusion.1
  14.8 2.6 %all_gather.10 = bf16[512,512]{1,0:T(8,128)(2,1)} all-gather(bf16[512,256]{1,0:T(8,128)(2,1)S(1)} %convolution_convert_fusion.1), channel_id=1, replica_groups=mesh['groups'=2,'seq'=8,'tp'=2] {'tp'}, dimensions={1}, use_global_device_ids=true | all-gather | bytes 786432 | tf_op jit(solution)/shard_map/all_gather | solution.py:22
  17.4 0.0 all-gather.3.cloned.1.call-update
  17.4 0.0 all-reduce.2.cloned.1.call-start
  17.5 0.1 copy.11
  17.7 21.0 %all-gather = s32[8,1,512]{2,1,0:T(1,128)S(1)} all-gather(s32[1,1,512]{2,1,0:T(1,128)S(1)} %bitcast.61), channel_id=1, replica_groups=mesh['groups'=2,'seq'=8,'tp'=2] {'seq'}, dimensions={0}, use_global_device_ids=true | all-gather | bytes 18432 | tf_op jit(solution)/shard_map/all_gather | solution.py:25
  38.7 51.6 %all-gather.3.cloned.1.call-done = bf16[4096,512]{1,0:T(8,128)(2,1)} async-done(((bf16[512,512]{1,0:T(8,128)(2,1)}), bf16[4096,512]{1,0:T(8,128)(2,1)}) %all-gather.3.cloned.1.call-update) | async-done | bytes 4194320 | tf_op jit(solution)/shard_map/all_gather | solution.py:24
  90.3 10.6 %fusion.11 = (f32[512]{0:T(512)S(1)}, f32[4096,512]{1,0:T(8,128)}) fusion(s32[512]{0:T(512)S(1)} %iota_add_fusion, s32[512]{0:T(512)S(1)} %copy-done.5, s32[4096]{0:T(1024)S(1)} %bitcast.58, bf16[4096,256]{1,0:T(8,128)(2,1)S(1)} %copy-done, bf16[4096,512]{1,0:T(8,128)(2,1)} %all-gather.3.cloned.1.call-done, bf16[512,4096]{1,0:T(8,128)(2,1)} %param.8, ...), kind=kOutput, calls=%fused_computation.19 | convolution fusion | flops 2170682880 | bytes 16820224 | tf_op jit(solution)/shard_map/qhd,kd->hqk/dot_general | solution.py:28
  100.9 5.5 %fusion.15 = f32[512]{0:T(512)S(1)} fusion(f32[4096,512]{1,0:T(8,128)} %get-tuple-element.6, f32[512]{0:T(512)S(1)} %broadcast_maximum_fusion, s32[512]{0:T(512)S(1)} %iota_add_fusion, s32[512]{0:T(512)S(1)} %copy-done.5, s32[4096]{0:T(1024)S(1)} %bitcast.59), kind=kLoop, calls=%fused_computation.24 | loop fusion | flops 14679552 | bytes 8413184 | tf_op jit(solution)/shard_map/reduce_sum | solution.py:35
  106.5 5.5 %broadcast_in_dim.13 = f32[512,32,128]{2,1,0:T(8,128)} broadcast(f32[512,32]{1,0:T(8,128)S(1)} %copy.11), dimensions={0,1} | broadcast | bytes 8454144 | tf_op jit(solution)/shard_map/broadcast_in_dim | solution.py:43
  112.0 17.3 %fusion.10 = bf16[512,4096]{1,0:T(8,128)(2,1)} fusion(f32[64,8,32,128]{3,2,1,0:T(8,128)} %bitcast.56, bf16[256,4096]{1,0:T(8,128)(2,1)} %param.13, bf16[4096,512]{1,0:T(8,128)(2,1)} %all-gather.3.cloned.1.call-done, f32[4096,512]{1,0:T(8,128)} %get-tuple-element.6, f32[512]{0:T(512)S(1)} %broadcast_maximum_fusion, s32[512]{0:T(512)S(1)} %iota_add_fusion, ...), kind=kOutput, calls=%fused_computation.16 | convolution fusion | flops 2168717312 | bytes 25190400 | tf_op jit(solution)/shard_map/dot_general | solution.py:42
  129.3 0.0 all-reduce.2.cloned.1.call-update
  129.4 0.1 copy.12
  129.5 29.1 %all-reduce.2.cloned.1.call-done = bf16[512,4096]{1,0:T(8,128)(2,1)} async-done(((bf16[512,4096]{1,0:T(8,128)(2,1)}), bf16[512,4096]{1,0:T(8,128)(2,1)}) %all-reduce.2.cloned.1.call-update) | async-done | bytes 4194320 | tf_op jit(solution)/shard_map/psum | solution.py:46
  158.6 2.3 %broadcast_in_dim.30 = f32[512,32,128]{2,1,0:T(8,128)S(1)} broadcast(f32[512,32]{1,0:T(8,128)S(1)} %copy.12), dimensions={0,1} | broadcast | bytes 8454144 | tf_op jit(solution)/shard_map/broadcast_in_dim | solution.py:44
  160.9 17.8 %fusion.7 = bf16[512,4096]{1,0:T(8,128)(2,1)} fusion(bf16[512,4096]{1,0:T(8,128)(2,1)S(1)} %copy-done.2, bf16[512,4096]{1,0:T(8,128)(2,1)} %all-reduce.2.cloned.1.call-done, f32[64,8,32,128]{3,2,1,0:T(8,128)S(1)} %bitcast.54, f32[64,8,32,128]{3,2,1,0:T(8,128)} %bitcast.57), kind=kLoop, calls=%fused_computation.10 | loop fusion | flops 14680064 | bytes 29360128 | tf_op jit(solution)/shard_map/convert_element_type | solution.py:49
  178.7 9.4 %fusion.8 = bf16[512,4096]{1,0:T(8,128)(2,1)} fusion(bf16[512,4096]{1,0:T(8,128)(2,1)} %fusion.7, f32[64,8,32,128]{3,2,1,0:T(8,128)S(1)} %bitcast.55), kind=kLoop, calls=%fused_computation.12 | loop fusion | flops 6291456 | bytes 16777216 | tf_op jit(solution)/shard_map/convert_element_type | solution.py:51
  (18 shorter events, 0.1 us)
Async XLA Ops:
  6.5 83.8 %copy-start = (bf16[4096,256]{1,0:T(8,128)(2,1)S(1)}, bf16[4096,256]{1,0:T(8,128)(2,1)}, u32[]{:S(2)}) copy-start(bf16[4096,256]{1,0:T(8,128)(2,1)} %param.11) | copy-start | bytes 6291460
  6.5 6.7 %copy-start.7 = (f32[4096]{0:T(1024)S(1)}, f32[4096]{0:T(1024)}, u32[]{:S(2)}) copy-start(f32[4096]{0:T(1024)} %param.9) | copy-start | bytes 49156
  6.5 83.8 %all-gather.3.cloned.1.call-start = ((), (), s32[]{:S(2)}) async-start(), calls=%async_computation | async-start | bytes 4718592 | tf_op jit(solution)/shard_map/all_gather | solution.py:24
  6.5 6.7 %copy-start.1 = (bf16[512,4096]{1,0:T(8,128)(2,1)S(1)}, bf16[512,4096]{1,0:T(8,128)(2,1)}, u32[]{:S(2)}) copy-start(bf16[512,4096]{1,0:T(8,128)(2,1)} %param.8) | copy-start | bytes 12582916
  6.5 6.8 %copy-start.6 = (bf16[4096,256]{1,0:T(8,128)(2,1)S(1)}, bf16[4096,256]{1,0:T(8,128)(2,1)}, u32[]{:S(2)}) copy-start(bf16[4096,256]{1,0:T(8,128)(2,1)} %param.12) | copy-start | bytes 6291460
  13.2 4.2 %copy-start.3 = (s32[512,32]{0,1:T(8,128)S(1)}, s32[512,32]{0,1:T(8,128)}, u32[]{:S(2)}) copy-start(s32[512,32]{0,1:T(8,128)} %param.14) | copy-start | bytes 196612
  13.3 4.4 %copy-start.5 = (s32[512]{0:T(512)S(1)}, s32[512]{0:T(512)}, u32[]{:S(2)}) copy-start(s32[512]{0:T(512)} %param.10) | copy-start | bytes 6148
  17.4 141.2 %all-reduce.2.cloned.1.call-start = ((), (), s32[]{:S(2)}) async-start(), calls=%async_computation.1 | async-start | bytes 8388608 | tf_op jit(solution)/shard_map/psum | solution.py:46
  112.0 17.4 %copy-start.4 = (s32[512,32]{0,1:T(8,128)S(1)}, s32[512,32]{0,1:T(8,128)}, u32[]{:S(2)}) copy-start(s32[512,32]{0,1:T(8,128)} %param.15) | copy-start | bytes 196612
  158.6 2.3 %copy-start.2 = (bf16[512,4096]{1,0:T(8,128)(2,1)S(1)}, bf16[512,4096]{1,0:T(8,128)(2,1)}, u32[]{:S(2)}) copy-start(bf16[512,4096]{1,0:T(8,128)(2,1)} %param.8) | copy-start | bytes 12582916
Sparse Core Ops, SparseCore 0:
  17.5 72.7 all-gather.2
  129.5 29.0 all-reduce.1
where the time goes:
time: 196 us; the launch traced here: 195 us
  waiting for transfers between devices  80.7 us (41%)
  other arithmetic  39.5 us (20%)
  matrix products  29.4 us (15%)
  blocking collectives  23.6 us (12%)
  between operations  13.6 us (7%)
  local copies, waits for them, and re-layouts  8.06 us (4%)
    all_gather x1, waiting for transfers between devices, on_device(): absorb_keyval = lax.all_gather(keyval, 'seq', axis=0, tiled=True)  51.6 us
    psum x1, waiting for transfers between devices, on_device(): summed = lax.psum(quant.astype(jnp.bfloat16), 'tp').astype(jnp.float32)  29.1 us
    all_gather x1, blocking collectives, on_device(): seg_ids = lax.all_gather(segments, 'seq', axis=0, tiled=True)  21 us
    convert_element_type x1, other arithmetic, on_device(): jnp.clip(combined / out_scale, -448.0, 448.0).astype(jnp.bfloat16)  17.8 us
    dot_general x1, matrix products, on_device(): term = jnp.dot(attended, w_out, preferred_element_type=jnp.float32)  17.3 us
    dot_general x1, matrix products, on_device(): jnp.einsum('qhd,kd->hqk', query, key_rows, preferred_element_type=jnp.flo...  10.6 us
    convert_element_type x1, other arithmetic, on_device(): return (coded.astype(jnp.float32) * out_scale).astype(jnp.bfloat16)  9.37 us
    reduce_sum x1, other arithmetic, on_device(): total = jnp.sum(weights, axis=2)  5.54 us
  transfers between devices with their start and end apart: 2, of which 2 were waited for; matrix products, arithmetic and copies ran while one was open for 0% of the time, Pallas kernels for 0%

commit v1 on v0

v1 whole, which is shorter than its diff:
```python
import functools

import jax
import jax.numpy as jnp
from jax import lax
from jax.experimental import pallas as pl
from jax.experimental.pallas import tpu as pltpu
from jax.sharding import PartitionSpec as P

HD = 256
LANES = 128
SEG_ROWS = 16
LIMIT = 448.0
MIN_EXP = -9
NEG = -1e30
VMEM_BYTES = 56 * 1024 * 1024
NT = (((1,), (1,)), ((), ()))


def norm_kv_kernel(x_ref, gain_ref, w_ref, seg_ref, msg_ref, normed_ref):
    step = pl.program_id(0)
    rows = x_ref.shape[0]
    count = msg_ref.shape[0] - SEG_ROWS
    x = x_ref[...].astype(jnp.float32)
    center = x - jnp.mean(x, axis=1, keepdims=True)
    spread = jnp.mean(center * center, axis=1, keepdims=True)
    normed = (center * lax.rsqrt(spread + 1e-05) * gain_ref[...]).astype(jnp.bfloat16)
    normed_ref[...] = normed
    kv = jnp.dot(normed, w_ref[...], preferred_element_type=jnp.float32)
    msg_ref[pl.ds(pl.multiple_of(step * rows, rows), rows), :] = kv.astype(jnp.bfloat16)

    @pl.when(step == 0)
    def _():
        seg = seg_ref[...].astype(jnp.float32)
        low = jnp.broadcast_to(seg[:, :HD], (8, HD))
        high = jnp.broadcast_to(seg[:, HD:], (8, HD))
        msg_ref[pl.ds(count, SEG_ROWS), :] = jnp.concatenate([low, high], axis=0).astype(jnp.bfloat16)


def norm_kv(tokens, gain, w_keyval, segments, tile):
    rows, width = tokens.shape
    cols = w_keyval.shape[1]
    return pl.pallas_call(
        norm_kv_kernel,
        grid=(rows // tile,),
        in_specs=[
            pl.BlockSpec((tile, width), lambda i: (i, 0)),
            pl.BlockSpec((1, width), lambda i: (0, 0)),
            pl.BlockSpec((width, cols), lambda i: (0, 0)),
            pl.BlockSpec((1, rows), lambda i: (0, 0)),
        ],
        out_specs=[
            pl.BlockSpec((rows + SEG_ROWS, cols), lambda i: (0, 0)),
            pl.BlockSpec((tile, width), lambda i: (i, 0)),
        ],
        out_shape=[
            jax.ShapeDtypeStruct((rows + SEG_ROWS, cols), jnp.bfloat16),
            jax.ShapeDtypeStruct((rows, width), jnp.bfloat16),
        ],
        compiler_params=pltpu.CompilerParams(vmem_limit_bytes=VMEM_BYTES),
        cost_estimate=pl.CostEstimate(
            flops=2 * rows * width * cols + 10 * rows * width, bytes_accessed=4 * rows * width + 2 * width * cols, transcendentals=rows
        ),
        name="norm_kv",
    )(tokens, gain.reshape(1, width), w_keyval, segments.reshape(1, rows))


def query_kernel(x_ref, w_ref, out_ref):
    out_ref[...] = jnp.dot(x_ref[...], w_ref[...], preferred_element_type=jnp.float32).astype(jnp.bfloat16)


def project_query(normed, w_query):
    rows, width = normed.shape
    cols = w_query.shape[1]
    tile = rows // 2
    return pl.pallas_call(
        query_kernel,
        grid=(rows // tile,),
        in_specs=[pl.BlockSpec((tile, width), lambda i: (i, 0)), pl.BlockSpec((width, cols), lambda i: (0, 0))],
        out_specs=pl.BlockSpec((tile, cols), lambda i: (i, 0)),
        out_shape=jax.ShapeDtypeStruct((rows, cols), jnp.bfloat16),
        compiler_params=pltpu.CompilerParams(vmem_limit_bytes=VMEM_BYTES),
        cost_estimate=pl.CostEstimate(
            flops=2 * rows * width * cols, bytes_accessed=2 * rows * width + 2 * width * cols, transcendentals=0
        ),
        name="project_query",
    )(normed, w_query)


def attend_kernel(count, blocks, q_ref, seg_ref, *refs):
    mine, other = refs[:blocks + 1], refs[blocks + 1:2 * blocks + 2]
    out_ref, keys, values, segs, scores, sems = refs[2 * blocks + 2:]
    rows = q_ref.shape[0]
    part = lax.axis_index("tp")
    place = lax.axis_index("seq")
    odd = lax.rem(place, 2)

    def pieces(here, there, slot):
        return (
            (here.at[pl.ds(0, rows)], keys.at[slot], there.at[pl.ds(0, rows)], values.at[slot]),
            (there.at[pl.ds(0, rows)], keys.at[slot], here.at[pl.ds(0, rows)], values.at[slot]),
        )

    def fetch(here, there, slot):
        for value, (key_src, key_dst, val_src, val_dst) in enumerate(pieces(here, there, slot)):
            @pl.when(part == value)
            def _():
                pltpu.make_async_copy(key_src, key_dst, sems.at[0, slot]).start()
                pltpu.make_async_copy(val_src, val_dst, sems.at[1, slot]).start()

        pltpu.make_async_copy(here.at[pl.ds(rows, SEG_ROWS)], segs.at[slot], sems.at[2, slot]).start()

    for slot in range(blocks - 1):
        fetch(mine[slot], other[slot], slot)
    for value in range(2):
        @pl.when(odd == 1 - value)
        def _():
            fetch(mine[blocks - 1 + value], other[blocks - 1 + value], blocks - 1)

    evens = blocks // 2
    back = [0] + [2 * k for k in range(1, evens + 1)]
    back += [2 * k - 1 + 2 * odd for k in range(1, evens)] + [(2 * evens - 1) - (2 * evens - 2) * odd]
    wide = jnp.broadcast_to(seg_ref[...].astype(jnp.float32), (8, rows))
    own_seg = jnp.transpose(wide)[:, 0:1]
    top = jnp.full((rows, 1), NEG, jnp.float32)
    for slot in range(blocks):
        pltpu.make_async_copy(mine[0].at[pl.ds(0, rows)], keys.at[slot], sems.at[0, slot]).wait()
        pltpu.make_async_copy(mine[0].at[pl.ds(0, rows)], values.at[slot], sems.at[1, slot]).wait()
        pltpu.make_async_copy(mine[0].at[pl.ds(rows, SEG_ROWS)], segs.at[slot], sems.at[2, slot]).wait()
        raw = lax.dot_general(q_ref[...], keys[slot], NT, preferred_element_type=jnp.float32)
        packed = segs[slot].astype(jnp.float32)
        key_seg = jnp.concatenate([packed[0:1, :], packed[8:9, :]], axis=1)
        if slot == 0:
            row_pos = lax.broadcasted_iota(jnp.int32, (rows, rows), 0)
            col_pos = lax.broadcasted_iota(jnp.int32, (rows, rows), 1)
            allowed = (key_seg == own_seg) & (col_pos <= row_pos)
        else:
            key_seg = jnp.where(place >= back[slot], key_seg, -1.0)
            allowed = key_seg == own_seg
        masked = jnp.where(allowed, raw, NEG)
        scores[slot] = masked
        top = jnp.maximum(top, jnp.max(masked, axis=1, keepdims=True))
    factor = HD ** (-0.5) * 1.4426950408889634
    total = jnp.zeros((rows, 1), jnp.float32)
    weighted = jnp.zeros((rows, HD), jnp.float32)
    for slot in range(blocks):
        weights = jnp.exp2((scores[slot] - top) * factor)
        total = total + jnp.sum(weights, axis=1, keepdims=True)
        weighted = weighted + jnp.dot(weights.astype(jnp.bfloat16), values[slot], preferred_element_type=jnp.float32)
    out_ref[...] = (weighted / total).astype(jnp.bfloat16)


def attend(query, segments, mine, other, blocks):
    rows = query.shape[0]
    operands = 2 * (blocks + 1)
    return pl.pallas_call(
        functools.partial(attend_kernel, rows, blocks),
        in_specs=[pl.BlockSpec(memory_space=pltpu.VMEM)] * 2 + [pl.BlockSpec(memory_space=pl.ANY)] * operands,
        out_specs=pl.BlockSpec(memory_space=pltpu.VMEM),
        out_shape=jax.ShapeDtypeStruct((rows, HD), jnp.bfloat16),
        scratch_shapes=[
            pltpu.VMEM((blocks, rows, HD), jnp.bfloat16),
            pltpu.VMEM((blocks, rows, HD), jnp.bfloat16),
            pltpu.VMEM((blocks, SEG_ROWS, HD), jnp.bfloat16),
            pltpu.VMEM((blocks, rows, rows), jnp.float32),
            pltpu.SemaphoreType.DMA((3, blocks)),
        ],
        compiler_params=pltpu.CompilerParams(vmem_limit_bytes=VMEM_BYTES),
        cost_estimate=pl.CostEstimate(
            flops=4 * rows * rows * blocks * HD, bytes_accessed=4 * rows * blocks * HD, transcendentals=rows * rows * blocks
        ),
        name="attend",
    )(query, segments.reshape(1, rows), *mine, *other)


def output_kernel(a_ref, b_ref, wa_ref, wb_ref, x_ref, sum_ref, out_exp_ref, out_ref):
    width = x_ref.shape[1]
    groups = sum_ref.shape[0]

    def bounds(ref):
        power = jnp.left_shift(jnp.int32(1), ref[...] - MIN_EXP).astype(jnp.float32)
        return jnp.transpose(power * (LIMIT * 2.0 ** MIN_EXP))

    sum_bound, out_bound = bounds(sum_ref), bounds(out_exp_ref)
    per = width // groups
    chunk = 2 * per
    a, b = a_ref[...], b_ref[...]
    for start in range(0, width, chunk):
        term_a = jnp.dot(a, wa_ref[:, start:start + chunk], preferred_element_type=jnp.float32)
        term_b = jnp.dot(b, wb_ref[:, start:start + chunk], preferred_element_type=jnp.float32)
        for part in range(2):
            cols = slice(part * per, (part + 1) * per)
            group = (start + part * per) // per
            bound = sum_bound[:, group:group + 1]
            quant_a = jnp.clip(term_a[:, cols], -bound, bound).astype(jnp.bfloat16).astype(jnp.float32)
            quant_b = jnp.clip(term_b[:, cols], -bound, bound).astype(jnp.bfloat16).astype(jnp.float32)
            span = slice(start + part * per, start + (part + 1) * per)
            combined = x_ref[:, span].astype(jnp.float32) + (quant_a + quant_b)
            last = out_bound[:, group:group + 1]
            out_ref[:, span] = jnp.clip(combined, -last, last).astype(jnp.bfloat16)


def project_out(att_a, att_b, w_a, w_b, tokens, sum_exps, out_exps):
    rows, width = tokens.shape
    depth = att_a.shape[1]
    groups = sum_exps.shape[1]
    steps = groups // 8
    tile = width // steps
    whole = pl.BlockSpec((rows, depth), lambda i: (0, 0))
    weight = pl.BlockSpec((depth, tile), lambda i: (0, i))
    wide = pl.BlockSpec((rows, tile), lambda i: (0, i))
    exps = pl.BlockSpec((groups // steps, rows), lambda i: (i, 0))
    return pl.pallas_call(
        output_kernel,
        grid=(steps,),
        in_specs=[whole, whole, weight, weight, wide, exps, exps],
        out_specs=wide,
        out_shape=jax.ShapeDtypeStruct((rows, width), jnp.bfloat16),
        compiler_params=pltpu.CompilerParams(vmem_limit_bytes=VMEM_BYTES),
        cost_estimate=pl.CostEstimate(
            flops=4 * rows * width * depth, bytes_accessed=4 * rows * width + 4 * width * depth, transcendentals=0
        ),
        name="project_out",
    )(att_a, att_b, w_a, w_b, tokens, sum_exps.T, out_exps.T)


def on_device(seq_size, tokens, gain, segments, w_query, w_keyval, w_out, sum_exps, out_exps):
    window = seq_size // 2
    ahead = [(i, i + 2) for i in range(seq_size - 2)]
    across = [(i, i ^ 1) for i in range(seq_size)]
    to_odd = [(i, i + 1) for i in range(0, seq_size, 2)]
    to_even = [(i + 1, i) for i in range(0, seq_size, 2)]

    def swap(x):
        return lax.ppermute(x, "tp", [(0, 1), (1, 0)])

    w_other = swap(w_out)
    message, normed = norm_kv(tokens, gain, w_keyval, segments, 128)
    evens, odds = [], []
    held = message
    pair = lax.ppermute(message, "seq", to_odd)
    for k in range(window // 2):
        held = lax.ppermute(held, "seq", ahead)
        evens.append(held)
        if k < window // 2 - 1:
            odds.append(lax.ppermute(held, "seq", across))
    far = lax.ppermute(held, "seq", to_even)
    mine = [message] + evens + odds + [pair, far]
    other = [swap(m) for m in mine]
    query = project_query(normed, w_query)
    attended = attend(query, segments, mine, other, window + 1)
    return project_out(attended, swap(attended), w_out, w_other, tokens, sum_exps, out_exps)


def solution(mesh):
    in_specs = (
        P(("groups", "seq"), None),
        P(),
        P(("groups", "seq")),
        P(None, "tp"),
        P(None, "tp"),
        P("tp", None),
        P(("groups", "seq"), None),
        P(("groups", "seq"), None),
    )
    out_specs = P(("groups", "seq"), None)
    return jax.shard_map(
        functools.partial(on_device, mesh.shape["seq"]),
        mesh=mesh, in_specs=in_specs, out_specs=out_specs, check_vma=False,
    )
```

time: 196 us -> 66 us (0.34)
  waiting for transfers between devices: 80.7 us -> 12.8 us
  other arithmetic: 39.5 us -> 0 us
  Pallas kernels: 0 us -> 29.9 us
  matrix products: 29.4 us -> 0 us
  blocking collectives: 23.6 us -> 0 us
  starting transfers between devices: 0.04 us -> 19.7 us
  between operations: 13.6 us -> 0.17 us
  local copies, waits for them, and re-layouts: 8.06 us -> 2.96 us
    all_gather x1 -> x0, waiting for transfers between devices: 51.6 us -> none  [on_device(): absorb_keyval = lax.all_gather(keyval, 'seq', axis=0, tiled=True)]
    pallas_call x0 -> x4, Pallas kernels: none -> 29.9 us  [the longest x1 10.7 us: project_out(): pl.pallas_call(output_kernel, grid=(steps,), in_specs=[whole, whole, weig...]
    dot_general x3 -> x0, matrix products: 29.4 us -> none  [the longest x1 17.3 us: on_device(): term = jnp.dot(attended, w_out, preferred_element_type=jnp.float32)]
    psum x1 -> x0, waiting for transfers between devices: 29.1 us -> none  [on_device(): summed = lax.psum(quant.astype(jnp.bfloat16), 'tp').astype(jnp.float32)]
    convert_element_type x2 -> x0, other arithmetic: 27.2 us -> none  [the longest x1 17.8 us: on_device(): jnp.clip(combined / out_scale, -448.0, 448.0).astype(jnp.bfloat16)]
    all_gather x2 -> x0, blocking collectives: 23.6 us -> none  [the longest x1 21 us: on_device(): seg_ids = lax.all_gather(segments, 'seq', axis=0, tiled=True)]
    ppermute x0 -> x13, starting transfers between devices: none -> 19.7 us  [the longest x8 7.62 us: swap(): return lax.ppermute(x, 'tp', [(0, 1), (1, 0)])]
    ppermute x0 -> x13, waiting for transfers between devices: none -> 12.8 us  [the longest x2 6.97 us: on_device(): held = lax.ppermute(held, 'seq', ahead)]
  transfers between devices with their start and end apart: 2 -> 13, of which waited for: 2 -> 5; matrix products, arithmetic and copies ran while one was open for 0% -> 0% of each run, Pallas kernels for 0% -> 29%
where the time goes in v1:
time: 66 us; the launch traced here: 65.5 us
  Pallas kernels  29.9 us (45%)
  starting transfers between devices  19.7 us (30%)
  waiting for transfers between devices  12.8 us (19%)
  local copies, waits for them, and re-layouts  2.96 us (4%)
    pallas_call x1, Pallas kernels, project_out(): pl.pallas_call(output_kernel, grid=(steps,), in_specs=[whole, whole, weig...  10.7 us
    pallas_call x1, Pallas kernels, norm_kv(): pl.pallas_call(norm_kv_kernel, grid=(rows // tile,), in_specs=[pl.BlockSp...  7.78 us
    ppermute x8, starting transfers between devices, swap(): return lax.ppermute(x, 'tp', [(0, 1), (1, 0)])  7.62 us
    pallas_call x1, Pallas kernels, attend(): pl.pallas_call(functools.partial(attend_kernel, rows, blocks), in_specs=[...  7.13 us
    ppermute x2, waiting for transfers between devices, on_device(): held = lax.ppermute(held, 'seq', ahead)  6.97 us
    ppermute x2, starting transfers between devices, on_device(): held = lax.ppermute(held, 'seq', ahead)  6.39 us
    pallas_call x1, Pallas kernels, project_query(): pl.pallas_call(query_kernel, grid=(rows // tile,), in_specs=[pl.BlockSpec...  4.3 us
    ppermute x1, waiting for transfers between devices, on_device(): far = lax.ppermute(held, 'seq', to_even)  3.93 us
  transfers between devices with their start and end apart: 13, of which 5 were waited for; matrix products, arithmetic and copies ran while one was open for 0% of the time, Pallas kernels for 29%

profile of v1, /device:TPU:11, one launch (start us, length us, event | category | flops | bytes accessed | tf_op | source)
XLA Modules:
  0.0 65.5 jit_solution(3139846645930324509)
XLA Ops:
  0.0 0.7 %collective-permute-start.12 = (bf16[256,4096]{1,0:T(8,128)(2,1)}, bf16[256,4096]{1,0:T(8,128)(2,1)S(1)}, u32[]{:S(2)}, u32[]{:S(2)}) collective-permute-start(bf16[256,4096]{1,0:T(8,128)(2,1)} %wa_ref.1), channel_id=1, source_target_pairs={{0,1},{1,0},{2,3},{3,2},{4,5},{5,4},{6,7},{7,6},{8,9},{9,8},{10,11... | collective-permute-start | bytes 6291464 | tf_op jit(solution)/shard_map/ppermute | solution.py:235
  0.7 7.8 %norm_kv.1 = (bf16[528,256]{1,0:T(8,128)(2,1)}, bf16[512,4096]{1,0:T(8,128)(2,1)}) custom-call(bf16[512,4096]{1,0:T(8,128)(2,1)} %x_ref.3, f32[1,4096]{1,0:T(1,128)} %bitcast.6, bf16[4096,256]{1,0:T(8,128)(2,1)} %w_ref.2, s32[1,512]{1,0:T(1,128)} %bitcast.7), custom_call_target="tpu_custom_call" | custom-call | flops 1094713344 | bytes 10485760 | tf_op jit(solution)/shard_map/norm_kv/pallas_call | solution.py:43
  8.5 3.2 %collective-permute-start = (bf16[528,256]{1,0:T(8,128)(2,1)}, bf16[528,256]{1,0:T(8,128)(2,1)S(1)}, u32[]{:S(2)}, u32[]{:S(2)}) collective-permute-start(bf16[528,256]{1,0:T(8,128)(2,1)} %get-tuple-element.8.refs_0_), channel_id=1, source_target_pairs={{0,4},{2,6},{4,8},{6,10},{8,12},{10,14},{1,5},{3,7},{5,9},{7,11},{... | collective-permute-start | bytes 811016 | tf_op jit(solution)/shard_map/ppermute | solution.py:243
  11.7 3.2 %collective-permute-start.3 = (bf16[528,256]{1,0:T(8,128)(2,1)}, bf16[528,256]{1,0:T(8,128)(2,1)S(1)}, u32[]{:S(2)}, u32[]{:S(2)}) collective-permute-start(bf16[528,256]{1,0:T(8,128)(2,1)} %get-tuple-element.8.refs_0_), channel_id=1, source_target_pairs={{0,2},{4,6},{8,10},{12,14},{1,3},{5,7},{9,11},{13,15},{16,18},{20,... | collective-permute-start | bytes 811016 | tf_op jit(solution)/shard_map/ppermute | solution.py:241
  14.8 3.8 %collective-permute-done.refs_1_ = bf16[528,256]{1,0:T(8,128)(2,1)S(1)} collective-permute-done((bf16[528,256]{1,0:T(8,128)(2,1)}, bf16[528,256]{1,0:T(8,128)(2,1)S(1)}, u32[]{:S(2)}, u32[]{:S(2)}) %collective-permute-start) | collective-permute-done | bytes 270368 | tf_op jit(solution)/shard_map/ppermute | solution.py:243
  18.7 3.2 %collective-permute-start.1 = (bf16[528,256]{1,0:T(8,128)(2,1)S(1)}, bf16[528,256]{1,0:T(8,128)(2,1)S(1)}, u32[]{:S(2)}, u32[]{:S(2)}) collective-permute-start(bf16[528,256]{1,0:T(8,128)(2,1)S(1)} %collective-permute-done.refs_1_), channel_id=1, source_target_pairs={{0,4},{2,6},{4,8},{6,10},{8,12},{10,14},{1,5},{3,7},{5,9},{7,11},{... | collective-permute-start | bytes 811016 | tf_op jit(solution)/shard_map/ppermute | solution.py:243
  21.9 1.1 %collective-permute-start.5 = (bf16[528,256]{1,0:T(8,128)(2,1)}, bf16[528,256]{1,0:T(8,128)(2,1)S(1)}, u32[]{:S(2)}, u32[]{:S(2)}) collective-permute-start(bf16[528,256]{1,0:T(8,128)(2,1)} %get-tuple-element.8.refs_0_), channel_id=1, source_target_pairs={{0,1},{1,0},{2,3},{3,2},{4,5},{5,4},{6,7},{7,6},{8,9},{9,8},{10,11... | collective-permute-start | bytes 811016 | tf_op jit(solution)/shard_map/ppermute | solution.py:235
  23.0 1.3 %collective-permute-start.2 = (bf16[528,256]{1,0:T(8,128)(2,1)S(1)}, bf16[528,256]{1,0:T(8,128)(2,1)S(1)}, u32[]{:S(2)}, u32[]{:S(2)}) collective-permute-start(bf16[528,256]{1,0:T(8,128)(2,1)S(1)} %collective-permute-done.refs_1_), channel_id=1, source_target_pairs={{0,2},{2,0},{4,6},{6,4},{8,10},{10,8},{12,14},{14,12},{1,3},{3,1},... | collective-permute-start | bytes 811016 | tf_op jit(solution)/shard_map/ppermute | solution.py:246
  24.3 0.3 collective-permute-start.6
  24.6 3.1 %collective-permute-done.1.refs_2_ = bf16[528,256]{1,0:T(8,128)(2,1)S(1)} collective-permute-done((bf16[528,256]{1,0:T(8,128)(2,1)S(1)}, bf16[528,256]{1,0:T(8,128)(2,1)S(1)}, u32[]{:S(2)}, u32[]{:S(2)}) %collective-permute-start.1) | collective-permute-done | bytes 270368 | tf_op jit(solution)/shard_map/ppermute | solution.py:243
  27.8 1.3 %collective-permute-start.4 = (bf16[528,256]{1,0:T(8,128)(2,1)S(1)}, bf16[528,256]{1,0:T(8,128)(2,1)S(1)}, u32[]{:S(2)}, u32[]{:S(2)}) collective-permute-start(bf16[528,256]{1,0:T(8,128)(2,1)S(1)} %collective-permute-done.1.refs_2_), channel_id=1, source_target_pairs={{2,0},{6,4},{10,8},{14,12},{3,1},{7,5},{11,9},{15,13},{18,16},{22,... | collective-permute-start | bytes 811016 | tf_op jit(solution)/shard_map/ppermute | solution.py:247
  29.1 1.7 %collective-permute-start.9 = (bf16[528,256]{1,0:T(8,128)(2,1)S(1)}, bf16[528,256]{1,0:T(8,128)(2,1)S(1)}, u32[]{:S(2)}, u32[]{:S(2)}) collective-permute-start(bf16[528,256]{1,0:T(8,128)(2,1)S(1)} %collective-permute-done.3.refs_4_), channel_id=1, source_target_pairs={{0,1},{1,0},{2,3},{3,2},{4,5},{5,4},{6,7},{7,6},{8,9},{9,8},{10,11... | collective-permute-start | bytes 811016 | tf_op jit(solution)/shard_map/ppermute | solution.py:235
  30.8 0.2 collective-permute-done.2.refs_3_
  31.1 0.8 %collective-permute-start.7 = (bf16[528,256]{1,0:T(8,128)(2,1)S(1)}, bf16[528,256]{1,0:T(8,128)(2,1)S(1)}, u32[]{:S(2)}, u32[]{:S(2)}) collective-permute-start(bf16[528,256]{1,0:T(8,128)(2,1)S(1)} %collective-permute-done.1.refs_2_), channel_id=1, source_target_pairs={{0,1},{1,0},{2,3},{3,2},{4,5},{5,4},{6,7},{7,6},{8,9},{9,8},{10,11... | collective-permute-start | bytes 811016 | tf_op jit(solution)/shard_map/ppermute | solution.py:235
  32.0 3.9 %collective-permute-done.4.refs_5_ = bf16[528,256]{1,0:T(8,128)(2,1)S(1)} collective-permute-done((bf16[528,256]{1,0:T(8,128)(2,1)S(1)}, bf16[528,256]{1,0:T(8,128)(2,1)S(1)}, u32[]{:S(2)}, u32[]{:S(2)}) %collective-permute-start.4) | collective-permute-done | bytes 270368 | tf_op jit(solution)/shard_map/ppermute | solution.py:247
  35.9 2.6 %collective-permute-start.10 = (bf16[528,256]{1,0:T(8,128)(2,1)S(1)}, bf16[528,256]{1,0:T(8,128)(2,1)S(1)}, u32[]{:S(2)}, u32[]{:S(2)}) collective-permute-start(bf16[528,256]{1,0:T(8,128)(2,1)S(1)} %collective-permute-done.4.refs_5_), channel_id=1, source_target_pairs={{0,1},{1,0},{2,3},{3,2},{4,5},{5,4},{6,7},{7,6},{8,9},{9,8},{10,11... | collective-permute-start | bytes 811016 | tf_op jit(solution)/shard_map/ppermute | solution.py:235
  38.5 4.3 %project_query.1.q_ref = bf16[512,256]{1,0:T(8,128)(2,1)} custom-call(bf16[512,4096]{1,0:T(8,128)(2,1)} %get-tuple-element.7.x_ref, bf16[4096,256]{1,0:T(8,128)(2,1)} %w_ref.3), custom_call_target="tpu_custom_call" | custom-call | flops 1073741824 | bytes 6291456 | tf_op jit(solution)/shard_map/project_query/pallas_call | solution.py:76
  43.0 0.7 %copy-done.9 = bf16[528,256]{1,0:T(8,128)(2,1)} copy-done((bf16[528,256]{1,0:T(8,128)(2,1)}, bf16[528,256]{1,0:T(8,128)(2,1)S(1)}, u32[]{:S(2)}) %copy-start.9) | copy-done | bytes 270360
  43.8 0.7 %copy-done.12 = bf16[528,256]{1,0:T(8,128)(2,1)} copy-done((bf16[528,256]{1,0:T(8,128)(2,1)}, bf16[528,256]{1,0:T(8,128)(2,1)S(1)}, u32[]{:S(2)}) %copy-start.12) | copy-done | bytes 270360
  44.5 7.1 %attend.1.a_ref = bf16[512,256]{1,0:T(8,128)(2,1)} custom-call(bf16[512,256]{1,0:T(8,128)(2,1)} %project_query.1.q_ref, s32[1,512]{1,0:T(1,128)} %bitcast.8, bf16[528,256]{1,0:T(8,128)(2,1)} %get-tuple-element.8.refs_0_, bf16[528,256]{1,0:T(8,128)(2,1)} %copy-done.2, bf16[528,256]{1,0:T(8,128)(2,1)} %copy-done.4, bf16[528,256]{1,0:T(8,128)(2,1)} %copy-done.6, ...), custom_call_target="tpu_custom_call" | custom-call | flops 1342177280 | bytes 2621440 | tf_op jit(solution)/shard_map/attend/pallas_call | solution.py:156
  51.8 1.6 %collective-permute-done.11.b_ref = bf16[512,256]{1,0:T(8,128)(2,1)S(1)} collective-permute-done((bf16[512,256]{1,0:T(8,128)(2,1)}, bf16[512,256]{1,0:T(8,128)(2,1)S(1)}, u32[]{:S(2)}, u32[]{:S(2)}) %collective-permute-start.11) | collective-permute-done | bytes 262176 | tf_op jit(solution)/shard_map/ppermute | solution.py:235
  53.4 0.7 %copy-done.1 = bf16[512,256]{1,0:T(8,128)(2,1)} copy-done((bf16[512,256]{1,0:T(8,128)(2,1)}, bf16[512,256]{1,0:T(8,128)(2,1)S(1)}, u32[]{:S(2)}) %copy-start.1) | copy-done | bytes 262168
  54.1 0.7 %copy-done = bf16[256,4096]{1,0:T(8,128)(2,1)} copy-done((bf16[256,4096]{1,0:T(8,128)(2,1)}, bf16[256,4096]{1,0:T(8,128)(2,1)S(1)}, u32[]{:S(2)}) %copy-start) | copy-done | bytes 2097176
  54.8 10.7 %project_out.1 = bf16[512,4096]{1,0:T(8,128)(2,1)} custom-call(bf16[512,256]{1,0:T(8,128)(2,1)} %attend.1.a_ref, bf16[512,256]{1,0:T(8,128)(2,1)} %copy-done.1, bf16[256,4096]{1,0:T(8,128)(2,1)} %wa_ref.1, bf16[256,4096]{1,0:T(8,128)(2,1)} %copy-done, bf16[512,4096]{1,0:T(8,128)(2,1)} %x_ref.3, s32[32,512]{1,0:T(8,128)} %bitcast.4, s32[32,512]{1,0:T(8,128)} %bitcast.5), custom_call_target="tpu_custom_call" | custom-call | flops 2147483648 | bytes 12582912 | tf_op jit(solution)/shard_map/project_out/pallas_call | solution.py:213
  (32 shorter events, 0.5 us)
Async XLA Ops:
  0.0 53.4 %collective-permute-start.12 = (bf16[256,4096]{1,0:T(8,128)(2,1)}, bf16[256,4096]{1,0:T(8,128)(2,1)S(1)}, u32[]{:S(2)}, u32[]{:S(2)}) collective-permute-start(bf16[256,4096]{1,0:T(8,128)(2,1)} %wa_ref.1), channel_id=1, source_target_pairs={{0,1},{1,0},{2,3},{3,2},{4,5},{5,4},{6,7},{7,6},{8,9},{9,8},{10,11... | collective-permute-start | bytes 6291464 | tf_op jit(solution)/shard_map/ppermute | solution.py:235
  8.5 10.2 %collective-permute-start = (bf16[528,256]{1,0:T(8,128)(2,1)}, bf16[528,256]{1,0:T(8,128)(2,1)S(1)}, u32[]{:S(2)}, u32[]{:S(2)}) collective-permute-start(bf16[528,256]{1,0:T(8,128)(2,1)} %get-tuple-element.8.refs_0_), channel_id=1, source_target_pairs={{0,4},{2,6},{4,8},{6,10},{8,12},{10,14},{1,5},{3,7},{5,9},{7,11},{... | collective-permute-start | bytes 811016 | tf_op jit(solution)/shard_map/ppermute | solution.py:243
  11.7 12.6 %collective-permute-start.3 = (bf16[528,256]{1,0:T(8,128)(2,1)}, bf16[528,256]{1,0:T(8,128)(2,1)S(1)}, u32[]{:S(2)}, u32[]{:S(2)}) collective-permute-start(bf16[528,256]{1,0:T(8,128)(2,1)} %get-tuple-element.8.refs_0_), channel_id=1, source_target_pairs={{0,2},{4,6},{8,10},{12,14},{1,3},{5,7},{9,11},{13,15},{16,18},{20,... | collective-permute-start | bytes 811016 | tf_op jit(solution)/shard_map/ppermute | solution.py:241
  18.7 24.2 %copy-start.2 = (bf16[528,256]{1,0:T(8,128)(2,1)}, bf16[528,256]{1,0:T(8,128)(2,1)S(1)}, u32[]{:S(2)}) copy-start(bf16[528,256]{1,0:T(8,128)(2,1)S(1)} %collective-permute-done.refs_1_) | copy-start | bytes 811012
  18.7 9.1 %collective-permute-start.1 = (bf16[528,256]{1,0:T(8,128)(2,1)S(1)}, bf16[528,256]{1,0:T(8,128)(2,1)S(1)}, u32[]{:S(2)}, u32[]{:S(2)}) collective-permute-start(bf16[528,256]{1,0:T(8,128)(2,1)S(1)} %collective-permute-done.refs_1_), channel_id=1, source_target_pairs={{0,4},{2,6},{4,8},{6,10},{8,12},{10,14},{1,5},{3,7},{5,9},{7,11},{... | collective-permute-start | bytes 811016 | tf_op jit(solution)/shard_map/ppermute | solution.py:243
  21.9 7.2 %collective-permute-start.5 = (bf16[528,256]{1,0:T(8,128)(2,1)}, bf16[528,256]{1,0:T(8,128)(2,1)S(1)}, u32[]{:S(2)}, u32[]{:S(2)}) collective-permute-start(bf16[528,256]{1,0:T(8,128)(2,1)} %get-tuple-element.8.refs_0_), channel_id=1, source_target_pairs={{0,1},{1,0},{2,3},{3,2},{4,5},{5,4},{6,7},{7,6},{8,9},{9,8},{10,11... | collective-permute-start | bytes 811016 | tf_op jit(solution)/shard_map/ppermute | solution.py:235
  23.0 8.1 %collective-permute-start.2 = (bf16[528,256]{1,0:T(8,128)(2,1)S(1)}, bf16[528,256]{1,0:T(8,128)(2,1)S(1)}, u32[]{:S(2)}, u32[]{:S(2)}) collective-permute-start(bf16[528,256]{1,0:T(8,128)(2,1)S(1)} %collective-permute-done.refs_1_), channel_id=1, source_target_pairs={{0,2},{2,0},{4,6},{6,4},{8,10},{10,8},{12,14},{14,12},{1,3},{3,1},... | collective-permute-start | bytes 811016 | tf_op jit(solution)/shard_map/ppermute | solution.py:246
  24.3 18.6 %copy-start.3 = (bf16[528,256]{1,0:T(8,128)(2,1)}, bf16[528,256]{1,0:T(8,128)(2,1)S(1)}, u32[]{:S(2)}) copy-start(bf16[528,256]{1,0:T(8,128)(2,1)S(1)} %collective-permute-done.3.refs_4_) | copy-start | bytes 811012
  24.3 7.7 %collective-permute-start.6 = (bf16[528,256]{1,0:T(8,128)(2,1)S(1)}, bf16[528,256]{1,0:T(8,128)(2,1)S(1)}, u32[]{:S(2)}, u32[]{:S(2)}) collective-permute-start(bf16[528,256]{1,0:T(8,128)(2,1)S(1)} %collective-permute-done.refs_1_), channel_id=1, source_target_pairs={{0,1},{1,0},{2,3},{3,2},{4,5},{5,4},{6,7},{7,6},{8,9},{9,8},{10,11... | collective-permute-start | bytes 811016 | tf_op jit(solution)/shard_map/ppermute | solution.py:235
  27.8 15.1 %copy-start.4 = (bf16[528,256]{1,0:T(8,128)(2,1)}, bf16[528,256]{1,0:T(8,128)(2,1)S(1)}, u32[]{:S(2)}) copy-start(bf16[528,256]{1,0:T(8,128)(2,1)S(1)} %collective-permute-done.1.refs_2_) | copy-start | bytes 811012
  27.8 8.2 %collective-permute-start.4 = (bf16[528,256]{1,0:T(8,128)(2,1)S(1)}, bf16[528,256]{1,0:T(8,128)(2,1)S(1)}, u32[]{:S(2)}, u32[]{:S(2)}) collective-permute-start(bf16[528,256]{1,0:T(8,128)(2,1)S(1)} %collective-permute-done.1.refs_2_), channel_id=1, source_target_pairs={{2,0},{6,4},{10,8},{14,12},{3,1},{7,5},{11,9},{15,13},{18,16},{22,... | collective-permute-start | bytes 811016 | tf_op jit(solution)/shard_map/ppermute | solution.py:247
  29.1 13.8 %copy-start.5 = (bf16[528,256]{1,0:T(8,128)(2,1)}, bf16[528,256]{1,0:T(8,128)(2,1)S(1)}, u32[]{:S(2)}) copy-start(bf16[528,256]{1,0:T(8,128)(2,1)S(1)} %collective-permute-done.5.refs_6_) | copy-start | bytes 811012
  29.1 13.8 %collective-permute-start.9 = (bf16[528,256]{1,0:T(8,128)(2,1)S(1)}, bf16[528,256]{1,0:T(8,128)(2,1)S(1)}, u32[]{:S(2)}, u32[]{:S(2)}) collective-permute-start(bf16[528,256]{1,0:T(8,128)(2,1)S(1)} %collective-permute-done.3.refs_4_), channel_id=1, source_target_pairs={{0,1},{1,0},{2,3},{3,2},{4,5},{5,4},{6,7},{7,6},{8,9},{9,8},{10,11... | collective-permute-start | bytes 811016 | tf_op jit(solution)/shard_map/ppermute | solution.py:235
  31.1 11.8 %copy-start.6 = (bf16[528,256]{1,0:T(8,128)(2,1)}, bf16[528,256]{1,0:T(8,128)(2,1)S(1)}, u32[]{:S(2)}) copy-start(bf16[528,256]{1,0:T(8,128)(2,1)S(1)} %collective-permute-done.2.refs_3_) | copy-start | bytes 811012
  31.1 11.8 %collective-permute-start.7 = (bf16[528,256]{1,0:T(8,128)(2,1)S(1)}, bf16[528,256]{1,0:T(8,128)(2,1)S(1)}, u32[]{:S(2)}, u32[]{:S(2)}) collective-permute-start(bf16[528,256]{1,0:T(8,128)(2,1)S(1)} %collective-permute-done.1.refs_2_), channel_id=1, source_target_pairs={{0,1},{1,0},{2,3},{3,2},{4,5},{5,4},{6,7},{7,6},{8,9},{9,8},{10,11... | collective-permute-start | bytes 811016 | tf_op jit(solution)/shard_map/ppermute | solution.py:235
  31.9 11.0 %copy-start.7 = (bf16[528,256]{1,0:T(8,128)(2,1)}, bf16[528,256]{1,0:T(8,128)(2,1)S(1)}, u32[]{:S(2)}) copy-start(bf16[528,256]{1,0:T(8,128)(2,1)S(1)} %collective-permute-done.6.refs_7_) | copy-start | bytes 811012
  31.9 11.0 %collective-permute-start.8 = (bf16[528,256]{1,0:T(8,128)(2,1)S(1)}, bf16[528,256]{1,0:T(8,128)(2,1)S(1)}, u32[]{:S(2)}, u32[]{:S(2)}) collective-permute-start(bf16[528,256]{1,0:T(8,128)(2,1)S(1)} %collective-permute-done.2.refs_3_), channel_id=1, source_target_pairs={{0,1},{1,0},{2,3},{3,2},{4,5},{5,4},{6,7},{7,6},{8,9},{9,8},{10,11... | collective-permute-start | bytes 811016 | tf_op jit(solution)/shard_map/ppermute | solution.py:235
  35.9 7.0 %copy-start.8 = (bf16[528,256]{1,0:T(8,128)(2,1)}, bf16[528,256]{1,0:T(8,128)(2,1)S(1)}, u32[]{:S(2)}) copy-start(bf16[528,256]{1,0:T(8,128)(2,1)S(1)} %collective-permute-done.4.refs_5_) | copy-start | bytes 811012
  35.9 7.0 %collective-permute-start.10 = (bf16[528,256]{1,0:T(8,128)(2,1)S(1)}, bf16[528,256]{1,0:T(8,128)(2,1)S(1)}, u32[]{:S(2)}, u32[]{:S(2)}) collective-permute-start(bf16[528,256]{1,0:T(8,128)(2,1)S(1)} %collective-permute-done.4.refs_5_), channel_id=1, source_target_pairs={{0,1},{1,0},{2,3},{3,2},{4,5},{5,4},{6,7},{7,6},{8,9},{9,8},{10,11... | collective-permute-start | bytes 811016 | tf_op jit(solution)/shard_map/ppermute | solution.py:235
  42.9 0.7 %copy-start.9 = (bf16[528,256]{1,0:T(8,128)(2,1)}, bf16[528,256]{1,0:T(8,128)(2,1)S(1)}, u32[]{:S(2)}) copy-start(bf16[528,256]{1,0:T(8,128)(2,1)S(1)} %collective-permute-done.9.refs_10_) | copy-start | bytes 811012
  42.9 0.8 %copy-start.10 = (bf16[528,256]{1,0:T(8,128)(2,1)}, bf16[528,256]{1,0:T(8,128)(2,1)S(1)}, u32[]{:S(2)}) copy-start(bf16[528,256]{1,0:T(8,128)(2,1)S(1)} %collective-permute-done.7.refs_8_) | copy-start | bytes 811012
  42.9 0.8 %copy-start.11 = (bf16[528,256]{1,0:T(8,128)(2,1)}, bf16[528,256]{1,0:T(8,128)(2,1)S(1)}, u32[]{:S(2)}) copy-start(bf16[528,256]{1,0:T(8,128)(2,1)S(1)} %collective-permute-done.8.refs_9_) | copy-start | bytes 811012
  51.6 1.8 %collective-permute-start.11 = (bf16[512,256]{1,0:T(8,128)(2,1)}, bf16[512,256]{1,0:T(8,128)(2,1)S(1)}, u32[]{:S(2)}, u32[]{:S(2)}) collective-permute-start(bf16[512,256]{1,0:T(8,128)(2,1)} %attend.1.a_ref), channel_id=1, source_target_pairs={{0,1},{1,0},{2,3},{3,2},{4,5},{5,4},{6,7},{7,6},{8,9},{9,8},{10,11... | collective-permute-start | bytes 786440 | tf_op jit(solution)/shard_map/ppermute | solution.py:235
  53.4 1.4 %copy-start = (bf16[256,4096]{1,0:T(8,128)(2,1)}, bf16[256,4096]{1,0:T(8,128)(2,1)S(1)}, u32[]{:S(2)}) copy-start(bf16[256,4096]{1,0:T(8,128)(2,1)S(1)} %collective-permute-done.12.wb_ref) | copy-start | bytes 6291460
  (2 other events, 1.4 us)

commit v2 on v1

v2 whole, which is shorter than its diff:
```python
import functools

import jax
import jax.numpy as jnp
from jax import lax
from jax.experimental import pallas as pl
from jax.experimental.pallas import tpu as pltpu
from jax.sharding import PartitionSpec as P

HD = 256
LANES = 128
SEG_ROWS = 16
LIMIT = 448.0
MIN_EXP = -9
NEG = -1e30
MIB = 1024 * 1024
NT = (((1,), (1,)), ((), ()))
FACTOR = HD ** (-0.5) * 1.4426950408889634


def norm_kv_kernel(x_ref, gain_ref, w_ref, seg_ref, msg_ref, normed_ref):
    step = pl.program_id(0)
    rows, width = x_ref.shape
    count = msg_ref.shape[0] - SEG_ROWS

    def wide(start):
        return x_ref[:, start:start + LANES].astype(jnp.float32)

    total = wide(0)
    for start in range(LANES, width, LANES):
        total = total + wide(start)
    mean = jnp.broadcast_to(jnp.sum(total, axis=1, keepdims=True) * (1.0 / width), (rows, LANES))
    square = jnp.zeros((rows, LANES), jnp.float32)
    for start in range(0, width, LANES):
        center = wide(start) - mean
        square = square + center * center
    spread = jnp.sum(square, axis=1, keepdims=True) * (1.0 / width)
    scale = jnp.broadcast_to(lax.rsqrt(spread + 1e-05), (rows, LANES))
    kv = jnp.zeros((rows, w_ref.shape[1]), jnp.float32)
    for start in range(0, width, HD):
        for at in (start, start + LANES):
            normed = (wide(at) - mean) * scale * gain_ref[:, at:at + LANES]
            normed_ref[:, at:at + LANES] = normed.astype(jnp.bfloat16)
        kv = kv + jnp.dot(
            normed_ref[:, start:start + HD], w_ref[start:start + HD, :], preferred_element_type=jnp.float32
        )
    msg_ref[pl.ds(pl.multiple_of(step * rows, rows), rows), :] = kv.astype(jnp.bfloat16)

    @pl.when(step == 0)
    def _():
        seg = seg_ref[...].astype(jnp.float32)
        low = jnp.broadcast_to(seg[:, :HD], (8, HD))
        high = jnp.broadcast_to(seg[:, HD:], (8, HD))
        msg_ref[pl.ds(count, SEG_ROWS), :] = jnp.concatenate([low, high], axis=0).astype(jnp.bfloat16)


def norm_kv(tokens, gain, w_keyval, segments, tile):
    rows, width = tokens.shape
    cols = w_keyval.shape[1]
    return pl.pallas_call(
        norm_kv_kernel,
        grid=(rows // tile,),
        in_specs=[
            pl.BlockSpec((tile, width), lambda i: (i, 0)),
            pl.BlockSpec((1, width), lambda i: (0, 0)),
            pl.BlockSpec((width, cols), lambda i: (0, 0)),
            pl.BlockSpec((1, rows), lambda i: (0, 0)),
        ],
        out_specs=[
            pl.BlockSpec((rows + SEG_ROWS, cols), lambda i: (0, 0)),
            pl.BlockSpec((tile, width), lambda i: (i, 0)),
        ],
        out_shape=[
            jax.ShapeDtypeStruct((rows + SEG_ROWS, cols), jnp.bfloat16),
            jax.ShapeDtypeStruct((rows, width), jnp.bfloat16),
        ],
        compiler_params=pltpu.CompilerParams(vmem_limit_bytes=24 * MIB),
        cost_estimate=pl.CostEstimate(
            flops=2 * rows * width * cols, bytes_accessed=4 * rows * width + 2 * width * cols, transcendentals=0
        ),
        name="norm_kv",
    )(tokens, gain.reshape(1, width), w_keyval, segments.reshape(1, rows))


def turn():
    return lax.rem(lax.div(lax.axis_index("seq"), 2), 2)


def query_kernel(x_ref, w_ref, out_ref, turn_ref):
    out_ref[...] = jnp.dot(x_ref[...], w_ref[...], preferred_element_type=jnp.float32).astype(jnp.bfloat16)
    turn_ref[...] = jnp.full(turn_ref.shape, turn(), jnp.int32)


def project_query(normed, w_query):
    rows, width = normed.shape
    cols = w_query.shape[1]
    tile = rows // 2
    return pl.pallas_call(
        query_kernel,
        grid=(rows // tile,),
        in_specs=[pl.BlockSpec((tile, width), lambda i: (i, 0)), pl.BlockSpec((width, cols), lambda i: (0, 0))],
        out_specs=[pl.BlockSpec((tile, cols), lambda i: (i, 0)), pl.BlockSpec((8, LANES), lambda i: (0, 0))],
        out_shape=[jax.ShapeDtypeStruct((rows, cols), jnp.bfloat16), jax.ShapeDtypeStruct((8, LANES), jnp.int32)],
        compiler_params=pltpu.CompilerParams(vmem_limit_bytes=20 * MIB),
        cost_estimate=pl.CostEstimate(
            flops=2 * rows * width * cols, bytes_accessed=2 * rows * width + 2 * width * cols, transcendentals=0
        ),
        name="project_query",
    )(normed, w_query)


def attend_kernel(plan, first, last, *refs):
    blocks = len(plan)
    q_ref, seg_ref = refs[:2]
    mine, other = refs[2:2 + blocks], refs[2 + blocks:2 + 2 * blocks]
    refs = refs[2 + 2 * blocks:]
    state_ref = None
    if not first:
        state_ref, refs = refs[0], refs[1:]
    out_ref, refs = refs[0], refs[1:]
    if not last:
        turn_ref, refs = refs[0], refs[1:]
        turn_ref[...] = jnp.full(turn_ref.shape, turn(), jnp.int32)
    keys, values, segs, scores, sems = refs
    rows = q_ref.shape[0]
    tile = rows // 2
    part = lax.axis_index("tp")
    place = lax.axis_index("seq")
    odd = lax.rem(place, 2)

    for slot in range(blocks):
        for value in range(2):
            key_src, val_src = (mine[slot], other[slot]) if value == 0 else (other[slot], mine[slot])

            @pl.when(part == value)
            def _():
                pltpu.make_async_copy(key_src.at[pl.ds(0, rows)], keys.at[slot], sems.at[0, slot]).start()
                pltpu.make_async_copy(val_src.at[pl.ds(0, rows)], values.at[slot], sems.at[1, slot]).start()

        pltpu.make_async_copy(mine[slot].at[pl.ds(rows, SEG_ROWS)], segs.at[slot], sems.at[2, slot]).start()

    own_seg = jnp.transpose(jnp.broadcast_to(seg_ref[...].astype(jnp.float32), (8, rows)))[:, 0:1]
    for slot in range(blocks):
        pltpu.make_async_copy(mine[slot].at[pl.ds(0, rows)], keys.at[slot], sems.at[0, slot]).wait()
        pltpu.make_async_copy(mine[slot].at[pl.ds(0, rows)], values.at[slot], sems.at[1, slot]).wait()
        pltpu.make_async_copy(mine[slot].at[pl.ds(rows, SEG_ROWS)], segs.at[slot], sems.at[2, slot]).wait()
    key_segs = []
    for slot, kind in enumerate(plan):
        packed = segs[slot].astype(jnp.float32)
        key_seg = jnp.concatenate([packed[0:1, :], packed[8:9, :]], axis=1)
        if kind != "own":
            back = jnp.where(odd == 1, kind[1], kind[0])
            key_seg = jnp.where((back > 0) & (place >= back), key_seg, -1.0)
        key_segs.append(key_seg)

    for start in range(0, rows, tile):
        span = slice(start, start + tile)
        query = q_ref[span, :]
        best = None if first else state_ref[span, HD:HD + LANES]
        bounds = []
        for slot, kind in enumerate(plan):
            low, high = 0, rows
            if kind == "own":
                high = start + tile
            elif kind[2]:
                low = start
            bounds.append((low, high))
            raw = lax.dot_general(query, keys[slot, low:high, :], NT, preferred_element_type=jnp.float32)
            allowed = key_segs[slot][:, low:high] == own_seg[span, :]
            if kind == "own":
                row_pos = start + lax.broadcasted_iota(jnp.int32, raw.shape, 0)
                allowed = allowed & (lax.broadcasted_iota(jnp.int32, raw.shape, 1) <= row_pos)
            masked = jnp.where(allowed, raw, NEG)
            scores[slot, :, low:high] = masked
            for at in range(0, high - low, LANES):
                piece = masked[:, at:at + LANES]
                best = piece if best is None else jnp.maximum(best, piece)
        top = jnp.broadcast_to(jnp.max(best, axis=1, keepdims=True), (tile, LANES))
        if first:
            total = jnp.zeros((tile, LANES), jnp.float32)
            weighted = jnp.zeros((tile, HD), jnp.float32)
        else:
            shrink = jnp.exp2((state_ref[span, HD:HD + LANES] - top) * FACTOR)
            total = state_ref[span, HD + LANES:] * shrink
            weighted = state_ref[span, :HD] * jnp.concatenate([shrink, shrink], axis=1)
        for slot in range(blocks):
            low, high = bounds[slot]
            pieces = []
            for at in range(low, high, LANES):
                weights = jnp.exp2((scores[slot, :, at:at + LANES] - top) * FACTOR)
                total = total + weights
                pieces.append(weights.astype(jnp.bfloat16))
            probs = jnp.concatenate(pieces, axis=1)
            weighted = weighted + jnp.dot(probs, values[slot, low:high, :], preferred_element_type=jnp.float32)
        if last:
            out_ref[span, :] = (weighted / jnp.sum(total, axis=1, keepdims=True)).astype(jnp.bfloat16)
        else:
            out_ref[span, :HD] = weighted
            out_ref[span, HD:HD + LANES] = top
            out_ref[span, HD + LANES:] = total


def attend(query, segments, plan, mine, other, state, last):
    rows = query.shape[0]
    blocks = len(plan)
    vmem = pl.BlockSpec(memory_space=pltpu.VMEM)
    first = state is None
    operands = [query, segments.reshape(1, rows), *mine, *other] + ([] if first else [state])
    if last:
        out_shape = jax.ShapeDtypeStruct((rows, HD), jnp.bfloat16)
        out_specs = vmem
    else:
        out_shape = [
            jax.ShapeDtypeStruct((rows, HD + 2 * LANES), jnp.float32),
            jax.ShapeDtypeStruct((8, LANES), jnp.int32),
        ]
        out_specs = [vmem, vmem]
    return pl.pallas_call(
        functools.partial(attend_kernel, plan, first, last),
        in_specs=[vmem] * 2 + [pl.BlockSpec(memory_space=pl.ANY)] * (2 * blocks) + ([] if first else [vmem]),
        out_specs=out_specs,
        out_shape=out_shape,
        scratch_shapes=[
            pltpu.VMEM((blocks, rows, HD), jnp.bfloat16),
            pltpu.VMEM((blocks, rows, HD), jnp.bfloat16),
            pltpu.VMEM((blocks, SEG_ROWS, HD), jnp.bfloat16),
            pltpu.VMEM((blocks, rows // 2, rows), jnp.float32),
            pltpu.SemaphoreType.DMA((3, blocks)),
        ],
        compiler_params=pltpu.CompilerParams(vmem_limit_bytes=(12 + 2 * blocks) * MIB),
        cost_estimate=pl.CostEstimate(
            flops=4 * rows * rows * blocks * HD, bytes_accessed=4 * rows * blocks * HD, transcendentals=rows * rows * blocks
        ),
        name="attend_last" if last else "attend_first" if first else "attend_more",
    )(*operands)


def output_kernel(a_ref, b_ref, wa_ref, wb_ref, x_ref, sum_ref, out_exp_ref, out_ref):
    rows, width = x_ref.shape
    groups = sum_ref.shape[0]

    def bounds(ref):
        power = jnp.left_shift(jnp.int32(1), ref[...] - MIN_EXP).astype(jnp.float32)
        return jnp.transpose(power * (LIMIT * 2.0 ** MIN_EXP))

    def clip(value, bound):
        return jnp.minimum(jnp.maximum(value.astype(jnp.bfloat16), -bound), bound)

    sum_bound, out_bound = bounds(sum_ref), bounds(out_exp_ref)
    per = width // groups
    chunk = 2 * per
    a, b = a_ref[...], b_ref[...]
    for start in range(0, width, chunk):
        term_a = jnp.dot(a, wa_ref[:, start:start + chunk], preferred_element_type=jnp.float32)
        term_b = jnp.dot(b, wb_ref[:, start:start + chunk], preferred_element_type=jnp.float32)
        for part in range(2):
            cols = slice(part * per, (part + 1) * per)
            group = (start + part * per) // per
            span = slice(start + part * per, start + (part + 1) * per)
            bound = jnp.broadcast_to(sum_bound[:, group:group + 1], (rows, per)).astype(jnp.bfloat16)
            last = jnp.broadcast_to(out_bound[:, group:group + 1], (rows, per)).astype(jnp.bfloat16)
            quant_a = clip(term_a[:, cols], bound).astype(jnp.float32)
            quant_b = clip(term_b[:, cols], bound).astype(jnp.float32)
            combined = x_ref[:, span].astype(jnp.float32) + (quant_a + quant_b)
            out_ref[:, span] = clip(combined, last)


def project_out(att_a, att_b, w_a, w_b, tokens, sum_exps, out_exps):
    rows, width = tokens.shape
    depth = att_a.shape[1]
    groups = sum_exps.shape[1]
    steps = groups // 8
    tile = width // steps
    whole = pl.BlockSpec((rows, depth), lambda i: (0, 0))
    weight = pl.BlockSpec((depth, tile), lambda i: (0, i))
    wide = pl.BlockSpec((rows, tile), lambda i: (0, i))
    exps = pl.BlockSpec((groups // steps, rows), lambda i: (i, 0))
    return pl.pallas_call(
        output_kernel,
        grid=(steps,),
        in_specs=[whole, whole, weight, weight, wide, exps, exps],
        out_specs=wide,
        out_shape=jax.ShapeDtypeStruct((rows, width), jnp.bfloat16),
        compiler_params=pltpu.CompilerParams(vmem_limit_bytes=20 * MIB),
        cost_estimate=pl.CostEstimate(
            flops=4 * rows * width * depth, bytes_accessed=4 * rows * width + 4 * width * depth, transcendentals=0
        ),
        name="project_out",
    )(att_a, att_b, w_a, w_b, tokens, sum_exps.T, out_exps.T)


def on_device(seq_size, tokens, gain, segments, w_query, w_keyval, w_out, sum_exps, out_exps):
    window = seq_size // 2

    def swap_cores(x):
        return lax.ppermute(x, "tp", [(0, 1), (1, 0)])

    def swap_pair(x):
        return lax.ppermute(x, "seq", [(i, i ^ 1) for i in range(seq_size)])

    def exchange(x, colour):
        low = [i for i in range(seq_size - 2) if (i // 2) % 2 == colour]
        return lax.ppermute(x, "seq", [(i, i + 2) for i in low] + [(i + 2, i) for i in low])

    def pick(flag, if_odd, if_even):
        return jnp.where(flag[:1, :1] == 1, if_odd, if_even)

    w_other = swap_cores(w_out)
    message, normed = norm_kv(tokens, gain, w_keyval, segments, 256)
    at_odd, at_even = exchange(message, 0), exchange(message, 1)
    pair = swap_pair(message)
    query, flag = project_query(normed, w_query)
    state = None
    mine, plan = [message, pair], ["own", (0, 1, False)]
    for k in range(1, window // 2 + 1):
        held = pick(flag, at_odd, at_even)
        mine.append(held)
        plan.append((2 * k, 2 * k, 2 * k == window))
        if k < window // 2:
            at_odd, at_even = exchange(at_even, 0), exchange(at_odd, 1)
        beside = swap_pair(held)
        if k == 1 or k == window // 2:
            state, flag = attend(query, segments, plan, mine, [swap_cores(m) for m in mine], state, False)
            mine, plan = [], []
        mine.append(beside)
        plan.append((2 * k - 1, 2 * k + 1 if k < window // 2 else 0, False))
    attended = attend(query, segments, plan, mine, [swap_cores(m) for m in mine], state, True)
    return project_out(attended, swap_cores(attended), w_out, w_other, tokens, sum_exps, out_exps)


def solution(mesh):
    in_specs = (
        P(("groups", "seq"), None),
        P(),
        P(("groups", "seq")),
        P(None, "tp"),
        P(None, "tp"),
        P("tp", None),
        P(("groups", "seq"), None),
        P(("groups", "seq"), None),
    )
    out_specs = P(("groups", "seq"), None)
    return jax.shard_map(
        functools.partial(on_device, mesh.shape["seq"]),
        mesh=mesh, in_specs=in_specs, out_specs=out_specs, check_vma=False,
    )
```

time: 66 us -> 54.4 us (0.82)
  Pallas kernels: 29.9 us -> 17.6 us
  local copies, waits for them, and re-layouts: 2.96 us -> 6.23 us
  starting transfers between devices: 19.7 us -> 17.2 us
  waiting for transfers between devices: 12.8 us -> 11.5 us
  between operations: 0.17 us -> 1.45 us
    pallas_call x1, Pallas kernels: 10.7 us -> 7.05 us  [project_out(): pl.pallas_call(output_kernel, grid=(steps,), in_specs=[whole, whole, weig...]
    pallas_call x1, Pallas kernels: 7.78 us -> 4.46 us  [norm_kv(): pl.pallas_call(norm_kv_kernel, grid=(rows // tile,), in_specs=[pl.BlockSp...]
    pallas_call x1, Pallas kernels: 4.3 us -> 1.43 us  [project_query(): pl.pallas_call(query_kernel, grid=(rows // tile,), in_specs=[pl.BlockSpec...]
    ppermute x13 -> x15, starting transfers between devices: 19.7 us -> 17.2 us  [the longest x8 6.69 us: swap_cores(): return lax.ppermute(x, 'tp', [(0, 1), (1, 0)])]
    pallas_call x1 -> x3, Pallas kernels: 7.13 us -> 4.69 us  [attend(): pl.pallas_call(functools.partial(attend_kernel, plan, first, last), in_sp...]
    unnamed x26 -> x18, local copies, waits for them, and re-layouts: 2.96 us -> 5.2 us
    ppermute x13 -> x15, waiting for transfers between devices: 12.8 us -> 11.5 us  [the longest x4 5.15 us: exchange(): lax.ppermute(x, 'seq', [(i, i + 2) for i in low] + [(i + 2, i) for i in l...]
    slice x0 -> x2, local copies, waits for them, and re-layouts: none -> 1.03 us  [pick(): return jnp.where(flag[:1, :1] == 1, if_odd, if_even)]
  transfers between devices with their start and end apart: 13 -> 15, of which waited for: 5 -> 5; matrix products, arithmetic and copies ran while one was open for 0% -> 2% of each run, Pallas kernels for 29% -> 20%
where the time goes in v2:
time: 54.4 us; the launch traced here: 54.1 us
  Pallas kernels  17.6 us (32%)
  starting transfers between devices  17.2 us (32%)
  waiting for transfers between devices  11.5 us (21%)
  local copies, waits for them, and re-layouts  6.23 us (11%)
  between operations  1.45 us (3%)
    pallas_call x1, Pallas kernels, project_out(): pl.pallas_call(output_kernel, grid=(steps,), in_specs=[whole, whole, weig...  7.05 us
    ppermute x8, starting transfers between devices, swap_cores(): return lax.ppermute(x, 'tp', [(0, 1), (1, 0)])  6.69 us
    ppermute x4, starting transfers between devices, exchange(): lax.ppermute(x, 'seq', [(i, i + 2) for i in low] + [(i + 2, i) for i in l...  6.56 us
    unnamed x18, local copies, waits for them, and re-layouts  5.2 us
    ppermute x4, waiting for transfers between devices, exchange(): lax.ppermute(x, 'seq', [(i, i + 2) for i in low] + [(i + 2, i) for i in l...  5.15 us
    ppermute x3, waiting for transfers between devices, swap_pair(): return lax.ppermute(x, 'seq', [(i, i ^ 1) for i in range(seq_size)])  4.91 us
    pallas_call x3, Pallas kernels, attend(): pl.pallas_call(functools.partial(attend_kernel, plan, first, last), in_sp...  4.69 us
    pallas_call x1, Pallas kernels, norm_kv(): pl.pallas_call(norm_kv_kernel, grid=(rows // tile,), in_specs=[pl.BlockSp...  4.46 us
  transfers between devices with their start and end apart: 15, of which 5 were waited for; matrix products, arithmetic and copies ran while one was open for 2% of the time, Pallas kernels for 20%

profile of v2, /device:TPU:11, one launch (start us, length us, event | category | flops | bytes accessed | tf_op | source)
XLA Modules:
  0.0 54.1 jit_solution(5585177415710857102)
XLA Ops:
  0.7 2.2 %copy-done = bf16[512,4096]{1,0:T(8,128)(2,1)S(1)} copy-done((bf16[512,4096]{1,0:T(8,128)(2,1)S(1)}, bf16[512,4096]{1,0:T(8,128)(2,1)}, u32[]{:S(2)}) %copy-start) | copy-done | bytes 4194328
  2.9 1.6 %copy-done.4 = bf16[4096,256]{1,0:T(8,128)(2,1)S(1)} copy-done((bf16[4096,256]{1,0:T(8,128)(2,1)S(1)}, bf16[4096,256]{1,0:T(8,128)(2,1)}, u32[]{:S(2)}) %copy-start.4) | copy-done | bytes 2097176
  5.1 0.7 %copy-done.8 = f32[4096]{0:T(1024)S(1)} copy-done((f32[4096]{0:T(1024)S(1)}, f32[4096]{0:T(1024)}, u32[]{:S(2)}) %copy-start.8) | copy-done | bytes 16408
  5.9 4.5 %norm_kv.1 = (bf16[528,256]{1,0:T(8,128)(2,1)S(1)}, bf16[512,4096]{1,0:T(8,128)(2,1)S(1)}) custom-call(bf16[512,4096]{1,0:T(8,128)(2,1)S(1)} %copy-done, f32[1,4096]{1,0:T(1,128)S(1)} %bitcast.12, bf16[4096,256]{1,0:T(8,128)(2,1)S(1)} %copy-done.4, s32[1,512]{1,0:T(1,128)S(1)} %bitcast.8), custom_call_target="tpu_custom_call" | custom-call | flops 1073741824 | bytes 10485760 | tf_op jit(solution)/shard_map/norm_kv/pallas_call | solution.py:60
  10.6 4.3 %collective-permute-start.2 = (bf16[528,256]{1,0:T(8,128)(2,1)S(1)}, bf16[528,256]{1,0:T(8,128)(2,1)S(1)}, u32[]{:S(2)}, u32[]{:S(2)}) collective-permute-start(bf16[528,256]{1,0:T(8,128)(2,1)S(1)} %get-tuple-element.14.refs_2_), channel_id=1, source_target_pairs={{4,8},{6,10},{8,4},{10,6},{5,9},{7,11},{9,5},{11,7},{20,24},{22,26... | collective-permute-start | bytes 811016 | tf_op jit(solution)/shard_map/ppermute | solution.py:303
  14.9 1.3 %collective-permute-start = (bf16[528,256]{1,0:T(8,128)(2,1)S(1)}, bf16[528,256]{1,0:T(8,128)(2,1)S(1)}, u32[]{:S(2)}, u32[]{:S(2)}) collective-permute-start(bf16[528,256]{1,0:T(8,128)(2,1)S(1)} %get-tuple-element.14.refs_2_), channel_id=1, source_target_pairs={{0,2},{2,0},{4,6},{6,4},{8,10},{10,8},{12,14},{14,12},{1,3},{3,1},... | collective-permute-start | bytes 811016 | tf_op jit(solution)/shard_map/ppermute | solution.py:299
  16.2 0.8 %collective-permute-start.3 = (bf16[528,256]{1,0:T(8,128)(2,1)S(1)}, bf16[528,256]{1,0:T(8,128)(2,1)S(1)}, u32[]{:S(2)}, u32[]{:S(2)}) collective-permute-start(bf16[528,256]{1,0:T(8,128)(2,1)S(1)} %get-tuple-element.14.refs_2_), channel_id=1, source_target_pairs={{0,1},{1,0},{2,3},{3,2},{4,5},{5,4},{6,7},{7,6},{8,9},{9,8},{10,11... | collective-permute-start | bytes 811016 | tf_op jit(solution)/shard_map/ppermute | solution.py:296
  17.0 1.4 %project_query.1 = (bf16[512,256]{1,0:T(8,128)(2,1)S(1)}, s32[8,128]{1,0:T(8,128)S(1)}) custom-call(bf16[512,4096]{1,0:T(8,128)(2,1)S(1)} %get-tuple-element.12.x_ref, bf16[4096,256]{1,0:T(8,128)(2,1)S(1)} %copy-done.2), custom_call_target="tpu_custom_call" | custom-call | flops 1073741824 | bytes 6291456 | tf_op jit(solution)/shard_map/project_query/pallas_call | solution.py:98
  19.7 1.9 %collective-permute-done.2 = bf16[528,256]{1,0:T(8,128)(2,1)S(1)} collective-permute-done((bf16[528,256]{1,0:T(8,128)(2,1)S(1)}, bf16[528,256]{1,0:T(8,128)(2,1)S(1)}, u32[]{:S(2)}, u32[]{:S(2)}) %collective-permute-start.2) | collective-permute-done | bytes 270368 | tf_op jit(solution)/shard_map/ppermute | solution.py:303
  21.6 0.8 %collective-permute-start.5 = (bf16[528,256]{1,0:T(8,128)(2,1)S(1)}, bf16[528,256]{1,0:T(8,128)(2,1)S(1)}, u32[]{:S(2)}, u32[]{:S(2)}) collective-permute-start(bf16[528,256]{1,0:T(8,128)(2,1)S(1)} %broadcast_select_fusion.1.refs_4_), channel_id=1, source_target_pairs={{0,1},{1,0},{2,3},{3,2},{4,5},{5,4},{6,7},{7,6},{8,9},{9,8},{10,11... | collective-permute-start | bytes 811016 | tf_op jit(solution)/shard_map/ppermute | solution.py:296
  22.4 1.4 %collective-permute-start.4 = (bf16[528,256]{1,0:T(8,128)(2,1)S(1)}, bf16[528,256]{1,0:T(8,128)(2,1)S(1)}, u32[]{:S(2)}, u32[]{:S(2)}) collective-permute-start(bf16[528,256]{1,0:T(8,128)(2,1)S(1)} %collective-permute-done.refs_3_), channel_id=1, source_target_pairs={{0,1},{1,0},{2,3},{3,2},{4,5},{5,4},{6,7},{7,6},{8,9},{9,8},{10,11... | collective-permute-start | bytes 811016 | tf_op jit(solution)/shard_map/ppermute | solution.py:296
  23.9 2.0 %collective-permute-start.7 = (bf16[528,256]{1,0:T(8,128)(2,1)S(1)}, bf16[528,256]{1,0:T(8,128)(2,1)S(1)}, u32[]{:S(2)}, u32[]{:S(2)}) collective-permute-start(bf16[528,256]{1,0:T(8,128)(2,1)S(1)} %collective-permute-done.1), channel_id=1, source_target_pairs={{4,8},{6,10},{8,4},{10,6},{5,9},{7,11},{9,5},{11,7},{20,24},{22,26... | collective-permute-start | bytes 811016 | tf_op jit(solution)/shard_map/ppermute | solution.py:303
  25.9 1.3 %collective-permute-start.10 = (bf16[528,256]{1,0:T(8,128)(2,1)S(1)}, bf16[528,256]{1,0:T(8,128)(2,1)S(1)}, u32[]{:S(2)}, u32[]{:S(2)}) collective-permute-start(bf16[528,256]{1,0:T(8,128)(2,1)S(1)} %broadcast_select_fusion.1.refs_4_), channel_id=1, source_target_pairs={{0,2},{2,0},{4,6},{6,4},{8,10},{10,8},{12,14},{14,12},{1,3},{3,1},... | collective-permute-start | bytes 811016 | tf_op jit(solution)/shard_map/ppermute | solution.py:299
  27.2 2.2 %attend_first.1 = (f32[512,512]{1,0:T(8,128)S(1)}, s32[8,128]{1,0:T(8,128)S(1)}) custom-call(bf16[512,256]{1,0:T(8,128)(2,1)S(1)} %get-tuple-element.13.refs_0_, s32[1,512]{1,0:T(1,128)S(1)} %bitcast.9, bf16[528,256]{1,0:T(8,128)(2,1)S(1)} %get-tuple-element.14.refs_2_, bf16[528,256]{1,0:T(8,128)(2,1)S(1)} %collective-permute-done.refs_3_, ...), custom_call_target="tpu_custom_call" | custom-call | flops 805306368 | bytes 1572864 | tf_op jit(solution)/shard_map/attend_first/pallas_call | solution.py:218
  30.6 1.4 %collective-permute-done.6 = bf16[528,256]{1,0:T(8,128)(2,1)S(1)} collective-permute-done((bf16[528,256]{1,0:T(8,128)(2,1)S(1)}, bf16[528,256]{1,0:T(8,128)(2,1)S(1)}, u32[]{:S(2)}, u32[]{:S(2)}) %collective-permute-start.6) | collective-permute-done | bytes 270368 | tf_op jit(solution)/shard_map/ppermute | solution.py:303
  32.0 1.9 %collective-permute-done.7 = bf16[528,256]{1,0:T(8,128)(2,1)S(1)} collective-permute-done((bf16[528,256]{1,0:T(8,128)(2,1)S(1)}, bf16[528,256]{1,0:T(8,128)(2,1)S(1)}, u32[]{:S(2)}, u32[]{:S(2)}) %collective-permute-start.7) | collective-permute-done | bytes 270368 | tf_op jit(solution)/shard_map/ppermute | solution.py:303
  33.9 1.3 %collective-permute-start.8 = (bf16[528,256]{1,0:T(8,128)(2,1)S(1)}, bf16[528,256]{1,0:T(8,128)(2,1)S(1)}, u32[]{:S(2)}, u32[]{:S(2)}) collective-permute-start(bf16[528,256]{1,0:T(8,128)(2,1)S(1)} %broadcast_select_fusion.refs_3_), channel_id=1, source_target_pairs={{0,2},{2,0},{4,6},{6,4},{8,10},{10,8},{12,14},{14,12},{1,3},{3,1},... | collective-permute-start | bytes 811016 | tf_op jit(solution)/shard_map/ppermute | solution.py:299
  35.2 1.1 %collective-permute-start.12 = (bf16[528,256]{1,0:T(8,128)(2,1)S(1)}, bf16[528,256]{1,0:T(8,128)(2,1)S(1)}, u32[]{:S(2)}, u32[]{:S(2)}) collective-permute-start(bf16[528,256]{1,0:T(8,128)(2,1)S(1)} %broadcast_select_fusion.refs_3_), channel_id=1, source_target_pairs={{0,1},{1,0},{2,3},{3,2},{4,5},{5,4},{6,7},{7,6},{8,9},{9,8},{10,11... | collective-permute-start | bytes 811016 | tf_op jit(solution)/shard_map/ppermute | solution.py:296
  36.3 4.9 %collective-permute-done.8.refs_2_ = bf16[528,256]{1,0:T(8,128)(2,1)S(1)} collective-permute-done((bf16[528,256]{1,0:T(8,128)(2,1)S(1)}, bf16[528,256]{1,0:T(8,128)(2,1)S(1)}, u32[]{:S(2)}, u32[]{:S(2)}) %collective-permute-start.8) | collective-permute-done | bytes 270368 | tf_op jit(solution)/shard_map/ppermute | solution.py:299
  41.2 1.7 %collective-permute-start.9 = (bf16[528,256]{1,0:T(8,128)(2,1)S(1)}, bf16[528,256]{1,0:T(8,128)(2,1)S(1)}, u32[]{:S(2)}, u32[]{:S(2)}) collective-permute-start(bf16[528,256]{1,0:T(8,128)(2,1)S(1)} %collective-permute-done.8.refs_2_), channel_id=1, source_target_pairs={{0,1},{1,0},{2,3},{3,2},{4,5},{5,4},{6,7},{7,6},{8,9},{9,8},{10,11... | collective-permute-start | bytes 811016 | tf_op jit(solution)/shard_map/ppermute | solution.py:296
  42.9 1.4 %attend_more.1 = (f32[512,512]{1,0:T(8,128)S(1)}, s32[8,128]{1,0:T(8,128)}) custom-call(bf16[512,256]{1,0:T(8,128)(2,1)S(1)} %get-tuple-element.13.refs_0_, s32[1,512]{1,0:T(1,128)S(1)} %bitcast.10, bf16[528,256]{1,0:T(8,128)(2,1)S(1)} %collective-permute-done.10.refs_2_, bf16[528,256]{1,0:T(8,128)(2,1)S(1)} %broadcast_select_fusion.refs_3_, ...), custom_call_target="tpu_custom_call" | custom-call | flops 536870912 | bytes 1048576 | tf_op jit(solution)/shard_map/attend_more/pallas_call | solution.py:218
  44.3 1.1 %attend_last.1.a_ref = bf16[512,256]{1,0:T(8,128)(2,1)S(1)} custom-call(bf16[512,256]{1,0:T(8,128)(2,1)S(1)} %get-tuple-element.13.refs_0_, s32[1,512]{1,0:T(1,128)S(1)} %bitcast.11, bf16[528,256]{1,0:T(8,128)(2,1)S(1)} %collective-permute-done.8.refs_2_, bf16[528,256]{1,0:T(8,128)(2,1)S(1)} %collective-permute-done.9.refs_3_, ...), custom_call_target="tpu_custom_call" | custom-call | flops 268435456 | bytes 524288 | tf_op jit(solution)/shard_map/attend_last/pallas_call | solution.py:218
  45.5 1.5 %collective-permute-done.13.b_ref = bf16[512,256]{1,0:T(8,128)(2,1)S(1)} collective-permute-done((bf16[512,256]{1,0:T(8,128)(2,1)S(1)}, bf16[512,256]{1,0:T(8,128)(2,1)S(1)}, u32[]{:S(2)}, u32[]{:S(2)}) %collective-permute-start.13) | collective-permute-done | bytes 262176 | tf_op jit(solution)/shard_map/ppermute | solution.py:296
  47.0 7.1 %project_out.1 = bf16[512,4096]{1,0:T(8,128)(2,1)} custom-call(bf16[512,256]{1,0:T(8,128)(2,1)S(1)} %attend_last.1.a_ref, bf16[512,256]{1,0:T(8,128)(2,1)S(1)} %collective-permute-done.13.b_ref, bf16[256,4096]{1,0:T(8,128)(2,1)S(1)} %copy-done.3, bf16[256,4096]{1,0:T(8,128)(2,1)S(1)} %collective-permute-done.14.wb_ref, bf16[512,4096]{1,0:T(8,128)(2,1)S(1)} %copy-done.1, ...), custom_call_target="tpu_custom_call" | custom-call | flops 2147483648 | bytes 12582912 | tf_op jit(solution)/shard_map/project_out/pallas_call | solution.py:278
  (34 shorter events, 2.9 us)
Async XLA Ops:
  0.0 47.0 %collective-permute-start.14 = (bf16[256,4096]{1,0:T(8,128)(2,1)}, bf16[256,4096]{1,0:T(8,128)(2,1)S(1)}, u32[]{:S(2)}, u32[]{:S(2)}) collective-permute-start(bf16[256,4096]{1,0:T(8,128)(2,1)} %wa_ref.1), channel_id=1, source_target_pairs={{0,1},{1,0},{2,3},{3,2},{4,5},{5,4},{6,7},{7,6},{8,9},{9,8},{10,11... | collective-permute-start | bytes 6291464 | tf_op jit(solution)/shard_map/ppermute | solution.py:296
  0.7 2.2 %copy-start = (bf16[512,4096]{1,0:T(8,128)(2,1)S(1)}, bf16[512,4096]{1,0:T(8,128)(2,1)}, u32[]{:S(2)}) copy-start(bf16[512,4096]{1,0:T(8,128)(2,1)} %x_ref.3) | copy-start | bytes 12582916
  2.9 1.6 %copy-start.4 = (bf16[4096,256]{1,0:T(8,128)(2,1)S(1)}, bf16[4096,256]{1,0:T(8,128)(2,1)}, u32[]{:S(2)}) copy-start(bf16[4096,256]{1,0:T(8,128)(2,1)} %w_ref.2) | copy-start | bytes 6291460
  4.5 0.7 %copy-start.7 = (s32[512]{0:T(512)S(1)}, s32[512]{0:T(512)}, u32[]{:S(2)}) copy-start(s32[512]{0:T(512)} %param.10) | copy-start | bytes 6148
  5.1 0.7 %copy-start.8 = (f32[4096]{0:T(1024)S(1)}, f32[4096]{0:T(1024)}, u32[]{:S(2)}) copy-start(f32[4096]{0:T(1024)} %param.9) | copy-start | bytes 49156
  5.9 11.2 %copy-start.2 = (bf16[4096,256]{1,0:T(8,128)(2,1)S(1)}, bf16[4096,256]{1,0:T(8,128)(2,1)}, u32[]{:S(2)}) copy-start(bf16[4096,256]{1,0:T(8,128)(2,1)} %w_ref.3) | copy-start | bytes 6291460
  10.3 9.3 %collective-permute-start.1 = (bf16[528,256]{1,0:T(8,128)(2,1)S(1)}, bf16[528,256]{1,0:T(8,128)(2,1)S(1)}, u32[]{:S(2)}, u32[]{:S(2)}) collective-permute-start(bf16[528,256]{1,0:T(8,128)(2,1)S(1)} %get-tuple-element.14.refs_2_), channel_id=1, source_target_pairs={{0,4},{2,6},{8,12},{10,14},{4,0},{6,2},{12,8},{14,10},{1,5},{3,7},... | collective-permute-start | bytes 811016 | tf_op jit(solution)/shard_map/ppermute | solution.py:303
  10.6 11.0 %collective-permute-start.2 = (bf16[528,256]{1,0:T(8,128)(2,1)S(1)}, bf16[528,256]{1,0:T(8,128)(2,1)S(1)}, u32[]{:S(2)}, u32[]{:S(2)}) collective-permute-start(bf16[528,256]{1,0:T(8,128)(2,1)S(1)} %get-tuple-element.14.refs_2_), channel_id=1, source_target_pairs={{4,8},{6,10},{8,4},{10,6},{5,9},{7,11},{9,5},{11,7},{20,24},{22,26... | collective-permute-start | bytes 811016 | tf_op jit(solution)/shard_map/ppermute | solution.py:303
  14.9 7.5 %collective-permute-start = (bf16[528,256]{1,0:T(8,128)(2,1)S(1)}, bf16[528,256]{1,0:T(8,128)(2,1)S(1)}, u32[]{:S(2)}, u32[]{:S(2)}) collective-permute-start(bf16[528,256]{1,0:T(8,128)(2,1)S(1)} %get-tuple-element.14.refs_2_), channel_id=1, source_target_pairs={{0,2},{2,0},{4,6},{6,4},{8,10},{10,8},{12,14},{14,12},{1,3},{3,1},... | collective-permute-start | bytes 811016 | tf_op jit(solution)/shard_map/ppermute | solution.py:299
  16.2 7.7 %collective-permute-start.3 = (bf16[528,256]{1,0:T(8,128)(2,1)S(1)}, bf16[528,256]{1,0:T(8,128)(2,1)S(1)}, u32[]{:S(2)}, u32[]{:S(2)}) collective-permute-start(bf16[528,256]{1,0:T(8,128)(2,1)S(1)} %get-tuple-element.14.refs_2_), channel_id=1, source_target_pairs={{0,1},{1,0},{2,3},{3,2},{4,5},{5,4},{6,7},{7,6},{8,9},{9,8},{10,11... | collective-permute-start | bytes 811016 | tf_op jit(solution)/shard_map/ppermute | solution.py:296
  21.6 4.3 %collective-permute-start.5 = (bf16[528,256]{1,0:T(8,128)(2,1)S(1)}, bf16[528,256]{1,0:T(8,128)(2,1)S(1)}, u32[]{:S(2)}, u32[]{:S(2)}) collective-permute-start(bf16[528,256]{1,0:T(8,128)(2,1)S(1)} %broadcast_select_fusion.1.refs_4_), channel_id=1, source_target_pairs={{0,1},{1,0},{2,3},{3,2},{4,5},{5,4},{6,7},{7,6},{8,9},{9,8},{10,11... | collective-permute-start | bytes 811016 | tf_op jit(solution)/shard_map/ppermute | solution.py:296
  22.4 4.8 %collective-permute-start.4 = (bf16[528,256]{1,0:T(8,128)(2,1)S(1)}, bf16[528,256]{1,0:T(8,128)(2,1)S(1)}, u32[]{:S(2)}, u32[]{:S(2)}) collective-permute-start(bf16[528,256]{1,0:T(8,128)(2,1)S(1)} %collective-permute-done.refs_3_), channel_id=1, source_target_pairs={{0,1},{1,0},{2,3},{3,2},{4,5},{5,4},{6,7},{7,6},{8,9},{9,8},{10,11... | collective-permute-start | bytes 811016 | tf_op jit(solution)/shard_map/ppermute | solution.py:296
  23.9 8.1 %collective-permute-start.6 = (bf16[528,256]{1,0:T(8,128)(2,1)S(1)}, bf16[528,256]{1,0:T(8,128)(2,1)S(1)}, u32[]{:S(2)}, u32[]{:S(2)}) collective-permute-start(bf16[528,256]{1,0:T(8,128)(2,1)S(1)} %collective-permute-done.2), channel_id=1, source_target_pairs={{0,4},{2,6},{8,12},{10,14},{4,0},{6,2},{12,8},{14,10},{1,5},{3,7},... | collective-permute-start | bytes 811016 | tf_op jit(solution)/shard_map/ppermute | solution.py:303
  23.9 10.0 %collective-permute-start.7 = (bf16[528,256]{1,0:T(8,128)(2,1)S(1)}, bf16[528,256]{1,0:T(8,128)(2,1)S(1)}, u32[]{:S(2)}, u32[]{:S(2)}) collective-permute-start(bf16[528,256]{1,0:T(8,128)(2,1)S(1)} %collective-permute-done.1), channel_id=1, source_target_pairs={{4,8},{6,10},{8,4},{10,6},{5,9},{7,11},{9,5},{11,7},{20,24},{22,26... | collective-permute-start | bytes 811016 | tf_op jit(solution)/shard_map/ppermute | solution.py:303
  25.9 10.4 %collective-permute-start.10 = (bf16[528,256]{1,0:T(8,128)(2,1)S(1)}, bf16[528,256]{1,0:T(8,128)(2,1)S(1)}, u32[]{:S(2)}, u32[]{:S(2)}) collective-permute-start(bf16[528,256]{1,0:T(8,128)(2,1)S(1)} %broadcast_select_fusion.1.refs_4_), channel_id=1, source_target_pairs={{0,2},{2,0},{4,6},{6,4},{8,10},{10,8},{12,14},{14,12},{1,3},{3,1},... | collective-permute-start | bytes 811016 | tf_op jit(solution)/shard_map/ppermute | solution.py:299
  27.2 19.8 %copy-start.3 = (bf16[256,4096]{1,0:T(8,128)(2,1)S(1)}, bf16[256,4096]{1,0:T(8,128)(2,1)}, u32[]{:S(2)}) copy-start(bf16[256,4096]{1,0:T(8,128)(2,1)} %wa_ref.1) | copy-start | bytes 6291460
  33.9 7.3 %collective-permute-start.8 = (bf16[528,256]{1,0:T(8,128)(2,1)S(1)}, bf16[528,256]{1,0:T(8,128)(2,1)S(1)}, u32[]{:S(2)}, u32[]{:S(2)}) collective-permute-start(bf16[528,256]{1,0:T(8,128)(2,1)S(1)} %broadcast_select_fusion.refs_3_), channel_id=1, source_target_pairs={{0,2},{2,0},{4,6},{6,4},{8,10},{10,8},{12,14},{14,12},{1,3},{3,1},... | collective-permute-start | bytes 811016 | tf_op jit(solution)/shard_map/ppermute | solution.py:299
  35.2 7.7 %collective-permute-start.12 = (bf16[528,256]{1,0:T(8,128)(2,1)S(1)}, bf16[528,256]{1,0:T(8,128)(2,1)S(1)}, u32[]{:S(2)}, u32[]{:S(2)}) collective-permute-start(bf16[528,256]{1,0:T(8,128)(2,1)S(1)} %broadcast_select_fusion.refs_3_), channel_id=1, source_target_pairs={{0,1},{1,0},{2,3},{3,2},{4,5},{5,4},{6,7},{7,6},{8,9},{9,8},{10,11... | collective-permute-start | bytes 811016 | tf_op jit(solution)/shard_map/ppermute | solution.py:296
  36.3 6.6 %collective-permute-start.11 = (bf16[528,256]{1,0:T(8,128)(2,1)S(1)}, bf16[528,256]{1,0:T(8,128)(2,1)S(1)}, u32[]{:S(2)}, u32[]{:S(2)}) collective-permute-start(bf16[528,256]{1,0:T(8,128)(2,1)S(1)} %collective-permute-done.10.refs_2_), channel_id=1, source_target_pairs={{0,1},{1,0},{2,3},{3,2},{4,5},{5,4},{6,7},{7,6},{8,9},{9,8},{10,11... | collective-permute-start | bytes 811016 | tf_op jit(solution)/shard_map/ppermute | solution.py:296
  41.2 3.1 %collective-permute-start.9 = (bf16[528,256]{1,0:T(8,128)(2,1)S(1)}, bf16[528,256]{1,0:T(8,128)(2,1)S(1)}, u32[]{:S(2)}, u32[]{:S(2)}) collective-permute-start(bf16[528,256]{1,0:T(8,128)(2,1)S(1)} %collective-permute-done.8.refs_2_), channel_id=1, source_target_pairs={{0,1},{1,0},{2,3},{3,2},{4,5},{5,4},{6,7},{7,6},{8,9},{9,8},{10,11... | collective-permute-start | bytes 811016 | tf_op jit(solution)/shard_map/ppermute | solution.py:296
  42.8 4.2 %copy-start.1 = (bf16[512,4096]{1,0:T(8,128)(2,1)S(1)}, bf16[512,4096]{1,0:T(8,128)(2,1)}, u32[]{:S(2)}) copy-start(bf16[512,4096]{1,0:T(8,128)(2,1)} %x_ref.3) | copy-start | bytes 12582916
  42.9 4.2 %copy-start.5 = (s32[512,32]{0,1:T(8,128)S(1)}, s32[512,32]{0,1:T(8,128)}, u32[]{:S(2)}) copy-start(s32[512,32]{0,1:T(8,128)} %param.14) | copy-start | bytes 196612
  42.9 4.1 %copy-start.6 = (s32[512,32]{0,1:T(8,128)S(1)}, s32[512,32]{0,1:T(8,128)}, u32[]{:S(2)}) copy-start(s32[512,32]{0,1:T(8,128)} %param.15) | copy-start | bytes 196612
  45.4 1.6 %collective-permute-start.13 = (bf16[512,256]{1,0:T(8,128)(2,1)S(1)}, bf16[512,256]{1,0:T(8,128)(2,1)S(1)}, u32[]{:S(2)}, u32[]{:S(2)}) collective-permute-start(bf16[512,256]{1,0:T(8,128)(2,1)S(1)} %attend_last.1.a_ref), channel_id=1, source_target_pairs={{0,1},{1,0},{2,3},{3,2},{4,5},{5,4},{6,7},{7,6},{8,9},{9,8},{10,11... | collective-permute-start | bytes 786440 | tf_op jit(solution)/shard_map/ppermute | solution.py:296

commit v3 on v2

--- a/solution.py
+++ b/solution.py
@@ -18,77 +18,89 @@
 FACTOR = HD ** (-0.5) * 1.4426950408889634
 
 
-def norm_kv_kernel(x_ref, gain_ref, w_ref, seg_ref, msg_ref, normed_ref):
-    step = pl.program_id(0)
-    rows, width = x_ref.shape
-    count = msg_ref.shape[0] - SEG_ROWS
-
-    def wide(start):
-        return x_ref[:, start:start + LANES].astype(jnp.float32)
-
-    total = wide(0)
-    for start in range(LANES, width, LANES):
-        total = total + wide(start)
-    mean = jnp.broadcast_to(jnp.sum(total, axis=1, keepdims=True) * (1.0 / width), (rows, LANES))
-    square = jnp.zeros((rows, LANES), jnp.float32)
-    for start in range(0, width, LANES):
-        center = wide(start) - mean
-        square = square + center * center
-    spread = jnp.sum(square, axis=1, keepdims=True) * (1.0 / width)
-    scale = jnp.broadcast_to(lax.rsqrt(spread + 1e-05), (rows, LANES))
-    kv = jnp.zeros((rows, w_ref.shape[1]), jnp.float32)
-    for start in range(0, width, HD):
-        for at in (start, start + LANES):
-            normed = (wide(at) - mean) * scale * gain_ref[:, at:at + LANES]
-            normed_ref[:, at:at + LANES] = normed.astype(jnp.bfloat16)
-        kv = kv + jnp.dot(
-            normed_ref[:, start:start + HD], w_ref[start:start + HD, :], preferred_element_type=jnp.float32
-        )
-    msg_ref[pl.ds(pl.multiple_of(step * rows, rows), rows), :] = kv.astype(jnp.bfloat16)
-
-    @pl.when(step == 0)
-    def _():
-        seg = seg_ref[...].astype(jnp.float32)
-        low = jnp.broadcast_to(seg[:, :HD], (8, HD))
-        high = jnp.broadcast_to(seg[:, HD:], (8, HD))
-        msg_ref[pl.ds(count, SEG_ROWS), :] = jnp.concatenate([low, high], axis=0).astype(jnp.bfloat16)
-
-
-def norm_kv(tokens, gain, w_keyval, segments, tile):
+def norm_kv_kernel(x_ref, gain_ref, w_ref, seg_ref, msg_ref, normed_ref, xs, ws, sems):
+    rows, width = xs.shape
+    tile, part = rows // 2, rows // 4
+
+    def tokens_copy(i):
+        return pltpu.make_async_copy(x_ref.at[pl.ds(i * part, part)], xs.at[pl.ds(i * part, part)], sems.at[i])
+
+    def weights_copy():
+        return pltpu.make_async_copy(w_ref, ws, sems.at[4])
+
+    tokens_copy(0).start()
+    tokens_copy(1).start()
+    weights_copy().start()
+    tokens_copy(2).start()
+    tokens_copy(3).start()
+    seg = seg_ref[...].astype(jnp.float32)
+    low = jnp.broadcast_to(seg[:, :HD], (8, HD))
+    high = jnp.broadcast_to(seg[:, HD:], (8, HD))
+    msg_ref[rows:, :] = jnp.concatenate([low, high], axis=0).astype(jnp.bfloat16)
+
+    def wide(first, count, start):
+        return xs[first:first + count, start:start + LANES].astype(jnp.float32)
+
+    def stats(first):
+        total = wide(first, part, 0)
+        for start in range(LANES, width, LANES):
+            total = total + wide(first, part, start)
+        mean = jnp.broadcast_to(jnp.sum(total, axis=1, keepdims=True) * (1.0 / width), (part, LANES))
+        square = jnp.zeros((part, LANES), jnp.float32)
+        for start in range(0, width, LANES):
+            center = wide(first, part, start) - mean
+            square = square + center * center
+        spread = jnp.sum(square, axis=1, keepdims=True) * (1.0 / width)
+        return mean, jnp.broadcast_to(lax.rsqrt(spread + 1e-05), (part, LANES))
+
+    for first in range(0, rows, tile):
+        halves = []
+        for at in range(first, first + tile, part):
+            tokens_copy(at // part).wait()
+            halves.append(stats(at))
+        mean = jnp.concatenate([h[0] for h in halves], axis=0)
+        scale = jnp.concatenate([h[1] for h in halves], axis=0)
+        if first == 0:
+            weights_copy().wait()
+        kv = jnp.zeros((tile, ws.shape[1]), jnp.float32)
+        span = slice(first, first + tile)
+        for start in range(0, width, HD):
+            for at in (start, start + LANES):
+                normed = (wide(first, tile, at) - mean) * scale * gain_ref[:, at:at + LANES]
+                normed_ref[span, at:at + LANES] = normed.astype(jnp.bfloat16)
+            kv = kv + jnp.dot(
+                normed_ref[span, start:start + HD], ws[start:start + HD, :], preferred_element_type=jnp.float32
+            )
+        msg_ref[span, :] = kv.astype(jnp.bfloat16)
+
+
+def norm_kv(tokens, gain, w_keyval, segments):
     rows, width = tokens.shape
     cols = w_keyval.shape[1]
+    vmem, hbm = pl.BlockSpec(memory_space=pltpu.VMEM), pl.BlockSpec(memory_space=pltpu.HBM)
     return pl.pallas_call(
         norm_kv_kernel,
-        grid=(rows // tile,),
-        in_specs=[
-            pl.BlockSpec((tile, width), lambda i: (i, 0)),
-            pl.BlockSpec((1, width), lambda i: (0, 0)),
-            pl.BlockSpec((width, cols), lambda i: (0, 0)),
-            pl.BlockSpec((1, rows), lambda i: (0, 0)),
-        ],
-        out_specs=[
-            pl.BlockSpec((rows + SEG_ROWS, cols), lambda i: (0, 0)),
-            pl.BlockSpec((tile, width), lambda i: (i, 0)),
-        ],
+        in_specs=[hbm, vmem, hbm, vmem],
+        out_specs=[vmem, vmem],
         out_shape=[
             jax.ShapeDtypeStruct((rows + SEG_ROWS, cols), jnp.bfloat16),
             jax.ShapeDtypeStruct((rows, width), jnp.bfloat16),
         ],
-        compiler_params=pltpu.CompilerParams(vmem_limit_bytes=24 * MIB),
+        scratch_shapes=[
+            pltpu.VMEM((rows, width), jnp.bfloat16),
+            pltpu.VMEM((width, cols), jnp.bfloat16),
+            pltpu.SemaphoreType.DMA((5,)),
+        ],
+        compiler_params=pltpu.CompilerParams(vmem_limit_bytes=56 * MIB),
         cost_estimate=pl.CostEstimate(
-            flops=2 * rows * width * cols, bytes_accessed=4 * rows * width + 2 * width * cols, transcendentals=0
+            flops=40 * rows * width * cols, bytes_accessed=4 * rows * width + 2 * width * cols, transcendentals=0
         ),
         name="norm_kv",
     )(tokens, gain.reshape(1, width), w_keyval, segments.reshape(1, rows))
 
 
-def turn():
-    return lax.rem(lax.div(lax.axis_index("seq"), 2), 2)
-
-
-def query_kernel(x_ref, w_ref, out_ref, turn_ref):
+def query_kernel(x_ref, w_ref, out_ref):
     out_ref[...] = jnp.dot(x_ref[...], w_ref[...], preferred_element_type=jnp.float32).astype(jnp.bfloat16)
-    turn_ref[...] = jnp.full(turn_ref.shape, turn(), jnp.int32)
 
 
 def project_query(normed, w_query):
@@ -99,11 +111,11 @@
         query_kernel,
         grid=(rows // tile,),
         in_specs=[pl.BlockSpec((tile, width), lambda i: (i, 0)), pl.BlockSpec((width, cols), lambda i: (0, 0))],
-        out_specs=[pl.BlockSpec((tile, cols), lambda i: (i, 0)), pl.BlockSpec((8, LANES), lambda i: (0, 0))],
-        out_shape=[jax.ShapeDtypeStruct((rows, cols), jnp.bfloat16), jax.ShapeDtypeStruct((8, LANES), jnp.int32)],
+        out_specs=pl.BlockSpec((tile, cols), lambda i: (i, 0)),
+        out_shape=jax.ShapeDtypeStruct((rows, cols), jnp.bfloat16),
         compiler_params=pltpu.CompilerParams(vmem_limit_bytes=20 * MIB),
         cost_estimate=pl.CostEstimate(
-            flops=2 * rows * width * cols, bytes_accessed=2 * rows * width + 2 * width * cols, transcendentals=0
+            flops=20 * rows * width * cols, bytes_accessed=2 * rows * width + 2 * width * cols, transcendentals=0
         ),
         name="project_query",
     )(normed, w_query)
@@ -118,9 +130,6 @@
     if not first:
         state_ref, refs = refs[0], refs[1:]
     out_ref, refs = refs[0], refs[1:]
-    if not last:
-        turn_ref, refs = refs[0], refs[1:]
-        turn_ref[...] = jnp.full(turn_ref.shape, turn(), jnp.int32)
     keys, values, segs, scores, sems = refs
     rows = q_ref.shape[0]
     tile = rows // 2
@@ -208,17 +217,12 @@
     operands = [query, segments.reshape(1, rows), *mine, *other] + ([] if first else [state])
     if last:
         out_shape = jax.ShapeDtypeStruct((rows, HD), jnp.bfloat16)
-        out_specs = vmem
     else:
-        out_shape = [
-            jax.ShapeDtypeStruct((rows, HD + 2 * LANES), jnp.float32),
-            jax.ShapeDtypeStruct((8, LANES), jnp.int32),
-        ]
-        out_specs = [vmem, vmem]
+        out_shape = jax.ShapeDtypeStruct((rows, HD + 2 * LANES), jnp.float32)
     return pl.pallas_call(
         functools.partial(attend_kernel, plan, first, last),
         in_specs=[vmem] * 2 + [pl.BlockSpec(memory_space=pl.ANY)] * (2 * blocks) + ([] if first else [vmem]),
-        out_specs=out_specs,
+        out_specs=vmem,
         out_shape=out_shape,
         scratch_shapes=[
             pltpu.VMEM((blocks, rows, HD), jnp.bfloat16),
@@ -229,7 +233,7 @@
         ],
         compiler_params=pltpu.CompilerParams(vmem_limit_bytes=(12 + 2 * blocks) * MIB),
         cost_estimate=pl.CostEstimate(
-            flops=4 * rows * rows * blocks * HD, bytes_accessed=4 * rows * blocks * HD, transcendentals=rows * rows * blocks
+            flops=80 * rows * rows * blocks * HD, bytes_accessed=4 * rows * blocks * HD, transcendentals=rows * rows * blocks
         ),
         name="attend_last" if last else "attend_first" if first else "attend_more",
     )(*operands)
@@ -298,29 +302,24 @@
     def swap_pair(x):
         return lax.ppermute(x, "seq", [(i, i ^ 1) for i in range(seq_size)])
 
-    def exchange(x, colour):
-        low = [i for i in range(seq_size - 2) if (i // 2) % 2 == colour]
-        return lax.ppermute(x, "seq", [(i, i + 2) for i in low] + [(i + 2, i) for i in low])
-
-    def pick(flag, if_odd, if_even):
-        return jnp.where(flag[:1, :1] == 1, if_odd, if_even)
+    def shift(x):
+        return lax.ppermute(x, "seq", [(i, (i + 2) % seq_size) for i in range(seq_size)])
 
     w_other = swap_cores(w_out)
-    message, normed = norm_kv(tokens, gain, w_keyval, segments, 256)
-    at_odd, at_even = exchange(message, 0), exchange(message, 1)
+    message, normed = norm_kv(tokens, gain, w_keyval, segments)
+    held = shift(message)
     pair = swap_pair(message)
-    query, flag = project_query(normed, w_query)
+    query = project_query(normed, w_query)
     state = None
     mine, plan = [message, pair], ["own", (0, 1, False)]
     for k in range(1, window // 2 + 1):
-        held = pick(flag, at_odd, at_even)
         mine.append(held)
         plan.append((2 * k, 2 * k, 2 * k == window))
+        beside = swap_pair(held)
         if k < window // 2:
-            at_odd, at_even = exchange(at_even, 0), exchange(at_odd, 1)
-        beside = swap_pair(held)
+            held = shift(held)
         if k == 1 or k == window // 2:
-            state, flag = attend(query, segments, plan, mine, [swap_cores(m) for m in mine], state, False)
+            state = attend(query, segments, plan, mine, [swap_cores(m) for m in mine], state, False)
             mine, plan = [], []
         mine.append(beside)
         plan.append((2 * k - 1, 2 * k + 1 if k < window // 2 else 0, False))

time: 54.4 us -> 51.5 us (0.947)
  the two profiles are of different devices: /device:TPU:11 before, /device:TPU:0 now
where the time goes in v3:
time: 51.5 us; the launch traced here: 51.3 us
  Pallas kernels  21.8 us (42%)
  waiting for transfers between devices  18.2 us (35%)
  starting transfers between devices  8.89 us (17%)
  local copies, waits for them, and re-layouts  2.35 us (5%)
    ppermute x2, waiting for transfers between devices, shift(): lax.ppermute(x, 'seq', [(i, (i + 2) % seq_size) for i in range(seq_size)])  12.1 us
    pallas_call x1, Pallas kernels, norm_kv(): pl.pallas_call(norm_kv_kernel, in_specs=[hbm, vmem, hbm, vmem], out_specs...  8.56 us
    pallas_call x1, Pallas kernels, project_out(): pl.pallas_call(output_kernel, grid=(steps,), in_specs=[whole, whole, weig...  7.06 us
    ppermute x3, waiting for transfers between devices, swap_pair(): return lax.ppermute(x, 'seq', [(i, i ^ 1) for i in range(seq_size)])  4.87 us
    pallas_call x3, Pallas kernels, attend(): pl.pallas_call(functools.partial(attend_kernel, plan, first, last), in_sp...  4.74 us
    ppermute x3, starting transfers between devices, swap_pair(): return lax.ppermute(x, 'seq', [(i, i ^ 1) for i in range(seq_size)])  4.56 us
    ppermute x2, starting transfers between devices, shift(): lax.ppermute(x, 'seq', [(i, (i + 2) % seq_size) for i in range(seq_size)])  3.08 us
    unnamed x16, local copies, waits for them, and re-layouts  2.35 us
  transfers between devices with their start and end apart: 13, of which 5 were waited for; matrix products, arithmetic and copies ran while one was open for 0% of the time, Pallas kernels for 12%

profile of v3, /device:TPU:0, one launch (start us, length us, event | category | flops | bytes accessed | tf_op | source)
XLA Modules:
  0.0 51.3 jit_solution(13494637408808252924)
XLA Ops:
  0.0 8.6 %norm_kv.1 = (bf16[528,256]{1,0:T(8,128)(2,1)}, bf16[512,4096]{1,0:T(8,128)(2,1)}) custom-call(bf16[512,4096]{1,0:T(8,128)(2,1)} %x_ref.3, f32[1,4096]{1,0:T(1,128)} %bitcast.10, bf16[4096,256]{1,0:T(8,128)(2,1)} %w_ref.2, s32[1,512]{1,0:T(1,128)} %bitcast.6), custom_call_target="tpu_custom_call" | custom-call | flops 21474836480 | bytes 10485760 | tf_op jit(solution)/shard_map/norm_kv/pallas_call | solution.py:81
  8.6 3.1 %collective-permute-start = (bf16[528,256]{1,0:T(8,128)(2,1)}, bf16[528,256]{1,0:T(8,128)(2,1)S(1)}, u32[]{:S(2)}, u32[]{:S(2)}) collective-permute-start(bf16[528,256]{1,0:T(8,128)(2,1)} %get-tuple-element.8.refs_2_), channel_id=1, source_target_pairs={{0,4},{2,6},{4,8},{6,10},{8,12},{10,14},{12,0},{14,2},{1,5},{3,7},... | collective-permute-start | bytes 811016 | tf_op jit(solution)/shard_map/ppermute | solution.py:306
  11.6 1.5 %collective-permute-start.7 = (bf16[528,256]{1,0:T(8,128)(2,1)}, bf16[528,256]{1,0:T(8,128)(2,1)S(1)}, u32[]{:S(2)}, u32[]{:S(2)}) collective-permute-start(bf16[528,256]{1,0:T(8,128)(2,1)} %get-tuple-element.8.refs_2_), channel_id=1, source_target_pairs={{0,2},{2,0},{4,6},{6,4},{8,10},{10,8},{12,14},{14,12},{1,3},{3,1},... | collective-permute-start | bytes 811016 | tf_op jit(solution)/shard_map/ppermute | solution.py:303
  13.2 7.2 %collective-permute-done.refs_4_ = bf16[528,256]{1,0:T(8,128)(2,1)S(1)} collective-permute-done((bf16[528,256]{1,0:T(8,128)(2,1)}, bf16[528,256]{1,0:T(8,128)(2,1)S(1)}, u32[]{:S(2)}, u32[]{:S(2)}) %collective-permute-start) | collective-permute-done | bytes 270368 | tf_op jit(solution)/shard_map/ppermute | solution.py:306
  20.4 1.5 %collective-permute-start.4 = (bf16[528,256]{1,0:T(8,128)(2,1)S(1)}, bf16[528,256]{1,0:T(8,128)(2,1)S(1)}, u32[]{:S(2)}, u32[]{:S(2)}) collective-permute-start(bf16[528,256]{1,0:T(8,128)(2,1)S(1)} %collective-permute-done.refs_4_), channel_id=1, source_target_pairs={{0,2},{2,0},{4,6},{6,4},{8,10},{10,8},{12,14},{14,12},{1,3},{3,1},... | collective-permute-start | bytes 811016 | tf_op jit(solution)/shard_map/ppermute | solution.py:303
  21.9 0.0 collective-permute-done.7.refs_3_
  21.9 0.2 collective-permute-start.9
  22.1 2.2 %copy-done.7 = bf16[512,4096]{1,0:T(8,128)(2,1)S(1)} copy-done((bf16[512,4096]{1,0:T(8,128)(2,1)S(1)}, bf16[512,4096]{1,0:T(8,128)(2,1)}, u32[]{:S(2)}) %copy-start.7) | copy-done | bytes 4194328
  24.3 1.4 %project_query.1.refs_0_ = bf16[512,256]{1,0:T(8,128)(2,1)S(1)} custom-call(bf16[512,4096]{1,0:T(8,128)(2,1)S(1)} %copy-done.7, bf16[4096,256]{1,0:T(8,128)(2,1)S(1)} %copy-done.4), custom_call_target="tpu_custom_call" | custom-call | flops 10737418240 | bytes 6291456 | tf_op jit(solution)/shard_map/project_query/pallas_call | solution.py:110
  25.8 0.1 copy-done.1
  25.9 0.3 collective-permute-start.12
  26.2 4.9 %collective-permute-done.1.refs_3_ = bf16[528,256]{1,0:T(8,128)(2,1)S(1)} collective-permute-done((bf16[528,256]{1,0:T(8,128)(2,1)S(1)}, bf16[528,256]{1,0:T(8,128)(2,1)S(1)}, u32[]{:S(2)}, u32[]{:S(2)}) %collective-permute-start.1) | collective-permute-done | bytes 270368 | tf_op jit(solution)/shard_map/ppermute | solution.py:306
  31.1 1.5 %collective-permute-start.2 = (bf16[528,256]{1,0:T(8,128)(2,1)S(1)}, bf16[528,256]{1,0:T(8,128)(2,1)S(1)}, u32[]{:S(2)}, u32[]{:S(2)}) collective-permute-start(bf16[528,256]{1,0:T(8,128)(2,1)S(1)} %collective-permute-done.1.refs_3_), channel_id=1, source_target_pairs={{0,2},{2,0},{4,6},{6,4},{8,10},{10,8},{12,14},{14,12},{1,3},{3,1},... | collective-permute-start | bytes 811016 | tf_op jit(solution)/shard_map/ppermute | solution.py:303
  32.6 0.2 collective-permute-start.5
  32.8 2.3 %attend_first.1.refs_6_ = f32[512,512]{1,0:T(8,128)S(1)} custom-call(bf16[512,256]{1,0:T(8,128)(2,1)S(1)} %project_query.1.refs_0_, s32[1,512]{1,0:T(1,128)S(1)} %bitcast.7, bf16[528,256]{1,0:T(8,128)(2,1)S(1)} %copy-done.5, bf16[528,256]{1,0:T(8,128)(2,1)S(1)} %collective-permute-done.7.refs_3_, bf16[528,256]{1,0:T(8,128)(2,1)S(1)} %collective-permute-done.refs_4_, ...), custom_call_target="tpu_custom_call" | custom-call | flops 16106127360 | bytes 1572864 | tf_op jit(solution)/shard_map/attend_first/pallas_call | solution.py:222
  35.1 4.9 %collective-permute-done.2.refs_2_ = bf16[528,256]{1,0:T(8,128)(2,1)S(1)} collective-permute-done((bf16[528,256]{1,0:T(8,128)(2,1)S(1)}, bf16[528,256]{1,0:T(8,128)(2,1)S(1)}, u32[]{:S(2)}, u32[]{:S(2)}) %collective-permute-start.2) | collective-permute-done | bytes 270368 | tf_op jit(solution)/shard_map/ppermute | solution.py:303
  40.0 1.4 %attend_more.1.refs_4_ = f32[512,512]{1,0:T(8,128)S(1)} custom-call(bf16[512,256]{1,0:T(8,128)(2,1)S(1)} %project_query.1.refs_0_, s32[1,512]{1,0:T(1,128)S(1)} %bitcast.8, bf16[528,256]{1,0:T(8,128)(2,1)S(1)} %collective-permute-done.4.refs_2_, bf16[528,256]{1,0:T(8,128)(2,1)S(1)} %collective-permute-done.1.refs_3_, ...), custom_call_target="tpu_custom_call" | custom-call | flops 10737418240 | bytes 1048576 | tf_op jit(solution)/shard_map/attend_more/pallas_call | solution.py:222
  41.4 0.0 copy-start.2
  41.4 0.0 copy-start.3
  41.4 0.1 collective-permute-done.3.refs_3_
  41.5 1.1 %attend_last.1.a_ref = bf16[512,256]{1,0:T(8,128)(2,1)S(1)} custom-call(bf16[512,256]{1,0:T(8,128)(2,1)S(1)} %project_query.1.refs_0_, s32[1,512]{1,0:T(1,128)S(1)} %bitcast.9, bf16[528,256]{1,0:T(8,128)(2,1)S(1)} %collective-permute-done.2.refs_2_, bf16[528,256]{1,0:T(8,128)(2,1)S(1)} %collective-permute-done.3.refs_3_, f32[512,512]{1,0:T(8,128)S(1)} %attend_more.1.refs_4_), custom_call_target="tpu_custom_call" | custom-call | flops 5368709120 | bytes 524288 | tf_op jit(solution)/shard_map/attend_last/pallas_call | solution.py:222
  42.6 0.5 collective-permute-start.11
  43.1 1.2 %collective-permute-done.11.b_ref = bf16[512,256]{1,0:T(8,128)(2,1)S(1)} collective-permute-done((bf16[512,256]{1,0:T(8,128)(2,1)S(1)}, bf16[512,256]{1,0:T(8,128)(2,1)S(1)}, u32[]{:S(2)}, u32[]{:S(2)}) %collective-permute-start.11) | collective-permute-done | bytes 262176 | tf_op jit(solution)/shard_map/ppermute | solution.py:300
  44.3 7.1 %project_out.1 = bf16[512,4096]{1,0:T(8,128)(2,1)} custom-call(bf16[512,256]{1,0:T(8,128)(2,1)S(1)} %attend_last.1.a_ref, bf16[512,256]{1,0:T(8,128)(2,1)S(1)} %collective-permute-done.11.b_ref, bf16[256,4096]{1,0:T(8,128)(2,1)S(1)} %copy-done.1, bf16[256,4096]{1,0:T(8,128)(2,1)S(1)} %collective-permute-done.12.wb_ref, bf16[512,4096]{1,0:T(8,128)(2,1)S(1)} %copy-done, ...), custom_call_target="tpu_custom_call" | custom-call | flops 2147483648 | bytes 12582912 | tf_op jit(solution)/shard_map/project_out/pallas_call | solution.py:282
  (24 shorter events, 0.1 us)
Async XLA Ops:
  0.0 22.1 %copy-start.4 = (bf16[4096,256]{1,0:T(8,128)(2,1)S(1)}, bf16[4096,256]{1,0:T(8,128)(2,1)}, u32[]{:S(2)}) copy-start(bf16[4096,256]{1,0:T(8,128)(2,1)} %w_ref.3) | copy-start | bytes 6291460
  8.6 11.8 %collective-permute-start = (bf16[528,256]{1,0:T(8,128)(2,1)}, bf16[528,256]{1,0:T(8,128)(2,1)S(1)}, u32[]{:S(2)}, u32[]{:S(2)}) collective-permute-start(bf16[528,256]{1,0:T(8,128)(2,1)} %get-tuple-element.8.refs_2_), channel_id=1, source_target_pairs={{0,4},{2,6},{4,8},{6,10},{8,12},{10,14},{12,0},{14,2},{1,5},{3,7},... | collective-permute-start | bytes 811016 | tf_op jit(solution)/shard_map/ppermute | solution.py:306
  11.6 10.2 %collective-permute-start.7 = (bf16[528,256]{1,0:T(8,128)(2,1)}, bf16[528,256]{1,0:T(8,128)(2,1)S(1)}, u32[]{:S(2)}, u32[]{:S(2)}) collective-permute-start(bf16[528,256]{1,0:T(8,128)(2,1)} %get-tuple-element.8.refs_2_), channel_id=1, source_target_pairs={{0,2},{2,0},{4,6},{6,4},{8,10},{10,8},{12,14},{14,12},{1,3},{3,1},... | collective-permute-start | bytes 811016 | tf_op jit(solution)/shard_map/ppermute | solution.py:303
  13.2 12.6 %collective-permute-start.8 = (bf16[528,256]{1,0:T(8,128)(2,1)}, bf16[528,256]{1,0:T(8,128)(2,1)S(1)}, u32[]{:S(2)}, u32[]{:S(2)}) collective-permute-start(bf16[528,256]{1,0:T(8,128)(2,1)} %get-tuple-element.8.refs_2_), channel_id=1, source_target_pairs={{0,1},{1,0},{2,3},{3,2},{4,5},{5,4},{6,7},{7,6},{8,9},{9,8},{10,11... | collective-permute-start | bytes 811016 | tf_op jit(solution)/shard_map/ppermute | solution.py:300
  20.4 10.7 %collective-permute-start.10 = (bf16[528,256]{1,0:T(8,128)(2,1)S(1)}, bf16[528,256]{1,0:T(8,128)(2,1)S(1)}, u32[]{:S(2)}, u32[]{:S(2)}) collective-permute-start(bf16[528,256]{1,0:T(8,128)(2,1)S(1)} %collective-permute-done.refs_4_), channel_id=1, source_target_pairs={{0,1},{1,0},{2,3},{3,2},{4,5},{5,4},{6,7},{7,6},{8,9},{9,8},{10,11... | collective-permute-start | bytes 811016 | tf_op jit(solution)/shard_map/ppermute | solution.py:300
  20.4 10.7 %collective-permute-start.1 = (bf16[528,256]{1,0:T(8,128)(2,1)S(1)}, bf16[528,256]{1,0:T(8,128)(2,1)S(1)}, u32[]{:S(2)}, u32[]{:S(2)}) collective-permute-start(bf16[528,256]{1,0:T(8,128)(2,1)S(1)} %collective-permute-done.refs_4_), channel_id=1, source_target_pairs={{0,4},{2,6},{4,8},{6,10},{8,12},{10,14},{12,0},{14,2},{1,5},{3,7},... | collective-permute-start | bytes 811016 | tf_op jit(solution)/shard_map/ppermute | solution.py:306
  20.4 12.2 %collective-permute-start.4 = (bf16[528,256]{1,0:T(8,128)(2,1)S(1)}, bf16[528,256]{1,0:T(8,128)(2,1)S(1)}, u32[]{:S(2)}, u32[]{:S(2)}) collective-permute-start(bf16[528,256]{1,0:T(8,128)(2,1)S(1)} %collective-permute-done.refs_4_), channel_id=1, source_target_pairs={{0,2},{2,0},{4,6},{6,4},{8,10},{10,8},{12,14},{14,12},{1,3},{3,1},... | collective-permute-start | bytes 811016 | tf_op jit(solution)/shard_map/ppermute | solution.py:303
  21.9 10.9 %collective-permute-start.9 = (bf16[528,256]{1,0:T(8,128)(2,1)S(1)}, bf16[528,256]{1,0:T(8,128)(2,1)S(1)}, u32[]{:S(2)}, u32[]{:S(2)}) collective-permute-start(bf16[528,256]{1,0:T(8,128)(2,1)S(1)} %collective-permute-done.7.refs_3_), channel_id=1, source_target_pairs={{0,1},{1,0},{2,3},{3,2},{4,5},{5,4},{6,7},{7,6},{8,9},{9,8},{10,11... | collective-permute-start | bytes 811016 | tf_op jit(solution)/shard_map/ppermute | solution.py:300
  22.1 2.2 %copy-start.7 = (bf16[512,4096]{1,0:T(8,128)(2,1)S(1)}, bf16[512,4096]{1,0:T(8,128)(2,1)}, u32[]{:S(2)}) copy-start(bf16[512,4096]{1,0:T(8,128)(2,1)} %get-tuple-element.7.x_ref) | copy-start | bytes 12582916
  24.3 1.6 %copy-start.1 = (bf16[256,4096]{1,0:T(8,128)(2,1)S(1)}, bf16[256,4096]{1,0:T(8,128)(2,1)}, u32[]{:S(2)}) copy-start(bf16[256,4096]{1,0:T(8,128)(2,1)} %wa_ref.1) | copy-start | bytes 6291460
  24.3 8.5 %copy-start.5 = (bf16[528,256]{1,0:T(8,128)(2,1)S(1)}, bf16[528,256]{1,0:T(8,128)(2,1)}, u32[]{:S(2)}) copy-start(bf16[528,256]{1,0:T(8,128)(2,1)} %get-tuple-element.8.refs_2_) | copy-start | bytes 811012
  24.3 8.5 %copy-start.6 = (s32[512]{0:T(512)S(1)}, s32[512]{0:T(512)}, u32[]{:S(2)}) copy-start(s32[512]{0:T(512)} %param.10) | copy-start | bytes 6148
  25.9 18.3 %collective-permute-start.12 = (bf16[256,4096]{1,0:T(8,128)(2,1)S(1)}, bf16[256,4096]{1,0:T(8,128)(2,1)S(1)}, u32[]{:S(2)}, u32[]{:S(2)}) collective-permute-start(bf16[256,4096]{1,0:T(8,128)(2,1)S(1)} %copy-done.1), channel_id=1, source_target_pairs={{0,1},{1,0},{2,3},{3,2},{4,5},{5,4},{6,7},{7,6},{8,9},{9,8},{10,11... | collective-permute-start | bytes 6291464 | tf_op jit(solution)/shard_map/ppermute | solution.py:300
  31.1 8.9 %collective-permute-start.6 = (bf16[528,256]{1,0:T(8,128)(2,1)S(1)}, bf16[528,256]{1,0:T(8,128)(2,1)S(1)}, u32[]{:S(2)}, u32[]{:S(2)}) collective-permute-start(bf16[528,256]{1,0:T(8,128)(2,1)S(1)} %collective-permute-done.1.refs_3_), channel_id=1, source_target_pairs={{0,1},{1,0},{2,3},{3,2},{4,5},{5,4},{6,7},{7,6},{8,9},{9,8},{10,11... | collective-permute-start | bytes 811016 | tf_op jit(solution)/shard_map/ppermute | solution.py:300
  31.1 8.9 %collective-permute-start.2 = (bf16[528,256]{1,0:T(8,128)(2,1)S(1)}, bf16[528,256]{1,0:T(8,128)(2,1)S(1)}, u32[]{:S(2)}, u32[]{:S(2)}) collective-permute-start(bf16[528,256]{1,0:T(8,128)(2,1)S(1)} %collective-permute-done.1.refs_3_), channel_id=1, source_target_pairs={{0,2},{2,0},{4,6},{6,4},{8,10},{10,8},{12,14},{14,12},{1,3},{3,1},... | collective-permute-start | bytes 811016 | tf_op jit(solution)/shard_map/ppermute | solution.py:303
  32.6 7.4 %collective-permute-start.5 = (bf16[528,256]{1,0:T(8,128)(2,1)S(1)}, bf16[528,256]{1,0:T(8,128)(2,1)S(1)}, u32[]{:S(2)}, u32[]{:S(2)}) collective-permute-start(bf16[528,256]{1,0:T(8,128)(2,1)S(1)} %collective-permute-done.4.refs_2_), channel_id=1, source_target_pairs={{0,1},{1,0},{2,3},{3,2},{4,5},{5,4},{6,7},{7,6},{8,9},{9,8},{10,11... | collective-permute-start | bytes 811016 | tf_op jit(solution)/shard_map/ppermute | solution.py:300
  40.0 1.5 %collective-permute-start.3 = (bf16[528,256]{1,0:T(8,128)(2,1)S(1)}, bf16[528,256]{1,0:T(8,128)(2,1)S(1)}, u32[]{:S(2)}, u32[]{:S(2)}) collective-permute-start(bf16[528,256]{1,0:T(8,128)(2,1)S(1)} %collective-permute-done.2.refs_2_), channel_id=1, source_target_pairs={{0,1},{1,0},{2,3},{3,2},{4,5},{5,4},{6,7},{7,6},{8,9},{9,8},{10,11... | collective-permute-start | bytes 811016 | tf_op jit(solution)/shard_map/ppermute | solution.py:300
  41.4 2.9 %copy-start.2 = (s32[512,32]{0,1:T(8,128)S(1)}, s32[512,32]{0,1:T(8,128)}, u32[]{:S(2)}) copy-start(s32[512,32]{0,1:T(8,128)} %param.14) | copy-start | bytes 196612
  41.4 2.8 %copy-start.3 = (s32[512,32]{0,1:T(8,128)S(1)}, s32[512,32]{0,1:T(8,128)}, u32[]{:S(2)}) copy-start(s32[512,32]{0,1:T(8,128)} %param.15) | copy-start | bytes 196612
  41.5 2.7 %copy-start = (bf16[512,4096]{1,0:T(8,128)(2,1)S(1)}, bf16[512,4096]{1,0:T(8,128)(2,1)}, u32[]{:S(2)}) copy-start(bf16[512,4096]{1,0:T(8,128)(2,1)} %x_ref.3) | copy-start | bytes 12582916
  42.6 1.7 %collective-permute-start.11 = (bf16[512,256]{1,0:T(8,128)(2,1)S(1)}, bf16[512,256]{1,0:T(8,128)(2,1)S(1)}, u32[]{:S(2)}, u32[]{:S(2)}) collective-permute-start(bf16[512,256]{1,0:T(8,128)(2,1)S(1)} %attend_last.1.a_ref), channel_id=1, source_target_pairs={{0,1},{1,0},{2,3},{3,2},{4,5},{5,4},{6,7},{7,6},{8,9},{9,8},{10,11... | collective-permute-start | bytes 786440 | tf_op jit(solution)/shard_map/ppermute | solution.py:300

commit v4 on v3

--- a/solution.py
+++ b/solution.py
@@ -18,7 +18,7 @@
 FACTOR = HD ** (-0.5) * 1.4426950408889634
 
 
-def norm_kv_kernel(x_ref, gain_ref, w_ref, seg_ref, msg_ref, normed_ref, xs, ws, sems):
+def norm_kv_kernel(x_ref, gain_hbm, w_ref, seg_hbm, msg_ref, normed_ref, xs, ws, gain_ref, seg_ref, sems):
     rows, width = xs.shape
     tile, part = rows // 2, rows // 4
 
@@ -28,16 +28,19 @@
     def weights_copy():
         return pltpu.make_async_copy(w_ref, ws, sems.at[4])
 
+    def gain_copy():
+        return pltpu.make_async_copy(gain_hbm, gain_ref, sems.at[5])
+
+    def segments_copy():
+        return pltpu.make_async_copy(seg_hbm, seg_ref, sems.at[6])
+
     tokens_copy(0).start()
     tokens_copy(1).start()
+    gain_copy().start()
+    segments_copy().start()
     weights_copy().start()
     tokens_copy(2).start()
     tokens_copy(3).start()
-    seg = seg_ref[...].astype(jnp.float32)
-    low = jnp.broadcast_to(seg[:, :HD], (8, HD))
-    high = jnp.broadcast_to(seg[:, HD:], (8, HD))
-    msg_ref[rows:, :] = jnp.concatenate([low, high], axis=0).astype(jnp.bfloat16)
-
     def wide(first, count, start):
         return xs[first:first + count, start:start + LANES].astype(jnp.float32)
 
@@ -61,6 +64,7 @@
         mean = jnp.concatenate([h[0] for h in halves], axis=0)
         scale = jnp.concatenate([h[1] for h in halves], axis=0)
         if first == 0:
+            gain_copy().wait()
             weights_copy().wait()
         kv = jnp.zeros((tile, ws.shape[1]), jnp.float32)
         span = slice(first, first + tile)
@@ -72,6 +76,15 @@
                 normed_ref[span, start:start + HD], ws[start:start + HD, :], preferred_element_type=jnp.float32
             )
         msg_ref[span, :] = kv.astype(jnp.bfloat16)
+    segments_copy().wait()
+    seg = seg_ref[...].astype(jnp.float32)
+    low = jnp.broadcast_to(seg[:, :HD], (8, HD))
+    high = jnp.broadcast_to(seg[:, HD:], (8, HD))
+    msg_ref[rows:, :] = jnp.concatenate([low, high], axis=0).astype(jnp.bfloat16)
+
+
+def in_hbm(x):
+    return pltpu.with_memory_space_constraint(x, pltpu.HBM)
 
 
 def norm_kv(tokens, gain, w_keyval, segments):
@@ -80,23 +93,22 @@
     vmem, hbm = pl.BlockSpec(memory_space=pltpu.VMEM), pl.BlockSpec(memory_space=pltpu.HBM)
     return pl.pallas_call(
         norm_kv_kernel,
-        in_specs=[hbm, vmem, hbm, vmem],
+        in_specs=[hbm] * 4,
         out_specs=[vmem, vmem],
-        out_shape=[
-            jax.ShapeDtypeStruct((rows + SEG_ROWS, cols), jnp.bfloat16),
-            jax.ShapeDtypeStruct((rows, width), jnp.bfloat16),
-        ],
+        out_shape=[pltpu.VMEM((rows + SEG_ROWS, cols), jnp.bfloat16), pltpu.VMEM((rows, width), jnp.bfloat16)],
         scratch_shapes=[
             pltpu.VMEM((rows, width), jnp.bfloat16),
             pltpu.VMEM((width, cols), jnp.bfloat16),
-            pltpu.SemaphoreType.DMA((5,)),
+            pltpu.VMEM((1, width), jnp.float32),
+            pltpu.VMEM((1, rows), jnp.int32),
+            pltpu.SemaphoreType.DMA((7,)),
         ],
-        compiler_params=pltpu.CompilerParams(vmem_limit_bytes=56 * MIB),
+        compiler_params=pltpu.CompilerParams(vmem_limit_bytes=24 * MIB),
         cost_estimate=pl.CostEstimate(
             flops=40 * rows * width * cols, bytes_accessed=4 * rows * width + 2 * width * cols, transcendentals=0
         ),
         name="norm_kv",
-    )(tokens, gain.reshape(1, width), w_keyval, segments.reshape(1, rows))
+    )(in_hbm(tokens), in_hbm(gain.reshape(1, width)), in_hbm(w_keyval), in_hbm(segments.reshape(1, rows)))
 
 
 def query_kernel(x_ref, w_ref, out_ref):
@@ -299,25 +311,26 @@
     def swap_cores(x):
         return lax.ppermute(x, "tp", [(0, 1), (1, 0)])
 
-    def swap_pair(x):
-        return lax.ppermute(x, "seq", [(i, i ^ 1) for i in range(seq_size)])
-
-    def shift(x):
-        return lax.ppermute(x, "seq", [(i, (i + 2) % seq_size) for i in range(seq_size)])
+    def swap_pair(x, first):
+        return lax.ppermute(x, "seq", [(i, i ^ 1 if i >= first else i) for i in range(seq_size)])
+
+    def shift(x, first):
+        cycle = seq_size - first
+        return lax.ppermute(x, "seq", [(i, first + (i - first + 2) % cycle if i >= first else i) for i in range(seq_size)])
 
     w_other = swap_cores(w_out)
     message, normed = norm_kv(tokens, gain, w_keyval, segments)
-    held = shift(message)
-    pair = swap_pair(message)
+    held = shift(message, 0)
+    pair = swap_pair(message, 0)
     query = project_query(normed, w_query)
     state = None
     mine, plan = [message, pair], ["own", (0, 1, False)]
     for k in range(1, window // 2 + 1):
         mine.append(held)
         plan.append((2 * k, 2 * k, 2 * k == window))
-        beside = swap_pair(held)
+        beside = swap_pair(held, 2 * k)
         if k < window // 2:
-            held = shift(held)
+            held = shift(held, 2 * k)
         if k == 1 or k == window // 2:
             state = attend(query, segments, plan, mine, [swap_cores(m) for m in mine], state, False)
             mine, plan = [], []

time: 51.5 us -> 48 us (0.932)
  the two profiles are of different devices: /device:TPU:0 before, /device:TPU:25 now
where the time goes in v4:
time: 48 us; the launch traced here: 47.8 us
  Pallas kernels  19.2 us (40%)
  starting transfers between devices  15 us (31%)
  waiting for transfers between devices  13.3 us (28%)
    ppermute x3, starting transfers between devices, swap_pair(): lax.ppermute(x, 'seq', [(i, i ^ 1 if i >= first else i) for i in range(se...  7.59 us
    ppermute x2, waiting for transfers between devices, shift(): lax.ppermute(x, 'seq', [(i, first + (i - first + 2) % cycle if i >= first...  7.55 us
    pallas_call x1, Pallas kernels, project_out(): pl.pallas_call(output_kernel, grid=(steps,), in_specs=[whole, whole, weig...  7.05 us
    pallas_call x1, Pallas kernels, norm_kv(): pl.pallas_call(norm_kv_kernel, in_specs=[hbm] * 4, out_specs=[vmem, vmem]...  6.03 us
    ppermute x8, starting transfers between devices, swap_cores(): return lax.ppermute(x, 'tp', [(0, 1), (1, 0)])  5.36 us
    pallas_call x3, Pallas kernels, attend(): pl.pallas_call(functools.partial(attend_kernel, plan, first, last), in_sp...  4.71 us
    ppermute x3, waiting for transfers between devices, swap_pair(): lax.ppermute(x, 'seq', [(i, i ^ 1 if i >= first else i) for i in range(se...  4.25 us
    ppermute x2, starting transfers between devices, shift(): lax.ppermute(x, 'seq', [(i, first + (i - first + 2) % cycle if i >= first...  2.01 us
  transfers between devices with their start and end apart: 13, of which 4 were waited for; matrix products, arithmetic and copies ran while one was open for 0% of the time, Pallas kernels for 13%

profile of v4, /device:TPU:25, one launch (start us, length us, event | category | flops | bytes accessed | tf_op | source)
XLA Modules:
  0.0 47.8 jit_solution(8066683494920439582)
XLA Ops:
  0.0 6.0 %norm_kv.1 = (bf16[528,256]{1,0:T(8,128)(2,1)S(1)}, bf16[512,4096]{1,0:T(8,128)(2,1)S(1)}) custom-call(bf16[512,4096]{1,0:T(8,128)(2,1)} %x_ref.3, f32[1,4096]{1,0:T(1,128)} %bitcast.10, bf16[4096,256]{1,0:T(8,128)(2,1)} %w_ref.2, s32[1,512]{1,0:T(1,128)} %bitcast.6), custom_call_target="tpu_custom_call" | custom-call | flops 21474836480 | bytes 10485760 | tf_op jit(solution)/shard_map/norm_kv/pallas_call | solution.py:94
  6.0 0.1 collective-permute-start
  6.1 1.3 %collective-permute-start.7 = (bf16[528,256]{1,0:T(8,128)(2,1)S(1)}, bf16[528,256]{1,0:T(8,128)(2,1)S(1)}, u32[]{:S(2)}, u32[]{:S(2)}) collective-permute-start(bf16[528,256]{1,0:T(8,128)(2,1)S(1)} %get-tuple-element.8.refs_2_), channel_id=1, source_target_pairs={{0,2},{2,0},{4,6},{6,4},{8,10},{10,8},{12,14},{14,12},{1,3},{3,1},... | collective-permute-start | bytes 811016 | tf_op jit(solution)/shard_map/ppermute | solution.py:315
  7.4 1.1 %collective-permute-start.8 = (bf16[528,256]{1,0:T(8,128)(2,1)S(1)}, bf16[528,256]{1,0:T(8,128)(2,1)S(1)}, u32[]{:S(2)}, u32[]{:S(2)}) collective-permute-start(bf16[528,256]{1,0:T(8,128)(2,1)S(1)} %get-tuple-element.8.refs_2_), channel_id=1, source_target_pairs={{0,1},{1,0},{2,3},{3,2},{4,5},{5,4},{6,7},{7,6},{8,9},{9,8},{10,11... | collective-permute-start | bytes 811016 | tf_op jit(solution)/shard_map/ppermute | solution.py:312
  8.5 4.9 %collective-permute-done.refs_4_ = bf16[528,256]{1,0:T(8,128)(2,1)S(1)} collective-permute-done((bf16[528,256]{1,0:T(8,128)(2,1)S(1)}, bf16[528,256]{1,0:T(8,128)(2,1)S(1)}, u32[]{:S(2)}, u32[]{:S(2)}) %collective-permute-start) | collective-permute-done | bytes 270368 | tf_op jit(solution)/shard_map/ppermute | solution.py:319
  13.4 1.5 %collective-permute-start.10 = (bf16[528,256]{1,0:T(8,128)(2,1)S(1)}, bf16[528,256]{1,0:T(8,128)(2,1)S(1)}, u32[]{:S(2)}, u32[]{:S(2)}) collective-permute-start(bf16[528,256]{1,0:T(8,128)(2,1)S(1)} %collective-permute-done.refs_4_), channel_id=1, source_target_pairs={{0,1},{1,0},{2,3},{3,2},{4,5},{5,4},{6,7},{7,6},{8,9},{9,8},{10,11... | collective-permute-start | bytes 811016 | tf_op jit(solution)/shard_map/ppermute | solution.py:312
  15.0 2.0 %collective-permute-start.1 = (bf16[528,256]{1,0:T(8,128)(2,1)S(1)}, bf16[528,256]{1,0:T(8,128)(2,1)S(1)}, u32[]{:S(2)}, u32[]{:S(2)}) collective-permute-start(bf16[528,256]{1,0:T(8,128)(2,1)S(1)} %collective-permute-done.refs_4_), channel_id=1, source_target_pairs={{0,0},{2,2},{4,8},{6,10},{8,12},{10,14},{12,4},{14,6},{1,1},{3,3},... | collective-permute-start | bytes 811016 | tf_op jit(solution)/shard_map/ppermute | solution.py:319
  17.0 3.1 %collective-permute-start.4 = (bf16[528,256]{1,0:T(8,128)(2,1)S(1)}, bf16[528,256]{1,0:T(8,128)(2,1)S(1)}, u32[]{:S(2)}, u32[]{:S(2)}) collective-permute-start(bf16[528,256]{1,0:T(8,128)(2,1)S(1)} %collective-permute-done.refs_4_), channel_id=1, source_target_pairs={{0,0},{2,2},{4,6},{6,4},{8,10},{10,8},{12,14},{14,12},{1,1},{3,3},... | collective-permute-start | bytes 811016 | tf_op jit(solution)/shard_map/ppermute | solution.py:315
  20.1 0.6 %collective-permute-start.9 = (bf16[528,256]{1,0:T(8,128)(2,1)S(1)}, bf16[528,256]{1,0:T(8,128)(2,1)S(1)}, u32[]{:S(2)}, u32[]{:S(2)}) collective-permute-start(bf16[528,256]{1,0:T(8,128)(2,1)S(1)} %collective-permute-done.7.refs_3_), channel_id=1, source_target_pairs={{0,1},{1,0},{2,3},{3,2},{4,5},{5,4},{6,7},{7,6},{8,9},{9,8},{10,11... | collective-permute-start | bytes 811016 | tf_op jit(solution)/shard_map/ppermute | solution.py:312
  20.8 1.4 %project_query.1.refs_0_ = bf16[512,256]{1,0:T(8,128)(2,1)S(1)} custom-call(bf16[512,4096]{1,0:T(8,128)(2,1)S(1)} %get-tuple-element.7.x_ref, bf16[4096,256]{1,0:T(8,128)(2,1)S(1)} %copy-done.4), custom_call_target="tpu_custom_call" | custom-call | flops 10737418240 | bytes 6291456 | tf_op jit(solution)/shard_map/project_query/pallas_call | solution.py:122
  22.2 0.1 copy-done.1
  22.3 0.0 collective-permute-start.12
  22.4 2.6 %collective-permute-done.1.refs_3_ = bf16[528,256]{1,0:T(8,128)(2,1)S(1)} collective-permute-done((bf16[528,256]{1,0:T(8,128)(2,1)S(1)}, bf16[528,256]{1,0:T(8,128)(2,1)S(1)}, u32[]{:S(2)}, u32[]{:S(2)}) %collective-permute-start.1) | collective-permute-done | bytes 270368 | tf_op jit(solution)/shard_map/ppermute | solution.py:319
  25.0 0.8 %collective-permute-start.6 = (bf16[528,256]{1,0:T(8,128)(2,1)S(1)}, bf16[528,256]{1,0:T(8,128)(2,1)S(1)}, u32[]{:S(2)}, u32[]{:S(2)}) collective-permute-start(bf16[528,256]{1,0:T(8,128)(2,1)S(1)} %collective-permute-done.1.refs_3_), channel_id=1, source_target_pairs={{0,1},{1,0},{2,3},{3,2},{4,5},{5,4},{6,7},{7,6},{8,9},{9,8},{10,11... | collective-permute-start | bytes 811016 | tf_op jit(solution)/shard_map/ppermute | solution.py:312
  25.8 3.1 %collective-permute-start.2 = (bf16[528,256]{1,0:T(8,128)(2,1)S(1)}, bf16[528,256]{1,0:T(8,128)(2,1)S(1)}, u32[]{:S(2)}, u32[]{:S(2)}) collective-permute-start(bf16[528,256]{1,0:T(8,128)(2,1)S(1)} %collective-permute-done.1.refs_3_), channel_id=1, source_target_pairs={{0,0},{2,2},{4,4},{6,6},{8,10},{10,8},{12,14},{14,12},{1,1},{3,3},... | collective-permute-start | bytes 811016 | tf_op jit(solution)/shard_map/ppermute | solution.py:315
  28.9 0.3 collective-permute-start.5
  29.3 2.2 %attend_first.1.refs_6_ = f32[512,512]{1,0:T(8,128)S(1)} custom-call(bf16[512,256]{1,0:T(8,128)(2,1)S(1)} %project_query.1.refs_0_, s32[1,512]{1,0:T(1,128)S(1)} %bitcast.7, bf16[528,256]{1,0:T(8,128)(2,1)S(1)} %get-tuple-element.8.refs_2_, bf16[528,256]{1,0:T(8,128)(2,1)S(1)} %collective-permute-done.7.refs_3_, ...), custom_call_target="tpu_custom_call" | custom-call | flops 16106127360 | bytes 1572864 | tf_op jit(solution)/shard_map/attend_first/pallas_call | solution.py:234
  31.5 4.2 %collective-permute-done.2.refs_2_ = bf16[528,256]{1,0:T(8,128)(2,1)S(1)} collective-permute-done((bf16[528,256]{1,0:T(8,128)(2,1)S(1)}, bf16[528,256]{1,0:T(8,128)(2,1)S(1)}, u32[]{:S(2)}, u32[]{:S(2)}) %collective-permute-start.2) | collective-permute-done | bytes 270368 | tf_op jit(solution)/shard_map/ppermute | solution.py:315
  35.8 0.8 %collective-permute-start.3 = (bf16[528,256]{1,0:T(8,128)(2,1)S(1)}, bf16[528,256]{1,0:T(8,128)(2,1)S(1)}, u32[]{:S(2)}, u32[]{:S(2)}) collective-permute-start(bf16[528,256]{1,0:T(8,128)(2,1)S(1)} %collective-permute-done.2.refs_2_), channel_id=1, source_target_pairs={{0,1},{1,0},{2,3},{3,2},{4,5},{5,4},{6,7},{7,6},{8,9},{9,8},{10,11... | collective-permute-start | bytes 811016 | tf_op jit(solution)/shard_map/ppermute | solution.py:312
  36.6 1.4 %attend_more.1.refs_4_ = f32[512,512]{1,0:T(8,128)S(1)} custom-call(bf16[512,256]{1,0:T(8,128)(2,1)S(1)} %project_query.1.refs_0_, s32[1,512]{1,0:T(1,128)S(1)} %bitcast.8, bf16[528,256]{1,0:T(8,128)(2,1)S(1)} %collective-permute-done.4.refs_2_, bf16[528,256]{1,0:T(8,128)(2,1)S(1)} %collective-permute-done.1.refs_3_, ...), custom_call_target="tpu_custom_call" | custom-call | flops 10737418240 | bytes 1048576 | tf_op jit(solution)/shard_map/attend_more/pallas_call | solution.py:234
  38.0 1.1 %attend_last.1.a_ref = bf16[512,256]{1,0:T(8,128)(2,1)S(1)} custom-call(bf16[512,256]{1,0:T(8,128)(2,1)S(1)} %project_query.1.refs_0_, s32[1,512]{1,0:T(1,128)S(1)} %bitcast.9, bf16[528,256]{1,0:T(8,128)(2,1)S(1)} %collective-permute-done.2.refs_2_, bf16[528,256]{1,0:T(8,128)(2,1)S(1)} %collective-permute-done.3.refs_3_, f32[512,512]{1,0:T(8,128)S(1)} %attend_more.1.refs_4_), custom_call_target="tpu_custom_call" | custom-call | flops 5368709120 | bytes 524288 | tf_op jit(solution)/shard_map/attend_last/pallas_call | solution.py:234
  39.1 0.1 collective-permute-start.11
  39.2 1.5 %collective-permute-done.11.b_ref = bf16[512,256]{1,0:T(8,128)(2,1)S(1)} collective-permute-done((bf16[512,256]{1,0:T(8,128)(2,1)S(1)}, bf16[512,256]{1,0:T(8,128)(2,1)S(1)}, u32[]{:S(2)}, u32[]{:S(2)}) %collective-permute-start.11) | collective-permute-done | bytes 262176 | tf_op jit(solution)/shard_map/ppermute | solution.py:312
  40.7 7.1 %project_out.1 = bf16[512,4096]{1,0:T(8,128)(2,1)} custom-call(bf16[512,256]{1,0:T(8,128)(2,1)S(1)} %attend_last.1.a_ref, bf16[512,256]{1,0:T(8,128)(2,1)S(1)} %collective-permute-done.11.b_ref, bf16[256,4096]{1,0:T(8,128)(2,1)S(1)} %copy-done.1, bf16[256,4096]{1,0:T(8,128)(2,1)S(1)} %collective-permute-done.12.wb_ref, bf16[512,4096]{1,0:T(8,128)(2,1)S(1)} %copy-done, ...), custom_call_target="tpu_custom_call" | custom-call | flops 2147483648 | bytes 12582912 | tf_op jit(solution)/shard_map/project_out/pallas_call | solution.py:294
  (20 shorter events, 0.1 us)
Async XLA Ops:
  0.0 20.7 %copy-start.4 = (bf16[4096,256]{1,0:T(8,128)(2,1)S(1)}, bf16[4096,256]{1,0:T(8,128)(2,1)}, u32[]{:S(2)}) copy-start(bf16[4096,256]{1,0:T(8,128)(2,1)} %w_ref.3) | copy-start | bytes 6291460
  6.0 7.4 %collective-permute-start = (bf16[528,256]{1,0:T(8,128)(2,1)S(1)}, bf16[528,256]{1,0:T(8,128)(2,1)S(1)}, u32[]{:S(2)}, u32[]{:S(2)}) collective-permute-start(bf16[528,256]{1,0:T(8,128)(2,1)S(1)} %get-tuple-element.8.refs_2_), channel_id=1, source_target_pairs={{0,4},{2,6},{4,8},{6,10},{8,12},{10,14},{12,0},{14,2},{1,5},{3,7},... | collective-permute-start | bytes 811016 | tf_op jit(solution)/shard_map/ppermute | solution.py:319
  6.1 14.0 %collective-permute-start.7 = (bf16[528,256]{1,0:T(8,128)(2,1)S(1)}, bf16[528,256]{1,0:T(8,128)(2,1)S(1)}, u32[]{:S(2)}, u32[]{:S(2)}) collective-permute-start(bf16[528,256]{1,0:T(8,128)(2,1)S(1)} %get-tuple-element.8.refs_2_), channel_id=1, source_target_pairs={{0,2},{2,0},{4,6},{6,4},{8,10},{10,8},{12,14},{14,12},{1,3},{3,1},... | collective-permute-start | bytes 811016 | tf_op jit(solution)/shard_map/ppermute | solution.py:315
  7.4 14.8 %collective-permute-start.8 = (bf16[528,256]{1,0:T(8,128)(2,1)S(1)}, bf16[528,256]{1,0:T(8,128)(2,1)S(1)}, u32[]{:S(2)}, u32[]{:S(2)}) collective-permute-start(bf16[528,256]{1,0:T(8,128)(2,1)S(1)} %get-tuple-element.8.refs_2_), channel_id=1, source_target_pairs={{0,1},{1,0},{2,3},{3,2},{4,5},{5,4},{6,7},{7,6},{8,9},{9,8},{10,11... | collective-permute-start | bytes 811016 | tf_op jit(solution)/shard_map/ppermute | solution.py:312
  13.4 12.3 %collective-permute-start.10 = (bf16[528,256]{1,0:T(8,128)(2,1)S(1)}, bf16[528,256]{1,0:T(8,128)(2,1)S(1)}, u32[]{:S(2)}, u32[]{:S(2)}) collective-permute-start(bf16[528,256]{1,0:T(8,128)(2,1)S(1)} %collective-permute-done.refs_4_), channel_id=1, source_target_pairs={{0,1},{1,0},{2,3},{3,2},{4,5},{5,4},{6,7},{7,6},{8,9},{9,8},{10,11... | collective-permute-start | bytes 811016 | tf_op jit(solution)/shard_map/ppermute | solution.py:312
  15.0 10.0 %collective-permute-start.1 = (bf16[528,256]{1,0:T(8,128)(2,1)S(1)}, bf16[528,256]{1,0:T(8,128)(2,1)S(1)}, u32[]{:S(2)}, u32[]{:S(2)}) collective-permute-start(bf16[528,256]{1,0:T(8,128)(2,1)S(1)} %collective-permute-done.refs_4_), channel_id=1, source_target_pairs={{0,0},{2,2},{4,8},{6,10},{8,12},{10,14},{12,4},{14,6},{1,1},{3,3},... | collective-permute-start | bytes 811016 | tf_op jit(solution)/shard_map/ppermute | solution.py:319
  17.0 12.0 %collective-permute-start.4 = (bf16[528,256]{1,0:T(8,128)(2,1)S(1)}, bf16[528,256]{1,0:T(8,128)(2,1)S(1)}, u32[]{:S(2)}, u32[]{:S(2)}) collective-permute-start(bf16[528,256]{1,0:T(8,128)(2,1)S(1)} %collective-permute-done.refs_4_), channel_id=1, source_target_pairs={{0,0},{2,2},{4,6},{6,4},{8,10},{10,8},{12,14},{14,12},{1,1},{3,3},... | collective-permute-start | bytes 811016 | tf_op jit(solution)/shard_map/ppermute | solution.py:315
  20.1 9.2 %collective-permute-start.9 = (bf16[528,256]{1,0:T(8,128)(2,1)S(1)}, bf16[528,256]{1,0:T(8,128)(2,1)S(1)}, u32[]{:S(2)}, u32[]{:S(2)}) collective-permute-start(bf16[528,256]{1,0:T(8,128)(2,1)S(1)} %collective-permute-done.7.refs_3_), channel_id=1, source_target_pairs={{0,1},{1,0},{2,3},{3,2},{4,5},{5,4},{6,7},{7,6},{8,9},{9,8},{10,11... | collective-permute-start | bytes 811016 | tf_op jit(solution)/shard_map/ppermute | solution.py:312
  20.8 1.6 %copy-start.1 = (bf16[256,4096]{1,0:T(8,128)(2,1)S(1)}, bf16[256,4096]{1,0:T(8,128)(2,1)}, u32[]{:S(2)}) copy-start(bf16[256,4096]{1,0:T(8,128)(2,1)} %wa_ref.1) | copy-start | bytes 6291460
  20.8 8.5 %copy-start.5 = (s32[512]{0:T(512)S(1)}, s32[512]{0:T(512)}, u32[]{:S(2)}) copy-start(s32[512]{0:T(512)} %param.10) | copy-start | bytes 6148
  22.3 18.4 %collective-permute-start.12 = (bf16[256,4096]{1,0:T(8,128)(2,1)S(1)}, bf16[256,4096]{1,0:T(8,128)(2,1)S(1)}, u32[]{:S(2)}, u32[]{:S(2)}) collective-permute-start(bf16[256,4096]{1,0:T(8,128)(2,1)S(1)} %copy-done.1), channel_id=1, source_target_pairs={{0,1},{1,0},{2,3},{3,2},{4,5},{5,4},{6,7},{7,6},{8,9},{9,8},{10,11... | collective-permute-start | bytes 6291464 | tf_op jit(solution)/shard_map/ppermute | solution.py:312
  25.0 11.6 %collective-permute-start.6 = (bf16[528,256]{1,0:T(8,128)(2,1)S(1)}, bf16[528,256]{1,0:T(8,128)(2,1)S(1)}, u32[]{:S(2)}, u32[]{:S(2)}) collective-permute-start(bf16[528,256]{1,0:T(8,128)(2,1)S(1)} %collective-permute-done.1.refs_3_), channel_id=1, source_target_pairs={{0,1},{1,0},{2,3},{3,2},{4,5},{5,4},{6,7},{7,6},{8,9},{9,8},{10,11... | collective-permute-start | bytes 811016 | tf_op jit(solution)/shard_map/ppermute | solution.py:312
  25.8 10.0 %collective-permute-start.2 = (bf16[528,256]{1,0:T(8,128)(2,1)S(1)}, bf16[528,256]{1,0:T(8,128)(2,1)S(1)}, u32[]{:S(2)}, u32[]{:S(2)}) collective-permute-start(bf16[528,256]{1,0:T(8,128)(2,1)S(1)} %collective-permute-done.1.refs_3_), channel_id=1, source_target_pairs={{0,0},{2,2},{4,4},{6,6},{8,10},{10,8},{12,14},{14,12},{1,1},{3,3},... | collective-permute-start | bytes 811016 | tf_op jit(solution)/shard_map/ppermute | solution.py:315
  28.9 7.6 %collective-permute-start.5 = (bf16[528,256]{1,0:T(8,128)(2,1)S(1)}, bf16[528,256]{1,0:T(8,128)(2,1)S(1)}, u32[]{:S(2)}, u32[]{:S(2)}) collective-permute-start(bf16[528,256]{1,0:T(8,128)(2,1)S(1)} %collective-permute-done.4.refs_2_), channel_id=1, source_target_pairs={{0,1},{1,0},{2,3},{3,2},{4,5},{5,4},{6,7},{7,6},{8,9},{9,8},{10,11... | collective-permute-start | bytes 811016 | tf_op jit(solution)/shard_map/ppermute | solution.py:312
  35.8 2.2 %collective-permute-start.3 = (bf16[528,256]{1,0:T(8,128)(2,1)S(1)}, bf16[528,256]{1,0:T(8,128)(2,1)S(1)}, u32[]{:S(2)}, u32[]{:S(2)}) collective-permute-start(bf16[528,256]{1,0:T(8,128)(2,1)S(1)} %collective-permute-done.2.refs_2_), channel_id=1, source_target_pairs={{0,1},{1,0},{2,3},{3,2},{4,5},{5,4},{6,7},{7,6},{8,9},{9,8},{10,11... | collective-permute-start | bytes 811016 | tf_op jit(solution)/shard_map/ppermute | solution.py:312
  38.0 2.7 %copy-start.2 = (s32[512,32]{0,1:T(8,128)S(1)}, s32[512,32]{0,1:T(8,128)}, u32[]{:S(2)}) copy-start(s32[512,32]{0,1:T(8,128)} %param.14) | copy-start | bytes 196612
  38.0 2.7 %copy-start.3 = (s32[512,32]{0,1:T(8,128)S(1)}, s32[512,32]{0,1:T(8,128)}, u32[]{:S(2)}) copy-start(s32[512,32]{0,1:T(8,128)} %param.15) | copy-start | bytes 196612
  38.0 2.7 %copy-start = (bf16[512,4096]{1,0:T(8,128)(2,1)S(1)}, bf16[512,4096]{1,0:T(8,128)(2,1)}, u32[]{:S(2)}) copy-start(bf16[512,4096]{1,0:T(8,128)(2,1)} %x_ref.3) | copy-start | bytes 12582916
  39.1 1.6 %collective-permute-start.11 = (bf16[512,256]{1,0:T(8,128)(2,1)S(1)}, bf16[512,256]{1,0:T(8,128)(2,1)S(1)}, u32[]{:S(2)}, u32[]{:S(2)}) collective-permute-start(bf16[512,256]{1,0:T(8,128)(2,1)S(1)} %attend_last.1.a_ref), channel_id=1, source_target_pairs={{0,1},{1,0},{2,3},{3,2},{4,5},{5,4},{6,7},{7,6},{8,9},{9,8},{10,11... | collective-permute-start | bytes 786440 | tf_op jit(solution)/shard_map/ppermute | solution.py:312

commit v5 on v4

--- a/solution.py
+++ b/solution.py
@@ -105,7 +105,7 @@
         ],
         compiler_params=pltpu.CompilerParams(vmem_limit_bytes=24 * MIB),
         cost_estimate=pl.CostEstimate(
-            flops=40 * rows * width * cols, bytes_accessed=4 * rows * width + 2 * width * cols, transcendentals=0
+            flops=2 * rows * width * cols, bytes_accessed=4 * rows * width + 2 * width * cols, transcendentals=0
         ),
         name="norm_kv",
     )(in_hbm(tokens), in_hbm(gain.reshape(1, width)), in_hbm(w_keyval), in_hbm(segments.reshape(1, rows)))
@@ -127,7 +127,7 @@
         out_shape=jax.ShapeDtypeStruct((rows, cols), jnp.bfloat16),
         compiler_params=pltpu.CompilerParams(vmem_limit_bytes=20 * MIB),
         cost_estimate=pl.CostEstimate(
-            flops=20 * rows * width * cols, bytes_accessed=2 * rows * width + 2 * width * cols, transcendentals=0
+            flops=2 * rows * width * cols, bytes_accessed=2 * rows * width + 2 * width * cols, transcendentals=0
         ),
         name="project_query",
     )(normed, w_query)
@@ -147,7 +147,6 @@
     tile = rows // 2
     part = lax.axis_index("tp")
     place = lax.axis_index("seq")
-    odd = lax.rem(place, 2)
 
     for slot in range(blocks):
         for value in range(2):
@@ -166,12 +165,11 @@
         pltpu.make_async_copy(mine[slot].at[pl.ds(0, rows)], values.at[slot], sems.at[1, slot]).wait()
         pltpu.make_async_copy(mine[slot].at[pl.ds(rows, SEG_ROWS)], segs.at[slot], sems.at[2, slot]).wait()
     key_segs = []
-    for slot, kind in enumerate(plan):
+    for slot, (back, _) in enumerate(plan):
         packed = segs[slot].astype(jnp.float32)
         key_seg = jnp.concatenate([packed[0:1, :], packed[8:9, :]], axis=1)
-        if kind != "own":
-            back = jnp.where(odd == 1, kind[1], kind[0])
-            key_seg = jnp.where((back > 0) & (place >= back), key_seg, -1.0)
+        if back > 0:
+            key_seg = jnp.where(place >= back, key_seg, -1.0)
         key_segs.append(key_seg)
 
     for start in range(0, rows, tile):
@@ -179,16 +177,16 @@
         query = q_ref[span, :]
         best = None if first else state_ref[span, HD:HD + LANES]
         bounds = []
-        for slot, kind in enumerate(plan):
+        for slot, (back, furthest) in enumerate(plan):
             low, high = 0, rows
-            if kind == "own":
+            if back == 0:
                 high = start + tile
-            elif kind[2]:
+            elif furthest:
                 low = start
             bounds.append((low, high))
             raw = lax.dot_general(query, keys[slot, low:high, :], NT, preferred_element_type=jnp.float32)
             allowed = key_segs[slot][:, low:high] == own_seg[span, :]
-            if kind == "own":
+            if back == 0:
                 row_pos = start + lax.broadcasted_iota(jnp.int32, raw.shape, 0)
                 allowed = allowed & (lax.broadcasted_iota(jnp.int32, raw.shape, 1) <= row_pos)
             masked = jnp.where(allowed, raw, NEG)
@@ -245,7 +243,7 @@
         ],
         compiler_params=pltpu.CompilerParams(vmem_limit_bytes=(12 + 2 * blocks) * MIB),
         cost_estimate=pl.CostEstimate(
-            flops=80 * rows * rows * blocks * HD, bytes_accessed=4 * rows * blocks * HD, transcendentals=rows * rows * blocks
+            flops=4 * rows * rows * blocks * HD, bytes_accessed=4 * rows * blocks * HD, transcendentals=rows * rows * blocks
         ),
         name="attend_last" if last else "attend_first" if first else "attend_more",
     )(*operands)
@@ -311,33 +309,32 @@
     def swap_cores(x):
         return lax.ppermute(x, "tp", [(0, 1), (1, 0)])
 
-    def swap_pair(x, first):
-        return lax.ppermute(x, "seq", [(i, i ^ 1 if i >= first else i) for i in range(seq_size)])
-
-    def shift(x, first):
-        cycle = seq_size - first
-        return lax.ppermute(x, "seq", [(i, first + (i - first + 2) % cycle if i >= first else i) for i in range(seq_size)])
+    def shift(x, step):
+        return lax.ppermute(x, "seq", [(i, (i + step) % seq_size) for i in range(seq_size)])
 
     w_other = swap_cores(w_out)
     message, normed = norm_kv(tokens, gain, w_keyval, segments)
-    held = shift(message, 0)
-    pair = swap_pair(message, 0)
     query = project_query(normed, w_query)
+    held, query = lax.optimization_barrier((shift(message, 2), query))
+    odd = lax.rem(lax.axis_index("seq"), 2) == 1
+    beside = lax.ppermute(jnp.where(odd, held, message), "seq", [(i, i ^ 1) for i in range(seq_size)])
+    parts = [[(0, message), (2, held)], [(1, beside)]]
+    for back in range(2, window, 2):
+        parts[-1].append((back + 1, shift(held, 1)))
+        held = shift(held, 2)
+        if back + 2 < window:
+            parts[-1].append((back + 2, held))
+        else:
+            parts.append([(window, held)])
     state = None
-    mine, plan = [message, pair], ["own", (0, 1, False)]
-    for k in range(1, window // 2 + 1):
-        mine.append(held)
-        plan.append((2 * k, 2 * k, 2 * k == window))
-        beside = swap_pair(held, 2 * k)
-        if k < window // 2:
-            held = shift(held, 2 * k)
-        if k == 1 or k == window // 2:
-            state = attend(query, segments, plan, mine, [swap_cores(m) for m in mine], state, False)
-            mine, plan = [], []
-        mine.append(beside)
-        plan.append((2 * k - 1, 2 * k + 1 if k < window // 2 else 0, False))
-    attended = attend(query, segments, plan, mine, [swap_cores(m) for m in mine], state, True)
-    return project_out(attended, swap_cores(attended), w_out, w_other, tokens, sum_exps, out_exps)
+    for number, blocks in enumerate(parts):
+        plan = [(back, back == window) for back, _ in blocks]
+        mine = [block for _, block in blocks]
+        if number == len(parts) - 1:
+            mine[0], early = lax.optimization_barrier((mine[0], early))
+        early = state
+        state = attend(query, segments, plan, mine, [swap_cores(m) for m in mine], state, number == len(parts) - 1)
+    return project_out(state, swap_cores(state), w_out, w_other, tokens, sum_exps, out_exps)
 
 
 def solution(mesh):

time: 48 us -> 49.3 us (1.027)
  the two profiles are of different devices: /device:TPU:25 before, /device:TPU:0 now
where the time goes in v5:
time: 49.3 us; the launch traced here: 49.1 us
  Pallas kernels  19.7 us (40%)
  waiting for transfers between devices  18.6 us (38%)
  starting transfers between devices  6.48 us (13%)
  local copies, waits for them, and re-layouts  4.23 us (9%)
    ppermute x1, waiting for transfers between devices, on_device(): lax.ppermute(jnp.where(odd, held, message), 'seq', [(i, i ^ 1) for i in r...  12.1 us
    pallas_call x1, Pallas kernels, project_out(): pl.pallas_call(output_kernel, grid=(steps,), in_specs=[whole, whole, weig...  7.77 us
    pallas_call x1, Pallas kernels, norm_kv(): pl.pallas_call(norm_kv_kernel, in_specs=[hbm] * 4, out_specs=[vmem, vmem]...  6.14 us
    ppermute x3, waiting for transfers between devices, shift(): lax.ppermute(x, 'seq', [(i, (i + step) % seq_size) for i in range(seq_siz...  5.32 us
    pallas_call x3, Pallas kernels, attend(): pl.pallas_call(functools.partial(attend_kernel, plan, first, last), in_sp...  4.33 us
    unnamed x16, local copies, waits for them, and re-layouts  4.23 us
    ppermute x3, starting transfers between devices, shift(): lax.ppermute(x, 'seq', [(i, (i + step) % seq_size) for i in range(seq_siz...  3.08 us
    ppermute x7, starting transfers between devices, swap_cores(): return lax.ppermute(x, 'tp', [(0, 1), (1, 0)])  1.81 us
  transfers between devices with their start and end apart: 11, of which 3 were waited for; matrix products, arithmetic and copies ran while one was open for 0% of the time, Pallas kernels for 24%

profile of v5, /device:TPU:0, one launch (start us, length us, event | category | flops | bytes accessed | tf_op | source)
XLA Modules:
  0.0 49.1 jit_solution(9638144612222746964)
XLA Ops:
  0.0 0.5 collective-permute-start.10
  0.5 6.1 %norm_kv.1 = (bf16[528,256]{1,0:T(8,128)(2,1)S(1)}, bf16[512,4096]{1,0:T(8,128)(2,1)S(1)}) custom-call(bf16[512,4096]{1,0:T(8,128)(2,1)} %x_ref.3, f32[1,4096]{1,0:T(1,128)} %bitcast.10, bf16[4096,256]{1,0:T(8,128)(2,1)} %w_ref.2, s32[1,512]{1,0:T(1,128)} %bitcast.6), custom_call_target="tpu_custom_call" | custom-call | flops 1073741824 | bytes 10485760 | tf_op jit(solution)/shard_map/norm_kv/pallas_call | solution.py:94
  6.6 0.0 copy-start.1
  6.6 2.0 %copy-done.1 = bf16[512,4096]{1,0:T(8,128)(2,1)} copy-done((bf16[512,4096]{1,0:T(8,128)(2,1)}, bf16[512,4096]{1,0:T(8,128)(2,1)S(1)}, u32[]{:S(2)}) %copy-start.1) | copy-done | bytes 4194328
  8.6 2.6 %collective-permute-start = (bf16[528,256]{1,0:T(8,128)(2,1)S(1)}, bf16[528,256]{1,0:T(8,128)(2,1)S(1)}, u32[]{:S(2)}, u32[]{:S(2)}) collective-permute-start(bf16[528,256]{1,0:T(8,128)(2,1)S(1)} %get-tuple-element.10.refs_2_), channel_id=1, source_target_pairs={{0,4},{2,6},{4,8},{6,10},{8,12},{10,14},{12,0},{14,2},{1,5},{3,7},... | collective-permute-start | bytes 811016 | tf_op jit(solution)/shard_map/ppermute | solution.py:313
  11.2 0.2 collective-permute-start.2
  11.4 2.2 %copy-done.2 = bf16[512,4096]{1,0:T(8,128)(2,1)S(1)} copy-done((bf16[512,4096]{1,0:T(8,128)(2,1)S(1)}, bf16[512,4096]{1,0:T(8,128)(2,1)}, u32[]{:S(2)}) %copy-start.2) | copy-done | bytes 4194328
  13.6 1.4 %project_query.1.refs_0_ = bf16[512,256]{1,0:T(8,128)(2,1)S(1)} custom-call(bf16[512,4096]{1,0:T(8,128)(2,1)S(1)} %copy-done.2, bf16[4096,256]{1,0:T(8,128)(2,1)S(1)} %copy-done.3), custom_call_target="tpu_custom_call" | custom-call | flops 1073741824 | bytes 6291456 | tf_op jit(solution)/shard_map/project_query/pallas_call | solution.py:122
  15.1 5.3 %collective-permute-done.refs_3_ = bf16[528,256]{1,0:T(8,128)(2,1)S(1)} collective-permute-done((bf16[528,256]{1,0:T(8,128)(2,1)S(1)}, bf16[528,256]{1,0:T(8,128)(2,1)S(1)}, u32[]{:S(2)}, u32[]{:S(2)}) %collective-permute-start) | collective-permute-done | bytes 270368 | tf_op jit(solution)/shard_map/ppermute | solution.py:313
  20.4 1.6 %collective-permute-start.5 = (bf16[528,256]{1,0:T(8,128)(2,1)S(1)}, bf16[528,256]{1,0:T(8,128)(2,1)S(1)}, u32[]{:S(2)}, u32[]{:S(2)}) collective-permute-start(bf16[528,256]{1,0:T(8,128)(2,1)S(1)} %broadcast_select_fusion), channel_id=1, source_target_pairs={{0,2},{2,0},{4,6},{6,4},{8,10},{10,8},{12,14},{14,12},{1,3},{3,1},... | collective-permute-start | bytes 811016 | tf_op jit(solution)/shard_map/ppermute | solution.py:320
  22.0 0.5 %collective-permute-start.6 = (bf16[528,256]{1,0:T(8,128)(2,1)S(1)}, bf16[528,256]{1,0:T(8,128)(2,1)S(1)}, u32[]{:S(2)}, u32[]{:S(2)}) collective-permute-start(bf16[528,256]{1,0:T(8,128)(2,1)S(1)} %collective-permute-done.refs_3_), channel_id=1, source_target_pairs={{0,2},{2,4},{4,6},{6,8},{8,10},{10,12},{12,14},{14,0},{1,3},{3,5},... | collective-permute-start | bytes 811016 | tf_op jit(solution)/shard_map/ppermute | solution.py:313
  22.5 12.1 %collective-permute-done.5.refs_2_ = bf16[528,256]{1,0:T(8,128)(2,1)S(1)} collective-permute-done((bf16[528,256]{1,0:T(8,128)(2,1)S(1)}, bf16[528,256]{1,0:T(8,128)(2,1)S(1)}, u32[]{:S(2)}, u32[]{:S(2)}) %collective-permute-start.5) | collective-permute-done | bytes 270368 | tf_op jit(solution)/shard_map/ppermute | solution.py:320
  34.6 0.0 collective-permute-start.7
  34.6 0.5 %collective-permute-start.8 = (bf16[528,256]{1,0:T(8,128)(2,1)S(1)}, bf16[528,256]{1,0:T(8,128)(2,1)S(1)}, u32[]{:S(2)}, u32[]{:S(2)}) collective-permute-start(bf16[528,256]{1,0:T(8,128)(2,1)S(1)} %collective-permute-done.6.refs_3_), channel_id=1, source_target_pairs={{0,1},{1,0},{2,3},{3,2},{4,5},{5,4},{6,7},{7,6},{8,9},{9,8},{10,11... | collective-permute-start | bytes 811016 | tf_op jit(solution)/shard_map/ppermute | solution.py:310
  35.1 1.7 %attend_first.1.refs_6_ = f32[512,512]{1,0:T(8,128)S(1)} custom-call(bf16[512,256]{1,0:T(8,128)(2,1)S(1)} %project_query.1.refs_0_, s32[1,512]{1,0:T(1,128)S(1)} %bitcast.7, bf16[528,256]{1,0:T(8,128)(2,1)S(1)} %get-tuple-element.10.refs_2_, bf16[528,256]{1,0:T(8,128)(2,1)S(1)} %collective-permute-done.refs_3_, ...), custom_call_target="tpu_custom_call" | custom-call | flops 536870912 | bytes 1048576 | tf_op jit(solution)/shard_map/attend_first/pallas_call | solution.py:232
  36.8 0.0 copy-start
  36.8 0.0 copy-start.5
  36.8 0.0 copy-start.6
  36.8 0.1 collective-permute-start.4
  36.9 1.6 %attend_more.1.refs_4_ = f32[512,512]{1,0:T(8,128)S(1)} custom-call(bf16[512,256]{1,0:T(8,128)(2,1)S(1)} %project_query.1.refs_0_, s32[1,512]{1,0:T(1,128)S(1)} %bitcast.8, bf16[528,256]{1,0:T(8,128)(2,1)S(1)} %collective-permute-done.5.refs_2_, bf16[528,256]{1,0:T(8,128)(2,1)S(1)} %collective-permute-done.6.refs_3_, ...), custom_call_target="tpu_custom_call" | custom-call | flops 536870912 | bytes 1048576 | tf_op jit(solution)/shard_map/attend_more/pallas_call | solution.py:232
  38.5 1.1 %attend_last.1.a_ref = bf16[512,256]{1,0:T(8,128)(2,1)S(1)} custom-call(bf16[512,256]{1,0:T(8,128)(2,1)S(1)} %project_query.1.refs_0_, s32[1,512]{1,0:T(1,128)S(1)} %bitcast.9, bf16[528,256]{1,0:T(8,128)(2,1)S(1)} %collective-permute-done.1.refs_2_, bf16[528,256]{1,0:T(8,128)(2,1)S(1)} %collective-permute-done.4.refs_3_, f32[512,512]{1,0:T(8,128)S(1)} %attend_more.1.refs_4_), custom_call_target="tpu_custom_call" | custom-call | flops 268435456 | bytes 524288 | tf_op jit(solution)/shard_map/attend_last/pallas_call | solution.py:232
  39.6 0.5 %collective-permute-start.9 = (bf16[512,256]{1,0:T(8,128)(2,1)S(1)}, bf16[512,256]{1,0:T(8,128)(2,1)S(1)}, u32[]{:S(2)}, u32[]{:S(2)}) collective-permute-start(bf16[512,256]{1,0:T(8,128)(2,1)S(1)} %attend_last.1.a_ref), channel_id=1, source_target_pairs={{0,1},{1,0},{2,3},{3,2},{4,5},{5,4},{6,7},{7,6},{8,9},{9,8},{10,11... | collective-permute-start | bytes 786440 | tf_op jit(solution)/shard_map/ppermute | solution.py:310
  40.1 1.2 %collective-permute-done.9.b_ref = bf16[512,256]{1,0:T(8,128)(2,1)S(1)} collective-permute-done((bf16[512,256]{1,0:T(8,128)(2,1)S(1)}, bf16[512,256]{1,0:T(8,128)(2,1)S(1)}, u32[]{:S(2)}, u32[]{:S(2)}) %collective-permute-start.9) | collective-permute-done | bytes 262176 | tf_op jit(solution)/shard_map/ppermute | solution.py:310
  41.3 7.8 %project_out.1 = bf16[512,4096]{1,0:T(8,128)(2,1)} custom-call(bf16[512,256]{1,0:T(8,128)(2,1)S(1)} %attend_last.1.a_ref, bf16[512,256]{1,0:T(8,128)(2,1)S(1)} %collective-permute-done.9.b_ref, bf16[256,4096]{1,0:T(8,128)(2,1)S(1)} %copy-done.4, bf16[256,4096]{1,0:T(8,128)(2,1)} %collective-permute-done.10.wb_ref, bf16[512,4096]{1,0:T(8,128)(2,1)S(1)} %copy-done, ...), custom_call_target="tpu_custom_call" | custom-call | flops 2147483648 | bytes 12582912 | tf_op jit(solution)/shard_map/project_out/pallas_call | solution.py:292
  (21 shorter events, 0.1 us)
Async XLA Ops:
  0.0 41.3 %collective-permute-start.10 = (bf16[256,4096]{1,0:T(8,128)(2,1)}, bf16[256,4096]{1,0:T(8,128)(2,1)}, u32[]{:S(2)}, u32[]{:S(2)}) collective-permute-start(bf16[256,4096]{1,0:T(8,128)(2,1)} %wa_ref.1), channel_id=1, source_target_pairs={{0,1},{1,0},{2,3},{3,2},{4,5},{5,4},{6,7},{7,6},{8,9},{9,8},{10,11... | collective-permute-start | bytes 6291464 | tf_op jit(solution)/shard_map/ppermute | solution.py:310
  0.5 11.0 %copy-start.3 = (bf16[4096,256]{1,0:T(8,128)(2,1)S(1)}, bf16[4096,256]{1,0:T(8,128)(2,1)}, u32[]{:S(2)}) copy-start(bf16[4096,256]{1,0:T(8,128)(2,1)} %w_ref.3) | copy-start | bytes 6291460
  6.6 2.0 %copy-start.1 = (bf16[512,4096]{1,0:T(8,128)(2,1)}, bf16[512,4096]{1,0:T(8,128)(2,1)S(1)}, u32[]{:S(2)}) copy-start(bf16[512,4096]{1,0:T(8,128)(2,1)S(1)} %get-tuple-element.11.x_ref) | copy-start | bytes 12582916
  8.6 11.8 %collective-permute-start = (bf16[528,256]{1,0:T(8,128)(2,1)S(1)}, bf16[528,256]{1,0:T(8,128)(2,1)S(1)}, u32[]{:S(2)}, u32[]{:S(2)}) collective-permute-start(bf16[528,256]{1,0:T(8,128)(2,1)S(1)} %get-tuple-element.10.refs_2_), channel_id=1, source_target_pairs={{0,4},{2,6},{4,8},{6,10},{8,12},{10,14},{12,0},{14,2},{1,5},{3,7},... | collective-permute-start | bytes 811016 | tf_op jit(solution)/shard_map/ppermute | solution.py:313
  11.2 11.3 %collective-permute-start.2 = (bf16[528,256]{1,0:T(8,128)(2,1)S(1)}, bf16[528,256]{1,0:T(8,128)(2,1)S(1)}, u32[]{:S(2)}, u32[]{:S(2)}) collective-permute-start(bf16[528,256]{1,0:T(8,128)(2,1)S(1)} %get-tuple-element.10.refs_2_), channel_id=1, source_target_pairs={{0,1},{1,0},{2,3},{3,2},{4,5},{5,4},{6,7},{7,6},{8,9},{9,8},{10,11... | collective-permute-start | bytes 811016 | tf_op jit(solution)/shard_map/ppermute | solution.py:310
  11.4 2.2 %copy-start.2 = (bf16[512,4096]{1,0:T(8,128)(2,1)S(1)}, bf16[512,4096]{1,0:T(8,128)(2,1)}, u32[]{:S(2)}) copy-start(bf16[512,4096]{1,0:T(8,128)(2,1)} %copy-done.1) | copy-start | bytes 12582916
  13.6 21.5 %copy-start.7 = (s32[512]{0:T(512)S(1)}, s32[512]{0:T(512)}, u32[]{:S(2)}) copy-start(s32[512]{0:T(512)} %param.10) | copy-start | bytes 6148
  20.4 14.2 %collective-permute-start.5 = (bf16[528,256]{1,0:T(8,128)(2,1)S(1)}, bf16[528,256]{1,0:T(8,128)(2,1)S(1)}, u32[]{:S(2)}, u32[]{:S(2)}) collective-permute-start(bf16[528,256]{1,0:T(8,128)(2,1)S(1)} %broadcast_select_fusion), channel_id=1, source_target_pairs={{0,2},{2,0},{4,6},{6,4},{8,10},{10,8},{12,14},{14,12},{1,3},{3,1},... | collective-permute-start | bytes 811016 | tf_op jit(solution)/shard_map/ppermute | solution.py:320
  22.0 12.6 %collective-permute-start.6 = (bf16[528,256]{1,0:T(8,128)(2,1)S(1)}, bf16[528,256]{1,0:T(8,128)(2,1)S(1)}, u32[]{:S(2)}, u32[]{:S(2)}) collective-permute-start(bf16[528,256]{1,0:T(8,128)(2,1)S(1)} %collective-permute-done.refs_3_), channel_id=1, source_target_pairs={{0,2},{2,4},{4,6},{6,8},{8,10},{10,12},{12,14},{14,0},{1,3},{3,5},... | collective-permute-start | bytes 811016 | tf_op jit(solution)/shard_map/ppermute | solution.py:313
  22.5 12.6 %collective-permute-start.3 = (bf16[528,256]{1,0:T(8,128)(2,1)S(1)}, bf16[528,256]{1,0:T(8,128)(2,1)S(1)}, u32[]{:S(2)}, u32[]{:S(2)}) collective-permute-start(bf16[528,256]{1,0:T(8,128)(2,1)S(1)} %collective-permute-done.refs_3_), channel_id=1, source_target_pairs={{0,1},{1,0},{2,3},{3,2},{4,5},{5,4},{6,7},{7,6},{8,9},{9,8},{10,11... | collective-permute-start | bytes 811016 | tf_op jit(solution)/shard_map/ppermute | solution.py:310
  22.5 14.3 %collective-permute-start.1 = (bf16[528,256]{1,0:T(8,128)(2,1)S(1)}, bf16[528,256]{1,0:T(8,128)(2,1)S(1)}, u32[]{:S(2)}, u32[]{:S(2)}) collective-permute-start(bf16[528,256]{1,0:T(8,128)(2,1)S(1)} %collective-permute-done.refs_3_), channel_id=1, source_target_pairs={{0,4},{2,6},{4,8},{6,10},{8,12},{10,14},{12,0},{14,2},{1,5},{3,7},... | collective-permute-start | bytes 811016 | tf_op jit(solution)/shard_map/ppermute | solution.py:313
  34.6 2.3 %collective-permute-start.7 = (bf16[528,256]{1,0:T(8,128)(2,1)S(1)}, bf16[528,256]{1,0:T(8,128)(2,1)S(1)}, u32[]{:S(2)}, u32[]{:S(2)}) collective-permute-start(bf16[528,256]{1,0:T(8,128)(2,1)S(1)} %collective-permute-done.5.refs_2_), channel_id=1, source_target_pairs={{0,1},{1,0},{2,3},{3,2},{4,5},{5,4},{6,7},{7,6},{8,9},{9,8},{10,11... | collective-permute-start | bytes 811016 | tf_op jit(solution)/shard_map/ppermute | solution.py:310
  34.6 2.3 %collective-permute-start.8 = (bf16[528,256]{1,0:T(8,128)(2,1)S(1)}, bf16[528,256]{1,0:T(8,128)(2,1)S(1)}, u32[]{:S(2)}, u32[]{:S(2)}) collective-permute-start(bf16[528,256]{1,0:T(8,128)(2,1)S(1)} %collective-permute-done.6.refs_3_), channel_id=1, source_target_pairs={{0,1},{1,0},{2,3},{3,2},{4,5},{5,4},{6,7},{7,6},{8,9},{9,8},{10,11... | collective-permute-start | bytes 811016 | tf_op jit(solution)/shard_map/ppermute | solution.py:310
  35.1 6.2 %copy-start.4 = (bf16[256,4096]{1,0:T(8,128)(2,1)S(1)}, bf16[256,4096]{1,0:T(8,128)(2,1)}, u32[]{:S(2)}) copy-start(bf16[256,4096]{1,0:T(8,128)(2,1)} %wa_ref.1) | copy-start | bytes 6291460
  36.8 4.6 %copy-start = (bf16[512,4096]{1,0:T(8,128)(2,1)S(1)}, bf16[512,4096]{1,0:T(8,128)(2,1)}, u32[]{:S(2)}) copy-start(bf16[512,4096]{1,0:T(8,128)(2,1)} %x_ref.3) | copy-start | bytes 12582916
  36.8 4.5 %copy-start.5 = (s32[512,32]{0,1:T(8,128)S(1)}, s32[512,32]{0,1:T(8,128)}, u32[]{:S(2)}) copy-start(s32[512,32]{0,1:T(8,128)} %param.14) | copy-start | bytes 196612
  36.8 4.5 %copy-start.6 = (s32[512,32]{0,1:T(8,128)S(1)}, s32[512,32]{0,1:T(8,128)}, u32[]{:S(2)}) copy-start(s32[512,32]{0,1:T(8,128)} %param.15) | copy-start | bytes 196612
  36.8 1.7 %collective-permute-start.4 = (bf16[528,256]{1,0:T(8,128)(2,1)S(1)}, bf16[528,256]{1,0:T(8,128)(2,1)S(1)}, u32[]{:S(2)}, u32[]{:S(2)}) collective-permute-start(bf16[528,256]{1,0:T(8,128)(2,1)S(1)} %collective-permute-done.1.refs_2_), channel_id=1, source_target_pairs={{0,1},{1,0},{2,3},{3,2},{4,5},{5,4},{6,7},{7,6},{8,9},{9,8},{10,11... | collective-permute-start | bytes 811016 | tf_op jit(solution)/shard_map/ppermute | solution.py:310
  39.6 1.7 %collective-permute-start.9 = (bf16[512,256]{1,0:T(8,128)(2,1)S(1)}, bf16[512,256]{1,0:T(8,128)(2,1)S(1)}, u32[]{:S(2)}, u32[]{:S(2)}) collective-permute-start(bf16[512,256]{1,0:T(8,128)(2,1)S(1)} %attend_last.1.a_ref), channel_id=1, source_target_pairs={{0,1},{1,0},{2,3},{3,2},{4,5},{5,4},{6,7},{7,6},{8,9},{9,8},{10,11... | collective-permute-start | bytes 786440 | tf_op jit(solution)/shard_map/ppermute | solution.py:310

commit v6 on v5

v6 whole, which is shorter than its diff:
```python
import functools

import jax
import jax.numpy as jnp
from jax import lax
from jax.experimental import pallas as pl
from jax.experimental.pallas import tpu as pltpu
from jax.sharding import PartitionSpec as P

HD = 256
LANES = 128
SEG_ROWS = 16
LIMIT = 448.0
MIN_EXP = -9
NEG = -1e30
MIB = 1024 * 1024
NT = (((1,), (1,)), ((), ()))
FACTOR = HD ** (-0.5) * 1.4426950408889634


def norm_kv_kernel(x_ref, gain_hbm, w_ref, seg_hbm, msg_ref, normed_ref, xs, ws, gain_ref, seg_ref, sems):
    rows, width = xs.shape
    tile, part = rows // 2, rows // 4

    def tokens_copy(i):
        return pltpu.make_async_copy(x_ref.at[pl.ds(i * part, part)], xs.at[pl.ds(i * part, part)], sems.at[i])

    def weights_copy():
        return pltpu.make_async_copy(w_ref, ws, sems.at[4])

    def gain_copy():
        return pltpu.make_async_copy(gain_hbm, gain_ref, sems.at[5])

    def segments_copy():
        return pltpu.make_async_copy(seg_hbm, seg_ref, sems.at[6])

    tokens_copy(0).start()
    tokens_copy(1).start()
    gain_copy().start()
    segments_copy().start()
    weights_copy().start()
    tokens_copy(2).start()
    tokens_copy(3).start()
    def wide(first, count, start):
        return xs[first:first + count, start:start + LANES].astype(jnp.float32)

    ones = jnp.ones((width, LANES), jnp.bfloat16)

    def stats(first):
        total = jnp.dot(xs[first:first + part, :], ones, preferred_element_type=jnp.float32)
        mean = total * (1.0 / width)
        square = jnp.zeros((part, LANES), jnp.float32)
        for start in range(0, width, LANES):
            center = wide(first, part, start) - mean
            square = square + center * center
        spread = jnp.sum(square, axis=1, keepdims=True) * (1.0 / width)
        return mean, jnp.broadcast_to(lax.rsqrt(spread + 1e-05), (part, LANES))

    for first in range(0, rows, tile):
        halves = []
        for at in range(first, first + tile, part):
            tokens_copy(at // part).wait()
            halves.append(stats(at))
        mean = jnp.concatenate([h[0] for h in halves], axis=0)
        scale = jnp.concatenate([h[1] for h in halves], axis=0)
        if first == 0:
            gain_copy().wait()
            weights_copy().wait()
        kv = jnp.zeros((tile, ws.shape[1]), jnp.float32)
        span = slice(first, first + tile)
        for start in range(0, width, HD):
            for at in (start, start + LANES):
                normed = (wide(first, tile, at) - mean) * scale * gain_ref[:, at:at + LANES]
                normed_ref[span, at:at + LANES] = normed.astype(jnp.bfloat16)
            kv = kv + jnp.dot(
                normed_ref[span, start:start + HD], ws[start:start + HD, :], preferred_element_type=jnp.float32
            )
        msg_ref[span, :] = kv.astype(jnp.bfloat16)
    segments_copy().wait()
    seg = seg_ref[...].astype(jnp.float32)
    low = jnp.broadcast_to(seg[:, :HD], (8, HD))
    high = jnp.broadcast_to(seg[:, HD:], (8, HD))
    msg_ref[rows:, :] = jnp.concatenate([low, high], axis=0).astype(jnp.bfloat16)


def in_hbm(x):
    return pltpu.with_memory_space_constraint(x, pltpu.HBM)


def in_vmem(x):
    return pltpu.with_memory_space_constraint(x, pltpu.VMEM)


def norm_kv(tokens, gain, w_keyval, segments):
    rows, width = tokens.shape
    cols = w_keyval.shape[1]
    vmem, hbm = pl.BlockSpec(memory_space=pltpu.VMEM), pl.BlockSpec(memory_space=pltpu.HBM)
    return pl.pallas_call(
        norm_kv_kernel,
        in_specs=[hbm] * 4,
        out_specs=[vmem, vmem],
        out_shape=[pltpu.VMEM((rows + SEG_ROWS, cols), jnp.bfloat16), pltpu.VMEM((rows, width), jnp.bfloat16)],
        scratch_shapes=[
            pltpu.VMEM((rows, width), jnp.bfloat16),
            pltpu.VMEM((width, cols), jnp.bfloat16),
            pltpu.VMEM((1, width), jnp.float32),
            pltpu.VMEM((1, rows), jnp.int32),
            pltpu.SemaphoreType.DMA((7,)),
        ],
        compiler_params=pltpu.CompilerParams(vmem_limit_bytes=24 * MIB),
        cost_estimate=pl.CostEstimate(
            flops=2 * rows * width * cols, bytes_accessed=4 * rows * width + 2 * width * cols, transcendentals=0
        ),
        name="norm_kv",
    )(in_hbm(tokens), in_hbm(gain.reshape(1, width)), in_hbm(w_keyval), in_hbm(segments.reshape(1, rows)))


def query_kernel(x_ref, w_ref, out_ref):
    out_ref[...] = jnp.dot(x_ref[...], w_ref[...], preferred_element_type=jnp.float32).astype(jnp.bfloat16)


def project_query(normed, w_query):
    rows, width = normed.shape
    cols = w_query.shape[1]
    vmem = pl.BlockSpec(memory_space=pltpu.VMEM)
    return pl.pallas_call(
        query_kernel,
        in_specs=[vmem, vmem],
        out_specs=vmem,
        out_shape=pltpu.VMEM((rows, cols), jnp.bfloat16),
        compiler_params=pltpu.CompilerParams(vmem_limit_bytes=8 * MIB),
        cost_estimate=pl.CostEstimate(
            flops=2 * rows * width * cols, bytes_accessed=2 * rows * width + 2 * width * cols, transcendentals=0
        ),
        name="project_query",
    )(in_vmem(normed), in_vmem(w_query))


def attend_kernel(plan, first, last, *refs):
    blocks = len(plan)
    q_ref, seg_ref = refs[:2]
    mine, other = refs[2:2 + blocks], refs[2 + blocks:2 + 2 * blocks]
    refs = refs[2 + 2 * blocks:]
    state_ref = None
    if not first:
        state_ref, refs = refs[0], refs[1:]
    out_ref, scores = refs
    rows = q_ref.shape[0]
    tile = rows // 2
    part = lax.axis_index("tp")
    place = lax.axis_index("seq")

    def finish(span, weighted, total):
        out_ref[span, :] = (weighted / jnp.sum(total, axis=1, keepdims=True)).astype(jnp.bfloat16)

    def update(count, keys, values):
        own_seg = jnp.transpose(jnp.broadcast_to(seg_ref[...].astype(jnp.float32), (8, rows)))[:, 0:1]
        key_segs = []
        for slot in range(count):
            packed = mine[slot][rows:, :].astype(jnp.float32)
            key_segs.append(jnp.concatenate([packed[0:1, :], packed[8:9, :]], axis=1))
        for start in range(0, rows, tile):
            span = slice(start, start + tile)
            query = q_ref[span, :]
            best = None if first else state_ref[span, HD:HD + LANES]
            bounds = []
            for slot, (back, furthest) in enumerate(plan[:count]):
                low, high = 0, rows
                if back == 0:
                    high = start + tile
                elif furthest:
                    low = start
                bounds.append((low, high))
                raw = lax.dot_general(query, keys[slot][low:high, :], NT, preferred_element_type=jnp.float32)
                allowed = key_segs[slot][:, low:high] == own_seg[span, :]
                if back == 0:
                    row_pos = start + lax.broadcasted_iota(jnp.int32, raw.shape, 0)
                    allowed = allowed & (lax.broadcasted_iota(jnp.int32, raw.shape, 1) <= row_pos)
                masked = jnp.where(allowed, raw, NEG)
                scores[slot, :, low:high] = masked
                for at in range(0, high - low, LANES):
                    piece = masked[:, at:at + LANES]
                    best = piece if best is None else jnp.maximum(best, piece)
            top = jnp.broadcast_to(jnp.max(best, axis=1, keepdims=True), (tile, LANES))
            if first:
                total = jnp.zeros((tile, LANES), jnp.float32)
                weighted = jnp.zeros((tile, HD), jnp.float32)
            else:
                shrink = jnp.exp2((state_ref[span, HD:HD + LANES] - top) * FACTOR)
                total = state_ref[span, HD + LANES:] * shrink
                weighted = state_ref[span, :HD] * jnp.concatenate([shrink, shrink], axis=1)
            for slot in range(count):
                low, high = bounds[slot]
                pieces = []
                for at in range(low, high, LANES):
                    weights = jnp.exp2((scores[slot, :, at:at + LANES] - top) * FACTOR)
                    total = total + weights
                    pieces.append(weights.astype(jnp.bfloat16))
                probs = jnp.concatenate(pieces, axis=1)
                weighted = weighted + jnp.dot(probs, values[slot][low:high, :], preferred_element_type=jnp.float32)
            if last:
                finish(span, weighted, total)
            else:
                out_ref[span, :HD] = weighted
                out_ref[span, HD:HD + LANES] = top
                out_ref[span, HD + LANES:] = total

    for count in range(1 if first else 0, blocks + 1):
        reached = place >= (plan[count - 1][0] if count > 0 else 0)
        if count < blocks:
            reached = reached & (place < plan[count][0])
        if count > 0:
            pl.when(reached & (part == 0))(functools.partial(update, count, mine, other))
            pl.when(reached & (part == 1))(functools.partial(update, count, other, mine))
        elif last:

            @pl.when(reached)
            def _():
                finish(slice(0, rows), state_ref[:, :HD], state_ref[:, HD + LANES:])


def attend(query, segments, plan, mine, other, state, last):
    rows = query.shape[0]
    blocks = len(plan)
    vmem = pl.BlockSpec(memory_space=pltpu.VMEM)
    first = state is None
    operands = [query, segments.reshape(1, rows), *mine, *other] + ([] if first else [state])
    return pl.pallas_call(
        functools.partial(attend_kernel, plan, first, last),
        in_specs=[vmem] * len(operands),
        out_specs=vmem,
        out_shape=pltpu.VMEM((rows, HD), jnp.bfloat16) if last else pltpu.VMEM((rows, HD + 2 * LANES), jnp.float32),
        scratch_shapes=[pltpu.VMEM((blocks, rows // 2, rows), jnp.float32)],
        input_output_aliases={} if first or last else {len(operands) - 1: 0},
        compiler_params=pltpu.CompilerParams(vmem_limit_bytes=12 * MIB),
        cost_estimate=pl.CostEstimate(
            flops=4 * rows * rows * blocks * HD, bytes_accessed=4 * rows * blocks * HD, transcendentals=rows * rows * blocks
        ),
        name="attend_last" if last else "attend_first" if first else "attend_more",
    )(*[in_vmem(operand) for operand in operands])


def bounds_kernel(sum_ref, out_exp_ref, sum_bound_ref, out_bound_ref):
    groups, rows = sum_ref.shape
    per = sum_bound_ref.shape[1] // groups
    for exps, bound_ref in ((sum_ref, sum_bound_ref), (out_exp_ref, out_bound_ref)):
        power = jnp.left_shift(jnp.int32(1), exps[...] - MIN_EXP).astype(jnp.float32)
        bound = jnp.transpose(power * (LIMIT * 2.0 ** MIN_EXP))
        for group in range(groups):
            wide = jnp.broadcast_to(bound[:, group:group + 1], (rows, per))
            bound_ref[:, group * per:(group + 1) * per] = wide.astype(jnp.bfloat16)


def spread_bounds(sum_exps, out_exps, width):
    rows, groups = sum_exps.shape
    vmem = pl.BlockSpec(memory_space=pltpu.VMEM)
    return pl.pallas_call(
        bounds_kernel,
        in_specs=[vmem, vmem],
        out_specs=[vmem, vmem],
        out_shape=[pltpu.VMEM((rows, width), jnp.bfloat16)] * 2,
        compiler_params=pltpu.CompilerParams(vmem_limit_bytes=8 * MIB),
        cost_estimate=pl.CostEstimate(flops=8 * rows * width, bytes_accessed=8 * rows * groups, transcendentals=0),
        name="spread_bounds",
    )(sum_exps.T, out_exps.T)


def output_kernel(a_ref, b_ref, wa_ref, wb_ref, x_ref, sum_ref, last_ref, out_ref, staged, sems):
    rows, width = x_ref.shape
    steps = sems.shape[0]
    chunk = width // steps
    tile = rows // 2

    def clip(value, bound):
        return jnp.minimum(jnp.maximum(value.astype(jnp.bfloat16), -bound), bound)

    def copy(step):
        span = pl.ds(pl.multiple_of(step * chunk, chunk), chunk)
        return pltpu.make_async_copy(staged.at[:, span], out_ref.at[:, span], sems.at[step])

    def body(step, carry):
        for at in range(0, chunk, HD):
            cols = pl.ds(pl.multiple_of(step * chunk + at, HD), HD)
            weights_a, weights_b = wa_ref[:, cols], wb_ref[:, cols]
            for start in range(0, rows, tile):
                span = slice(start, start + tile)
                term_a = jnp.dot(a_ref[span, :], weights_a, preferred_element_type=jnp.float32)
                term_b = jnp.dot(b_ref[span, :], weights_b, preferred_element_type=jnp.float32)
                bound = sum_ref[span, cols]
                quant = clip(term_a, bound).astype(jnp.float32) + clip(term_b, bound).astype(jnp.float32)
                staged[span, cols] = clip(x_ref[span, cols].astype(jnp.float32) + quant, last_ref[span, cols])
        copy(step).start()
        return carry

    lax.fori_loop(0, steps, body, 0)
    for step in range(steps):
        copy(step).wait()


def project_out(att_a, att_b, w_a, w_b, tokens, sum_bound, out_bound):
    rows, width = tokens.shape
    depth = att_a.shape[1]
    steps = 4
    vmem = pl.BlockSpec(memory_space=pltpu.VMEM)
    operands = [att_a, att_b, w_a, w_b, tokens, sum_bound, out_bound]
    return pl.pallas_call(
        output_kernel,
        in_specs=[vmem] * len(operands),
        out_specs=pl.BlockSpec(memory_space=pltpu.HBM),
        out_shape=jax.ShapeDtypeStruct((rows, width), jnp.bfloat16),
        scratch_shapes=[pltpu.VMEM((rows, width), jnp.bfloat16), pltpu.SemaphoreType.DMA((steps,))],
        compiler_params=pltpu.CompilerParams(vmem_limit_bytes=12 * MIB),
        cost_estimate=pl.CostEstimate(
            flops=4 * rows * width * depth, bytes_accessed=4 * rows * width + 4 * width * depth, transcendentals=0
        ),
        name="project_out",
    )(*[in_vmem(operand) for operand in operands])


def on_device(seq_size, tokens, gain, segments, w_query, w_keyval, w_out, sum_exps, out_exps):
    window = seq_size // 2

    def swap_cores(x):
        return lax.ppermute(x, "tp", [(0, 1), (1, 0)])

    def shift(x, step):
        return lax.ppermute(x, "seq", [(i, (i + step) % seq_size) for i in range(seq_size)])

    w_other = swap_cores(w_out)
    message, normed = norm_kv(tokens, gain, w_keyval, segments)
    query = project_query(normed, w_query)
    held, query = lax.optimization_barrier((shift(message, 2), query))
    odd = lax.rem(lax.axis_index("seq"), 2) == 1
    beside = lax.ppermute(jnp.where(odd, held, message), "seq", [(i, i ^ 1) for i in range(seq_size)])
    parts = [[(0, message), (2, held)]]
    for back in range(2, window, 2):
        step = shift(held, 1)
        held = shift(held, 2)
        parts.append([(back + 1, step)] + ([(back + 2, held)] if back + 2 < window else []))
    parts.append([(1, beside), (window, held)])
    exps = lax.optimization_barrier((sum_exps, out_exps, query))[:2]
    bounds = spread_bounds(*exps, tokens.shape[1])
    state = None
    for number, blocks in enumerate(parts):
        plan = [(back, back == window) for back, _ in blocks]
        mine = [block for _, block in blocks]
        if number == 1:
            bounds, state = early = lax.optimization_barrier((bounds, state))
        if number > 0:
            mine = [lax.optimization_barrier((block, early))[0] for block in mine]
        other = [swap_cores(m) for m in mine]
        state = attend(query, segments, plan, mine, other, state, number == len(parts) - 1)
    return project_out(state, swap_cores(state), w_out, w_other, tokens, *bounds)


def solution(mesh):
    in_specs = (
        P(("groups", "seq"), None),
        P(),
        P(("groups", "seq")),
        P(None, "tp"),
        P(None, "tp"),
        P("tp", None),
        P(("groups", "seq"), None),
        P(("groups", "seq"), None),
    )
    out_specs = P(("groups", "seq"), None)
    return jax.shard_map(
        functools.partial(on_device, mesh.shape["seq"]),
        mesh=mesh, in_specs=in_specs, out_specs=out_specs, check_vma=False,
    )
```

time: 49.3 us -> 46.3 us (0.939)
  local copies, waits for them, and re-layouts: 4.23 us -> 0.04 us
  waiting for transfers between devices: 18.6 us -> 20.3 us
  Pallas kernels: 19.7 us -> 18.8 us
    ppermute x3, waiting for transfers between devices: 5.32 us -> 13.3 us  [shift(): lax.ppermute(x, 'seq', [(i, (i + step) % seq_size) for i in range(seq_siz...]
    ppermute x1, waiting for transfers between devices: 12.1 us -> 4.22 us  [on_device(): lax.ppermute(jnp.where(odd, held, message), 'seq', [(i, i ^ 1) for i in r...]
    unnamed x16 -> x12, local copies, waits for them, and re-layouts: 4.23 us -> 0.04 us
    pallas_call x3, Pallas kernels: 4.33 us -> 1.32 us  [attend(): pl.pallas_call(functools.partial(attend_kernel, plan, first, last), in_sp...]
    pallas_call x1, Pallas kernels: 6.14 us -> 7.87 us  [norm_kv(): pl.pallas_call(norm_kv_kernel, in_specs=[hbm] * 4, out_specs=[vmem, vmem]...]
    ppermute x7, waiting for transfers between devices: 1.18 us -> 2.83 us  [swap_cores(): return lax.ppermute(x, 'tp', [(0, 1), (1, 0)])]
    ppermute x3, starting transfers between devices: 3.08 us -> 4.12 us  [shift(): lax.ppermute(x, 'seq', [(i, (i + step) % seq_size) for i in range(seq_siz...]
    ppermute x7, starting transfers between devices: 1.81 us -> 1.24 us  [swap_cores(): return lax.ppermute(x, 'tp', [(0, 1), (1, 0)])]
  transfers between devices with their start and end apart: 11 -> 11, of which waited for: 3 -> 6; matrix products, arithmetic and copies ran while one was open for 0% -> 0% of each run, Pallas kernels for 24% -> 28%
where the time goes in v6:
time: 46.3 us; the launch traced here: 46.1 us
  waiting for transfers between devices  20.3 us (44%)
  Pallas kernels  18.8 us (41%)
  starting transfers between devices  6.66 us (14%)
    ppermute x3, waiting for transfers between devices, shift(): lax.ppermute(x, 'seq', [(i, (i + step) % seq_size) for i in range(seq_siz...  13.3 us
    pallas_call x1, Pallas kernels, norm_kv(): pl.pallas_call(norm_kv_kernel, in_specs=[hbm] * 4, out_specs=[vmem, vmem]...  7.87 us
    pallas_call x1, Pallas kernels, project_out(): pl.pallas_call(output_kernel, in_specs=[vmem] * len(operands), out_specs=...  5.88 us
    ppermute x1, waiting for transfers between devices, on_device(): lax.ppermute(jnp.where(odd, held, message), 'seq', [(i, i ^ 1) for i in r...  4.22 us
    ppermute x3, starting transfers between devices, shift(): lax.ppermute(x, 'seq', [(i, (i + step) % seq_size) for i in range(seq_siz...  4.12 us
    ppermute x7, waiting for transfers between devices, swap_cores(): return lax.ppermute(x, 'tp', [(0, 1), (1, 0)])  2.83 us
    pallas_call x1, Pallas kernels, spread_bounds(): pl.pallas_call(bounds_kernel, in_specs=[vmem, vmem], out_specs=[vmem, vme...  2.48 us
    pallas_call x3, Pallas kernels, attend(): pl.pallas_call(functools.partial(attend_kernel, plan, first, last), in_sp...  1.32 us
  transfers between devices with their start and end apart: 11, of which 6 were waited for; matrix products, arithmetic and copies ran while one was open for 0% of the time, Pallas kernels for 28%

profile of v6, /device:TPU:0, one launch (start us, length us, event | category | flops | bytes accessed | tf_op | source)
XLA Modules:
  0.0 46.1 jit_solution(3832741263029379442)
XLA Ops:
  0.0 0.5 collective-permute-start.10
  0.5 7.9 %norm_kv.1 = (bf16[528,256]{1,0:T(8,128)(2,1)S(1)}, bf16[512,4096]{1,0:T(8,128)(2,1)S(1)}) custom-call(bf16[512,4096]{1,0:T(8,128)(2,1)} %x_ref.3, f32[1,4096]{1,0:T(1,128)} %bitcast.10, bf16[4096,256]{1,0:T(8,128)(2,1)} %w_ref.2, s32[1,512]{1,0:T(1,128)} %bitcast.6), custom_call_target="tpu_custom_call" | custom-call | flops 1073741824 | bytes 10485760 | tf_op jit(solution)/shard_map/norm_kv/pallas_call | solution.py:98
  8.3 0.0 copy-start.3
  8.3 0.0 copy-start.4
  8.4 0.0 copy-start.5
  8.4 2.6 %collective-permute-start = (bf16[528,256]{1,0:T(8,128)(2,1)S(1)}, bf16[528,256]{1,0:T(8,128)(2,1)S(1)}, u32[]{:S(2)}, u32[]{:S(2)}) collective-permute-start(bf16[528,256]{1,0:T(8,128)(2,1)S(1)} %get-tuple-element.19.refs_2_), channel_id=1, source_target_pairs={{0,4},{2,6},{4,8},{6,10},{8,12},{10,14},{12,0},{14,2},{1,5},{3,7},... | collective-permute-start | bytes 811016 | tf_op jit(solution)/shard_map/ppermute | solution.py:327
  11.0 0.1 collective-permute-start.2
  11.1 1.2 %project_query.1.refs_0_ = bf16[512,256]{1,0:T(8,128)(2,1)S(1)} custom-call(bf16[512,4096]{1,0:T(8,128)(2,1)S(1)} %get-tuple-element.20.x_ref, bf16[4096,256]{1,0:T(8,128)(2,1)S(1)} %copy-done.1), custom_call_target="tpu_custom_call" | custom-call | flops 1073741824 | bytes 6291456 | tf_op jit(solution)/shard_map/project_query/pallas_call | solution.py:126
  12.3 7.7 %collective-permute-done.refs_3_ = bf16[528,256]{1,0:T(8,128)(2,1)S(1)} collective-permute-done((bf16[528,256]{1,0:T(8,128)(2,1)S(1)}, bf16[528,256]{1,0:T(8,128)(2,1)S(1)}, u32[]{:S(2)}, u32[]{:S(2)}) %collective-permute-start) | collective-permute-done | bytes 270368 | tf_op jit(solution)/shard_map/ppermute | solution.py:327
  20.0 1.5 %collective-permute-start.7 = (bf16[528,256]{1,0:T(8,128)(2,1)S(1)}, bf16[528,256]{1,0:T(8,128)(2,1)S(1)}, u32[]{:S(2)}, u32[]{:S(2)}) collective-permute-start(bf16[528,256]{1,0:T(8,128)(2,1)S(1)} %collective-permute-done.refs_3_), channel_id=1, source_target_pairs={{0,2},{2,4},{4,6},{6,8},{8,10},{10,12},{12,14},{14,0},{1,3},{3,5},... | collective-permute-start | bytes 811016 | tf_op jit(solution)/shard_map/ppermute | solution.py:327
  21.6 0.0 copy-start
  21.6 0.0 copy-start.2
  21.6 1.3 %collective-permute-start.1 = (bf16[528,256]{1,0:T(8,128)(2,1)S(1)}, bf16[528,256]{1,0:T(8,128)(2,1)S(1)}, u32[]{:S(2)}, u32[]{:S(2)}) collective-permute-start(bf16[528,256]{1,0:T(8,128)(2,1)S(1)} %broadcast_select_fusion), channel_id=1, source_target_pairs={{0,2},{2,0},{4,6},{6,4},{8,10},{10,8},{12,14},{14,12},{1,3},{3,1},... | collective-permute-start | bytes 811016 | tf_op jit(solution)/shard_map/ppermute | solution.py:334
  22.9 2.5 %spread_bounds.1 = (bf16[512,4096]{1,0:T(8,128)(2,1)S(1)}, bf16[512,4096]{1,0:T(8,128)(2,1)S(1)}) custom-call(s32[32,512]{1,0:T(8,128)S(1)} %bitcast.4, s32[32,512]{1,0:T(8,128)S(1)} %bitcast.5), custom_call_target="tpu_custom_call" | custom-call | flops 16777216 | bytes 131072 | tf_op jit(solution)/shard_map/spread_bounds/pallas_call | solution.py:257
  25.4 1.1 %attend_first.1.refs_4_ = f32[512,512]{1,0:T(8,128)S(1)} custom-call(bf16[512,256]{1,0:T(8,128)(2,1)S(1)} %project_query.1.refs_0_, s32[1,512]{1,0:T(1,128)S(1)} %bitcast.7, bf16[528,256]{1,0:T(8,128)(2,1)S(1)} %get-tuple-element.19.refs_2_, bf16[528,256]{1,0:T(8,128)(2,1)S(1)} %collective-permute-done.refs_3_, ...), custom_call_target="tpu_custom_call" | custom-call | flops 536870912 | bytes 1048576 | tf_op jit(solution)/shard_map/attend_first/pallas_call | solution.py:228
  26.6 5.6 %collective-permute-done.7.refs_2_ = bf16[528,256]{1,0:T(8,128)(2,1)S(1)} collective-permute-done((bf16[528,256]{1,0:T(8,128)(2,1)S(1)}, bf16[528,256]{1,0:T(8,128)(2,1)S(1)}, u32[]{:S(2)}, u32[]{:S(2)}) %collective-permute-start.7) | collective-permute-done | bytes 270368 | tf_op jit(solution)/shard_map/ppermute | solution.py:327
  32.1 4.2 %collective-permute-done.1.refs_2_ = bf16[528,256]{1,0:T(8,128)(2,1)S(1)} collective-permute-done((bf16[528,256]{1,0:T(8,128)(2,1)S(1)}, bf16[528,256]{1,0:T(8,128)(2,1)S(1)}, u32[]{:S(2)}, u32[]{:S(2)}) %collective-permute-start.1) | collective-permute-done | bytes 270368 | tf_op jit(solution)/shard_map/ppermute | solution.py:334
  36.4 0.5 %collective-permute-start.6 = (bf16[528,256]{1,0:T(8,128)(2,1)S(1)}, bf16[528,256]{1,0:T(8,128)(2,1)S(1)}, u32[]{:S(2)}, u32[]{:S(2)}) collective-permute-start(bf16[528,256]{1,0:T(8,128)(2,1)S(1)} %collective-permute-done.4.refs_3_), channel_id=1, source_target_pairs={{0,1},{1,0},{2,3},{3,2},{4,5},{5,4},{6,7},{7,6},{8,9},{9,8},{10,11... | collective-permute-start | bytes 811016 | tf_op jit(solution)/shard_map/ppermute | solution.py:324
  36.9 1.0 %collective-permute-done.5.refs_4_ = bf16[528,256]{1,0:T(8,128)(2,1)S(1)} collective-permute-done((bf16[528,256]{1,0:T(8,128)(2,1)S(1)}, bf16[528,256]{1,0:T(8,128)(2,1)S(1)}, u32[]{:S(2)}, u32[]{:S(2)}) %collective-permute-start.5) | collective-permute-done | bytes 270368 | tf_op jit(solution)/shard_map/ppermute | solution.py:324
  37.9 0.4 collective-permute-done.6.refs_5_
  38.3 0.2 attend_last.1.a_ref
  38.5 0.2 collective-permute-start.9
  38.7 1.4 %collective-permute-done.9.b_ref = bf16[512,256]{1,0:T(8,128)(2,1)S(1)} collective-permute-done((bf16[512,256]{1,0:T(8,128)(2,1)S(1)}, bf16[512,256]{1,0:T(8,128)(2,1)S(1)}, u32[]{:S(2)}, u32[]{:S(2)}) %collective-permute-start.9) | collective-permute-done | bytes 262176 | tf_op jit(solution)/shard_map/ppermute | solution.py:324
  40.1 5.9 %project_out.1 = bf16[512,4096]{1,0:T(8,128)(2,1)} custom-call(bf16[512,256]{1,0:T(8,128)(2,1)S(1)} %attend_last.1.a_ref, bf16[512,256]{1,0:T(8,128)(2,1)S(1)} %collective-permute-done.9.b_ref, bf16[256,4096]{1,0:T(8,128)(2,1)S(1)} %copy-done.2, bf16[256,4096]{1,0:T(8,128)(2,1)S(1)} %collective-permute-done.10.wb_ref, bf16[512,4096]{1,0:T(8,128)(2,1)S(1)} %copy-done, ...), custom_call_target="tpu_custom_call" | custom-call | flops 2147483648 | bytes 12582912 | tf_op jit(solution)/shard_map/project_out/pallas_call | solution.py:306
  (18 shorter events, 0.1 us)
Async XLA Ops:
  0.0 11.1 %copy-start.1 = (bf16[4096,256]{1,0:T(8,128)(2,1)S(1)}, bf16[4096,256]{1,0:T(8,128)(2,1)}, u32[]{:S(2)}) copy-start(bf16[4096,256]{1,0:T(8,128)(2,1)} %w_ref.3) | copy-start | bytes 6291460
  0.0 40.1 %collective-permute-start.10 = (bf16[256,4096]{1,0:T(8,128)(2,1)}, bf16[256,4096]{1,0:T(8,128)(2,1)S(1)}, u32[]{:S(2)}, u32[]{:S(2)}) collective-permute-start(bf16[256,4096]{1,0:T(8,128)(2,1)} %wa_ref.1), channel_id=1, source_target_pairs={{0,1},{1,0},{2,3},{3,2},{4,5},{5,4},{6,7},{7,6},{8,9},{9,8},{10,11... | collective-permute-start | bytes 6291464 | tf_op jit(solution)/shard_map/ppermute | solution.py:324
  8.3 14.6 %copy-start.3 = (s32[512,32]{0,1:T(8,128)S(1)}, s32[512,32]{0,1:T(8,128)}, u32[]{:S(2)}) copy-start(s32[512,32]{0,1:T(8,128)} %param.14) | copy-start | bytes 196612
  8.3 14.6 %copy-start.4 = (s32[512,32]{0,1:T(8,128)S(1)}, s32[512,32]{0,1:T(8,128)}, u32[]{:S(2)}) copy-start(s32[512,32]{0,1:T(8,128)} %param.15) | copy-start | bytes 196612
  8.4 17.0 %copy-start.5 = (s32[512]{0:T(512)S(1)}, s32[512]{0:T(512)}, u32[]{:S(2)}) copy-start(s32[512]{0:T(512)} %param.10) | copy-start | bytes 6148
  8.4 11.6 %collective-permute-start = (bf16[528,256]{1,0:T(8,128)(2,1)S(1)}, bf16[528,256]{1,0:T(8,128)(2,1)S(1)}, u32[]{:S(2)}, u32[]{:S(2)}) collective-permute-start(bf16[528,256]{1,0:T(8,128)(2,1)S(1)} %get-tuple-element.19.refs_2_), channel_id=1, source_target_pairs={{0,4},{2,6},{4,8},{6,10},{8,12},{10,14},{12,0},{14,2},{1,5},{3,7},... | collective-permute-start | bytes 811016 | tf_op jit(solution)/shard_map/ppermute | solution.py:327
  11.0 10.6 %collective-permute-start.2 = (bf16[528,256]{1,0:T(8,128)(2,1)S(1)}, bf16[528,256]{1,0:T(8,128)(2,1)S(1)}, u32[]{:S(2)}, u32[]{:S(2)}) collective-permute-start(bf16[528,256]{1,0:T(8,128)(2,1)S(1)} %get-tuple-element.19.refs_2_), channel_id=1, source_target_pairs={{0,1},{1,0},{2,3},{3,2},{4,5},{5,4},{6,7},{7,6},{8,9},{9,8},{10,11... | collective-permute-start | bytes 811016 | tf_op jit(solution)/shard_map/ppermute | solution.py:324
  20.0 12.1 %collective-permute-start.7 = (bf16[528,256]{1,0:T(8,128)(2,1)S(1)}, bf16[528,256]{1,0:T(8,128)(2,1)S(1)}, u32[]{:S(2)}, u32[]{:S(2)}) collective-permute-start(bf16[528,256]{1,0:T(8,128)(2,1)S(1)} %collective-permute-done.refs_3_), channel_id=1, source_target_pairs={{0,2},{2,4},{4,6},{6,8},{8,10},{10,12},{12,14},{14,0},{1,3},{3,5},... | collective-permute-start | bytes 811016 | tf_op jit(solution)/shard_map/ppermute | solution.py:327
  21.5 10.6 %collective-permute-start.4 = (bf16[528,256]{1,0:T(8,128)(2,1)S(1)}, bf16[528,256]{1,0:T(8,128)(2,1)S(1)}, u32[]{:S(2)}, u32[]{:S(2)}) collective-permute-start(bf16[528,256]{1,0:T(8,128)(2,1)S(1)} %collective-permute-done.refs_3_), channel_id=1, source_target_pairs={{0,4},{2,6},{4,8},{6,10},{8,12},{10,14},{12,0},{14,2},{1,5},{3,7},... | collective-permute-start | bytes 811016 | tf_op jit(solution)/shard_map/ppermute | solution.py:327
  21.5 3.9 %collective-permute-start.3 = (bf16[528,256]{1,0:T(8,128)(2,1)S(1)}, bf16[528,256]{1,0:T(8,128)(2,1)S(1)}, u32[]{:S(2)}, u32[]{:S(2)}) collective-permute-start(bf16[528,256]{1,0:T(8,128)(2,1)S(1)} %collective-permute-done.refs_3_), channel_id=1, source_target_pairs={{0,1},{1,0},{2,3},{3,2},{4,5},{5,4},{6,7},{7,6},{8,9},{9,8},{10,11... | collective-permute-start | bytes 811016 | tf_op jit(solution)/shard_map/ppermute | solution.py:324
  21.6 18.5 %copy-start = (bf16[512,4096]{1,0:T(8,128)(2,1)S(1)}, bf16[512,4096]{1,0:T(8,128)(2,1)}, u32[]{:S(2)}) copy-start(bf16[512,4096]{1,0:T(8,128)(2,1)} %x_ref.3) | copy-start | bytes 12582916
  21.6 18.5 %copy-start.2 = (bf16[256,4096]{1,0:T(8,128)(2,1)S(1)}, bf16[256,4096]{1,0:T(8,128)(2,1)}, u32[]{:S(2)}) copy-start(bf16[256,4096]{1,0:T(8,128)(2,1)} %wa_ref.1) | copy-start | bytes 6291460
  21.6 14.8 %collective-permute-start.1 = (bf16[528,256]{1,0:T(8,128)(2,1)S(1)}, bf16[528,256]{1,0:T(8,128)(2,1)S(1)}, u32[]{:S(2)}, u32[]{:S(2)}) collective-permute-start(bf16[528,256]{1,0:T(8,128)(2,1)S(1)} %broadcast_select_fusion), channel_id=1, source_target_pairs={{0,2},{2,0},{4,6},{6,4},{8,10},{10,8},{12,14},{14,12},{1,3},{3,1},... | collective-permute-start | bytes 811016 | tf_op jit(solution)/shard_map/ppermute | solution.py:334
  32.1 4.7 %collective-permute-start.8 = (bf16[528,256]{1,0:T(8,128)(2,1)S(1)}, bf16[528,256]{1,0:T(8,128)(2,1)S(1)}, u32[]{:S(2)}, u32[]{:S(2)}) collective-permute-start(bf16[528,256]{1,0:T(8,128)(2,1)S(1)} %collective-permute-done.7.refs_2_), channel_id=1, source_target_pairs={{0,1},{1,0},{2,3},{3,2},{4,5},{5,4},{6,7},{7,6},{8,9},{9,8},{10,11... | collective-permute-start | bytes 811016 | tf_op jit(solution)/shard_map/ppermute | solution.py:324
  36.4 1.5 %collective-permute-start.5 = (bf16[528,256]{1,0:T(8,128)(2,1)S(1)}, bf16[528,256]{1,0:T(8,128)(2,1)S(1)}, u32[]{:S(2)}, u32[]{:S(2)}) collective-permute-start(bf16[528,256]{1,0:T(8,128)(2,1)S(1)} %collective-permute-done.1.refs_2_), channel_id=1, source_target_pairs={{0,1},{1,0},{2,3},{3,2},{4,5},{5,4},{6,7},{7,6},{8,9},{9,8},{10,11... | collective-permute-start | bytes 811016 | tf_op jit(solution)/shard_map/ppermute | solution.py:324
  36.4 1.9 %collective-permute-start.6 = (bf16[528,256]{1,0:T(8,128)(2,1)S(1)}, bf16[528,256]{1,0:T(8,128)(2,1)S(1)}, u32[]{:S(2)}, u32[]{:S(2)}) collective-permute-start(bf16[528,256]{1,0:T(8,128)(2,1)S(1)} %collective-permute-done.4.refs_3_), channel_id=1, source_target_pairs={{0,1},{1,0},{2,3},{3,2},{4,5},{5,4},{6,7},{7,6},{8,9},{9,8},{10,11... | collective-permute-start | bytes 811016 | tf_op jit(solution)/shard_map/ppermute | solution.py:324
  38.5 1.6 %collective-permute-start.9 = (bf16[512,256]{1,0:T(8,128)(2,1)S(1)}, bf16[512,256]{1,0:T(8,128)(2,1)S(1)}, u32[]{:S(2)}, u32[]{:S(2)}) collective-permute-start(bf16[512,256]{1,0:T(8,128)(2,1)S(1)} %attend_last.1.a_ref), channel_id=1, source_target_pairs={{0,1},{1,0},{2,3},{3,2},{4,5},{5,4},{6,7},{7,6},{8,9},{9,8},{10,11... | collective-permute-start | bytes 786440 | tf_op jit(solution)/shard_map/ppermute | solution.py:324

commit v7 on v6

--- a/solution.py
+++ b/solution.py
@@ -20,35 +20,39 @@
 
 def norm_kv_kernel(x_ref, gain_hbm, w_ref, seg_hbm, msg_ref, normed_ref, xs, ws, gain_ref, seg_ref, sems):
     rows, width = xs.shape
-    tile, part = rows // 2, rows // 4
+    tile, part = rows // 2, rows // 8
+    pieces = 4
+    deep = width // pieces
 
     def tokens_copy(i):
         return pltpu.make_async_copy(x_ref.at[pl.ds(i * part, part)], xs.at[pl.ds(i * part, part)], sems.at[i])
 
-    def weights_copy():
-        return pltpu.make_async_copy(w_ref, ws, sems.at[4])
+    def weights_copy(i):
+        return pltpu.make_async_copy(w_ref.at[pl.ds(i * deep, deep)], ws.at[pl.ds(i * deep, deep)], sems.at[8 + i])
 
     def gain_copy():
-        return pltpu.make_async_copy(gain_hbm, gain_ref, sems.at[5])
+        return pltpu.make_async_copy(gain_hbm, gain_ref, sems.at[12])
 
     def segments_copy():
-        return pltpu.make_async_copy(seg_hbm, seg_ref, sems.at[6])
-
-    tokens_copy(0).start()
-    tokens_copy(1).start()
+        return pltpu.make_async_copy(seg_hbm, seg_ref, sems.at[13])
+
+    for i in range(4):
+        tokens_copy(i).start()
     gain_copy().start()
+    for i in range(pieces):
+        weights_copy(i).start()
+    for i in range(4, 8):
+        tokens_copy(i).start()
     segments_copy().start()
-    weights_copy().start()
-    tokens_copy(2).start()
-    tokens_copy(3).start()
+
     def wide(first, count, start):
         return xs[first:first + count, start:start + LANES].astype(jnp.float32)
 
-    ones = jnp.ones((width, LANES), jnp.bfloat16)
-
     def stats(first):
-        total = jnp.dot(xs[first:first + part, :], ones, preferred_element_type=jnp.float32)
-        mean = total * (1.0 / width)
+        total = wide(first, part, 0)
+        for start in range(LANES, width, LANES):
+            total = total + wide(first, part, start)
+        mean = jnp.broadcast_to(jnp.sum(total, axis=1, keepdims=True) * (1.0 / width), (part, LANES))
         square = jnp.zeros((part, LANES), jnp.float32)
         for start in range(0, width, LANES):
             center = wide(first, part, start) - mean
@@ -65,7 +69,8 @@
         scale = jnp.concatenate([h[1] for h in halves], axis=0)
         if first == 0:
             gain_copy().wait()
-            weights_copy().wait()
+            for i in range(pieces):
+                weights_copy(i).wait()
         kv = jnp.zeros((tile, ws.shape[1]), jnp.float32)
         span = slice(first, first + tile)
         for start in range(0, width, HD):
@@ -105,7 +110,7 @@
             pltpu.VMEM((width, cols), jnp.bfloat16),
             pltpu.VMEM((1, width), jnp.float32),
             pltpu.VMEM((1, rows), jnp.int32),
-            pltpu.SemaphoreType.DMA((7,)),
+            pltpu.SemaphoreType.DMA((14,)),
         ],
         compiler_params=pltpu.CompilerParams(vmem_limit_bytes=24 * MIB),
         cost_estimate=pl.CostEstimate(
@@ -240,8 +245,10 @@
     )(*[in_vmem(operand) for operand in operands])
 
 
-def bounds_kernel(sum_ref, out_exp_ref, sum_bound_ref, out_bound_ref):
+def bounds_kernel(sum_ref, out_exp_ref, x_ref, sum_bound_ref, out_bound_ref, near_ref, sem):
     groups, rows = sum_ref.shape
+    fetch = pltpu.make_async_copy(x_ref, near_ref, sem)
+    fetch.start()
     per = sum_bound_ref.shape[1] // groups
     for exps, bound_ref in ((sum_ref, sum_bound_ref), (out_exp_ref, out_bound_ref)):
         power = jnp.left_shift(jnp.int32(1), exps[...] - MIN_EXP).astype(jnp.float32)
@@ -249,31 +256,70 @@
         for group in range(groups):
             wide = jnp.broadcast_to(bound[:, group:group + 1], (rows, per))
             bound_ref[:, group * per:(group + 1) * per] = wide.astype(jnp.bfloat16)
-
-
-def spread_bounds(sum_exps, out_exps, width):
-    rows, groups = sum_exps.shape
+    fetch.wait()
+
+
+def spread_bounds(sum_exps, out_exps, tokens):
+    rows, width = tokens.shape
+    groups = sum_exps.shape[1]
     vmem = pl.BlockSpec(memory_space=pltpu.VMEM)
     return pl.pallas_call(
         bounds_kernel,
-        in_specs=[vmem, vmem],
-        out_specs=[vmem, vmem],
-        out_shape=[pltpu.VMEM((rows, width), jnp.bfloat16)] * 2,
+        in_specs=[vmem, vmem, pl.BlockSpec(memory_space=pltpu.HBM)],
+        out_specs=[vmem] * 3,
+        out_shape=[pltpu.VMEM((rows, width), jnp.bfloat16)] * 3,
+        scratch_shapes=[pltpu.SemaphoreType.DMA(())],
         compiler_params=pltpu.CompilerParams(vmem_limit_bytes=8 * MIB),
         cost_estimate=pl.CostEstimate(flops=8 * rows * width, bytes_accessed=8 * rows * groups, transcendentals=0),
         name="spread_bounds",
-    )(sum_exps.T, out_exps.T)
-
-
-def output_kernel(a_ref, b_ref, wa_ref, wb_ref, x_ref, sum_ref, last_ref, out_ref, staged, sems):
+    )(in_vmem(sum_exps.T), in_vmem(out_exps.T), in_hbm(tokens))
+
+
+def clip(value, bound):
+    return jnp.minimum(jnp.maximum(value.astype(jnp.bfloat16), -bound), bound)
+
+
+def own_kernel(a_ref, w_ref, sum_ref, out_ref):
+    rows, width = out_ref.shape
+    tile = rows // 2
+    chunk = width // 4
+
+    def body(step, carry):
+        for at in range(0, chunk, HD):
+            cols = pl.ds(pl.multiple_of(step * chunk + at, HD), HD)
+            weights = w_ref[:, cols]
+            for start in range(0, rows, tile):
+                span = slice(start, start + tile)
+                term = jnp.dot(a_ref[span, :], weights, preferred_element_type=jnp.float32)
+                out_ref[span, cols] = clip(term, sum_ref[span, cols])
+        return carry
+
+    lax.fori_loop(0, 4, body, 0)
+
+
+def project_own(attended, w_out, sum_bound):
+    rows, depth = attended.shape
+    width = w_out.shape[1]
+    vmem = pl.BlockSpec(memory_space=pltpu.VMEM)
+    return pl.pallas_call(
+        own_kernel,
+        in_specs=[vmem] * 3,
+        out_specs=vmem,
+        out_shape=pltpu.VMEM((rows, width), jnp.bfloat16),
+        compiler_params=pltpu.CompilerParams(vmem_limit_bytes=8 * MIB),
+        cost_estimate=pl.CostEstimate(
+            flops=2 * rows * width * depth, bytes_accessed=4 * rows * width + 2 * width * depth, transcendentals=0
+        ),
+        name="project_own",
+    )(in_vmem(attended), in_vmem(w_out), in_vmem(sum_bound))
+
+
+def output_kernel(b_ref, wb_ref, quant_ref, x_ref, sum_ref, last_ref, out_ref, staged, sems):
     rows, width = x_ref.shape
     steps = sems.shape[0]
     chunk = width // steps
     tile = rows // 2
 
-    def clip(value, bound):
-        return jnp.minimum(jnp.maximum(value.astype(jnp.bfloat16), -bound), bound)
-
     def copy(step):
         span = pl.ds(pl.multiple_of(step * chunk, chunk), chunk)
         return pltpu.make_async_copy(staged.at[:, span], out_ref.at[:, span], sems.at[step])
@@ -281,13 +327,11 @@
     def body(step, carry):
         for at in range(0, chunk, HD):
             cols = pl.ds(pl.multiple_of(step * chunk + at, HD), HD)
-            weights_a, weights_b = wa_ref[:, cols], wb_ref[:, cols]
+            weights = wb_ref[:, cols]
             for start in range(0, rows, tile):
                 span = slice(start, start + tile)
-                term_a = jnp.dot(a_ref[span, :], weights_a, preferred_element_type=jnp.float32)
-                term_b = jnp.dot(b_ref[span, :], weights_b, preferred_element_type=jnp.float32)
-                bound = sum_ref[span, cols]
-                quant = clip(term_a, bound).astype(jnp.float32) + clip(term_b, bound).astype(jnp.float32)
+                term = jnp.dot(b_ref[span, :], weights, preferred_element_type=jnp.float32)
+                quant = clip(term, sum_ref[span, cols]).astype(jnp.float32) + quant_ref[span, cols].astype(jnp.float32)
                 staged[span, cols] = clip(x_ref[span, cols].astype(jnp.float32) + quant, last_ref[span, cols])
         copy(step).start()
         return carry
@@ -297,12 +341,12 @@
         copy(step).wait()
 
 
-def project_out(att_a, att_b, w_a, w_b, tokens, sum_bound, out_bound):
+def project_out(att_other, w_other, quant_own, sum_bound, out_bound, tokens):
     rows, width = tokens.shape
-    depth = att_a.shape[1]
+    depth = att_other.shape[1]
     steps = 4
     vmem = pl.BlockSpec(memory_space=pltpu.VMEM)
-    operands = [att_a, att_b, w_a, w_b, tokens, sum_bound, out_bound]
+    operands = [att_other, w_other, quant_own, tokens, sum_bound, out_bound]
     return pl.pallas_call(
         output_kernel,
         in_specs=[vmem] * len(operands),
@@ -311,7 +355,7 @@
         scratch_shapes=[pltpu.VMEM((rows, width), jnp.bfloat16), pltpu.SemaphoreType.DMA((steps,))],
         compiler_params=pltpu.CompilerParams(vmem_limit_bytes=12 * MIB),
         cost_estimate=pl.CostEstimate(
-            flops=4 * rows * width * depth, bytes_accessed=4 * rows * width + 4 * width * depth, transcendentals=0
+            flops=2 * rows * width * depth, bytes_accessed=4 * rows * width + 2 * width * depth, transcendentals=0
         ),
         name="project_out",
     )(*[in_vmem(operand) for operand in operands])
@@ -323,23 +367,29 @@
     def swap_cores(x):
         return lax.ppermute(x, "tp", [(0, 1), (1, 0)])
 
-    def shift(x, step):
-        return lax.ppermute(x, "seq", [(i, (i + step) % seq_size) for i in range(seq_size)])
+    def shift(x, step, first):
+        cycle = seq_size - first
+        pairs = []
+        for i in range(seq_size):
+            for core in range(2):
+                after = 2 * (first + (i - first + step) % cycle) + core if i >= first else 2 * i + 1 - core
+                pairs.append((2 * i + core, after))
+        return lax.ppermute(x, ("seq", "tp"), pairs)
 
     w_other = swap_cores(w_out)
     message, normed = norm_kv(tokens, gain, w_keyval, segments)
     query = project_query(normed, w_query)
-    held, query = lax.optimization_barrier((shift(message, 2), query))
+    held, query = lax.optimization_barrier((shift(message, 2, 0), query))
     odd = lax.rem(lax.axis_index("seq"), 2) == 1
     beside = lax.ppermute(jnp.where(odd, held, message), "seq", [(i, i ^ 1) for i in range(seq_size)])
     parts = [[(0, message), (2, held)]]
     for back in range(2, window, 2):
-        step = shift(held, 1)
-        held = shift(held, 2)
+        step = shift(held, 1, back)
+        held = shift(held, 2, back)
         parts.append([(back + 1, step)] + ([(back + 2, held)] if back + 2 < window else []))
     parts.append([(1, beside), (window, held)])
     exps = lax.optimization_barrier((sum_exps, out_exps, query))[:2]
-    bounds = spread_bounds(*exps, tokens.shape[1])
+    bounds = spread_bounds(*exps, tokens)
     state = None
     for number, blocks in enumerate(parts):
         plan = [(back, back == window) for back, _ in blocks]
@@ -350,7 +400,8 @@
             mine = [lax.optimization_barrier((block, early))[0] for block in mine]
         other = [swap_cores(m) for m in mine]
         state = attend(query, segments, plan, mine, other, state, number == len(parts) - 1)
-    return project_out(state, swap_cores(state), w_out, w_other, tokens, *bounds)
+    quant_own = project_own(state, w_out, bounds[0])
+    return project_out(swap_cores(state), w_other, quant_own, *bounds)
 
 
 def solution(mesh):

time: 46.3 us -> 42 us (0.907)
  the two profiles are of different devices: /device:TPU:0 before, /device:TPU:11 now
where the time goes in v7:
time: 42 us; the launch traced here: 41.9 us
  Pallas kernels  19.8 us (47%)
  starting transfers between devices  11.5 us (27%)
  waiting for transfers between devices  10.2 us (24%)
    pallas_call x1, Pallas kernels, norm_kv(): pl.pallas_call(norm_kv_kernel, in_specs=[hbm] * 4, out_specs=[vmem, vmem]...  6.28 us
    ppermute x7, starting transfers between devices, swap_cores(): return lax.ppermute(x, 'tp', [(0, 1), (1, 0)])  6.26 us
    pallas_call x1, Pallas kernels, project_out(): pl.pallas_call(output_kernel, in_specs=[vmem] * len(operands), out_specs=...  5.25 us
    ppermute x3, waiting for transfers between devices, shift(): return lax.ppermute(x, ('seq', 'tp'), pairs)  4.91 us
    ppermute x3, starting transfers between devices, shift(): return lax.ppermute(x, ('seq', 'tp'), pairs)  3.88 us
    ppermute x1, waiting for transfers between devices, on_device(): lax.ppermute(jnp.where(odd, held, message), 'seq', [(i, i ^ 1) for i in r...  3.83 us
    pallas_call x3, Pallas kernels, attend(): pl.pallas_call(functools.partial(attend_kernel, plan, first, last), in_sp...  2.67 us
    pallas_call x1, Pallas kernels, spread_bounds(): pl.pallas_call(bounds_kernel, in_specs=[vmem, vmem, pl.BlockSpec(memory_s...  2.49 us
  transfers between devices with their start and end apart: 11, of which 4 were waited for; matrix products, arithmetic and copies ran while one was open for 0% of the time, Pallas kernels for 35%

profile of v7, /device:TPU:11, one launch (start us, length us, event | category | flops | bytes accessed | tf_op | source)
XLA Modules:
  0.0 41.9 jit_solution(15841441456121928273)
XLA Ops:
  0.0 0.7 %collective-permute-start.10 = (bf16[256,4096]{1,0:T(8,128)(2,1)}, bf16[256,4096]{1,0:T(8,128)(2,1)S(1)}, u32[]{:S(2)}, u32[]{:S(2)}) collective-permute-start(bf16[256,4096]{1,0:T(8,128)(2,1)} %w_ref.5), channel_id=1, source_target_pairs={{0,1},{1,0},{2,3},{3,2},{4,5},{5,4},{6,7},{7,6},{8,9},{9,8},{10,11... | collective-permute-start | bytes 6291464 | tf_op jit(solution)/shard_map/ppermute | solution.py:368
  0.7 6.3 %norm_kv.1 = (bf16[528,256]{1,0:T(8,128)(2,1)S(1)}, bf16[512,4096]{1,0:T(8,128)(2,1)S(1)}) custom-call(bf16[512,4096]{1,0:T(8,128)(2,1)} %x_ref.3, f32[1,4096]{1,0:T(1,128)} %bitcast.10, bf16[4096,256]{1,0:T(8,128)(2,1)} %w_ref.3, s32[1,512]{1,0:T(1,128)} %bitcast.6), custom_call_target="tpu_custom_call" | custom-call | flops 1073741824 | bytes 10485760 | tf_op jit(solution)/shard_map/norm_kv/pallas_call | solution.py:103
  7.0 0.0 copy-start.2
  7.0 1.3 %collective-permute-start = (bf16[528,256]{1,0:T(8,128)(2,1)S(1)}, bf16[528,256]{1,0:T(8,128)(2,1)S(1)}, u32[]{:S(2)}, u32[]{:S(2)}) collective-permute-start(bf16[528,256]{1,0:T(8,128)(2,1)S(1)} %get-tuple-element.21.refs_2_), channel_id=1, source_target_pairs={{0,4},{1,5},{2,6},{3,7},{4,8},{5,9},{6,10},{7,11},{8,12},{9,13},{1... | collective-permute-start | bytes 811016 | tf_op jit(solution)/shard_map/ppermute | solution.py:377
  8.3 0.4 %collective-permute-start.2 = (bf16[528,256]{1,0:T(8,128)(2,1)S(1)}, bf16[528,256]{1,0:T(8,128)(2,1)S(1)}, u32[]{:S(2)}, u32[]{:S(2)}) collective-permute-start(bf16[528,256]{1,0:T(8,128)(2,1)S(1)} %get-tuple-element.21.refs_2_), channel_id=1, source_target_pairs={{0,1},{1,0},{2,3},{3,2},{4,5},{5,4},{6,7},{7,6},{8,9},{9,8},{10,11... | collective-permute-start | bytes 811016 | tf_op jit(solution)/shard_map/ppermute | solution.py:368
  8.8 1.2 %project_query.1.refs_0_ = bf16[512,256]{1,0:T(8,128)(2,1)S(1)} custom-call(bf16[512,4096]{1,0:T(8,128)(2,1)S(1)} %get-tuple-element.22.x_ref, bf16[4096,256]{1,0:T(8,128)(2,1)S(1)} %copy-done), custom_call_target="tpu_custom_call" | custom-call | flops 1073741824 | bytes 6291456 | tf_op jit(solution)/shard_map/project_query/pallas_call | solution.py:131
  10.0 0.0 copy-start.4
  10.1 4.9 %collective-permute-done.refs_3_ = bf16[528,256]{1,0:T(8,128)(2,1)S(1)} collective-permute-done((bf16[528,256]{1,0:T(8,128)(2,1)S(1)}, bf16[528,256]{1,0:T(8,128)(2,1)S(1)}, u32[]{:S(2)}, u32[]{:S(2)}) %collective-permute-start) | collective-permute-done | bytes 270368 | tf_op jit(solution)/shard_map/ppermute | solution.py:377
  15.0 1.2 %collective-permute-start.7 = (bf16[528,256]{1,0:T(8,128)(2,1)S(1)}, bf16[528,256]{1,0:T(8,128)(2,1)S(1)}, u32[]{:S(2)}, u32[]{:S(2)}) collective-permute-start(bf16[528,256]{1,0:T(8,128)(2,1)S(1)} %collective-permute-done.refs_3_), channel_id=1, source_target_pairs={{0,1},{1,0},{2,3},{3,2},{4,6},{5,7},{6,8},{7,9},{8,10},{9,11},{10,... | collective-permute-start | bytes 811016 | tf_op jit(solution)/shard_map/ppermute | solution.py:377
  16.2 1.3 %collective-permute-start.4 = (bf16[528,256]{1,0:T(8,128)(2,1)S(1)}, bf16[528,256]{1,0:T(8,128)(2,1)S(1)}, u32[]{:S(2)}, u32[]{:S(2)}) collective-permute-start(bf16[528,256]{1,0:T(8,128)(2,1)S(1)} %collective-permute-done.refs_3_), channel_id=1, source_target_pairs={{0,1},{1,0},{2,3},{3,2},{4,8},{5,9},{6,10},{7,11},{8,12},{9,13},{1... | collective-permute-start | bytes 811016 | tf_op jit(solution)/shard_map/ppermute | solution.py:377
  17.5 1.5 %collective-permute-start.3 = (bf16[528,256]{1,0:T(8,128)(2,1)S(1)}, bf16[528,256]{1,0:T(8,128)(2,1)S(1)}, u32[]{:S(2)}, u32[]{:S(2)}) collective-permute-start(bf16[528,256]{1,0:T(8,128)(2,1)S(1)} %collective-permute-done.refs_3_), channel_id=1, source_target_pairs={{0,1},{1,0},{2,3},{3,2},{4,5},{5,4},{6,7},{7,6},{8,9},{9,8},{10,11... | collective-permute-start | bytes 811016 | tf_op jit(solution)/shard_map/ppermute | solution.py:368
  19.1 1.3 %collective-permute-start.1 = (bf16[528,256]{1,0:T(8,128)(2,1)S(1)}, bf16[528,256]{1,0:T(8,128)(2,1)S(1)}, u32[]{:S(2)}, u32[]{:S(2)}) collective-permute-start(bf16[528,256]{1,0:T(8,128)(2,1)S(1)} %broadcast_select_fusion), channel_id=1, source_target_pairs={{0,2},{2,0},{4,6},{6,4},{8,10},{10,8},{12,14},{14,12},{1,3},{3,1},... | collective-permute-start | bytes 811016 | tf_op jit(solution)/shard_map/ppermute | solution.py:384
  20.4 2.5 %spread_bounds.1 = (bf16[512,4096]{1,0:T(8,128)(2,1)S(1)}, bf16[512,4096]{1,0:T(8,128)(2,1)S(1)}, bf16[512,4096]{1,0:T(8,128)(2,1)S(1)}) custom-call(s32[32,512]{1,0:T(8,128)S(1)} %bitcast.4, s32[32,512]{1,0:T(8,128)S(1)} %bitcast.5, bf16[512,4096]{1,0:T(8,128)(2,1)} %x_ref.3), custom_call_target="tpu_custom_call" | custom-call | flops 16777216 | bytes 131072 | tf_op jit(solution)/shard_map/spread_bounds/pallas_call | solution.py:266
  22.9 1.6 %attend_first.1.refs_4_ = f32[512,512]{1,0:T(8,128)S(1)} custom-call(bf16[512,256]{1,0:T(8,128)(2,1)S(1)} %project_query.1.refs_0_, s32[1,512]{1,0:T(1,128)S(1)} %bitcast.7, bf16[528,256]{1,0:T(8,128)(2,1)S(1)} %get-tuple-element.21.refs_2_, bf16[528,256]{1,0:T(8,128)(2,1)S(1)} %collective-permute-done.refs_3_, ...), custom_call_target="tpu_custom_call" | custom-call | flops 536870912 | bytes 1048576 | tf_op jit(solution)/shard_map/attend_first/pallas_call | solution.py:233
  24.5 2.7 %collective-permute-start.8 = (bf16[528,256]{1,0:T(8,128)(2,1)S(1)}, bf16[528,256]{1,0:T(8,128)(2,1)S(1)}, u32[]{:S(2)}, u32[]{:S(2)}) collective-permute-start(bf16[528,256]{1,0:T(8,128)(2,1)S(1)} %collective-permute-done.7.refs_2_), channel_id=1, source_target_pairs={{0,1},{1,0},{2,3},{3,2},{4,5},{5,4},{6,7},{7,6},{8,9},{9,8},{10,11... | collective-permute-start | bytes 811016 | tf_op jit(solution)/shard_map/ppermute | solution.py:368
  27.2 3.8 %collective-permute-done.1.refs_2_ = bf16[528,256]{1,0:T(8,128)(2,1)S(1)} collective-permute-done((bf16[528,256]{1,0:T(8,128)(2,1)S(1)}, bf16[528,256]{1,0:T(8,128)(2,1)S(1)}, u32[]{:S(2)}, u32[]{:S(2)}) %collective-permute-start.1) | collective-permute-done | bytes 270368 | tf_op jit(solution)/shard_map/ppermute | solution.py:384
  31.0 0.4 %collective-permute-start.5 = (bf16[528,256]{1,0:T(8,128)(2,1)S(1)}, bf16[528,256]{1,0:T(8,128)(2,1)S(1)}, u32[]{:S(2)}, u32[]{:S(2)}) collective-permute-start(bf16[528,256]{1,0:T(8,128)(2,1)S(1)} %collective-permute-done.1.refs_2_), channel_id=1, source_target_pairs={{0,1},{1,0},{2,3},{3,2},{4,5},{5,4},{6,7},{7,6},{8,9},{9,8},{10,11... | collective-permute-start | bytes 811016 | tf_op jit(solution)/shard_map/ppermute | solution.py:368
  31.5 0.1 collective-permute-start.6
  31.5 1.1 %collective-permute-done.5.refs_4_ = bf16[528,256]{1,0:T(8,128)(2,1)S(1)} collective-permute-done((bf16[528,256]{1,0:T(8,128)(2,1)S(1)}, bf16[528,256]{1,0:T(8,128)(2,1)S(1)}, u32[]{:S(2)}, u32[]{:S(2)}) %collective-permute-start.5) | collective-permute-done | bytes 270368 | tf_op jit(solution)/shard_map/ppermute | solution.py:368
  32.6 0.4 collective-permute-done.6.refs_5_
  33.0 1.1 %attend_last.1.a_ref = bf16[512,256]{1,0:T(8,128)(2,1)S(1)} custom-call(bf16[512,256]{1,0:T(8,128)(2,1)S(1)} %project_query.1.refs_0_, s32[1,512]{1,0:T(1,128)S(1)} %bitcast.9, bf16[528,256]{1,0:T(8,128)(2,1)S(1)} %collective-permute-done.1.refs_2_, bf16[528,256]{1,0:T(8,128)(2,1)S(1)} %collective-permute-done.4.refs_3_, ...), custom_call_target="tpu_custom_call" | custom-call | flops 536870912 | bytes 1048576 | tf_op jit(solution)/shard_map/attend_last/pallas_call | solution.py:233
  34.1 0.4 %collective-permute-start.9 = (bf16[512,256]{1,0:T(8,128)(2,1)S(1)}, bf16[512,256]{1,0:T(8,128)(2,1)S(1)}, u32[]{:S(2)}, u32[]{:S(2)}) collective-permute-start(bf16[512,256]{1,0:T(8,128)(2,1)S(1)} %attend_last.1.a_ref), channel_id=1, source_target_pairs={{0,1},{1,0},{2,3},{3,2},{4,5},{5,4},{6,7},{7,6},{8,9},{9,8},{10,11... | collective-permute-start | bytes 786440 | tf_op jit(solution)/shard_map/ppermute | solution.py:368
  34.6 1.9 %project_own.1.quant_ref = bf16[512,4096]{1,0:T(8,128)(2,1)S(1)} custom-call(bf16[512,256]{1,0:T(8,128)(2,1)S(1)} %attend_last.1.a_ref, bf16[256,4096]{1,0:T(8,128)(2,1)S(1)} %copy-done.1, bf16[512,4096]{1,0:T(8,128)(2,1)S(1)} %get-tuple-element.30.sum_ref), custom_call_target="tpu_custom_call" | custom-call | flops 1073741824 | bytes 10485760 | tf_op jit(solution)/shard_map/project_own/pallas_call | solution.py:304
  36.4 5.3 %project_out.1 = bf16[512,4096]{1,0:T(8,128)(2,1)} custom-call(bf16[512,256]{1,0:T(8,128)(2,1)S(1)} %collective-permute-done.9.b_ref, bf16[256,4096]{1,0:T(8,128)(2,1)S(1)} %collective-permute-done.10.wb_ref, bf16[512,4096]{1,0:T(8,128)(2,1)S(1)} %project_own.1.quant_ref, bf16[512,4096]{1,0:T(8,128)(2,1)S(1)} %get-tuple-element.32.x_ref, ...), custom_call_target="tpu_custom_call" | custom-call | flops 1073741824 | bytes 10485760 | tf_op jit(solution)/shard_map/project_out/pallas_call | solution.py:350
  (17 shorter events, 0.1 us)
Async XLA Ops:
  0.0 8.8 %copy-start = (bf16[4096,256]{1,0:T(8,128)(2,1)S(1)}, bf16[4096,256]{1,0:T(8,128)(2,1)}, u32[]{:S(2)}) copy-start(bf16[4096,256]{1,0:T(8,128)(2,1)} %w_ref.4) | copy-start | bytes 6291460
  0.0 36.4 %collective-permute-start.10 = (bf16[256,4096]{1,0:T(8,128)(2,1)}, bf16[256,4096]{1,0:T(8,128)(2,1)S(1)}, u32[]{:S(2)}, u32[]{:S(2)}) collective-permute-start(bf16[256,4096]{1,0:T(8,128)(2,1)} %w_ref.5), channel_id=1, source_target_pairs={{0,1},{1,0},{2,3},{3,2},{4,5},{5,4},{6,7},{7,6},{8,9},{9,8},{10,11... | collective-permute-start | bytes 6291464 | tf_op jit(solution)/shard_map/ppermute | solution.py:368
  7.0 13.4 %copy-start.2 = (s32[512,32]{0,1:T(8,128)S(1)}, s32[512,32]{0,1:T(8,128)}, u32[]{:S(2)}) copy-start(s32[512,32]{0,1:T(8,128)} %param.14) | copy-start | bytes 196612
  7.0 13.4 %copy-start.3 = (s32[512,32]{0,1:T(8,128)S(1)}, s32[512,32]{0,1:T(8,128)}, u32[]{:S(2)}) copy-start(s32[512,32]{0,1:T(8,128)} %param.15) | copy-start | bytes 196612
  7.0 8.0 %collective-permute-start = (bf16[528,256]{1,0:T(8,128)(2,1)S(1)}, bf16[528,256]{1,0:T(8,128)(2,1)S(1)}, u32[]{:S(2)}, u32[]{:S(2)}) collective-permute-start(bf16[528,256]{1,0:T(8,128)(2,1)S(1)} %get-tuple-element.21.refs_2_), channel_id=1, source_target_pairs={{0,4},{1,5},{2,6},{3,7},{4,8},{5,9},{6,10},{7,11},{8,12},{9,13},{1... | collective-permute-start | bytes 811016 | tf_op jit(solution)/shard_map/ppermute | solution.py:377
  8.3 10.7 %collective-permute-start.2 = (bf16[528,256]{1,0:T(8,128)(2,1)S(1)}, bf16[528,256]{1,0:T(8,128)(2,1)S(1)}, u32[]{:S(2)}, u32[]{:S(2)}) collective-permute-start(bf16[528,256]{1,0:T(8,128)(2,1)S(1)} %get-tuple-element.21.refs_2_), channel_id=1, source_target_pairs={{0,1},{1,0},{2,3},{3,2},{4,5},{5,4},{6,7},{7,6},{8,9},{9,8},{10,11... | collective-permute-start | bytes 811016 | tf_op jit(solution)/shard_map/ppermute | solution.py:368
  10.0 12.9 %copy-start.4 = (s32[512]{0:T(512)S(1)}, s32[512]{0:T(512)}, u32[]{:S(2)}) copy-start(s32[512]{0:T(512)} %param.10) | copy-start | bytes 6148
  15.0 9.6 %collective-permute-start.7 = (bf16[528,256]{1,0:T(8,128)(2,1)S(1)}, bf16[528,256]{1,0:T(8,128)(2,1)S(1)}, u32[]{:S(2)}, u32[]{:S(2)}) collective-permute-start(bf16[528,256]{1,0:T(8,128)(2,1)S(1)} %collective-permute-done.refs_3_), channel_id=1, source_target_pairs={{0,1},{1,0},{2,3},{3,2},{4,6},{5,7},{6,8},{7,9},{8,10},{9,11},{10,... | collective-permute-start | bytes 811016 | tf_op jit(solution)/shard_map/ppermute | solution.py:377
  16.2 11.0 %collective-permute-start.4 = (bf16[528,256]{1,0:T(8,128)(2,1)S(1)}, bf16[528,256]{1,0:T(8,128)(2,1)S(1)}, u32[]{:S(2)}, u32[]{:S(2)}) collective-permute-start(bf16[528,256]{1,0:T(8,128)(2,1)S(1)} %collective-permute-done.refs_3_), channel_id=1, source_target_pairs={{0,1},{1,0},{2,3},{3,2},{4,8},{5,9},{6,10},{7,11},{8,12},{9,13},{1... | collective-permute-start | bytes 811016 | tf_op jit(solution)/shard_map/ppermute | solution.py:377
  17.5 5.4 %collective-permute-start.3 = (bf16[528,256]{1,0:T(8,128)(2,1)S(1)}, bf16[528,256]{1,0:T(8,128)(2,1)S(1)}, u32[]{:S(2)}, u32[]{:S(2)}) collective-permute-start(bf16[528,256]{1,0:T(8,128)(2,1)S(1)} %collective-permute-done.refs_3_), channel_id=1, source_target_pairs={{0,1},{1,0},{2,3},{3,2},{4,5},{5,4},{6,7},{7,6},{8,9},{9,8},{10,11... | collective-permute-start | bytes 811016 | tf_op jit(solution)/shard_map/ppermute | solution.py:368
  19.1 11.9 %collective-permute-start.1 = (bf16[528,256]{1,0:T(8,128)(2,1)S(1)}, bf16[528,256]{1,0:T(8,128)(2,1)S(1)}, u32[]{:S(2)}, u32[]{:S(2)}) collective-permute-start(bf16[528,256]{1,0:T(8,128)(2,1)S(1)} %broadcast_select_fusion), channel_id=1, source_target_pairs={{0,2},{2,0},{4,6},{6,4},{8,10},{10,8},{12,14},{14,12},{1,3},{3,1},... | collective-permute-start | bytes 811016 | tf_op jit(solution)/shard_map/ppermute | solution.py:384
  22.9 11.7 %copy-start.1 = (bf16[256,4096]{1,0:T(8,128)(2,1)S(1)}, bf16[256,4096]{1,0:T(8,128)(2,1)}, u32[]{:S(2)}) copy-start(bf16[256,4096]{1,0:T(8,128)(2,1)} %w_ref.5) | copy-start | bytes 6291460
  24.5 7.0 %collective-permute-start.8 = (bf16[528,256]{1,0:T(8,128)(2,1)S(1)}, bf16[528,256]{1,0:T(8,128)(2,1)S(1)}, u32[]{:S(2)}, u32[]{:S(2)}) collective-permute-start(bf16[528,256]{1,0:T(8,128)(2,1)S(1)} %collective-permute-done.7.refs_2_), channel_id=1, source_target_pairs={{0,1},{1,0},{2,3},{3,2},{4,5},{5,4},{6,7},{7,6},{8,9},{9,8},{10,11... | collective-permute-start | bytes 811016 | tf_op jit(solution)/shard_map/ppermute | solution.py:368
  31.0 1.6 %collective-permute-start.5 = (bf16[528,256]{1,0:T(8,128)(2,1)S(1)}, bf16[528,256]{1,0:T(8,128)(2,1)S(1)}, u32[]{:S(2)}, u32[]{:S(2)}) collective-permute-start(bf16[528,256]{1,0:T(8,128)(2,1)S(1)} %collective-permute-done.1.refs_2_), channel_id=1, source_target_pairs={{0,1},{1,0},{2,3},{3,2},{4,5},{5,4},{6,7},{7,6},{8,9},{9,8},{10,11... | collective-permute-start | bytes 811016 | tf_op jit(solution)/shard_map/ppermute | solution.py:368
  31.5 1.6 %collective-permute-start.6 = (bf16[528,256]{1,0:T(8,128)(2,1)S(1)}, bf16[528,256]{1,0:T(8,128)(2,1)S(1)}, u32[]{:S(2)}, u32[]{:S(2)}) collective-permute-start(bf16[528,256]{1,0:T(8,128)(2,1)S(1)} %collective-permute-done.4.refs_3_), channel_id=1, source_target_pairs={{0,1},{1,0},{2,3},{3,2},{4,5},{5,4},{6,7},{7,6},{8,9},{9,8},{10,11... | collective-permute-start | bytes 811016 | tf_op jit(solution)/shard_map/ppermute | solution.py:368
  34.1 2.3 %collective-permute-start.9 = (bf16[512,256]{1,0:T(8,128)(2,1)S(1)}, bf16[512,256]{1,0:T(8,128)(2,1)S(1)}, u32[]{:S(2)}, u32[]{:S(2)}) collective-permute-start(bf16[512,256]{1,0:T(8,128)(2,1)S(1)} %attend_last.1.a_ref), channel_id=1, source_target_pairs={{0,1},{1,0},{2,3},{3,2},{4,5},{5,4},{6,7},{7,6},{8,9},{9,8},{10,11... | collective-permute-start | bytes 786440 | tf_op jit(solution)/shard_map/ppermute | solution.py:368

commit v8 on v7

--- a/solution.py
+++ b/solution.py
@@ -60,27 +60,24 @@
         spread = jnp.sum(square, axis=1, keepdims=True) * (1.0 / width)
         return mean, jnp.broadcast_to(lax.rsqrt(spread + 1e-05), (part, LANES))
 
-    for first in range(0, rows, tile):
-        halves = []
-        for at in range(first, first + tile, part):
-            tokens_copy(at // part).wait()
-            halves.append(stats(at))
-        mean = jnp.concatenate([h[0] for h in halves], axis=0)
-        scale = jnp.concatenate([h[1] for h in halves], axis=0)
-        if first == 0:
+    def project(first):
+        span = slice(first, first + tile)
+        kv = jnp.dot(normed_ref[span, :], ws[...], preferred_element_type=jnp.float32)
+        msg_ref[span, :] = kv.astype(jnp.bfloat16)
+
+    for at in range(0, rows, part):
+        tokens_copy(at // part).wait()
+        mean, scale = stats(at)
+        if at == 0:
             gain_copy().wait()
+        for start in range(0, width, LANES):
+            normed = (wide(at, part, start) - mean) * scale * gain_ref[:, start:start + LANES]
+            normed_ref[at:at + part, start:start + LANES] = normed.astype(jnp.bfloat16)
+        if at + part == rows - tile:
             for i in range(pieces):
                 weights_copy(i).wait()
-        kv = jnp.zeros((tile, ws.shape[1]), jnp.float32)
-        span = slice(first, first + tile)
-        for start in range(0, width, HD):
-            for at in (start, start + LANES):
-                normed = (wide(first, tile, at) - mean) * scale * gain_ref[:, at:at + LANES]
-                normed_ref[span, at:at + LANES] = normed.astype(jnp.bfloat16)
-            kv = kv + jnp.dot(
-                normed_ref[span, start:start + HD], ws[start:start + HD, :], preferred_element_type=jnp.float32
-            )
-        msg_ref[span, :] = kv.astype(jnp.bfloat16)
+            project(0)
+    project(rows - tile)
     segments_copy().wait()
     seg = seg_ref[...].astype(jnp.float32)
     low = jnp.broadcast_to(seg[:, :HD], (8, HD))
@@ -279,19 +276,30 @@
     return jnp.minimum(jnp.maximum(value.astype(jnp.bfloat16), -bound), bound)
 
 
+def in_tiles(a_ref, w_ref, first, count, tile, finish):
+    waiting = None
+    for at in range(0, count, HD):
+        cols = pl.ds(pl.multiple_of(first + at, HD), HD)
+        weights = w_ref[:, cols]
+        for start in range(0, a_ref.shape[0], tile):
+            span = slice(start, start + tile)
+            term = jnp.dot(a_ref[span, :], weights, preferred_element_type=jnp.float32)
+            if waiting is not None:
+                finish(*waiting)
+            waiting = (span, cols, term)
+    finish(*waiting)
+
+
 def own_kernel(a_ref, w_ref, sum_ref, out_ref):
     rows, width = out_ref.shape
     tile = rows // 2
     chunk = width // 4
 
     def body(step, carry):
-        for at in range(0, chunk, HD):
-            cols = pl.ds(pl.multiple_of(step * chunk + at, HD), HD)
-            weights = w_ref[:, cols]
-            for start in range(0, rows, tile):
-                span = slice(start, start + tile)
-                term = jnp.dot(a_ref[span, :], weights, preferred_element_type=jnp.float32)
-                out_ref[span, cols] = clip(term, sum_ref[span, cols])
+        def finish(span, cols, term):
+            out_ref[span, cols] = clip(term, sum_ref[span, cols])
+
+        in_tiles(a_ref, w_ref, step * chunk, chunk, tile, finish)
         return carry
 
     lax.fori_loop(0, 4, body, 0)
@@ -325,14 +333,11 @@
         return pltpu.make_async_copy(staged.at[:, span], out_ref.at[:, span], sems.at[step])
 
     def body(step, carry):
-        for at in range(0, chunk, HD):
-            cols = pl.ds(pl.multiple_of(step * chunk + at, HD), HD)
-            weights = wb_ref[:, cols]
-            for start in range(0, rows, tile):
-                span = slice(start, start + tile)
-                term = jnp.dot(b_ref[span, :], weights, preferred_element_type=jnp.float32)
-                quant = clip(term, sum_ref[span, cols]).astype(jnp.float32) + quant_ref[span, cols].astype(jnp.float32)
-                staged[span, cols] = clip(x_ref[span, cols].astype(jnp.float32) + quant, last_ref[span, cols])
+        def finish(span, cols, term):
+            quant = clip(term, sum_ref[span, cols]).astype(jnp.float32) + quant_ref[span, cols].astype(jnp.float32)
+            staged[span, cols] = clip(x_ref[span, cols].astype(jnp.float32) + quant, last_ref[span, cols])
+
+        in_tiles(b_ref, wb_ref, step * chunk, chunk, tile, finish)
         copy(step).start()
         return carry
 
@@ -344,7 +349,7 @@
 def project_out(att_other, w_other, quant_own, sum_bound, out_bound, tokens):
     rows, width = tokens.shape
     depth = att_other.shape[1]
-    steps = 4
+    steps = 8
     vmem = pl.BlockSpec(memory_space=pltpu.VMEM)
     operands = [att_other, w_other, quant_own, tokens, sum_bound, out_bound]
     return pl.pallas_call(

time: 42 us -> 43.2 us (1.029)
  Pallas kernels: 19.8 us -> 21 us
    pallas_call x1, Pallas kernels: 6.28 us -> 7 us  [norm_kv(): pl.pallas_call(norm_kv_kernel, in_specs=[hbm] * 4, out_specs=[vmem, vmem]...]
    pallas_call x1, Pallas kernels: 5.25 us -> 5.78 us  [project_out(): pl.pallas_call(output_kernel, in_specs=[vmem] * len(operands), out_specs=...]
where the time goes in v8:
time: 43.2 us; the launch traced here: 43.1 us
  Pallas kernels  21 us (49%)
  starting transfers between devices  11.5 us (27%)
  waiting for transfers between devices  10.2 us (24%)
    pallas_call x1, Pallas kernels, norm_kv(): pl.pallas_call(norm_kv_kernel, in_specs=[hbm] * 4, out_specs=[vmem, vmem]...  7 us
    ppermute x7, starting transfers between devices, swap_cores(): return lax.ppermute(x, 'tp', [(0, 1), (1, 0)])  6.26 us
    pallas_call x1, Pallas kernels, project_out(): pl.pallas_call(output_kernel, in_specs=[vmem] * len(operands), out_specs=...  5.78 us
    ppermute x3, waiting for transfers between devices, shift(): return lax.ppermute(x, ('seq', 'tp'), pairs)  4.91 us
    ppermute x3, starting transfers between devices, shift(): return lax.ppermute(x, ('seq', 'tp'), pairs)  3.89 us
    ppermute x1, waiting for transfers between devices, on_device(): lax.ppermute(jnp.where(odd, held, message), 'seq', [(i, i ^ 1) for i in r...  3.83 us
    pallas_call x3, Pallas kernels, attend(): pl.pallas_call(functools.partial(attend_kernel, plan, first, last), in_sp...  2.66 us
    pallas_call x1, Pallas kernels, spread_bounds(): pl.pallas_call(bounds_kernel, in_specs=[vmem, vmem, pl.BlockSpec(memory_s...  2.49 us
  transfers between devices with their start and end apart: 11, of which 4 were waited for; matrix products, arithmetic and copies ran while one was open for 0% of the time, Pallas kernels for 35%

profile of v8, /device:TPU:11, one launch (start us, length us, event | category | flops | bytes accessed | tf_op | source)
XLA Modules:
  0.0 43.1 jit_solution(4953236876501495791)
XLA Ops:
  0.0 0.7 %collective-permute-start.10 = (bf16[256,4096]{1,0:T(8,128)(2,1)}, bf16[256,4096]{1,0:T(8,128)(2,1)S(1)}, u32[]{:S(2)}, u32[]{:S(2)}) collective-permute-start(bf16[256,4096]{1,0:T(8,128)(2,1)} %w_ref.5), channel_id=1, source_target_pairs={{0,1},{1,0},{2,3},{3,2},{4,5},{5,4},{6,7},{7,6},{8,9},{9,8},{10,11... | collective-permute-start | bytes 6291464 | tf_op jit(solution)/shard_map/ppermute | solution.py:373
  0.7 7.0 %norm_kv.1 = (bf16[528,256]{1,0:T(8,128)(2,1)S(1)}, bf16[512,4096]{1,0:T(8,128)(2,1)S(1)}) custom-call(bf16[512,4096]{1,0:T(8,128)(2,1)} %x_ref.3, f32[1,4096]{1,0:T(1,128)} %bitcast.10, bf16[4096,256]{1,0:T(8,128)(2,1)} %w_ref.3, s32[1,512]{1,0:T(1,128)} %bitcast.6), custom_call_target="tpu_custom_call" | custom-call | flops 1073741824 | bytes 10485760 | tf_op jit(solution)/shard_map/norm_kv/pallas_call | solution.py:100
  7.7 0.0 copy-start.3
  7.7 1.3 %collective-permute-start = (bf16[528,256]{1,0:T(8,128)(2,1)S(1)}, bf16[528,256]{1,0:T(8,128)(2,1)S(1)}, u32[]{:S(2)}, u32[]{:S(2)}) collective-permute-start(bf16[528,256]{1,0:T(8,128)(2,1)S(1)} %get-tuple-element.21.refs_2_), channel_id=1, source_target_pairs={{0,4},{1,5},{2,6},{3,7},{4,8},{5,9},{6,10},{7,11},{8,12},{9,13},{1... | collective-permute-start | bytes 811016 | tf_op jit(solution)/shard_map/ppermute | solution.py:382
  9.1 0.4 %collective-permute-start.2 = (bf16[528,256]{1,0:T(8,128)(2,1)S(1)}, bf16[528,256]{1,0:T(8,128)(2,1)S(1)}, u32[]{:S(2)}, u32[]{:S(2)}) collective-permute-start(bf16[528,256]{1,0:T(8,128)(2,1)S(1)} %get-tuple-element.21.refs_2_), channel_id=1, source_target_pairs={{0,1},{1,0},{2,3},{3,2},{4,5},{5,4},{6,7},{7,6},{8,9},{9,8},{10,11... | collective-permute-start | bytes 811016 | tf_op jit(solution)/shard_map/ppermute | solution.py:373
  9.5 1.2 %project_query.1.refs_0_ = bf16[512,256]{1,0:T(8,128)(2,1)S(1)} custom-call(bf16[512,4096]{1,0:T(8,128)(2,1)S(1)} %get-tuple-element.22.x_ref, bf16[4096,256]{1,0:T(8,128)(2,1)S(1)} %copy-done), custom_call_target="tpu_custom_call" | custom-call | flops 1073741824 | bytes 6291456 | tf_op jit(solution)/shard_map/project_query/pallas_call | solution.py:128
  10.8 4.9 %collective-permute-done.refs_3_ = bf16[528,256]{1,0:T(8,128)(2,1)S(1)} collective-permute-done((bf16[528,256]{1,0:T(8,128)(2,1)S(1)}, bf16[528,256]{1,0:T(8,128)(2,1)S(1)}, u32[]{:S(2)}, u32[]{:S(2)}) %collective-permute-start) | collective-permute-done | bytes 270368 | tf_op jit(solution)/shard_map/ppermute | solution.py:382
  15.7 1.2 %collective-permute-start.7 = (bf16[528,256]{1,0:T(8,128)(2,1)S(1)}, bf16[528,256]{1,0:T(8,128)(2,1)S(1)}, u32[]{:S(2)}, u32[]{:S(2)}) collective-permute-start(bf16[528,256]{1,0:T(8,128)(2,1)S(1)} %collective-permute-done.refs_3_), channel_id=1, source_target_pairs={{0,1},{1,0},{2,3},{3,2},{4,6},{5,7},{6,8},{7,9},{8,10},{9,11},{10,... | collective-permute-start | bytes 811016 | tf_op jit(solution)/shard_map/ppermute | solution.py:382
  16.9 1.3 %collective-permute-start.4 = (bf16[528,256]{1,0:T(8,128)(2,1)S(1)}, bf16[528,256]{1,0:T(8,128)(2,1)S(1)}, u32[]{:S(2)}, u32[]{:S(2)}) collective-permute-start(bf16[528,256]{1,0:T(8,128)(2,1)S(1)} %collective-permute-done.refs_3_), channel_id=1, source_target_pairs={{0,1},{1,0},{2,3},{3,2},{4,8},{5,9},{6,10},{7,11},{8,12},{9,13},{1... | collective-permute-start | bytes 811016 | tf_op jit(solution)/shard_map/ppermute | solution.py:382
  18.2 1.5 %collective-permute-start.3 = (bf16[528,256]{1,0:T(8,128)(2,1)S(1)}, bf16[528,256]{1,0:T(8,128)(2,1)S(1)}, u32[]{:S(2)}, u32[]{:S(2)}) collective-permute-start(bf16[528,256]{1,0:T(8,128)(2,1)S(1)} %collective-permute-done.refs_3_), channel_id=1, source_target_pairs={{0,1},{1,0},{2,3},{3,2},{4,5},{5,4},{6,7},{7,6},{8,9},{9,8},{10,11... | collective-permute-start | bytes 811016 | tf_op jit(solution)/shard_map/ppermute | solution.py:373
  19.8 1.3 %collective-permute-start.1 = (bf16[528,256]{1,0:T(8,128)(2,1)S(1)}, bf16[528,256]{1,0:T(8,128)(2,1)S(1)}, u32[]{:S(2)}, u32[]{:S(2)}) collective-permute-start(bf16[528,256]{1,0:T(8,128)(2,1)S(1)} %broadcast_select_fusion), channel_id=1, source_target_pairs={{0,2},{2,0},{4,6},{6,4},{8,10},{10,8},{12,14},{14,12},{1,3},{3,1},... | collective-permute-start | bytes 811016 | tf_op jit(solution)/shard_map/ppermute | solution.py:389
  21.1 2.5 %spread_bounds.1 = (bf16[512,4096]{1,0:T(8,128)(2,1)S(1)}, bf16[512,4096]{1,0:T(8,128)(2,1)S(1)}, bf16[512,4096]{1,0:T(8,128)(2,1)S(1)}) custom-call(s32[32,512]{1,0:T(8,128)S(1)} %bitcast.4, s32[32,512]{1,0:T(8,128)S(1)} %bitcast.5, bf16[512,4096]{1,0:T(8,128)(2,1)} %x_ref.3), custom_call_target="tpu_custom_call" | custom-call | flops 16777216 | bytes 131072 | tf_op jit(solution)/shard_map/spread_bounds/pallas_call | solution.py:263
  23.6 0.0 copy-start.1
  23.6 1.6 %attend_first.1.refs_4_ = f32[512,512]{1,0:T(8,128)S(1)} custom-call(bf16[512,256]{1,0:T(8,128)(2,1)S(1)} %project_query.1.refs_0_, s32[1,512]{1,0:T(1,128)S(1)} %bitcast.7, bf16[528,256]{1,0:T(8,128)(2,1)S(1)} %get-tuple-element.21.refs_2_, bf16[528,256]{1,0:T(8,128)(2,1)S(1)} %collective-permute-done.refs_3_, ...), custom_call_target="tpu_custom_call" | custom-call | flops 536870912 | bytes 1048576 | tf_op jit(solution)/shard_map/attend_first/pallas_call | solution.py:230
  25.3 2.7 %collective-permute-start.8 = (bf16[528,256]{1,0:T(8,128)(2,1)S(1)}, bf16[528,256]{1,0:T(8,128)(2,1)S(1)}, u32[]{:S(2)}, u32[]{:S(2)}) collective-permute-start(bf16[528,256]{1,0:T(8,128)(2,1)S(1)} %collective-permute-done.7.refs_2_), channel_id=1, source_target_pairs={{0,1},{1,0},{2,3},{3,2},{4,5},{5,4},{6,7},{7,6},{8,9},{9,8},{10,11... | collective-permute-start | bytes 811016 | tf_op jit(solution)/shard_map/ppermute | solution.py:373
  27.9 3.8 %collective-permute-done.1.refs_2_ = bf16[528,256]{1,0:T(8,128)(2,1)S(1)} collective-permute-done((bf16[528,256]{1,0:T(8,128)(2,1)S(1)}, bf16[528,256]{1,0:T(8,128)(2,1)S(1)}, u32[]{:S(2)}, u32[]{:S(2)}) %collective-permute-start.1) | collective-permute-done | bytes 270368 | tf_op jit(solution)/shard_map/ppermute | solution.py:389
  31.7 0.4 %collective-permute-start.5 = (bf16[528,256]{1,0:T(8,128)(2,1)S(1)}, bf16[528,256]{1,0:T(8,128)(2,1)S(1)}, u32[]{:S(2)}, u32[]{:S(2)}) collective-permute-start(bf16[528,256]{1,0:T(8,128)(2,1)S(1)} %collective-permute-done.1.refs_2_), channel_id=1, source_target_pairs={{0,1},{1,0},{2,3},{3,2},{4,5},{5,4},{6,7},{7,6},{8,9},{9,8},{10,11... | collective-permute-start | bytes 811016 | tf_op jit(solution)/shard_map/ppermute | solution.py:373
  32.2 0.1 collective-permute-start.6
  32.3 1.1 %collective-permute-done.5.refs_4_ = bf16[528,256]{1,0:T(8,128)(2,1)S(1)} collective-permute-done((bf16[528,256]{1,0:T(8,128)(2,1)S(1)}, bf16[528,256]{1,0:T(8,128)(2,1)S(1)}, u32[]{:S(2)}, u32[]{:S(2)}) %collective-permute-start.5) | collective-permute-done | bytes 270368 | tf_op jit(solution)/shard_map/ppermute | solution.py:373
  33.4 0.4 collective-permute-done.6.refs_5_
  33.7 1.1 %attend_last.1.a_ref = bf16[512,256]{1,0:T(8,128)(2,1)S(1)} custom-call(bf16[512,256]{1,0:T(8,128)(2,1)S(1)} %project_query.1.refs_0_, s32[1,512]{1,0:T(1,128)S(1)} %bitcast.9, bf16[528,256]{1,0:T(8,128)(2,1)S(1)} %collective-permute-done.1.refs_2_, bf16[528,256]{1,0:T(8,128)(2,1)S(1)} %collective-permute-done.4.refs_3_, ...), custom_call_target="tpu_custom_call" | custom-call | flops 536870912 | bytes 1048576 | tf_op jit(solution)/shard_map/attend_last/pallas_call | solution.py:230
  34.8 0.4 %collective-permute-start.9 = (bf16[512,256]{1,0:T(8,128)(2,1)S(1)}, bf16[512,256]{1,0:T(8,128)(2,1)S(1)}, u32[]{:S(2)}, u32[]{:S(2)}) collective-permute-start(bf16[512,256]{1,0:T(8,128)(2,1)S(1)} %attend_last.1.a_ref), channel_id=1, source_target_pairs={{0,1},{1,0},{2,3},{3,2},{4,5},{5,4},{6,7},{7,6},{8,9},{9,8},{10,11... | collective-permute-start | bytes 786440 | tf_op jit(solution)/shard_map/ppermute | solution.py:373
  35.3 1.9 %project_own.1.quant_ref = bf16[512,4096]{1,0:T(8,128)(2,1)S(1)} custom-call(bf16[512,256]{1,0:T(8,128)(2,1)S(1)} %attend_last.1.a_ref, bf16[256,4096]{1,0:T(8,128)(2,1)S(1)} %copy-done.1, bf16[512,4096]{1,0:T(8,128)(2,1)S(1)} %get-tuple-element.30.sum_ref), custom_call_target="tpu_custom_call" | custom-call | flops 1073741824 | bytes 10485760 | tf_op jit(solution)/shard_map/project_own/pallas_call | solution.py:312
  37.2 5.8 %project_out.1 = bf16[512,4096]{1,0:T(8,128)(2,1)} custom-call(bf16[512,256]{1,0:T(8,128)(2,1)S(1)} %collective-permute-done.9.b_ref, bf16[256,4096]{1,0:T(8,128)(2,1)S(1)} %collective-permute-done.10.wb_ref, bf16[512,4096]{1,0:T(8,128)(2,1)S(1)} %project_own.1.quant_ref, bf16[512,4096]{1,0:T(8,128)(2,1)S(1)} %get-tuple-element.32.x_ref, ...), custom_call_target="tpu_custom_call" | custom-call | flops 1073741824 | bytes 10485760 | tf_op jit(solution)/shard_map/project_out/pallas_call | solution.py:355
  (17 shorter events, 0.1 us)
Async XLA Ops:
  0.0 9.5 %copy-start = (bf16[4096,256]{1,0:T(8,128)(2,1)S(1)}, bf16[4096,256]{1,0:T(8,128)(2,1)}, u32[]{:S(2)}) copy-start(bf16[4096,256]{1,0:T(8,128)(2,1)} %w_ref.4) | copy-start | bytes 6291460
  0.0 37.2 %collective-permute-start.10 = (bf16[256,4096]{1,0:T(8,128)(2,1)}, bf16[256,4096]{1,0:T(8,128)(2,1)S(1)}, u32[]{:S(2)}, u32[]{:S(2)}) collective-permute-start(bf16[256,4096]{1,0:T(8,128)(2,1)} %w_ref.5), channel_id=1, source_target_pairs={{0,1},{1,0},{2,3},{3,2},{4,5},{5,4},{6,7},{7,6},{8,9},{9,8},{10,11... | collective-permute-start | bytes 6291464 | tf_op jit(solution)/shard_map/ppermute | solution.py:373
  7.7 13.4 %copy-start.2 = (s32[512,32]{0,1:T(8,128)S(1)}, s32[512,32]{0,1:T(8,128)}, u32[]{:S(2)}) copy-start(s32[512,32]{0,1:T(8,128)} %param.14) | copy-start | bytes 196612
  7.7 13.4 %copy-start.3 = (s32[512,32]{0,1:T(8,128)S(1)}, s32[512,32]{0,1:T(8,128)}, u32[]{:S(2)}) copy-start(s32[512,32]{0,1:T(8,128)} %param.15) | copy-start | bytes 196612
  7.7 8.0 %collective-permute-start = (bf16[528,256]{1,0:T(8,128)(2,1)S(1)}, bf16[528,256]{1,0:T(8,128)(2,1)S(1)}, u32[]{:S(2)}, u32[]{:S(2)}) collective-permute-start(bf16[528,256]{1,0:T(8,128)(2,1)S(1)} %get-tuple-element.21.refs_2_), channel_id=1, source_target_pairs={{0,4},{1,5},{2,6},{3,7},{4,8},{5,9},{6,10},{7,11},{8,12},{9,13},{1... | collective-permute-start | bytes 811016 | tf_op jit(solution)/shard_map/ppermute | solution.py:382
  9.1 10.7 %collective-permute-start.2 = (bf16[528,256]{1,0:T(8,128)(2,1)S(1)}, bf16[528,256]{1,0:T(8,128)(2,1)S(1)}, u32[]{:S(2)}, u32[]{:S(2)}) collective-permute-start(bf16[528,256]{1,0:T(8,128)(2,1)S(1)} %get-tuple-element.21.refs_2_), channel_id=1, source_target_pairs={{0,1},{1,0},{2,3},{3,2},{4,5},{5,4},{6,7},{7,6},{8,9},{9,8},{10,11... | collective-permute-start | bytes 811016 | tf_op jit(solution)/shard_map/ppermute | solution.py:373
  10.8 12.9 %copy-start.4 = (s32[512]{0:T(512)S(1)}, s32[512]{0:T(512)}, u32[]{:S(2)}) copy-start(s32[512]{0:T(512)} %param.10) | copy-start | bytes 6148
  15.7 9.6 %collective-permute-start.7 = (bf16[528,256]{1,0:T(8,128)(2,1)S(1)}, bf16[528,256]{1,0:T(8,128)(2,1)S(1)}, u32[]{:S(2)}, u32[]{:S(2)}) collective-permute-start(bf16[528,256]{1,0:T(8,128)(2,1)S(1)} %collective-permute-done.refs_3_), channel_id=1, source_target_pairs={{0,1},{1,0},{2,3},{3,2},{4,6},{5,7},{6,8},{7,9},{8,10},{9,11},{10,... | collective-permute-start | bytes 811016 | tf_op jit(solution)/shard_map/ppermute | solution.py:382
  16.9 11.0 %collective-permute-start.4 = (bf16[528,256]{1,0:T(8,128)(2,1)S(1)}, bf16[528,256]{1,0:T(8,128)(2,1)S(1)}, u32[]{:S(2)}, u32[]{:S(2)}) collective-permute-start(bf16[528,256]{1,0:T(8,128)(2,1)S(1)} %collective-permute-done.refs_3_), channel_id=1, source_target_pairs={{0,1},{1,0},{2,3},{3,2},{4,8},{5,9},{6,10},{7,11},{8,12},{9,13},{1... | collective-permute-start | bytes 811016 | tf_op jit(solution)/shard_map/ppermute | solution.py:382
  18.2 5.4 %collective-permute-start.3 = (bf16[528,256]{1,0:T(8,128)(2,1)S(1)}, bf16[528,256]{1,0:T(8,128)(2,1)S(1)}, u32[]{:S(2)}, u32[]{:S(2)}) collective-permute-start(bf16[528,256]{1,0:T(8,128)(2,1)S(1)} %collective-permute-done.refs_3_), channel_id=1, source_target_pairs={{0,1},{1,0},{2,3},{3,2},{4,5},{5,4},{6,7},{7,6},{8,9},{9,8},{10,11... | collective-permute-start | bytes 811016 | tf_op jit(solution)/shard_map/ppermute | solution.py:373
  19.8 11.9 %collective-permute-start.1 = (bf16[528,256]{1,0:T(8,128)(2,1)S(1)}, bf16[528,256]{1,0:T(8,128)(2,1)S(1)}, u32[]{:S(2)}, u32[]{:S(2)}) collective-permute-start(bf16[528,256]{1,0:T(8,128)(2,1)S(1)} %broadcast_select_fusion), channel_id=1, source_target_pairs={{0,2},{2,0},{4,6},{6,4},{8,10},{10,8},{12,14},{14,12},{1,3},{3,1},... | collective-permute-start | bytes 811016 | tf_op jit(solution)/shard_map/ppermute | solution.py:389
  23.6 11.7 %copy-start.1 = (bf16[256,4096]{1,0:T(8,128)(2,1)S(1)}, bf16[256,4096]{1,0:T(8,128)(2,1)}, u32[]{:S(2)}) copy-start(bf16[256,4096]{1,0:T(8,128)(2,1)} %w_ref.5) | copy-start | bytes 6291460
  25.3 7.0 %collective-permute-start.8 = (bf16[528,256]{1,0:T(8,128)(2,1)S(1)}, bf16[528,256]{1,0:T(8,128)(2,1)S(1)}, u32[]{:S(2)}, u32[]{:S(2)}) collective-permute-start(bf16[528,256]{1,0:T(8,128)(2,1)S(1)} %collective-permute-done.7.refs_2_), channel_id=1, source_target_pairs={{0,1},{1,0},{2,3},{3,2},{4,5},{5,4},{6,7},{7,6},{8,9},{9,8},{10,11... | collective-permute-start | bytes 811016 | tf_op jit(solution)/shard_map/ppermute | solution.py:373
  31.7 1.6 %collective-permute-start.5 = (bf16[528,256]{1,0:T(8,128)(2,1)S(1)}, bf16[528,256]{1,0:T(8,128)(2,1)S(1)}, u32[]{:S(2)}, u32[]{:S(2)}) collective-permute-start(bf16[528,256]{1,0:T(8,128)(2,1)S(1)} %collective-permute-done.1.refs_2_), channel_id=1, source_target_pairs={{0,1},{1,0},{2,3},{3,2},{4,5},{5,4},{6,7},{7,6},{8,9},{9,8},{10,11... | collective-permute-start | bytes 811016 | tf_op jit(solution)/shard_map/ppermute | solution.py:373
  32.2 1.6 %collective-permute-start.6 = (bf16[528,256]{1,0:T(8,128)(2,1)S(1)}, bf16[528,256]{1,0:T(8,128)(2,1)S(1)}, u32[]{:S(2)}, u32[]{:S(2)}) collective-permute-start(bf16[528,256]{1,0:T(8,128)(2,1)S(1)} %collective-permute-done.4.refs_3_), channel_id=1, source_target_pairs={{0,1},{1,0},{2,3},{3,2},{4,5},{5,4},{6,7},{7,6},{8,9},{9,8},{10,11... | collective-permute-start | bytes 811016 | tf_op jit(solution)/shard_map/ppermute | solution.py:373
  34.8 2.3 %collective-permute-start.9 = (bf16[512,256]{1,0:T(8,128)(2,1)S(1)}, bf16[512,256]{1,0:T(8,128)(2,1)S(1)}, u32[]{:S(2)}, u32[]{:S(2)}) collective-permute-start(bf16[512,256]{1,0:T(8,128)(2,1)S(1)} %attend_last.1.a_ref), channel_id=1, source_target_pairs={{0,1},{1,0},{2,3},{3,2},{4,5},{5,4},{6,7},{7,6},{8,9},{9,8},{10,11... | collective-permute-start | bytes 786440 | tf_op jit(solution)/shard_map/ppermute | solution.py:373

commit v9 on v7

--- a/solution.py
+++ b/solution.py
@@ -48,25 +48,19 @@
     def wide(first, count, start):
         return xs[first:first + count, start:start + LANES].astype(jnp.float32)
 
-    def stats(first):
-        total = wide(first, part, 0)
+    for first in range(0, rows, tile):
+        for at in range(first, first + tile, part):
+            tokens_copy(at // part).wait()
+        total = wide(first, tile, 0)
         for start in range(LANES, width, LANES):
-            total = total + wide(first, part, start)
-        mean = jnp.broadcast_to(jnp.sum(total, axis=1, keepdims=True) * (1.0 / width), (part, LANES))
-        square = jnp.zeros((part, LANES), jnp.float32)
+            total = total + wide(first, tile, start)
+        mean = jnp.broadcast_to(jnp.sum(total, axis=1, keepdims=True) * (1.0 / width), (tile, LANES))
+        square = jnp.zeros((tile, LANES), jnp.float32)
         for start in range(0, width, LANES):
-            center = wide(first, part, start) - mean
+            center = wide(first, tile, start) - mean
             square = square + center * center
         spread = jnp.sum(square, axis=1, keepdims=True) * (1.0 / width)
-        return mean, jnp.broadcast_to(lax.rsqrt(spread + 1e-05), (part, LANES))
-
-    for first in range(0, rows, tile):
-        halves = []
-        for at in range(first, first + tile, part):
-            tokens_copy(at // part).wait()
-            halves.append(stats(at))
-        mean = jnp.concatenate([h[0] for h in halves], axis=0)
-        scale = jnp.concatenate([h[1] for h in halves], axis=0)
+        scale = jnp.broadcast_to(lax.rsqrt(spread + 1e-05), (tile, LANES))
         if first == 0:
             gain_copy().wait()
             for i in range(pieces):
@@ -245,18 +239,25 @@
     )(*[in_vmem(operand) for operand in operands])
 
 
-def bounds_kernel(sum_ref, out_exp_ref, x_ref, sum_bound_ref, out_bound_ref, near_ref, sem):
+def bounds_kernel(sum_ref, out_exp_ref, x_ref, sum_bound_ref, out_bound_ref, wide_ref, near, sem):
     groups, rows = sum_ref.shape
-    fetch = pltpu.make_async_copy(x_ref, near_ref, sem)
+    fetch = pltpu.make_async_copy(x_ref, near, sem)
     fetch.start()
     per = sum_bound_ref.shape[1] // groups
     for exps, bound_ref in ((sum_ref, sum_bound_ref), (out_exp_ref, out_bound_ref)):
         power = jnp.left_shift(jnp.int32(1), exps[...] - MIN_EXP).astype(jnp.float32)
         bound = jnp.transpose(power * (LIMIT * 2.0 ** MIN_EXP))
         for group in range(groups):
-            wide = jnp.broadcast_to(bound[:, group:group + 1], (rows, per))
-            bound_ref[:, group * per:(group + 1) * per] = wide.astype(jnp.bfloat16)
+            wide = jnp.broadcast_to(bound[:, group:group + 1], (rows, per)).astype(jnp.bfloat16)
+            bound_ref[:, group * per:(group + 1) * per] = wide
     fetch.wait()
+
+    def widen(step, carry):
+        span = pl.ds(pl.multiple_of(step * 64, 64), 64)
+        wide_ref[span, :] = near[span, :].astype(jnp.float32)
+        return carry
+
+    lax.fori_loop(0, rows // 64, widen, 0)
 
 
 def spread_bounds(sum_exps, out_exps, tokens):
@@ -267,9 +268,9 @@
         bounds_kernel,
         in_specs=[vmem, vmem, pl.BlockSpec(memory_space=pltpu.HBM)],
         out_specs=[vmem] * 3,
-        out_shape=[pltpu.VMEM((rows, width), jnp.bfloat16)] * 3,
-        scratch_shapes=[pltpu.SemaphoreType.DMA(())],
-        compiler_params=pltpu.CompilerParams(vmem_limit_bytes=8 * MIB),
+        out_shape=[pltpu.VMEM((rows, width), jnp.bfloat16)] * 2 + [pltpu.VMEM((rows, width), jnp.float32)],
+        scratch_shapes=[pltpu.VMEM((rows, width), jnp.bfloat16), pltpu.SemaphoreType.DMA(())],
+        compiler_params=pltpu.CompilerParams(vmem_limit_bytes=10 * MIB),
         cost_estimate=pl.CostEstimate(flops=8 * rows * width, bytes_accessed=8 * rows * groups, transcendentals=0),
         name="spread_bounds",
     )(in_vmem(sum_exps.T), in_vmem(out_exps.T), in_hbm(tokens))
@@ -316,13 +317,14 @@
 
 def output_kernel(b_ref, wb_ref, quant_ref, x_ref, sum_ref, last_ref, out_ref, staged, sems):
     rows, width = x_ref.shape
-    steps = sems.shape[0]
-    chunk = width // steps
+    pieces = sems.shape[0]
+    piece = width // pieces
+    chunk = width // 2
     tile = rows // 2
 
-    def copy(step):
-        span = pl.ds(pl.multiple_of(step * chunk, chunk), chunk)
-        return pltpu.make_async_copy(staged.at[:, span], out_ref.at[:, span], sems.at[step])
+    def copy(index):
+        span = pl.ds(pl.multiple_of(index * piece, piece), piece)
+        return pltpu.make_async_copy(staged.at[:, span], out_ref.at[:, span], sems.at[index])
 
     def body(step, carry):
         for at in range(0, chunk, HD):
@@ -331,20 +333,22 @@
             for start in range(0, rows, tile):
                 span = slice(start, start + tile)
                 term = jnp.dot(b_ref[span, :], weights, preferred_element_type=jnp.float32)
-                quant = clip(term, sum_ref[span, cols]).astype(jnp.float32) + quant_ref[span, cols].astype(jnp.float32)
-                staged[span, cols] = clip(x_ref[span, cols].astype(jnp.float32) + quant, last_ref[span, cols])
-        copy(step).start()
+                other = clip(term, sum_ref[span, cols])
+                quant = other.astype(jnp.float32) + quant_ref[span, cols].astype(jnp.float32)
+                staged[span, cols] = clip(x_ref[span, cols] + quant, last_ref[span, cols])
+            if (at + HD) % piece == 0:
+                copy(step * (chunk // piece) + at // piece).start()
         return carry
 
-    lax.fori_loop(0, steps, body, 0)
-    for step in range(steps):
-        copy(step).wait()
+    lax.fori_loop(0, width // chunk, body, 0)
+    for index in range(pieces):
+        copy(index).wait()
 
 
 def project_out(att_other, w_other, quant_own, sum_bound, out_bound, tokens):
     rows, width = tokens.shape
     depth = att_other.shape[1]
-    steps = 4
+    pieces = 8
     vmem = pl.BlockSpec(memory_space=pltpu.VMEM)
     operands = [att_other, w_other, quant_own, tokens, sum_bound, out_bound]
     return pl.pallas_call(
@@ -352,8 +356,8 @@
         in_specs=[vmem] * len(operands),
         out_specs=pl.BlockSpec(memory_space=pltpu.HBM),
         out_shape=jax.ShapeDtypeStruct((rows, width), jnp.bfloat16),
-        scratch_shapes=[pltpu.VMEM((rows, width), jnp.bfloat16), pltpu.SemaphoreType.DMA((steps,))],
-        compiler_params=pltpu.CompilerParams(vmem_limit_bytes=12 * MIB),
+        scratch_shapes=[pltpu.VMEM((rows, width), jnp.bfloat16), pltpu.SemaphoreType.DMA((pieces,))],
+        compiler_params=pltpu.CompilerParams(vmem_limit_bytes=10 * MIB),
         cost_estimate=pl.CostEstimate(
             flops=2 * rows * width * depth, bytes_accessed=4 * rows * width + 2 * width * depth, transcendentals=0
         ),

time: 42 us -> 41.3 us (0.983)
  starting transfers between devices: 11.5 us -> 10.9 us
    pallas_call x1, Pallas kernels: 5.25 us -> 4.62 us  [project_out(): pl.pallas_call(output_kernel, in_specs=[vmem] * len(operands), out_specs=...]
    pallas_call x1, Pallas kernels: 2.49 us -> 3.05 us  [spread_bounds(): pl.pallas_call(bounds_kernel, in_specs=[vmem, vmem, pl.BlockSpec(memory_s...]
    ppermute x7, starting transfers between devices: 6.26 us -> 5.71 us  [swap_cores(): return lax.ppermute(x, 'tp', [(0, 1), (1, 0)])]
  transfers between devices with their start and end apart: 11 -> 11, of which waited for: 4 -> 4; matrix products, arithmetic and copies ran while one was open for 0% -> 0% of each run, Pallas kernels for 35% -> 37%
where the time goes in v9:
time: 41.3 us; the launch traced here: 41.1 us
  Pallas kernels  19.6 us (47%)
  starting transfers between devices  10.9 us (26%)
  waiting for transfers between devices  10.2 us (25%)
    pallas_call x1, Pallas kernels, norm_kv(): pl.pallas_call(norm_kv_kernel, in_specs=[hbm] * 4, out_specs=[vmem, vmem]...  6.19 us
    ppermute x7, starting transfers between devices, swap_cores(): return lax.ppermute(x, 'tp', [(0, 1), (1, 0)])  5.71 us
    ppermute x3, waiting for transfers between devices, shift(): return lax.ppermute(x, ('seq', 'tp'), pairs)  4.91 us
    pallas_call x1, Pallas kernels, project_out(): pl.pallas_call(output_kernel, in_specs=[vmem] * len(operands), out_specs=...  4.62 us
    ppermute x3, starting transfers between devices, shift(): return lax.ppermute(x, ('seq', 'tp'), pairs)  3.88 us
    ppermute x1, waiting for transfers between devices, on_device(): lax.ppermute(jnp.where(odd, held, message), 'seq', [(i, i ^ 1) for i in r...  3.83 us
    pallas_call x1, Pallas kernels, spread_bounds(): pl.pallas_call(bounds_kernel, in_specs=[vmem, vmem, pl.BlockSpec(memory_s...  3.05 us
    pallas_call x3, Pallas kernels, attend(): pl.pallas_call(functools.partial(attend_kernel, plan, first, last), in_sp...  2.67 us
  transfers between devices with their start and end apart: 11, of which 4 were waited for; matrix products, arithmetic and copies ran while one was open for 0% of the time, Pallas kernels for 37%

profile of v9, /device:TPU:11, one launch (start us, length us, event | category | flops | bytes accessed | tf_op | source)
XLA Modules:
  0.0 41.1 jit_solution(11947777679993999783)
XLA Ops:
  0.0 0.7 %collective-permute-start.10 = (bf16[256,4096]{1,0:T(8,128)(2,1)}, bf16[256,4096]{1,0:T(8,128)(2,1)S(1)}, u32[]{:S(2)}, u32[]{:S(2)}) collective-permute-start(bf16[256,4096]{1,0:T(8,128)(2,1)} %w_ref.5), channel_id=1, source_target_pairs={{0,1},{1,0},{2,3},{3,2},{4,5},{5,4},{6,7},{7,6},{8,9},{9,8},{10,11... | collective-permute-start | bytes 6291464 | tf_op jit(solution)/shard_map/ppermute | solution.py:372
  0.7 6.2 %norm_kv.1 = (bf16[528,256]{1,0:T(8,128)(2,1)S(1)}, bf16[512,4096]{1,0:T(8,128)(2,1)S(1)}) custom-call(bf16[512,4096]{1,0:T(8,128)(2,1)} %x_ref.3, f32[1,4096]{1,0:T(1,128)} %bitcast.10, bf16[4096,256]{1,0:T(8,128)(2,1)} %w_ref.3, s32[1,512]{1,0:T(1,128)} %bitcast.6), custom_call_target="tpu_custom_call" | custom-call | flops 1073741824 | bytes 10485760 | tf_op jit(solution)/shard_map/norm_kv/pallas_call | solution.py:97
  6.9 0.0 copy-start.2
  6.9 0.0 copy-start.3
  6.9 1.3 %collective-permute-start = (bf16[528,256]{1,0:T(8,128)(2,1)S(1)}, bf16[528,256]{1,0:T(8,128)(2,1)S(1)}, u32[]{:S(2)}, u32[]{:S(2)}) collective-permute-start(bf16[528,256]{1,0:T(8,128)(2,1)S(1)} %get-tuple-element.21.refs_2_), channel_id=1, source_target_pairs={{0,4},{1,5},{2,6},{3,7},{4,8},{5,9},{6,10},{7,11},{8,12},{9,13},{1... | collective-permute-start | bytes 811016 | tf_op jit(solution)/shard_map/ppermute | solution.py:381
  8.3 0.4 %collective-permute-start.2 = (bf16[528,256]{1,0:T(8,128)(2,1)S(1)}, bf16[528,256]{1,0:T(8,128)(2,1)S(1)}, u32[]{:S(2)}, u32[]{:S(2)}) collective-permute-start(bf16[528,256]{1,0:T(8,128)(2,1)S(1)} %get-tuple-element.21.refs_2_), channel_id=1, source_target_pairs={{0,1},{1,0},{2,3},{3,2},{4,5},{5,4},{6,7},{7,6},{8,9},{9,8},{10,11... | collective-permute-start | bytes 811016 | tf_op jit(solution)/shard_map/ppermute | solution.py:372
  8.7 1.2 %project_query.1.refs_0_ = bf16[512,256]{1,0:T(8,128)(2,1)S(1)} custom-call(bf16[512,4096]{1,0:T(8,128)(2,1)S(1)} %get-tuple-element.22.x_ref, bf16[4096,256]{1,0:T(8,128)(2,1)S(1)} %copy-done), custom_call_target="tpu_custom_call" | custom-call | flops 1073741824 | bytes 6291456 | tf_op jit(solution)/shard_map/project_query/pallas_call | solution.py:125
  10.0 4.9 %collective-permute-done.refs_3_ = bf16[528,256]{1,0:T(8,128)(2,1)S(1)} collective-permute-done((bf16[528,256]{1,0:T(8,128)(2,1)S(1)}, bf16[528,256]{1,0:T(8,128)(2,1)S(1)}, u32[]{:S(2)}, u32[]{:S(2)}) %collective-permute-start) | collective-permute-done | bytes 270368 | tf_op jit(solution)/shard_map/ppermute | solution.py:381
  14.9 1.2 %collective-permute-start.7 = (bf16[528,256]{1,0:T(8,128)(2,1)S(1)}, bf16[528,256]{1,0:T(8,128)(2,1)S(1)}, u32[]{:S(2)}, u32[]{:S(2)}) collective-permute-start(bf16[528,256]{1,0:T(8,128)(2,1)S(1)} %collective-permute-done.refs_3_), channel_id=1, source_target_pairs={{0,1},{1,0},{2,3},{3,2},{4,6},{5,7},{6,8},{7,9},{8,10},{9,11},{10,... | collective-permute-start | bytes 811016 | tf_op jit(solution)/shard_map/ppermute | solution.py:381
  16.1 1.3 %collective-permute-start.4 = (bf16[528,256]{1,0:T(8,128)(2,1)S(1)}, bf16[528,256]{1,0:T(8,128)(2,1)S(1)}, u32[]{:S(2)}, u32[]{:S(2)}) collective-permute-start(bf16[528,256]{1,0:T(8,128)(2,1)S(1)} %collective-permute-done.refs_3_), channel_id=1, source_target_pairs={{0,1},{1,0},{2,3},{3,2},{4,8},{5,9},{6,10},{7,11},{8,12},{9,13},{1... | collective-permute-start | bytes 811016 | tf_op jit(solution)/shard_map/ppermute | solution.py:381
  17.4 1.5 %collective-permute-start.3 = (bf16[528,256]{1,0:T(8,128)(2,1)S(1)}, bf16[528,256]{1,0:T(8,128)(2,1)S(1)}, u32[]{:S(2)}, u32[]{:S(2)}) collective-permute-start(bf16[528,256]{1,0:T(8,128)(2,1)S(1)} %collective-permute-done.refs_3_), channel_id=1, source_target_pairs={{0,1},{1,0},{2,3},{3,2},{4,5},{5,4},{6,7},{7,6},{8,9},{9,8},{10,11... | collective-permute-start | bytes 811016 | tf_op jit(solution)/shard_map/ppermute | solution.py:372
  19.0 1.3 %collective-permute-start.1 = (bf16[528,256]{1,0:T(8,128)(2,1)S(1)}, bf16[528,256]{1,0:T(8,128)(2,1)S(1)}, u32[]{:S(2)}, u32[]{:S(2)}) collective-permute-start(bf16[528,256]{1,0:T(8,128)(2,1)S(1)} %broadcast_select_fusion), channel_id=1, source_target_pairs={{0,2},{2,0},{4,6},{6,4},{8,10},{10,8},{12,14},{14,12},{1,3},{3,1},... | collective-permute-start | bytes 811016 | tf_op jit(solution)/shard_map/ppermute | solution.py:388
  20.3 3.0 %spread_bounds.1 = (bf16[512,4096]{1,0:T(8,128)(2,1)S(1)}, bf16[512,4096]{1,0:T(8,128)(2,1)S(1)}, f32[512,4096]{1,0:T(8,128)S(1)}) custom-call(s32[32,512]{1,0:T(8,128)S(1)} %bitcast.4, s32[32,512]{1,0:T(8,128)S(1)} %bitcast.5, bf16[512,4096]{1,0:T(8,128)(2,1)} %x_ref.3), custom_call_target="tpu_custom_call" | custom-call | flops 16777216 | bytes 131072 | tf_op jit(solution)/shard_map/spread_bounds/pallas_call | solution.py:267
  23.4 1.6 %attend_first.1.refs_4_ = f32[512,512]{1,0:T(8,128)S(1)} custom-call(bf16[512,256]{1,0:T(8,128)(2,1)S(1)} %project_query.1.refs_0_, s32[1,512]{1,0:T(1,128)S(1)} %bitcast.7, bf16[528,256]{1,0:T(8,128)(2,1)S(1)} %get-tuple-element.21.refs_2_, bf16[528,256]{1,0:T(8,128)(2,1)S(1)} %collective-permute-done.refs_3_, ...), custom_call_target="tpu_custom_call" | custom-call | flops 536870912 | bytes 1048576 | tf_op jit(solution)/shard_map/attend_first/pallas_call | solution.py:227
  25.0 2.1 %collective-permute-start.8 = (bf16[528,256]{1,0:T(8,128)(2,1)S(1)}, bf16[528,256]{1,0:T(8,128)(2,1)S(1)}, u32[]{:S(2)}, u32[]{:S(2)}) collective-permute-start(bf16[528,256]{1,0:T(8,128)(2,1)S(1)} %collective-permute-done.7.refs_2_), channel_id=1, source_target_pairs={{0,1},{1,0},{2,3},{3,2},{4,5},{5,4},{6,7},{7,6},{8,9},{9,8},{10,11... | collective-permute-start | bytes 811016 | tf_op jit(solution)/shard_map/ppermute | solution.py:372
  27.1 3.8 %collective-permute-done.1.refs_2_ = bf16[528,256]{1,0:T(8,128)(2,1)S(1)} collective-permute-done((bf16[528,256]{1,0:T(8,128)(2,1)S(1)}, bf16[528,256]{1,0:T(8,128)(2,1)S(1)}, u32[]{:S(2)}, u32[]{:S(2)}) %collective-permute-start.1) | collective-permute-done | bytes 270368 | tf_op jit(solution)/shard_map/ppermute | solution.py:388
  30.9 0.4 %collective-permute-start.5 = (bf16[528,256]{1,0:T(8,128)(2,1)S(1)}, bf16[528,256]{1,0:T(8,128)(2,1)S(1)}, u32[]{:S(2)}, u32[]{:S(2)}) collective-permute-start(bf16[528,256]{1,0:T(8,128)(2,1)S(1)} %collective-permute-done.1.refs_2_), channel_id=1, source_target_pairs={{0,1},{1,0},{2,3},{3,2},{4,5},{5,4},{6,7},{7,6},{8,9},{9,8},{10,11... | collective-permute-start | bytes 811016 | tf_op jit(solution)/shard_map/ppermute | solution.py:372
  31.4 0.1 collective-permute-start.6
  31.5 1.1 %collective-permute-done.5.refs_4_ = bf16[528,256]{1,0:T(8,128)(2,1)S(1)} collective-permute-done((bf16[528,256]{1,0:T(8,128)(2,1)S(1)}, bf16[528,256]{1,0:T(8,128)(2,1)S(1)}, u32[]{:S(2)}, u32[]{:S(2)}) %collective-permute-start.5) | collective-permute-done | bytes 270368 | tf_op jit(solution)/shard_map/ppermute | solution.py:372
  32.6 0.4 collective-permute-done.6.refs_5_
  32.9 1.1 %attend_last.1.a_ref = bf16[512,256]{1,0:T(8,128)(2,1)S(1)} custom-call(bf16[512,256]{1,0:T(8,128)(2,1)S(1)} %project_query.1.refs_0_, s32[1,512]{1,0:T(1,128)S(1)} %bitcast.9, bf16[528,256]{1,0:T(8,128)(2,1)S(1)} %collective-permute-done.1.refs_2_, bf16[528,256]{1,0:T(8,128)(2,1)S(1)} %collective-permute-done.4.refs_3_, ...), custom_call_target="tpu_custom_call" | custom-call | flops 536870912 | bytes 1048576 | tf_op jit(solution)/shard_map/attend_last/pallas_call | solution.py:227
  34.0 0.4 %collective-permute-start.9 = (bf16[512,256]{1,0:T(8,128)(2,1)S(1)}, bf16[512,256]{1,0:T(8,128)(2,1)S(1)}, u32[]{:S(2)}, u32[]{:S(2)}) collective-permute-start(bf16[512,256]{1,0:T(8,128)(2,1)S(1)} %attend_last.1.a_ref), channel_id=1, source_target_pairs={{0,1},{1,0},{2,3},{3,2},{4,5},{5,4},{6,7},{7,6},{8,9},{9,8},{10,11... | collective-permute-start | bytes 786440 | tf_op jit(solution)/shard_map/ppermute | solution.py:372
  34.5 1.9 %project_own.1.quant_ref = bf16[512,4096]{1,0:T(8,128)(2,1)S(1)} custom-call(bf16[512,256]{1,0:T(8,128)(2,1)S(1)} %attend_last.1.a_ref, bf16[256,4096]{1,0:T(8,128)(2,1)S(1)} %copy-done.1, bf16[512,4096]{1,0:T(8,128)(2,1)S(1)} %get-tuple-element.30.sum_ref), custom_call_target="tpu_custom_call" | custom-call | flops 1073741824 | bytes 10485760 | tf_op jit(solution)/shard_map/project_own/pallas_call | solution.py:305
  36.4 4.6 %project_out.1 = bf16[512,4096]{1,0:T(8,128)(2,1)} custom-call(bf16[512,256]{1,0:T(8,128)(2,1)S(1)} %collective-permute-done.9.b_ref, bf16[256,4096]{1,0:T(8,128)(2,1)S(1)} %collective-permute-done.10.wb_ref, bf16[512,4096]{1,0:T(8,128)(2,1)S(1)} %project_own.1.quant_ref, f32[512,4096]{1,0:T(8,128)S(1)} %get-tuple-element.32.x_ref, ...), custom_call_target="tpu_custom_call" | custom-call | flops 1073741824 | bytes 10485760 | tf_op jit(solution)/shard_map/project_out/pallas_call | solution.py:354
  (17 shorter events, 0.1 us)
Async XLA Ops:
  0.0 8.7 %copy-start = (bf16[4096,256]{1,0:T(8,128)(2,1)S(1)}, bf16[4096,256]{1,0:T(8,128)(2,1)}, u32[]{:S(2)}) copy-start(bf16[4096,256]{1,0:T(8,128)(2,1)} %w_ref.4) | copy-start | bytes 6291460
  0.0 36.3 %collective-permute-start.10 = (bf16[256,4096]{1,0:T(8,128)(2,1)}, bf16[256,4096]{1,0:T(8,128)(2,1)S(1)}, u32[]{:S(2)}, u32[]{:S(2)}) collective-permute-start(bf16[256,4096]{1,0:T(8,128)(2,1)} %w_ref.5), channel_id=1, source_target_pairs={{0,1},{1,0},{2,3},{3,2},{4,5},{5,4},{6,7},{7,6},{8,9},{9,8},{10,11... | collective-permute-start | bytes 6291464 | tf_op jit(solution)/shard_map/ppermute | solution.py:372
  6.9 13.4 %copy-start.2 = (s32[512,32]{0,1:T(8,128)S(1)}, s32[512,32]{0,1:T(8,128)}, u32[]{:S(2)}) copy-start(s32[512,32]{0,1:T(8,128)} %param.14) | copy-start | bytes 196612
  6.9 13.4 %copy-start.3 = (s32[512,32]{0,1:T(8,128)S(1)}, s32[512,32]{0,1:T(8,128)}, u32[]{:S(2)}) copy-start(s32[512,32]{0,1:T(8,128)} %param.15) | copy-start | bytes 196612
  6.9 8.0 %collective-permute-start = (bf16[528,256]{1,0:T(8,128)(2,1)S(1)}, bf16[528,256]{1,0:T(8,128)(2,1)S(1)}, u32[]{:S(2)}, u32[]{:S(2)}) collective-permute-start(bf16[528,256]{1,0:T(8,128)(2,1)S(1)} %get-tuple-element.21.refs_2_), channel_id=1, source_target_pairs={{0,4},{1,5},{2,6},{3,7},{4,8},{5,9},{6,10},{7,11},{8,12},{9,13},{1... | collective-permute-start | bytes 811016 | tf_op jit(solution)/shard_map/ppermute | solution.py:381
  8.3 10.7 %collective-permute-start.2 = (bf16[528,256]{1,0:T(8,128)(2,1)S(1)}, bf16[528,256]{1,0:T(8,128)(2,1)S(1)}, u32[]{:S(2)}, u32[]{:S(2)}) collective-permute-start(bf16[528,256]{1,0:T(8,128)(2,1)S(1)} %get-tuple-element.21.refs_2_), channel_id=1, source_target_pairs={{0,1},{1,0},{2,3},{3,2},{4,5},{5,4},{6,7},{7,6},{8,9},{9,8},{10,11... | collective-permute-start | bytes 811016 | tf_op jit(solution)/shard_map/ppermute | solution.py:372
  10.0 13.4 %copy-start.4 = (s32[512]{0:T(512)S(1)}, s32[512]{0:T(512)}, u32[]{:S(2)}) copy-start(s32[512]{0:T(512)} %param.10) | copy-start | bytes 6148
  14.9 10.1 %collective-permute-start.7 = (bf16[528,256]{1,0:T(8,128)(2,1)S(1)}, bf16[528,256]{1,0:T(8,128)(2,1)S(1)}, u32[]{:S(2)}, u32[]{:S(2)}) collective-permute-start(bf16[528,256]{1,0:T(8,128)(2,1)S(1)} %collective-permute-done.refs_3_), channel_id=1, source_target_pairs={{0,1},{1,0},{2,3},{3,2},{4,6},{5,7},{6,8},{7,9},{8,10},{9,11},{10,... | collective-permute-start | bytes 811016 | tf_op jit(solution)/shard_map/ppermute | solution.py:381
  16.1 11.0 %collective-permute-start.4 = (bf16[528,256]{1,0:T(8,128)(2,1)S(1)}, bf16[528,256]{1,0:T(8,128)(2,1)S(1)}, u32[]{:S(2)}, u32[]{:S(2)}) collective-permute-start(bf16[528,256]{1,0:T(8,128)(2,1)S(1)} %collective-permute-done.refs_3_), channel_id=1, source_target_pairs={{0,1},{1,0},{2,3},{3,2},{4,8},{5,9},{6,10},{7,11},{8,12},{9,13},{1... | collective-permute-start | bytes 811016 | tf_op jit(solution)/shard_map/ppermute | solution.py:381
  17.4 6.0 %collective-permute-start.3 = (bf16[528,256]{1,0:T(8,128)(2,1)S(1)}, bf16[528,256]{1,0:T(8,128)(2,1)S(1)}, u32[]{:S(2)}, u32[]{:S(2)}) collective-permute-start(bf16[528,256]{1,0:T(8,128)(2,1)S(1)} %collective-permute-done.refs_3_), channel_id=1, source_target_pairs={{0,1},{1,0},{2,3},{3,2},{4,5},{5,4},{6,7},{7,6},{8,9},{9,8},{10,11... | collective-permute-start | bytes 811016 | tf_op jit(solution)/shard_map/ppermute | solution.py:372
  19.0 11.9 %collective-permute-start.1 = (bf16[528,256]{1,0:T(8,128)(2,1)S(1)}, bf16[528,256]{1,0:T(8,128)(2,1)S(1)}, u32[]{:S(2)}, u32[]{:S(2)}) collective-permute-start(bf16[528,256]{1,0:T(8,128)(2,1)S(1)} %broadcast_select_fusion), channel_id=1, source_target_pairs={{0,2},{2,0},{4,6},{6,4},{8,10},{10,8},{12,14},{14,12},{1,3},{3,1},... | collective-permute-start | bytes 811016 | tf_op jit(solution)/shard_map/ppermute | solution.py:388
  23.4 11.1 %copy-start.1 = (bf16[256,4096]{1,0:T(8,128)(2,1)S(1)}, bf16[256,4096]{1,0:T(8,128)(2,1)}, u32[]{:S(2)}) copy-start(bf16[256,4096]{1,0:T(8,128)(2,1)} %w_ref.5) | copy-start | bytes 6291460
  25.0 6.4 %collective-permute-start.8 = (bf16[528,256]{1,0:T(8,128)(2,1)S(1)}, bf16[528,256]{1,0:T(8,128)(2,1)S(1)}, u32[]{:S(2)}, u32[]{:S(2)}) collective-permute-start(bf16[528,256]{1,0:T(8,128)(2,1)S(1)} %collective-permute-done.7.refs_2_), channel_id=1, source_target_pairs={{0,1},{1,0},{2,3},{3,2},{4,5},{5,4},{6,7},{7,6},{8,9},{9,8},{10,11... | collective-permute-start | bytes 811016 | tf_op jit(solution)/shard_map/ppermute | solution.py:372
  30.9 1.6 %collective-permute-start.5 = (bf16[528,256]{1,0:T(8,128)(2,1)S(1)}, bf16[528,256]{1,0:T(8,128)(2,1)S(1)}, u32[]{:S(2)}, u32[]{:S(2)}) collective-permute-start(bf16[528,256]{1,0:T(8,128)(2,1)S(1)} %collective-permute-done.1.refs_2_), channel_id=1, source_target_pairs={{0,1},{1,0},{2,3},{3,2},{4,5},{5,4},{6,7},{7,6},{8,9},{9,8},{10,11... | collective-permute-start | bytes 811016 | tf_op jit(solution)/shard_map/ppermute | solution.py:372
  31.4 1.6 %collective-permute-start.6 = (bf16[528,256]{1,0:T(8,128)(2,1)S(1)}, bf16[528,256]{1,0:T(8,128)(2,1)S(1)}, u32[]{:S(2)}, u32[]{:S(2)}) collective-permute-start(bf16[528,256]{1,0:T(8,128)(2,1)S(1)} %collective-permute-done.4.refs_3_), channel_id=1, source_target_pairs={{0,1},{1,0},{2,3},{3,2},{4,5},{5,4},{6,7},{7,6},{8,9},{9,8},{10,11... | collective-permute-start | bytes 811016 | tf_op jit(solution)/shard_map/ppermute | solution.py:372
  34.0 2.3 %collective-permute-start.9 = (bf16[512,256]{1,0:T(8,128)(2,1)S(1)}, bf16[512,256]{1,0:T(8,128)(2,1)S(1)}, u32[]{:S(2)}, u32[]{:S(2)}) collective-permute-start(bf16[512,256]{1,0:T(8,128)(2,1)S(1)} %attend_last.1.a_ref), channel_id=1, source_target_pairs={{0,1},{1,0},{2,3},{3,2},{4,5},{5,4},{6,7},{7,6},{8,9},{9,8},{10,11... | collective-permute-start | bytes 786440 | tf_op jit(solution)/shard_map/ppermute | solution.py:372

commit v10 on v9

--- a/solution.py
+++ b/solution.py
@@ -15,10 +15,11 @@
 NEG = -1e30
 MIB = 1024 * 1024
 NT = (((1,), (1,)), ((), ()))
+EVEN, ODD, ALL, FURTHEST = 0, 1, 2, 3
 FACTOR = HD ** (-0.5) * 1.4426950408889634
 
 
-def norm_kv_kernel(x_ref, gain_hbm, w_ref, seg_hbm, msg_ref, normed_ref, xs, ws, gain_ref, seg_ref, sems):
+def norm_kv_kernel(x_ref, gain_hbm, w_ref, seg_hbm, next_ref, msg_ref, normed_ref, near_ref, xs, ws, gain_ref, seg_ref, sems):
     rows, width = xs.shape
     tile, part = rows // 2, rows // 8
     pieces = 4
@@ -35,6 +36,9 @@
 
     def segments_copy():
         return pltpu.make_async_copy(seg_hbm, seg_ref, sems.at[13])
+
+    def next_copy():
+        return pltpu.make_async_copy(next_ref, near_ref, sems.at[14])
 
     for i in range(4):
         tokens_copy(i).start()
@@ -44,6 +48,7 @@
     for i in range(4, 8):
         tokens_copy(i).start()
     segments_copy().start()
+    next_copy().start()
 
     def wide(first, count, start):
         return xs[first:first + count, start:start + LANES].astype(jnp.float32)
@@ -80,6 +85,7 @@
     low = jnp.broadcast_to(seg[:, :HD], (8, HD))
     high = jnp.broadcast_to(seg[:, HD:], (8, HD))
     msg_ref[rows:, :] = jnp.concatenate([low, high], axis=0).astype(jnp.bfloat16)
+    next_copy().wait()
 
 
 def in_hbm(x):
@@ -90,28 +96,32 @@
     return pltpu.with_memory_space_constraint(x, pltpu.VMEM)
 
 
-def norm_kv(tokens, gain, w_keyval, segments):
+def norm_kv(tokens, gain, w_keyval, segments, w_next):
     rows, width = tokens.shape
     cols = w_keyval.shape[1]
     vmem, hbm = pl.BlockSpec(memory_space=pltpu.VMEM), pl.BlockSpec(memory_space=pltpu.HBM)
     return pl.pallas_call(
         norm_kv_kernel,
-        in_specs=[hbm] * 4,
-        out_specs=[vmem, vmem],
-        out_shape=[pltpu.VMEM((rows + SEG_ROWS, cols), jnp.bfloat16), pltpu.VMEM((rows, width), jnp.bfloat16)],
+        in_specs=[hbm] * 5,
+        out_specs=[vmem] * 3,
+        out_shape=[
+            pltpu.VMEM((rows + SEG_ROWS, cols), jnp.bfloat16),
+            pltpu.VMEM((rows, width), jnp.bfloat16),
+            pltpu.VMEM(w_next.shape, w_next.dtype),
+        ],
         scratch_shapes=[
             pltpu.VMEM((rows, width), jnp.bfloat16),
             pltpu.VMEM((width, cols), jnp.bfloat16),
             pltpu.VMEM((1, width), jnp.float32),
             pltpu.VMEM((1, rows), jnp.int32),
-            pltpu.SemaphoreType.DMA((14,)),
+            pltpu.SemaphoreType.DMA((15,)),
         ],
         compiler_params=pltpu.CompilerParams(vmem_limit_bytes=24 * MIB),
         cost_estimate=pl.CostEstimate(
             flops=2 * rows * width * cols, bytes_accessed=4 * rows * width + 2 * width * cols, transcendentals=0
         ),
         name="norm_kv",
-    )(in_hbm(tokens), in_hbm(gain.reshape(1, width)), in_hbm(w_keyval), in_hbm(segments.reshape(1, rows)))
+    )(*[in_hbm(x) for x in (tokens, gain.reshape(1, width), w_keyval, segments.reshape(1, rows), w_next)])
 
 
 def query_kernel(x_ref, w_ref, out_ref):
@@ -152,24 +162,25 @@
     def finish(span, weighted, total):
         out_ref[span, :] = (weighted / jnp.sum(total, axis=1, keepdims=True)).astype(jnp.bfloat16)
 
-    def update(count, keys, values):
+    def update(slots, keys, values):
         own_seg = jnp.transpose(jnp.broadcast_to(seg_ref[...].astype(jnp.float32), (8, rows)))[:, 0:1]
-        key_segs = []
-        for slot in range(count):
+        key_segs = {}
+        for slot in slots:
             packed = mine[slot][rows:, :].astype(jnp.float32)
-            key_segs.append(jnp.concatenate([packed[0:1, :], packed[8:9, :]], axis=1))
+            key_segs[slot] = jnp.concatenate([packed[0:1, :], packed[8:9, :]], axis=1)
         for start in range(0, rows, tile):
             span = slice(start, start + tile)
             query = q_ref[span, :]
             best = None if first else state_ref[span, HD:HD + LANES]
-            bounds = []
-            for slot, (back, furthest) in enumerate(plan[:count]):
+            bounds = {}
+            for slot in slots:
+                back, kind = plan[slot]
                 low, high = 0, rows
                 if back == 0:
                     high = start + tile
-                elif furthest:
+                elif kind == FURTHEST:
                     low = start
-                bounds.append((low, high))
+                bounds[slot] = (low, high)
                 raw = lax.dot_general(query, keys[slot][low:high, :], NT, preferred_element_type=jnp.float32)
                 allowed = key_segs[slot][:, low:high] == own_seg[span, :]
                 if back == 0:
@@ -188,7 +199,7 @@
                 shrink = jnp.exp2((state_ref[span, HD:HD + LANES] - top) * FACTOR)
                 total = state_ref[span, HD + LANES:] * shrink
                 weighted = state_ref[span, :HD] * jnp.concatenate([shrink, shrink], axis=1)
-            for slot in range(count):
+            for slot in slots:
                 low, high = bounds[slot]
                 pieces = []
                 for at in range(low, high, LANES):
@@ -204,18 +215,22 @@
                 out_ref[span, HD:HD + LANES] = top
                 out_ref[span, HD + LANES:] = total
 
-    for count in range(1 if first else 0, blocks + 1):
-        reached = place >= (plan[count - 1][0] if count > 0 else 0)
-        if count < blocks:
-            reached = reached & (place < plan[count][0])
-        if count > 0:
-            pl.when(reached & (part == 0))(functools.partial(update, count, mine, other))
-            pl.when(reached & (part == 1))(functools.partial(update, count, other, mine))
-        elif last:
-
-            @pl.when(reached)
-            def _():
-                finish(slice(0, rows), state_ref[:, :HD], state_ref[:, HD + LANES:])
+    for parity in (0, 1):
+        slots = [slot for slot, (_, kind) in enumerate(plan) if kind in (ALL, FURTHEST, parity)]
+        for count in range(len(slots) + 1):
+            reached = lax.rem(place, 2) == parity
+            if count > 0:
+                reached = reached & (place >= plan[slots[count - 1]][0])
+            if count < len(slots):
+                reached = reached & (place < plan[slots[count]][0])
+            if count > 0:
+                pl.when(reached & (part == 0))(functools.partial(update, slots[:count], mine, other))
+                pl.when(reached & (part == 1))(functools.partial(update, slots[:count], other, mine))
+            elif last:
+
+                @pl.when(reached)
+                def _():
+                    finish(slice(0, rows), state_ref[:, :HD], state_ref[:, HD + LANES:])
 
 
 def attend(query, segments, plan, mine, other, state, last):
@@ -348,7 +363,7 @@
 def project_out(att_other, w_other, quant_own, sum_bound, out_bound, tokens):
     rows, width = tokens.shape
     depth = att_other.shape[1]
-    pieces = 8
+    pieces = 16
     vmem = pl.BlockSpec(memory_space=pltpu.VMEM)
     operands = [att_other, w_other, quant_own, tokens, sum_bound, out_bound]
     return pl.pallas_call(
@@ -381,23 +396,24 @@
         return lax.ppermute(x, ("seq", "tp"), pairs)
 
     w_other = swap_cores(w_out)
-    message, normed = norm_kv(tokens, gain, w_keyval, segments)
-    query = project_query(normed, w_query)
+    message, normed, w_near = norm_kv(tokens, gain, w_keyval, segments, w_query)
+    query = project_query(normed, w_near)
     held, query = lax.optimization_barrier((shift(message, 2, 0), query))
-    odd = lax.rem(lax.axis_index("seq"), 2) == 1
-    beside = lax.ppermute(jnp.where(odd, held, message), "seq", [(i, i ^ 1) for i in range(seq_size)])
-    parts = [[(0, message), (2, held)]]
+    pair = lax.ppermute(message, "seq", [(i, i ^ 1) for i in range(seq_size)])
+    along = [(i, min(i + 2, seq_size - 1)) for i in range(0, seq_size, 2)] + [(i, max(i - 2, 0)) for i in range(1, seq_size, 2)]
+    pair, held = lax.optimization_barrier((pair, held))
+    beside = lax.ppermute(pair, "seq", along)
+    parts = [[(0, ALL, message), (1, ODD, pair), (2, ALL, held)], [(1, EVEN, beside)]]
     for back in range(2, window, 2):
-        step = shift(held, 1, back)
+        parts[-1].append((back + 1, ALL, shift(held, 1, back)))
         held = shift(held, 2, back)
-        parts.append([(back + 1, step)] + ([(back + 2, held)] if back + 2 < window else []))
-    parts.append([(1, beside), (window, held)])
+        parts.append([(back + 2, ALL if back + 2 < window else FURTHEST, held)])
     exps = lax.optimization_barrier((sum_exps, out_exps, query))[:2]
     bounds = spread_bounds(*exps, tokens)
     state = None
     for number, blocks in enumerate(parts):
-        plan = [(back, back == window) for back, _ in blocks]
-        mine = [block for _, block in blocks]
+        plan = [(back, kind) for back, kind, _ in blocks]
+        mine = [block for _, _, block in blocks]
         if number == 1:
             bounds, state = early = lax.optimization_barrier((bounds, state))
         if number > 0:

time: 41.3 us -> 47.1 us (1.14)
  the two profiles are of different devices: /device:TPU:11 before, /device:TPU:13 now
where the time goes in v10:
time: 47.1 us; the launch traced here: 47 us
  Pallas kernels  20.5 us (44%)
  waiting for transfers between devices  17.2 us (37%)
  starting transfers between devices  8.92 us (19%)
    ppermute x3, waiting for transfers between devices, shift(): return lax.ppermute(x, ('seq', 'tp'), pairs)  8.33 us
    ppermute x1, waiting for transfers between devices, on_device(): beside = lax.ppermute(pair, 'seq', along)  7.91 us
    pallas_call x1, Pallas kernels, norm_kv(): pl.pallas_call(norm_kv_kernel, in_specs=[hbm] * 5, out_specs=[vmem] * 3,...  6.2 us
    ppermute x8, starting transfers between devices, swap_cores(): return lax.ppermute(x, 'tp', [(0, 1), (1, 0)])  4.64 us
    pallas_call x1, Pallas kernels, project_out(): pl.pallas_call(output_kernel, in_specs=[vmem] * len(operands), out_specs=...  4.61 us
    ppermute x3, starting transfers between devices, shift(): return lax.ppermute(x, ('seq', 'tp'), pairs)  4.05 us
    pallas_call x3, Pallas kernels, attend(): pl.pallas_call(functools.partial(attend_kernel, plan, first, last), in_sp...  3.52 us
    pallas_call x1, Pallas kernels, spread_bounds(): pl.pallas_call(bounds_kernel, in_specs=[vmem, vmem, pl.BlockSpec(memory_s...  3.05 us
  transfers between devices with their start and end apart: 13, of which 4 were waited for; matrix products, arithmetic and copies ran while one was open for 0% of the time, Pallas kernels for 34%

profile of v10, /device:TPU:13, one launch (start us, length us, event | category | flops | bytes accessed | tf_op | source)
XLA Modules:
  0.0 47.0 jit_solution(15823687117709915226)
XLA Ops:
  0.0 0.7 %collective-permute-start.12 = (bf16[256,4096]{1,0:T(8,128)(2,1)}, bf16[256,4096]{1,0:T(8,128)(2,1)S(1)}, u32[]{:S(2)}, u32[]{:S(2)}) collective-permute-start(bf16[256,4096]{1,0:T(8,128)(2,1)} %w_ref.3), channel_id=1, source_target_pairs={{0,1},{1,0},{2,3},{3,2},{4,5},{5,4},{6,7},{7,6},{8,9},{9,8},{10,11... | collective-permute-start | bytes 6291464 | tf_op jit(solution)/shard_map/ppermute | solution.py:387
  0.7 6.2 %norm_kv.1 = (bf16[528,256]{1,0:T(8,128)(2,1)S(1)}, bf16[512,4096]{1,0:T(8,128)(2,1)S(1)}, bf16[4096,256]{1,0:T(8,128)(2,1)S(1)}) custom-call(bf16[512,4096]{1,0:T(8,128)(2,1)} %x_ref.3, f32[1,4096]{1,0:T(1,128)} %bitcast.10, bf16[4096,256]{1,0:T(8,128)(2,1)} %w_ref.2, s32[1,512]{1,0:T(1,128)} %bitcast.6, bf16[4096,256]{1,0:T(8,128)(2,1)} %next_ref.1), custom_call_target="tpu_custom_call" | custom-call | flops 1073741824 | bytes 10485760 | tf_op jit(solution)/shard_map/norm_kv/pallas_call | solution.py:103
  6.9 0.0 copy-start.1
  6.9 1.3 %collective-permute-start = (bf16[528,256]{1,0:T(8,128)(2,1)S(1)}, bf16[528,256]{1,0:T(8,128)(2,1)S(1)}, u32[]{:S(2)}, u32[]{:S(2)}) collective-permute-start(bf16[528,256]{1,0:T(8,128)(2,1)S(1)} %get-tuple-element.24.refs_2_), channel_id=1, source_target_pairs={{0,4},{1,5},{2,6},{3,7},{4,8},{5,9},{6,10},{7,11},{8,12},{9,13},{1... | collective-permute-start | bytes 811016 | tf_op jit(solution)/shard_map/ppermute | solution.py:396
  8.3 0.2 collective-permute-start.1
  8.5 0.6 %collective-permute-start.3 = (bf16[528,256]{1,0:T(8,128)(2,1)S(1)}, bf16[528,256]{1,0:T(8,128)(2,1)S(1)}, u32[]{:S(2)}, u32[]{:S(2)}) collective-permute-start(bf16[528,256]{1,0:T(8,128)(2,1)S(1)} %get-tuple-element.24.refs_2_), channel_id=1, source_target_pairs={{0,1},{1,0},{2,3},{3,2},{4,5},{5,4},{6,7},{7,6},{8,9},{9,8},{10,11... | collective-permute-start | bytes 811016 | tf_op jit(solution)/shard_map/ppermute | solution.py:387
  9.1 1.2 %project_query.1.refs_0_ = bf16[512,256]{1,0:T(8,128)(2,1)S(1)} custom-call(bf16[512,4096]{1,0:T(8,128)(2,1)S(1)} %get-tuple-element.25.x_ref, bf16[4096,256]{1,0:T(8,128)(2,1)S(1)} %get-tuple-element.26.w_ref), custom_call_target="tpu_custom_call" | custom-call | flops 1073741824 | bytes 6291456 | tf_op jit(solution)/shard_map/project_query/pallas_call | solution.py:135
  10.3 4.8 %collective-permute-done.refs_4_ = bf16[528,256]{1,0:T(8,128)(2,1)S(1)} collective-permute-done((bf16[528,256]{1,0:T(8,128)(2,1)S(1)}, bf16[528,256]{1,0:T(8,128)(2,1)S(1)}, u32[]{:S(2)}, u32[]{:S(2)}) %collective-permute-start) | collective-permute-done | bytes 270368 | tf_op jit(solution)/shard_map/ppermute | solution.py:396
  15.1 1.0 %collective-permute-done.1.refs_3_ = bf16[528,256]{1,0:T(8,128)(2,1)S(1)} collective-permute-done((bf16[528,256]{1,0:T(8,128)(2,1)S(1)}, bf16[528,256]{1,0:T(8,128)(2,1)S(1)}, u32[]{:S(2)}, u32[]{:S(2)}) %collective-permute-start.1) | collective-permute-done | bytes 270368 | tf_op jit(solution)/shard_map/ppermute | solution.py:402
  16.1 1.1 %collective-permute-start.4 = (bf16[528,256]{1,0:T(8,128)(2,1)S(1)}, bf16[528,256]{1,0:T(8,128)(2,1)S(1)}, u32[]{:S(2)}, u32[]{:S(2)}) collective-permute-start(bf16[528,256]{1,0:T(8,128)(2,1)S(1)} %collective-permute-done.1.refs_3_), channel_id=1, source_target_pairs={{0,1},{1,0},{2,3},{3,2},{4,5},{5,4},{6,7},{7,6},{8,9},{9,8},{10,11... | collective-permute-start | bytes 811016 | tf_op jit(solution)/shard_map/ppermute | solution.py:387
  17.2 1.2 %collective-permute-start.8 = (bf16[528,256]{1,0:T(8,128)(2,1)S(1)}, bf16[528,256]{1,0:T(8,128)(2,1)S(1)}, u32[]{:S(2)}, u32[]{:S(2)}) collective-permute-start(bf16[528,256]{1,0:T(8,128)(2,1)S(1)} %collective-permute-done.refs_4_), channel_id=1, source_target_pairs={{0,1},{1,0},{2,3},{3,2},{4,6},{5,7},{6,8},{7,9},{8,10},{9,11},{10,... | collective-permute-start | bytes 811016 | tf_op jit(solution)/shard_map/ppermute | solution.py:396
  18.4 0.0 collective-permute-start.7
  18.4 1.5 %collective-permute-start.2 = (bf16[528,256]{1,0:T(8,128)(2,1)S(1)}, bf16[528,256]{1,0:T(8,128)(2,1)S(1)}, u32[]{:S(2)}, u32[]{:S(2)}) collective-permute-start(bf16[528,256]{1,0:T(8,128)(2,1)S(1)} %collective-permute-done.refs_4_), channel_id=1, source_target_pairs={{0,1},{1,0},{2,3},{3,2},{4,8},{5,9},{6,10},{7,11},{8,12},{9,13},{1... | collective-permute-start | bytes 811016 | tf_op jit(solution)/shard_map/ppermute | solution.py:396
  19.9 3.0 %spread_bounds.1 = (bf16[512,4096]{1,0:T(8,128)(2,1)S(1)}, bf16[512,4096]{1,0:T(8,128)(2,1)S(1)}, f32[512,4096]{1,0:T(8,128)S(1)}) custom-call(s32[32,512]{1,0:T(8,128)S(1)} %bitcast.4, s32[32,512]{1,0:T(8,128)S(1)} %bitcast.5, bf16[512,4096]{1,0:T(8,128)(2,1)} %x_ref.3), custom_call_target="tpu_custom_call" | custom-call | flops 16777216 | bytes 131072 | tf_op jit(solution)/shard_map/spread_bounds/pallas_call | solution.py:282
  23.0 2.1 %attend_first.1.refs_6_ = f32[512,512]{1,0:T(8,128)S(1)} custom-call(bf16[512,256]{1,0:T(8,128)(2,1)S(1)} %project_query.1.refs_0_, s32[1,512]{1,0:T(1,128)S(1)} %bitcast.7, bf16[528,256]{1,0:T(8,128)(2,1)S(1)} %get-tuple-element.24.refs_2_, bf16[528,256]{1,0:T(8,128)(2,1)S(1)} %collective-permute-done.1.refs_3_, ...), custom_call_target="tpu_custom_call" | custom-call | flops 805306368 | bytes 1572864 | tf_op jit(solution)/shard_map/attend_first/pallas_call | solution.py:242
  25.1 7.9 %collective-permute-done.7.refs_2_ = bf16[528,256]{1,0:T(8,128)(2,1)S(1)} collective-permute-done((bf16[528,256]{1,0:T(8,128)(2,1)S(1)}, bf16[528,256]{1,0:T(8,128)(2,1)S(1)}, u32[]{:S(2)}, u32[]{:S(2)}) %collective-permute-start.7) | collective-permute-done | bytes 270368 | tf_op jit(solution)/shard_map/ppermute | solution.py:405
  33.0 0.6 %collective-permute-start.9 = (bf16[528,256]{1,0:T(8,128)(2,1)S(1)}, bf16[528,256]{1,0:T(8,128)(2,1)S(1)}, u32[]{:S(2)}, u32[]{:S(2)}) collective-permute-start(bf16[528,256]{1,0:T(8,128)(2,1)S(1)} %collective-permute-done.7.refs_2_), channel_id=1, source_target_pairs={{0,1},{1,0},{2,3},{3,2},{4,5},{5,4},{6,7},{7,6},{8,9},{9,8},{10,11... | collective-permute-start | bytes 811016 | tf_op jit(solution)/shard_map/ppermute | solution.py:387
  33.6 3.6 %collective-permute-done.2.refs_2_ = bf16[528,256]{1,0:T(8,128)(2,1)S(1)} collective-permute-done((bf16[528,256]{1,0:T(8,128)(2,1)S(1)}, bf16[528,256]{1,0:T(8,128)(2,1)S(1)}, u32[]{:S(2)}, u32[]{:S(2)}) %collective-permute-start.2) | collective-permute-done | bytes 270368 | tf_op jit(solution)/shard_map/ppermute | solution.py:396
  37.2 1.4 %collective-permute-start.6 = (bf16[528,256]{1,0:T(8,128)(2,1)S(1)}, bf16[528,256]{1,0:T(8,128)(2,1)S(1)}, u32[]{:S(2)}, u32[]{:S(2)}) collective-permute-start(bf16[528,256]{1,0:T(8,128)(2,1)S(1)} %collective-permute-done.2.refs_2_), channel_id=1, source_target_pairs={{0,1},{1,0},{2,3},{3,2},{4,5},{5,4},{6,7},{7,6},{8,9},{9,8},{10,11... | collective-permute-start | bytes 811016 | tf_op jit(solution)/shard_map/ppermute | solution.py:387
  38.5 1.2 %attend_more.1.refs_4_ = f32[512,512]{1,0:T(8,128)S(1)} custom-call(bf16[512,256]{1,0:T(8,128)(2,1)S(1)} %project_query.1.refs_0_, s32[1,512]{1,0:T(1,128)S(1)} %bitcast.8, bf16[528,256]{1,0:T(8,128)(2,1)S(1)} %collective-permute-done.7.refs_2_, bf16[528,256]{1,0:T(8,128)(2,1)S(1)} %collective-permute-done.8.refs_3_, ...), custom_call_target="tpu_custom_call", output_to_operand_aliasing={{}: (6, {})} | custom-call | flops 536870912 | bytes 1048576 | tf_op jit(solution)/shard_map/attend_more/pallas_call | solution.py:242
  39.8 0.2 attend_last.1.a_ref
  40.0 0.3 collective-permute-start.11
  40.3 1.8 %project_own.1.quant_ref = bf16[512,4096]{1,0:T(8,128)(2,1)S(1)} custom-call(bf16[512,256]{1,0:T(8,128)(2,1)S(1)} %attend_last.1.a_ref, bf16[256,4096]{1,0:T(8,128)(2,1)S(1)} %copy-done, bf16[512,4096]{1,0:T(8,128)(2,1)S(1)} %get-tuple-element.36.sum_ref), custom_call_target="tpu_custom_call" | custom-call | flops 1073741824 | bytes 10485760 | tf_op jit(solution)/shard_map/project_own/pallas_call | solution.py:320
  42.2 4.6 %project_out.1 = bf16[512,4096]{1,0:T(8,128)(2,1)} custom-call(bf16[512,256]{1,0:T(8,128)(2,1)S(1)} %collective-permute-done.11.b_ref, bf16[256,4096]{1,0:T(8,128)(2,1)S(1)} %collective-permute-done.12.wb_ref, bf16[512,4096]{1,0:T(8,128)(2,1)S(1)} %project_own.1.quant_ref, f32[512,4096]{1,0:T(8,128)S(1)} %get-tuple-element.38.x_ref, ...), custom_call_target="tpu_custom_call" | custom-call | flops 1073741824 | bytes 10485760 | tf_op jit(solution)/shard_map/project_out/pallas_call | solution.py:369
  (18 shorter events, 0.0 us)
Async XLA Ops:
  0.0 42.2 %collective-permute-start.12 = (bf16[256,4096]{1,0:T(8,128)(2,1)}, bf16[256,4096]{1,0:T(8,128)(2,1)S(1)}, u32[]{:S(2)}, u32[]{:S(2)}) collective-permute-start(bf16[256,4096]{1,0:T(8,128)(2,1)} %w_ref.3), channel_id=1, source_target_pairs={{0,1},{1,0},{2,3},{3,2},{4,5},{5,4},{6,7},{7,6},{8,9},{9,8},{10,11... | collective-permute-start | bytes 6291464 | tf_op jit(solution)/shard_map/ppermute | solution.py:387
  6.9 13.0 %copy-start.1 = (s32[512,32]{0,1:T(8,128)S(1)}, s32[512,32]{0,1:T(8,128)}, u32[]{:S(2)}) copy-start(s32[512,32]{0,1:T(8,128)} %param.14) | copy-start | bytes 196612
  6.9 13.0 %copy-start.2 = (s32[512,32]{0,1:T(8,128)S(1)}, s32[512,32]{0,1:T(8,128)}, u32[]{:S(2)}) copy-start(s32[512,32]{0,1:T(8,128)} %param.15) | copy-start | bytes 196612
  6.9 8.2 %collective-permute-start = (bf16[528,256]{1,0:T(8,128)(2,1)S(1)}, bf16[528,256]{1,0:T(8,128)(2,1)S(1)}, u32[]{:S(2)}, u32[]{:S(2)}) collective-permute-start(bf16[528,256]{1,0:T(8,128)(2,1)S(1)} %get-tuple-element.24.refs_2_), channel_id=1, source_target_pairs={{0,4},{1,5},{2,6},{3,7},{4,8},{5,9},{6,10},{7,11},{8,12},{9,13},{1... | collective-permute-start | bytes 811016 | tf_op jit(solution)/shard_map/ppermute | solution.py:396
  8.3 7.8 %collective-permute-start.1 = (bf16[528,256]{1,0:T(8,128)(2,1)S(1)}, bf16[528,256]{1,0:T(8,128)(2,1)S(1)}, u32[]{:S(2)}, u32[]{:S(2)}) collective-permute-start(bf16[528,256]{1,0:T(8,128)(2,1)S(1)} %get-tuple-element.24.refs_2_), channel_id=1, source_target_pairs={{0,2},{2,0},{4,6},{6,4},{8,10},{10,8},{12,14},{14,12},{1,3},{3,1},... | collective-permute-start | bytes 811016 | tf_op jit(solution)/shard_map/ppermute | solution.py:402
  8.5 9.9 %collective-permute-start.3 = (bf16[528,256]{1,0:T(8,128)(2,1)S(1)}, bf16[528,256]{1,0:T(8,128)(2,1)S(1)}, u32[]{:S(2)}, u32[]{:S(2)}) collective-permute-start(bf16[528,256]{1,0:T(8,128)(2,1)S(1)} %get-tuple-element.24.refs_2_), channel_id=1, source_target_pairs={{0,1},{1,0},{2,3},{3,2},{4,5},{5,4},{6,7},{7,6},{8,9},{9,8},{10,11... | collective-permute-start | bytes 811016 | tf_op jit(solution)/shard_map/ppermute | solution.py:387
  9.1 13.9 %copy-start.3 = (s32[512]{0:T(512)S(1)}, s32[512]{0:T(512)}, u32[]{:S(2)}) copy-start(s32[512]{0:T(512)} %param.10) | copy-start | bytes 6148
  16.1 2.4 %collective-permute-start.4 = (bf16[528,256]{1,0:T(8,128)(2,1)S(1)}, bf16[528,256]{1,0:T(8,128)(2,1)S(1)}, u32[]{:S(2)}, u32[]{:S(2)}) collective-permute-start(bf16[528,256]{1,0:T(8,128)(2,1)S(1)} %collective-permute-done.1.refs_3_), channel_id=1, source_target_pairs={{0,1},{1,0},{2,3},{3,2},{4,5},{5,4},{6,7},{7,6},{8,9},{9,8},{10,11... | collective-permute-start | bytes 811016 | tf_op jit(solution)/shard_map/ppermute | solution.py:387
  17.2 5.8 %collective-permute-start.5 = (bf16[528,256]{1,0:T(8,128)(2,1)S(1)}, bf16[528,256]{1,0:T(8,128)(2,1)S(1)}, u32[]{:S(2)}, u32[]{:S(2)}) collective-permute-start(bf16[528,256]{1,0:T(8,128)(2,1)S(1)} %collective-permute-done.refs_4_), channel_id=1, source_target_pairs={{0,1},{1,0},{2,3},{3,2},{4,5},{5,4},{6,7},{7,6},{8,9},{9,8},{10,11... | collective-permute-start | bytes 811016 | tf_op jit(solution)/shard_map/ppermute | solution.py:387
  17.2 7.9 %collective-permute-start.8 = (bf16[528,256]{1,0:T(8,128)(2,1)S(1)}, bf16[528,256]{1,0:T(8,128)(2,1)S(1)}, u32[]{:S(2)}, u32[]{:S(2)}) collective-permute-start(bf16[528,256]{1,0:T(8,128)(2,1)S(1)} %collective-permute-done.refs_4_), channel_id=1, source_target_pairs={{0,1},{1,0},{2,3},{3,2},{4,6},{5,7},{6,8},{7,9},{8,10},{9,11},{10,... | collective-permute-start | bytes 811016 | tf_op jit(solution)/shard_map/ppermute | solution.py:396
  18.4 14.6 %collective-permute-start.7 = (bf16[528,256]{1,0:T(8,128)(2,1)S(1)}, bf16[528,256]{1,0:T(8,128)(2,1)S(1)}, u32[]{:S(2)}, u32[]{:S(2)}) collective-permute-start(bf16[528,256]{1,0:T(8,128)(2,1)S(1)} %collective-permute-done.1.refs_3_), channel_id=1, source_target_pairs={{0,4},{4,8},{8,12},{12,14},{2,0},{6,2},{10,6},{14,10},{1,5},{5,9},... | collective-permute-start | bytes 811016 | tf_op jit(solution)/shard_map/ppermute | solution.py:405
  18.4 18.8 %collective-permute-start.2 = (bf16[528,256]{1,0:T(8,128)(2,1)S(1)}, bf16[528,256]{1,0:T(8,128)(2,1)S(1)}, u32[]{:S(2)}, u32[]{:S(2)}) collective-permute-start(bf16[528,256]{1,0:T(8,128)(2,1)S(1)} %collective-permute-done.refs_4_), channel_id=1, source_target_pairs={{0,1},{1,0},{2,3},{3,2},{4,8},{5,9},{6,10},{7,11},{8,12},{9,13},{1... | collective-permute-start | bytes 811016 | tf_op jit(solution)/shard_map/ppermute | solution.py:396
  22.9 17.4 %copy-start = (bf16[256,4096]{1,0:T(8,128)(2,1)S(1)}, bf16[256,4096]{1,0:T(8,128)(2,1)}, u32[]{:S(2)}) copy-start(bf16[256,4096]{1,0:T(8,128)(2,1)} %w_ref.3) | copy-start | bytes 6291460
  33.0 5.5 %collective-permute-start.9 = (bf16[528,256]{1,0:T(8,128)(2,1)S(1)}, bf16[528,256]{1,0:T(8,128)(2,1)S(1)}, u32[]{:S(2)}, u32[]{:S(2)}) collective-permute-start(bf16[528,256]{1,0:T(8,128)(2,1)S(1)} %collective-permute-done.7.refs_2_), channel_id=1, source_target_pairs={{0,1},{1,0},{2,3},{3,2},{4,5},{5,4},{6,7},{7,6},{8,9},{9,8},{10,11... | collective-permute-start | bytes 811016 | tf_op jit(solution)/shard_map/ppermute | solution.py:387
  33.6 4.9 %collective-permute-start.10 = (bf16[528,256]{1,0:T(8,128)(2,1)S(1)}, bf16[528,256]{1,0:T(8,128)(2,1)S(1)}, u32[]{:S(2)}, u32[]{:S(2)}) collective-permute-start(bf16[528,256]{1,0:T(8,128)(2,1)S(1)} %collective-permute-done.8.refs_3_), channel_id=1, source_target_pairs={{0,1},{1,0},{2,3},{3,2},{4,5},{5,4},{6,7},{7,6},{8,9},{9,8},{10,11... | collective-permute-start | bytes 811016 | tf_op jit(solution)/shard_map/ppermute | solution.py:387
  37.2 2.6 %collective-permute-start.6 = (bf16[528,256]{1,0:T(8,128)(2,1)S(1)}, bf16[528,256]{1,0:T(8,128)(2,1)S(1)}, u32[]{:S(2)}, u32[]{:S(2)}) collective-permute-start(bf16[528,256]{1,0:T(8,128)(2,1)S(1)} %collective-permute-done.2.refs_2_), channel_id=1, source_target_pairs={{0,1},{1,0},{2,3},{3,2},{4,5},{5,4},{6,7},{7,6},{8,9},{9,8},{10,11... | collective-permute-start | bytes 811016 | tf_op jit(solution)/shard_map/ppermute | solution.py:387
  40.0 2.2 %collective-permute-start.11 = (bf16[512,256]{1,0:T(8,128)(2,1)S(1)}, bf16[512,256]{1,0:T(8,128)(2,1)S(1)}, u32[]{:S(2)}, u32[]{:S(2)}) collective-permute-start(bf16[512,256]{1,0:T(8,128)(2,1)S(1)} %attend_last.1.a_ref), channel_id=1, source_target_pairs={{0,1},{1,0},{2,3},{3,2},{4,5},{5,4},{6,7},{7,6},{8,9},{9,8},{10,11... | collective-permute-start | bytes 786440 | tf_op jit(solution)/shard_map/ppermute | solution.py:387

commit v11 on v9

--- a/solution.py
+++ b/solution.py
@@ -48,31 +48,38 @@
     def wide(first, count, start):
         return xs[first:first + count, start:start + LANES].astype(jnp.float32)
 
-    for first in range(0, rows, tile):
-        for at in range(first, first + tile, part):
-            tokens_copy(at // part).wait()
-        total = wide(first, tile, 0)
+    def stats(first, count):
+        total = wide(first, count, 0)
         for start in range(LANES, width, LANES):
-            total = total + wide(first, tile, start)
-        mean = jnp.broadcast_to(jnp.sum(total, axis=1, keepdims=True) * (1.0 / width), (tile, LANES))
-        square = jnp.zeros((tile, LANES), jnp.float32)
+            total = total + wide(first, count, start)
+        mean = jnp.broadcast_to(jnp.sum(total, axis=1, keepdims=True) * (1.0 / width), (count, LANES))
+        square = jnp.zeros((count, LANES), jnp.float32)
         for start in range(0, width, LANES):
-            center = wide(first, tile, start) - mean
+            center = wide(first, count, start) - mean
             square = square + center * center
         spread = jnp.sum(square, axis=1, keepdims=True) * (1.0 / width)
-        scale = jnp.broadcast_to(lax.rsqrt(spread + 1e-05), (tile, LANES))
+        return mean, jnp.broadcast_to(lax.rsqrt(spread + 1e-05), (count, LANES))
+
+    for first in range(0, rows, tile):
+        halves = []
+        for at in range(first, first + tile, 2 * part):
+            tokens_copy(at // part).wait()
+            tokens_copy(at // part + 1).wait()
+            halves.append(stats(at, 2 * part))
+        mean = jnp.concatenate([h[0] for h in halves], axis=0)
+        scale = jnp.concatenate([h[1] for h in halves], axis=0)
         if first == 0:
             gain_copy().wait()
-            for i in range(pieces):
-                weights_copy(i).wait()
         kv = jnp.zeros((tile, ws.shape[1]), jnp.float32)
         span = slice(first, first + tile)
-        for start in range(0, width, HD):
-            for at in (start, start + LANES):
+        for start in range(0, width, deep):
+            if first == 0:
+                weights_copy(start // deep).wait()
+            for at in range(start, start + deep, LANES):
                 normed = (wide(first, tile, at) - mean) * scale * gain_ref[:, at:at + LANES]
                 normed_ref[span, at:at + LANES] = normed.astype(jnp.bfloat16)
             kv = kv + jnp.dot(
-                normed_ref[span, start:start + HD], ws[start:start + HD, :], preferred_element_type=jnp.float32
+                normed_ref[span, start:start + deep], ws[start:start + deep, :], preferred_element_type=jnp.float32
             )
         msg_ref[span, :] = kv.astype(jnp.bfloat16)
     segments_copy().wait()
@@ -282,7 +289,7 @@
 
 def own_kernel(a_ref, w_ref, sum_ref, out_ref):
     rows, width = out_ref.shape
-    tile = rows // 2
+    tile = rows
     chunk = width // 4
 
     def body(step, carry):
@@ -320,7 +327,7 @@
     pieces = sems.shape[0]
     piece = width // pieces
     chunk = width // 2
-    tile = rows // 2
+    tile = rows
 
     def copy(index):
         span = pl.ds(pl.multiple_of(index * piece, piece), piece)

time: 41.3 us -> 41.8 us (1.012)
  Pallas kernels: 19.6 us -> 20.1 us
where the time goes in v11:
time: 41.8 us; the launch traced here: 41.6 us
  Pallas kernels  20.1 us (48%)
  starting transfers between devices  10.9 us (26%)
  waiting for transfers between devices  10.2 us (24%)
    pallas_call x1, Pallas kernels, norm_kv(): pl.pallas_call(norm_kv_kernel, in_specs=[hbm] * 4, out_specs=[vmem, vmem]...  6.46 us
    ppermute x7, starting transfers between devices, swap_cores(): return lax.ppermute(x, 'tp', [(0, 1), (1, 0)])  5.71 us
    ppermute x3, waiting for transfers between devices, shift(): return lax.ppermute(x, ('seq', 'tp'), pairs)  4.91 us
    pallas_call x1, Pallas kernels, project_out(): pl.pallas_call(output_kernel, in_specs=[vmem] * len(operands), out_specs=...  4.61 us
    ppermute x3, starting transfers between devices, shift(): return lax.ppermute(x, ('seq', 'tp'), pairs)  3.88 us
    ppermute x1, waiting for transfers between devices, on_device(): lax.ppermute(jnp.where(odd, held, message), 'seq', [(i, i ^ 1) for i in r...  3.83 us
    pallas_call x1, Pallas kernels, spread_bounds(): pl.pallas_call(bounds_kernel, in_specs=[vmem, vmem, pl.BlockSpec(memory_s...  3.05 us
    pallas_call x3, Pallas kernels, attend(): pl.pallas_call(functools.partial(attend_kernel, plan, first, last), in_sp...  2.66 us
  transfers between devices with their start and end apart: 11, of which 4 were waited for; matrix products, arithmetic and copies ran while one was open for 0% of the time, Pallas kernels for 37%

profile of v11, /device:TPU:11, one launch (start us, length us, event | category | flops | bytes accessed | tf_op | source)
XLA Modules:
  0.0 41.6 jit_solution(5572970318184209011)
XLA Ops:
  0.0 0.7 %collective-permute-start.10 = (bf16[256,4096]{1,0:T(8,128)(2,1)}, bf16[256,4096]{1,0:T(8,128)(2,1)S(1)}, u32[]{:S(2)}, u32[]{:S(2)}) collective-permute-start(bf16[256,4096]{1,0:T(8,128)(2,1)} %w_ref.5), channel_id=1, source_target_pairs={{0,1},{1,0},{2,3},{3,2},{4,5},{5,4},{6,7},{7,6},{8,9},{9,8},{10,11... | collective-permute-start | bytes 6291464 | tf_op jit(solution)/shard_map/ppermute | solution.py:379
  0.7 6.5 %norm_kv.1 = (bf16[528,256]{1,0:T(8,128)(2,1)S(1)}, bf16[512,4096]{1,0:T(8,128)(2,1)S(1)}) custom-call(bf16[512,4096]{1,0:T(8,128)(2,1)} %x_ref.3, f32[1,4096]{1,0:T(1,128)} %bitcast.10, bf16[4096,256]{1,0:T(8,128)(2,1)} %w_ref.3, s32[1,512]{1,0:T(1,128)} %bitcast.6), custom_call_target="tpu_custom_call" | custom-call | flops 1073741824 | bytes 10485760 | tf_op jit(solution)/shard_map/norm_kv/pallas_call | solution.py:104
  7.1 0.0 copy-start.2
  7.2 1.3 %collective-permute-start = (bf16[528,256]{1,0:T(8,128)(2,1)S(1)}, bf16[528,256]{1,0:T(8,128)(2,1)S(1)}, u32[]{:S(2)}, u32[]{:S(2)}) collective-permute-start(bf16[528,256]{1,0:T(8,128)(2,1)S(1)} %get-tuple-element.21.refs_2_), channel_id=1, source_target_pairs={{0,4},{1,5},{2,6},{3,7},{4,8},{5,9},{6,10},{7,11},{8,12},{9,13},{1... | collective-permute-start | bytes 811016 | tf_op jit(solution)/shard_map/ppermute | solution.py:388
  8.5 0.4 %collective-permute-start.2 = (bf16[528,256]{1,0:T(8,128)(2,1)S(1)}, bf16[528,256]{1,0:T(8,128)(2,1)S(1)}, u32[]{:S(2)}, u32[]{:S(2)}) collective-permute-start(bf16[528,256]{1,0:T(8,128)(2,1)S(1)} %get-tuple-element.21.refs_2_), channel_id=1, source_target_pairs={{0,1},{1,0},{2,3},{3,2},{4,5},{5,4},{6,7},{7,6},{8,9},{9,8},{10,11... | collective-permute-start | bytes 811016 | tf_op jit(solution)/shard_map/ppermute | solution.py:379
  9.0 1.2 %project_query.1.refs_0_ = bf16[512,256]{1,0:T(8,128)(2,1)S(1)} custom-call(bf16[512,4096]{1,0:T(8,128)(2,1)S(1)} %get-tuple-element.22.x_ref, bf16[4096,256]{1,0:T(8,128)(2,1)S(1)} %copy-done), custom_call_target="tpu_custom_call" | custom-call | flops 1073741824 | bytes 6291456 | tf_op jit(solution)/shard_map/project_query/pallas_call | solution.py:132
  10.2 0.0 copy-start.4
  10.2 4.9 %collective-permute-done.refs_3_ = bf16[528,256]{1,0:T(8,128)(2,1)S(1)} collective-permute-done((bf16[528,256]{1,0:T(8,128)(2,1)S(1)}, bf16[528,256]{1,0:T(8,128)(2,1)S(1)}, u32[]{:S(2)}, u32[]{:S(2)}) %collective-permute-start) | collective-permute-done | bytes 270368 | tf_op jit(solution)/shard_map/ppermute | solution.py:388
  15.1 1.2 %collective-permute-start.7 = (bf16[528,256]{1,0:T(8,128)(2,1)S(1)}, bf16[528,256]{1,0:T(8,128)(2,1)S(1)}, u32[]{:S(2)}, u32[]{:S(2)}) collective-permute-start(bf16[528,256]{1,0:T(8,128)(2,1)S(1)} %collective-permute-done.refs_3_), channel_id=1, source_target_pairs={{0,1},{1,0},{2,3},{3,2},{4,6},{5,7},{6,8},{7,9},{8,10},{9,11},{10,... | collective-permute-start | bytes 811016 | tf_op jit(solution)/shard_map/ppermute | solution.py:388
  16.4 1.3 %collective-permute-start.4 = (bf16[528,256]{1,0:T(8,128)(2,1)S(1)}, bf16[528,256]{1,0:T(8,128)(2,1)S(1)}, u32[]{:S(2)}, u32[]{:S(2)}) collective-permute-start(bf16[528,256]{1,0:T(8,128)(2,1)S(1)} %collective-permute-done.refs_3_), channel_id=1, source_target_pairs={{0,1},{1,0},{2,3},{3,2},{4,8},{5,9},{6,10},{7,11},{8,12},{9,13},{1... | collective-permute-start | bytes 811016 | tf_op jit(solution)/shard_map/ppermute | solution.py:388
  17.7 1.5 %collective-permute-start.3 = (bf16[528,256]{1,0:T(8,128)(2,1)S(1)}, bf16[528,256]{1,0:T(8,128)(2,1)S(1)}, u32[]{:S(2)}, u32[]{:S(2)}) collective-permute-start(bf16[528,256]{1,0:T(8,128)(2,1)S(1)} %collective-permute-done.refs_3_), channel_id=1, source_target_pairs={{0,1},{1,0},{2,3},{3,2},{4,5},{5,4},{6,7},{7,6},{8,9},{9,8},{10,11... | collective-permute-start | bytes 811016 | tf_op jit(solution)/shard_map/ppermute | solution.py:379
  19.3 1.3 %collective-permute-start.1 = (bf16[528,256]{1,0:T(8,128)(2,1)S(1)}, bf16[528,256]{1,0:T(8,128)(2,1)S(1)}, u32[]{:S(2)}, u32[]{:S(2)}) collective-permute-start(bf16[528,256]{1,0:T(8,128)(2,1)S(1)} %broadcast_select_fusion), channel_id=1, source_target_pairs={{0,2},{2,0},{4,6},{6,4},{8,10},{10,8},{12,14},{14,12},{1,3},{3,1},... | collective-permute-start | bytes 811016 | tf_op jit(solution)/shard_map/ppermute | solution.py:395
  20.6 3.0 %spread_bounds.1 = (bf16[512,4096]{1,0:T(8,128)(2,1)S(1)}, bf16[512,4096]{1,0:T(8,128)(2,1)S(1)}, f32[512,4096]{1,0:T(8,128)S(1)}) custom-call(s32[32,512]{1,0:T(8,128)S(1)} %bitcast.4, s32[32,512]{1,0:T(8,128)S(1)} %bitcast.5, bf16[512,4096]{1,0:T(8,128)(2,1)} %x_ref.3), custom_call_target="tpu_custom_call" | custom-call | flops 16777216 | bytes 131072 | tf_op jit(solution)/shard_map/spread_bounds/pallas_call | solution.py:274
  23.7 1.6 %attend_first.1.refs_4_ = f32[512,512]{1,0:T(8,128)S(1)} custom-call(bf16[512,256]{1,0:T(8,128)(2,1)S(1)} %project_query.1.refs_0_, s32[1,512]{1,0:T(1,128)S(1)} %bitcast.7, bf16[528,256]{1,0:T(8,128)(2,1)S(1)} %get-tuple-element.21.refs_2_, bf16[528,256]{1,0:T(8,128)(2,1)S(1)} %collective-permute-done.refs_3_, ...), custom_call_target="tpu_custom_call" | custom-call | flops 536870912 | bytes 1048576 | tf_op jit(solution)/shard_map/attend_first/pallas_call | solution.py:234
  25.3 2.1 %collective-permute-start.8 = (bf16[528,256]{1,0:T(8,128)(2,1)S(1)}, bf16[528,256]{1,0:T(8,128)(2,1)S(1)}, u32[]{:S(2)}, u32[]{:S(2)}) collective-permute-start(bf16[528,256]{1,0:T(8,128)(2,1)S(1)} %collective-permute-done.7.refs_2_), channel_id=1, source_target_pairs={{0,1},{1,0},{2,3},{3,2},{4,5},{5,4},{6,7},{7,6},{8,9},{9,8},{10,11... | collective-permute-start | bytes 811016 | tf_op jit(solution)/shard_map/ppermute | solution.py:379
  27.4 3.8 %collective-permute-done.1.refs_2_ = bf16[528,256]{1,0:T(8,128)(2,1)S(1)} collective-permute-done((bf16[528,256]{1,0:T(8,128)(2,1)S(1)}, bf16[528,256]{1,0:T(8,128)(2,1)S(1)}, u32[]{:S(2)}, u32[]{:S(2)}) %collective-permute-start.1) | collective-permute-done | bytes 270368 | tf_op jit(solution)/shard_map/ppermute | solution.py:395
  31.2 0.4 %collective-permute-start.5 = (bf16[528,256]{1,0:T(8,128)(2,1)S(1)}, bf16[528,256]{1,0:T(8,128)(2,1)S(1)}, u32[]{:S(2)}, u32[]{:S(2)}) collective-permute-start(bf16[528,256]{1,0:T(8,128)(2,1)S(1)} %collective-permute-done.1.refs_2_), channel_id=1, source_target_pairs={{0,1},{1,0},{2,3},{3,2},{4,5},{5,4},{6,7},{7,6},{8,9},{9,8},{10,11... | collective-permute-start | bytes 811016 | tf_op jit(solution)/shard_map/ppermute | solution.py:379
  31.6 0.1 collective-permute-start.6
  31.7 1.1 %collective-permute-done.5.refs_4_ = bf16[528,256]{1,0:T(8,128)(2,1)S(1)} collective-permute-done((bf16[528,256]{1,0:T(8,128)(2,1)S(1)}, bf16[528,256]{1,0:T(8,128)(2,1)S(1)}, u32[]{:S(2)}, u32[]{:S(2)}) %collective-permute-start.5) | collective-permute-done | bytes 270368 | tf_op jit(solution)/shard_map/ppermute | solution.py:379
  32.8 0.4 collective-permute-done.6.refs_5_
  33.2 1.1 %attend_last.1.a_ref = bf16[512,256]{1,0:T(8,128)(2,1)S(1)} custom-call(bf16[512,256]{1,0:T(8,128)(2,1)S(1)} %project_query.1.refs_0_, s32[1,512]{1,0:T(1,128)S(1)} %bitcast.9, bf16[528,256]{1,0:T(8,128)(2,1)S(1)} %collective-permute-done.1.refs_2_, bf16[528,256]{1,0:T(8,128)(2,1)S(1)} %collective-permute-done.4.refs_3_, ...), custom_call_target="tpu_custom_call" | custom-call | flops 536870912 | bytes 1048576 | tf_op jit(solution)/shard_map/attend_last/pallas_call | solution.py:234
  34.3 0.4 %collective-permute-start.9 = (bf16[512,256]{1,0:T(8,128)(2,1)S(1)}, bf16[512,256]{1,0:T(8,128)(2,1)S(1)}, u32[]{:S(2)}, u32[]{:S(2)}) collective-permute-start(bf16[512,256]{1,0:T(8,128)(2,1)S(1)} %attend_last.1.a_ref), channel_id=1, source_target_pairs={{0,1},{1,0},{2,3},{3,2},{4,5},{5,4},{6,7},{7,6},{8,9},{9,8},{10,11... | collective-permute-start | bytes 786440 | tf_op jit(solution)/shard_map/ppermute | solution.py:379
  34.7 2.1 %project_own.1.quant_ref = bf16[512,4096]{1,0:T(8,128)(2,1)S(1)} custom-call(bf16[512,256]{1,0:T(8,128)(2,1)S(1)} %attend_last.1.a_ref, bf16[256,4096]{1,0:T(8,128)(2,1)S(1)} %copy-done.1, bf16[512,4096]{1,0:T(8,128)(2,1)S(1)} %get-tuple-element.30.sum_ref), custom_call_target="tpu_custom_call" | custom-call | flops 1073741824 | bytes 10485760 | tf_op jit(solution)/shard_map/project_own/pallas_call | solution.py:312
  36.9 4.6 %project_out.1 = bf16[512,4096]{1,0:T(8,128)(2,1)} custom-call(bf16[512,256]{1,0:T(8,128)(2,1)S(1)} %collective-permute-done.9.b_ref, bf16[256,4096]{1,0:T(8,128)(2,1)S(1)} %collective-permute-done.10.wb_ref, bf16[512,4096]{1,0:T(8,128)(2,1)S(1)} %project_own.1.quant_ref, f32[512,4096]{1,0:T(8,128)S(1)} %get-tuple-element.32.x_ref, ...), custom_call_target="tpu_custom_call" | custom-call | flops 1073741824 | bytes 10485760 | tf_op jit(solution)/shard_map/project_out/pallas_call | solution.py:361
  (17 shorter events, 0.1 us)
Async XLA Ops:
  0.0 9.0 %copy-start = (bf16[4096,256]{1,0:T(8,128)(2,1)S(1)}, bf16[4096,256]{1,0:T(8,128)(2,1)}, u32[]{:S(2)}) copy-start(bf16[4096,256]{1,0:T(8,128)(2,1)} %w_ref.4) | copy-start | bytes 6291460
  0.0 36.9 %collective-permute-start.10 = (bf16[256,4096]{1,0:T(8,128)(2,1)}, bf16[256,4096]{1,0:T(8,128)(2,1)S(1)}, u32[]{:S(2)}, u32[]{:S(2)}) collective-permute-start(bf16[256,4096]{1,0:T(8,128)(2,1)} %w_ref.5), channel_id=1, source_target_pairs={{0,1},{1,0},{2,3},{3,2},{4,5},{5,4},{6,7},{7,6},{8,9},{9,8},{10,11... | collective-permute-start | bytes 6291464 | tf_op jit(solution)/shard_map/ppermute | solution.py:379
  7.1 13.4 %copy-start.2 = (s32[512,32]{0,1:T(8,128)S(1)}, s32[512,32]{0,1:T(8,128)}, u32[]{:S(2)}) copy-start(s32[512,32]{0,1:T(8,128)} %param.14) | copy-start | bytes 196612
  7.2 13.4 %copy-start.3 = (s32[512,32]{0,1:T(8,128)S(1)}, s32[512,32]{0,1:T(8,128)}, u32[]{:S(2)}) copy-start(s32[512,32]{0,1:T(8,128)} %param.15) | copy-start | bytes 196612
  7.2 8.0 %collective-permute-start = (bf16[528,256]{1,0:T(8,128)(2,1)S(1)}, bf16[528,256]{1,0:T(8,128)(2,1)S(1)}, u32[]{:S(2)}, u32[]{:S(2)}) collective-permute-start(bf16[528,256]{1,0:T(8,128)(2,1)S(1)} %get-tuple-element.21.refs_2_), channel_id=1, source_target_pairs={{0,4},{1,5},{2,6},{3,7},{4,8},{5,9},{6,10},{7,11},{8,12},{9,13},{1... | collective-permute-start | bytes 811016 | tf_op jit(solution)/shard_map/ppermute | solution.py:388
  8.5 10.7 %collective-permute-start.2 = (bf16[528,256]{1,0:T(8,128)(2,1)S(1)}, bf16[528,256]{1,0:T(8,128)(2,1)S(1)}, u32[]{:S(2)}, u32[]{:S(2)}) collective-permute-start(bf16[528,256]{1,0:T(8,128)(2,1)S(1)} %get-tuple-element.21.refs_2_), channel_id=1, source_target_pairs={{0,1},{1,0},{2,3},{3,2},{4,5},{5,4},{6,7},{7,6},{8,9},{9,8},{10,11... | collective-permute-start | bytes 811016 | tf_op jit(solution)/shard_map/ppermute | solution.py:379
  10.2 13.4 %copy-start.4 = (s32[512]{0:T(512)S(1)}, s32[512]{0:T(512)}, u32[]{:S(2)}) copy-start(s32[512]{0:T(512)} %param.10) | copy-start | bytes 6148
  15.1 10.1 %collective-permute-start.7 = (bf16[528,256]{1,0:T(8,128)(2,1)S(1)}, bf16[528,256]{1,0:T(8,128)(2,1)S(1)}, u32[]{:S(2)}, u32[]{:S(2)}) collective-permute-start(bf16[528,256]{1,0:T(8,128)(2,1)S(1)} %collective-permute-done.refs_3_), channel_id=1, source_target_pairs={{0,1},{1,0},{2,3},{3,2},{4,6},{5,7},{6,8},{7,9},{8,10},{9,11},{10,... | collective-permute-start | bytes 811016 | tf_op jit(solution)/shard_map/ppermute | solution.py:388
  16.4 11.0 %collective-permute-start.4 = (bf16[528,256]{1,0:T(8,128)(2,1)S(1)}, bf16[528,256]{1,0:T(8,128)(2,1)S(1)}, u32[]{:S(2)}, u32[]{:S(2)}) collective-permute-start(bf16[528,256]{1,0:T(8,128)(2,1)S(1)} %collective-permute-done.refs_3_), channel_id=1, source_target_pairs={{0,1},{1,0},{2,3},{3,2},{4,8},{5,9},{6,10},{7,11},{8,12},{9,13},{1... | collective-permute-start | bytes 811016 | tf_op jit(solution)/shard_map/ppermute | solution.py:388
  17.7 6.0 %collective-permute-start.3 = (bf16[528,256]{1,0:T(8,128)(2,1)S(1)}, bf16[528,256]{1,0:T(8,128)(2,1)S(1)}, u32[]{:S(2)}, u32[]{:S(2)}) collective-permute-start(bf16[528,256]{1,0:T(8,128)(2,1)S(1)} %collective-permute-done.refs_3_), channel_id=1, source_target_pairs={{0,1},{1,0},{2,3},{3,2},{4,5},{5,4},{6,7},{7,6},{8,9},{9,8},{10,11... | collective-permute-start | bytes 811016 | tf_op jit(solution)/shard_map/ppermute | solution.py:379
  19.3 11.9 %collective-permute-start.1 = (bf16[528,256]{1,0:T(8,128)(2,1)S(1)}, bf16[528,256]{1,0:T(8,128)(2,1)S(1)}, u32[]{:S(2)}, u32[]{:S(2)}) collective-permute-start(bf16[528,256]{1,0:T(8,128)(2,1)S(1)} %broadcast_select_fusion), channel_id=1, source_target_pairs={{0,2},{2,0},{4,6},{6,4},{8,10},{10,8},{12,14},{14,12},{1,3},{3,1},... | collective-permute-start | bytes 811016 | tf_op jit(solution)/shard_map/ppermute | solution.py:395
  23.6 11.1 %copy-start.1 = (bf16[256,4096]{1,0:T(8,128)(2,1)S(1)}, bf16[256,4096]{1,0:T(8,128)(2,1)}, u32[]{:S(2)}) copy-start(bf16[256,4096]{1,0:T(8,128)(2,1)} %w_ref.5) | copy-start | bytes 6291460
  25.3 6.4 %collective-permute-start.8 = (bf16[528,256]{1,0:T(8,128)(2,1)S(1)}, bf16[528,256]{1,0:T(8,128)(2,1)S(1)}, u32[]{:S(2)}, u32[]{:S(2)}) collective-permute-start(bf16[528,256]{1,0:T(8,128)(2,1)S(1)} %collective-permute-done.7.refs_2_), channel_id=1, source_target_pairs={{0,1},{1,0},{2,3},{3,2},{4,5},{5,4},{6,7},{7,6},{8,9},{9,8},{10,11... | collective-permute-start | bytes 811016 | tf_op jit(solution)/shard_map/ppermute | solution.py:379
  31.2 1.6 %collective-permute-start.5 = (bf16[528,256]{1,0:T(8,128)(2,1)S(1)}, bf16[528,256]{1,0:T(8,128)(2,1)S(1)}, u32[]{:S(2)}, u32[]{:S(2)}) collective-permute-start(bf16[528,256]{1,0:T(8,128)(2,1)S(1)} %collective-permute-done.1.refs_2_), channel_id=1, source_target_pairs={{0,1},{1,0},{2,3},{3,2},{4,5},{5,4},{6,7},{7,6},{8,9},{9,8},{10,11... | collective-permute-start | bytes 811016 | tf_op jit(solution)/shard_map/ppermute | solution.py:379
  31.6 1.6 %collective-permute-start.6 = (bf16[528,256]{1,0:T(8,128)(2,1)S(1)}, bf16[528,256]{1,0:T(8,128)(2,1)S(1)}, u32[]{:S(2)}, u32[]{:S(2)}) collective-permute-start(bf16[528,256]{1,0:T(8,128)(2,1)S(1)} %collective-permute-done.4.refs_3_), channel_id=1, source_target_pairs={{0,1},{1,0},{2,3},{3,2},{4,5},{5,4},{6,7},{7,6},{8,9},{9,8},{10,11... | collective-permute-start | bytes 811016 | tf_op jit(solution)/shard_map/ppermute | solution.py:379
  34.3 2.6 %collective-permute-start.9 = (bf16[512,256]{1,0:T(8,128)(2,1)S(1)}, bf16[512,256]{1,0:T(8,128)(2,1)S(1)}, u32[]{:S(2)}, u32[]{:S(2)}) collective-permute-start(bf16[512,256]{1,0:T(8,128)(2,1)S(1)} %attend_last.1.a_ref), channel_id=1, source_target_pairs={{0,1},{1,0},{2,3},{3,2},{4,5},{5,4},{6,7},{7,6},{8,9},{9,8},{10,11... | collective-permute-start | bytes 786440 | tf_op jit(solution)/shard_map/ppermute | solution.py:379

commit v12 on v9

--- a/solution.py
+++ b/solution.py
@@ -18,53 +18,43 @@
 FACTOR = HD ** (-0.5) * 1.4426950408889634
 
 
-def norm_kv_kernel(x_ref, gain_hbm, w_ref, seg_hbm, msg_ref, normed_ref, xs, ws, gain_ref, seg_ref, sems):
+def norm_kv_kernel(x_ref, gain_hbm, w_ref, seg_hbm, next_ref, msg_ref, normed_ref, near_ref, xs, ws, gain_ref, seg_ref, sems):
     rows, width = xs.shape
-    tile, part = rows // 2, rows // 8
-    pieces = 4
-    deep = width // pieces
+    tile, part = rows // 2, rows // 4
 
     def tokens_copy(i):
         return pltpu.make_async_copy(x_ref.at[pl.ds(i * part, part)], xs.at[pl.ds(i * part, part)], sems.at[i])
 
-    def weights_copy(i):
-        return pltpu.make_async_copy(w_ref.at[pl.ds(i * deep, deep)], ws.at[pl.ds(i * deep, deep)], sems.at[8 + i])
+    def weights_copy():
+        return pltpu.make_async_copy(w_ref, ws, sems.at[4])
 
     def gain_copy():
-        return pltpu.make_async_copy(gain_hbm, gain_ref, sems.at[12])
+        return pltpu.make_async_copy(gain_hbm, gain_ref, sems.at[5])
 
     def segments_copy():
-        return pltpu.make_async_copy(seg_hbm, seg_ref, sems.at[13])
-
-    for i in range(4):
-        tokens_copy(i).start()
-    gain_copy().start()
-    for i in range(pieces):
-        weights_copy(i).start()
-    for i in range(4, 8):
-        tokens_copy(i).start()
-    segments_copy().start()
+        return pltpu.make_async_copy(seg_hbm, seg_ref, sems.at[6])
+
+    def next_copy():
+        return pltpu.make_async_copy(next_ref, near_ref, sems.at[7])
 
     def wide(first, count, start):
         return xs[first:first + count, start:start + LANES].astype(jnp.float32)
 
-    for first in range(0, rows, tile):
-        for at in range(first, first + tile, part):
-            tokens_copy(at // part).wait()
-        total = wide(first, tile, 0)
+    def stats(first):
+        total = wide(first, part, 0)
         for start in range(LANES, width, LANES):
-            total = total + wide(first, tile, start)
-        mean = jnp.broadcast_to(jnp.sum(total, axis=1, keepdims=True) * (1.0 / width), (tile, LANES))
-        square = jnp.zeros((tile, LANES), jnp.float32)
+            total = total + wide(first, part, start)
+        mean = jnp.broadcast_to(jnp.sum(total, axis=1, keepdims=True) * (1.0 / width), (part, LANES))
+        square = jnp.zeros((part, LANES), jnp.float32)
         for start in range(0, width, LANES):
-            center = wide(first, tile, start) - mean
+            center = wide(first, part, start) - mean
             square = square + center * center
         spread = jnp.sum(square, axis=1, keepdims=True) * (1.0 / width)
-        scale = jnp.broadcast_to(lax.rsqrt(spread + 1e-05), (tile, LANES))
-        if first == 0:
-            gain_copy().wait()
-            for i in range(pieces):
-                weights_copy(i).wait()
+        return mean, jnp.broadcast_to(lax.rsqrt(spread + 1e-05), (part, LANES))
+
+    def project(first, halves):
+        mean = jnp.concatenate([h[0] for h in halves], axis=0)
+        scale = jnp.concatenate([h[1] for h in halves], axis=0)
         kv = jnp.zeros((tile, ws.shape[1]), jnp.float32)
         span = slice(first, first + tile)
         for start in range(0, width, HD):
@@ -75,11 +65,33 @@
                 normed_ref[span, start:start + HD], ws[start:start + HD, :], preferred_element_type=jnp.float32
             )
         msg_ref[span, :] = kv.astype(jnp.bfloat16)
+
+    tokens_copy(0).start()
+    tokens_copy(1).start()
+    tokens_copy(0).wait()
+    gain_copy().start()
+    weights_copy().start()
+    halves = [stats(0)]
+    tokens_copy(1).wait()
+    tokens_copy(2).start()
+    halves.append(stats(part))
+    gain_copy().wait()
+    weights_copy().wait()
+    tokens_copy(3).start()
+    segments_copy().start()
+    project(0, halves)
+    tokens_copy(2).wait()
+    halves = [stats(tile)]
+    tokens_copy(3).wait()
+    next_copy().start()
+    halves.append(stats(tile + part))
+    project(tile, halves)
     segments_copy().wait()
     seg = seg_ref[...].astype(jnp.float32)
     low = jnp.broadcast_to(seg[:, :HD], (8, HD))
     high = jnp.broadcast_to(seg[:, HD:], (8, HD))
     msg_ref[rows:, :] = jnp.concatenate([low, high], axis=0).astype(jnp.bfloat16)
+    next_copy().wait()
 
 
 def in_hbm(x):
@@ -90,28 +102,32 @@
     return pltpu.with_memory_space_constraint(x, pltpu.VMEM)
 
 
-def norm_kv(tokens, gain, w_keyval, segments):
+def norm_kv(tokens, gain, w_keyval, segments, w_next):
     rows, width = tokens.shape
     cols = w_keyval.shape[1]
     vmem, hbm = pl.BlockSpec(memory_space=pltpu.VMEM), pl.BlockSpec(memory_space=pltpu.HBM)
     return pl.pallas_call(
         norm_kv_kernel,
-        in_specs=[hbm] * 4,
-        out_specs=[vmem, vmem],
-        out_shape=[pltpu.VMEM((rows + SEG_ROWS, cols), jnp.bfloat16), pltpu.VMEM((rows, width), jnp.bfloat16)],
+        in_specs=[hbm] * 5,
+        out_specs=[vmem] * 3,
+        out_shape=[
+            pltpu.VMEM((rows + SEG_ROWS, cols), jnp.bfloat16),
+            pltpu.VMEM((rows, width), jnp.bfloat16),
+            pltpu.VMEM(w_next.shape, w_next.dtype),
+        ],
         scratch_shapes=[
             pltpu.VMEM((rows, width), jnp.bfloat16),
             pltpu.VMEM((width, cols), jnp.bfloat16),
             pltpu.VMEM((1, width), jnp.float32),
             pltpu.VMEM((1, rows), jnp.int32),
-            pltpu.SemaphoreType.DMA((14,)),
+            pltpu.SemaphoreType.DMA((8,)),
         ],
         compiler_params=pltpu.CompilerParams(vmem_limit_bytes=24 * MIB),
         cost_estimate=pl.CostEstimate(
             flops=2 * rows * width * cols, bytes_accessed=4 * rows * width + 2 * width * cols, transcendentals=0
         ),
         name="norm_kv",
-    )(in_hbm(tokens), in_hbm(gain.reshape(1, width)), in_hbm(w_keyval), in_hbm(segments.reshape(1, rows)))
+    )(*[in_hbm(x) for x in (tokens, gain.reshape(1, width), w_keyval, segments.reshape(1, rows), w_next)])
 
 
 def query_kernel(x_ref, w_ref, out_ref):
@@ -145,7 +161,7 @@
         state_ref, refs = refs[0], refs[1:]
     out_ref, scores = refs
     rows = q_ref.shape[0]
-    tile = rows // 2
+    tile = rows // 4
     part = lax.axis_index("tp")
     place = lax.axis_index("seq")
 
@@ -229,7 +245,7 @@
         in_specs=[vmem] * len(operands),
         out_specs=vmem,
         out_shape=pltpu.VMEM((rows, HD), jnp.bfloat16) if last else pltpu.VMEM((rows, HD + 2 * LANES), jnp.float32),
-        scratch_shapes=[pltpu.VMEM((blocks, rows // 2, rows), jnp.float32)],
+        scratch_shapes=[pltpu.VMEM((blocks, rows // 4, rows), jnp.float32)],
         input_output_aliases={} if first or last else {len(operands) - 1: 0},
         compiler_params=pltpu.CompilerParams(vmem_limit_bytes=12 * MIB),
         cost_estimate=pl.CostEstimate(
@@ -282,7 +298,7 @@
 
 def own_kernel(a_ref, w_ref, sum_ref, out_ref):
     rows, width = out_ref.shape
-    tile = rows // 2
+    tile = rows // 4
     chunk = width // 4
 
     def body(step, carry):
@@ -320,7 +336,7 @@
     pieces = sems.shape[0]
     piece = width // pieces
     chunk = width // 2
-    tile = rows // 2
+    tile = rows // 4
 
     def copy(index):
         span = pl.ds(pl.multiple_of(index * piece, piece), piece)
@@ -381,8 +397,8 @@
         return lax.ppermute(x, ("seq", "tp"), pairs)
 
     w_other = swap_cores(w_out)
-    message, normed = norm_kv(tokens, gain, w_keyval, segments)
-    query = project_query(normed, w_query)
+    message, normed, w_near = norm_kv(tokens, gain, w_keyval, segments, w_query)
+    query = project_query(normed, w_near)
     held, query = lax.optimization_barrier((shift(message, 2, 0), query))
     odd = lax.rem(lax.axis_index("seq"), 2) == 1
     beside = lax.ppermute(jnp.where(odd, held, message), "seq", [(i, i ^ 1) for i in range(seq_size)])

time: 41.3 us -> 42.6 us (1.031)
  Pallas kernels: 19.6 us -> 21.1 us
  starting transfers between devices: 10.9 us -> 10.1 us
  waiting for transfers between devices: 10.2 us -> 10.8 us
    pallas_call x3, Pallas kernels: 2.67 us -> 3.46 us  [attend(): pl.pallas_call(functools.partial(attend_kernel, plan, first, last), in_sp...]
    ppermute x7, starting transfers between devices: 5.71 us -> 4.95 us  [swap_cores(): return lax.ppermute(x, 'tp', [(0, 1), (1, 0)])]
    pallas_call x1, Pallas kernels: 6.19 us -> 6.66 us  [norm_kv(): pl.pallas_call(norm_kv_kernel, in_specs=[hbm] * 5, out_specs=[vmem] * 3,...]
  transfers between devices with their start and end apart: 11 -> 11, of which waited for: 4 -> 4; matrix products, arithmetic and copies ran while one was open for 0% -> 0% of each run, Pallas kernels for 37% -> 39%
where the time goes in v12:
time: 42.6 us; the launch traced here: 42.4 us
  Pallas kernels  21.1 us (50%)
  waiting for transfers between devices  10.8 us (25%)
  starting transfers between devices  10.1 us (24%)
    pallas_call x1, Pallas kernels, norm_kv(): pl.pallas_call(norm_kv_kernel, in_specs=[hbm] * 5, out_specs=[vmem] * 3,...  6.66 us
    ppermute x3, waiting for transfers between devices, shift(): return lax.ppermute(x, ('seq', 'tp'), pairs)  5.27 us
    ppermute x7, starting transfers between devices, swap_cores(): return lax.ppermute(x, 'tp', [(0, 1), (1, 0)])  4.95 us
    pallas_call x1, Pallas kernels, project_out(): pl.pallas_call(output_kernel, in_specs=[vmem] * len(operands), out_specs=...  4.78 us
    ppermute x1, waiting for transfers between devices, on_device(): lax.ppermute(jnp.where(odd, held, message), 'seq', [(i, i ^ 1) for i in r...  4.03 us
    ppermute x3, starting transfers between devices, shift(): return lax.ppermute(x, ('seq', 'tp'), pairs)  3.88 us
    pallas_call x3, Pallas kernels, attend(): pl.pallas_call(functools.partial(attend_kernel, plan, first, last), in_sp...  3.46 us
    pallas_call x1, Pallas kernels, spread_bounds(): pl.pallas_call(bounds_kernel, in_specs=[vmem, vmem, pl.BlockSpec(memory_s...  3.05 us
  transfers between devices with their start and end apart: 11, of which 4 were waited for; matrix products, arithmetic and copies ran while one was open for 0% of the time, Pallas kernels for 39%

profile of v12, /device:TPU:11, one launch (start us, length us, event | category | flops | bytes accessed | tf_op | source)
XLA Modules:
  0.0 42.4 jit_solution(5896857019602280397)
XLA Ops:
  0.0 0.7 %collective-permute-start.10 = (bf16[256,4096]{1,0:T(8,128)(2,1)}, bf16[256,4096]{1,0:T(8,128)(2,1)S(1)}, u32[]{:S(2)}, u32[]{:S(2)}) collective-permute-start(bf16[256,4096]{1,0:T(8,128)(2,1)} %w_ref.3), channel_id=1, source_target_pairs={{0,1},{1,0},{2,3},{3,2},{4,5},{5,4},{6,7},{7,6},{8,9},{9,8},{10,11... | collective-permute-start | bytes 6291464 | tf_op jit(solution)/shard_map/ppermute | solution.py:388
  0.7 6.7 %norm_kv.1 = (bf16[528,256]{1,0:T(8,128)(2,1)S(1)}, bf16[512,4096]{1,0:T(8,128)(2,1)S(1)}, bf16[4096,256]{1,0:T(8,128)(2,1)S(1)}) custom-call(bf16[512,4096]{1,0:T(8,128)(2,1)} %x_ref.3, f32[1,4096]{1,0:T(1,128)} %bitcast.10, bf16[4096,256]{1,0:T(8,128)(2,1)} %w_ref.2, s32[1,512]{1,0:T(1,128)} %bitcast.6, bf16[4096,256]{1,0:T(8,128)(2,1)} %next_ref.1), custom_call_target="tpu_custom_call" | custom-call | flops 1073741824 | bytes 10485760 | tf_op jit(solution)/shard_map/norm_kv/pallas_call | solution.py:109
  7.4 0.0 copy-start.2
  7.4 1.3 %collective-permute-start = (bf16[528,256]{1,0:T(8,128)(2,1)S(1)}, bf16[528,256]{1,0:T(8,128)(2,1)S(1)}, u32[]{:S(2)}, u32[]{:S(2)}) collective-permute-start(bf16[528,256]{1,0:T(8,128)(2,1)S(1)} %get-tuple-element.22.refs_2_), channel_id=1, source_target_pairs={{0,4},{1,5},{2,6},{3,7},{4,8},{5,9},{6,10},{7,11},{8,12},{9,13},{1... | collective-permute-start | bytes 811016 | tf_op jit(solution)/shard_map/ppermute | solution.py:397
  8.7 0.3 collective-permute-start.2
  9.0 1.2 %project_query.1.refs_0_ = bf16[512,256]{1,0:T(8,128)(2,1)S(1)} custom-call(bf16[512,4096]{1,0:T(8,128)(2,1)S(1)} %get-tuple-element.23.x_ref, bf16[4096,256]{1,0:T(8,128)(2,1)S(1)} %get-tuple-element.24.w_ref), custom_call_target="tpu_custom_call" | custom-call | flops 1073741824 | bytes 6291456 | tf_op jit(solution)/shard_map/project_query/pallas_call | solution.py:141
  10.3 0.0 copy-start.3
  10.3 5.3 %collective-permute-done.refs_3_ = bf16[528,256]{1,0:T(8,128)(2,1)S(1)} collective-permute-done((bf16[528,256]{1,0:T(8,128)(2,1)S(1)}, bf16[528,256]{1,0:T(8,128)(2,1)S(1)}, u32[]{:S(2)}, u32[]{:S(2)}) %collective-permute-start) | collective-permute-done | bytes 270368 | tf_op jit(solution)/shard_map/ppermute | solution.py:397
  15.5 1.2 %collective-permute-start.7 = (bf16[528,256]{1,0:T(8,128)(2,1)S(1)}, bf16[528,256]{1,0:T(8,128)(2,1)S(1)}, u32[]{:S(2)}, u32[]{:S(2)}) collective-permute-start(bf16[528,256]{1,0:T(8,128)(2,1)S(1)} %collective-permute-done.refs_3_), channel_id=1, source_target_pairs={{0,1},{1,0},{2,3},{3,2},{4,6},{5,7},{6,8},{7,9},{8,10},{9,11},{10,... | collective-permute-start | bytes 811016 | tf_op jit(solution)/shard_map/ppermute | solution.py:397
  16.8 1.3 %collective-permute-start.4 = (bf16[528,256]{1,0:T(8,128)(2,1)S(1)}, bf16[528,256]{1,0:T(8,128)(2,1)S(1)}, u32[]{:S(2)}, u32[]{:S(2)}) collective-permute-start(bf16[528,256]{1,0:T(8,128)(2,1)S(1)} %collective-permute-done.refs_3_), channel_id=1, source_target_pairs={{0,1},{1,0},{2,3},{3,2},{4,8},{5,9},{6,10},{7,11},{8,12},{9,13},{1... | collective-permute-start | bytes 811016 | tf_op jit(solution)/shard_map/ppermute | solution.py:397
  18.1 1.3 %collective-permute-start.3 = (bf16[528,256]{1,0:T(8,128)(2,1)S(1)}, bf16[528,256]{1,0:T(8,128)(2,1)S(1)}, u32[]{:S(2)}, u32[]{:S(2)}) collective-permute-start(bf16[528,256]{1,0:T(8,128)(2,1)S(1)} %collective-permute-done.refs_3_), channel_id=1, source_target_pairs={{0,1},{1,0},{2,3},{3,2},{4,5},{5,4},{6,7},{7,6},{8,9},{9,8},{10,11... | collective-permute-start | bytes 811016 | tf_op jit(solution)/shard_map/ppermute | solution.py:388
  19.5 1.3 %collective-permute-start.1 = (bf16[528,256]{1,0:T(8,128)(2,1)S(1)}, bf16[528,256]{1,0:T(8,128)(2,1)S(1)}, u32[]{:S(2)}, u32[]{:S(2)}) collective-permute-start(bf16[528,256]{1,0:T(8,128)(2,1)S(1)} %broadcast_select_fusion), channel_id=1, source_target_pairs={{0,2},{2,0},{4,6},{6,4},{8,10},{10,8},{12,14},{14,12},{1,3},{3,1},... | collective-permute-start | bytes 811016 | tf_op jit(solution)/shard_map/ppermute | solution.py:404
  20.8 3.0 %spread_bounds.1 = (bf16[512,4096]{1,0:T(8,128)(2,1)S(1)}, bf16[512,4096]{1,0:T(8,128)(2,1)S(1)}, f32[512,4096]{1,0:T(8,128)S(1)}) custom-call(s32[32,512]{1,0:T(8,128)S(1)} %bitcast.4, s32[32,512]{1,0:T(8,128)S(1)} %bitcast.5, bf16[512,4096]{1,0:T(8,128)(2,1)} %x_ref.3), custom_call_target="tpu_custom_call" | custom-call | flops 16777216 | bytes 131072 | tf_op jit(solution)/shard_map/spread_bounds/pallas_call | solution.py:283
  23.9 2.0 %attend_first.1.refs_4_ = f32[512,512]{1,0:T(8,128)S(1)} custom-call(bf16[512,256]{1,0:T(8,128)(2,1)S(1)} %project_query.1.refs_0_, s32[1,512]{1,0:T(1,128)S(1)} %bitcast.7, bf16[528,256]{1,0:T(8,128)(2,1)S(1)} %get-tuple-element.22.refs_2_, bf16[528,256]{1,0:T(8,128)(2,1)S(1)} %collective-permute-done.refs_3_, ...), custom_call_target="tpu_custom_call" | custom-call | flops 536870912 | bytes 1048576 | tf_op jit(solution)/shard_map/attend_first/pallas_call | solution.py:243
  25.9 1.7 %collective-permute-start.8 = (bf16[528,256]{1,0:T(8,128)(2,1)S(1)}, bf16[528,256]{1,0:T(8,128)(2,1)S(1)}, u32[]{:S(2)}, u32[]{:S(2)}) collective-permute-start(bf16[528,256]{1,0:T(8,128)(2,1)S(1)} %collective-permute-done.7.refs_2_), channel_id=1, source_target_pairs={{0,1},{1,0},{2,3},{3,2},{4,5},{5,4},{6,7},{7,6},{8,9},{9,8},{10,11... | collective-permute-start | bytes 811016 | tf_op jit(solution)/shard_map/ppermute | solution.py:388
  27.5 4.0 %collective-permute-done.1.refs_2_ = bf16[528,256]{1,0:T(8,128)(2,1)S(1)} collective-permute-done((bf16[528,256]{1,0:T(8,128)(2,1)S(1)}, bf16[528,256]{1,0:T(8,128)(2,1)S(1)}, u32[]{:S(2)}, u32[]{:S(2)}) %collective-permute-start.1) | collective-permute-done | bytes 270368 | tf_op jit(solution)/shard_map/ppermute | solution.py:404
  31.6 0.4 %collective-permute-start.5 = (bf16[528,256]{1,0:T(8,128)(2,1)S(1)}, bf16[528,256]{1,0:T(8,128)(2,1)S(1)}, u32[]{:S(2)}, u32[]{:S(2)}) collective-permute-start(bf16[528,256]{1,0:T(8,128)(2,1)S(1)} %collective-permute-done.1.refs_2_), channel_id=1, source_target_pairs={{0,1},{1,0},{2,3},{3,2},{4,5},{5,4},{6,7},{7,6},{8,9},{9,8},{10,11... | collective-permute-start | bytes 811016 | tf_op jit(solution)/shard_map/ppermute | solution.py:388
  32.0 0.1 collective-permute-start.6
  32.1 1.1 %collective-permute-done.5.refs_4_ = bf16[528,256]{1,0:T(8,128)(2,1)S(1)} collective-permute-done((bf16[528,256]{1,0:T(8,128)(2,1)S(1)}, bf16[528,256]{1,0:T(8,128)(2,1)S(1)}, u32[]{:S(2)}, u32[]{:S(2)}) %collective-permute-start.5) | collective-permute-done | bytes 270368 | tf_op jit(solution)/shard_map/ppermute | solution.py:388
  33.2 0.4 collective-permute-done.6.refs_5_
  33.6 1.5 %attend_last.1.a_ref = bf16[512,256]{1,0:T(8,128)(2,1)S(1)} custom-call(bf16[512,256]{1,0:T(8,128)(2,1)S(1)} %project_query.1.refs_0_, s32[1,512]{1,0:T(1,128)S(1)} %bitcast.9, bf16[528,256]{1,0:T(8,128)(2,1)S(1)} %collective-permute-done.1.refs_2_, bf16[528,256]{1,0:T(8,128)(2,1)S(1)} %collective-permute-done.4.refs_3_, ...), custom_call_target="tpu_custom_call" | custom-call | flops 536870912 | bytes 1048576 | tf_op jit(solution)/shard_map/attend_last/pallas_call | solution.py:243
  35.1 0.4 %collective-permute-start.9 = (bf16[512,256]{1,0:T(8,128)(2,1)S(1)}, bf16[512,256]{1,0:T(8,128)(2,1)S(1)}, u32[]{:S(2)}, u32[]{:S(2)}) collective-permute-start(bf16[512,256]{1,0:T(8,128)(2,1)S(1)} %attend_last.1.a_ref), channel_id=1, source_target_pairs={{0,1},{1,0},{2,3},{3,2},{4,5},{5,4},{6,7},{7,6},{8,9},{9,8},{10,11... | collective-permute-start | bytes 786440 | tf_op jit(solution)/shard_map/ppermute | solution.py:388
  35.5 2.0 %project_own.1.quant_ref = bf16[512,4096]{1,0:T(8,128)(2,1)S(1)} custom-call(bf16[512,256]{1,0:T(8,128)(2,1)S(1)} %attend_last.1.a_ref, bf16[256,4096]{1,0:T(8,128)(2,1)S(1)} %copy-done, bf16[512,4096]{1,0:T(8,128)(2,1)S(1)} %get-tuple-element.32.sum_ref), custom_call_target="tpu_custom_call" | custom-call | flops 1073741824 | bytes 10485760 | tf_op jit(solution)/shard_map/project_own/pallas_call | solution.py:321
  37.5 4.8 %project_out.1 = bf16[512,4096]{1,0:T(8,128)(2,1)} custom-call(bf16[512,256]{1,0:T(8,128)(2,1)S(1)} %collective-permute-done.9.b_ref, bf16[256,4096]{1,0:T(8,128)(2,1)S(1)} %collective-permute-done.10.wb_ref, bf16[512,4096]{1,0:T(8,128)(2,1)S(1)} %project_own.1.quant_ref, f32[512,4096]{1,0:T(8,128)S(1)} %get-tuple-element.34.x_ref, ...), custom_call_target="tpu_custom_call" | custom-call | flops 1073741824 | bytes 10485760 | tf_op jit(solution)/shard_map/project_out/pallas_call | solution.py:370
  (15 shorter events, 0.1 us)
Async XLA Ops:
  0.0 37.5 %collective-permute-start.10 = (bf16[256,4096]{1,0:T(8,128)(2,1)}, bf16[256,4096]{1,0:T(8,128)(2,1)S(1)}, u32[]{:S(2)}, u32[]{:S(2)}) collective-permute-start(bf16[256,4096]{1,0:T(8,128)(2,1)} %w_ref.3), channel_id=1, source_target_pairs={{0,1},{1,0},{2,3},{3,2},{4,5},{5,4},{6,7},{7,6},{8,9},{9,8},{10,11... | collective-permute-start | bytes 6291464 | tf_op jit(solution)/shard_map/ppermute | solution.py:388
  7.3 13.4 %copy-start.1 = (s32[512,32]{0,1:T(8,128)S(1)}, s32[512,32]{0,1:T(8,128)}, u32[]{:S(2)}) copy-start(s32[512,32]{0,1:T(8,128)} %param.14) | copy-start | bytes 196612
  7.4 13.4 %copy-start.2 = (s32[512,32]{0,1:T(8,128)S(1)}, s32[512,32]{0,1:T(8,128)}, u32[]{:S(2)}) copy-start(s32[512,32]{0,1:T(8,128)} %param.15) | copy-start | bytes 196612
  7.4 8.2 %collective-permute-start = (bf16[528,256]{1,0:T(8,128)(2,1)S(1)}, bf16[528,256]{1,0:T(8,128)(2,1)S(1)}, u32[]{:S(2)}, u32[]{:S(2)}) collective-permute-start(bf16[528,256]{1,0:T(8,128)(2,1)S(1)} %get-tuple-element.22.refs_2_), channel_id=1, source_target_pairs={{0,4},{1,5},{2,6},{3,7},{4,8},{5,9},{6,10},{7,11},{8,12},{9,13},{1... | collective-permute-start | bytes 811016 | tf_op jit(solution)/shard_map/ppermute | solution.py:397
  8.7 10.7 %collective-permute-start.2 = (bf16[528,256]{1,0:T(8,128)(2,1)S(1)}, bf16[528,256]{1,0:T(8,128)(2,1)S(1)}, u32[]{:S(2)}, u32[]{:S(2)}) collective-permute-start(bf16[528,256]{1,0:T(8,128)(2,1)S(1)} %get-tuple-element.22.refs_2_), channel_id=1, source_target_pairs={{0,1},{1,0},{2,3},{3,2},{4,5},{5,4},{6,7},{7,6},{8,9},{9,8},{10,11... | collective-permute-start | bytes 811016 | tf_op jit(solution)/shard_map/ppermute | solution.py:388
  10.3 13.6 %copy-start.3 = (s32[512]{0:T(512)S(1)}, s32[512]{0:T(512)}, u32[]{:S(2)}) copy-start(s32[512]{0:T(512)} %param.10) | copy-start | bytes 6148
  15.5 10.3 %collective-permute-start.7 = (bf16[528,256]{1,0:T(8,128)(2,1)S(1)}, bf16[528,256]{1,0:T(8,128)(2,1)S(1)}, u32[]{:S(2)}, u32[]{:S(2)}) collective-permute-start(bf16[528,256]{1,0:T(8,128)(2,1)S(1)} %collective-permute-done.refs_3_), channel_id=1, source_target_pairs={{0,1},{1,0},{2,3},{3,2},{4,6},{5,7},{6,8},{7,9},{8,10},{9,11},{10,... | collective-permute-start | bytes 811016 | tf_op jit(solution)/shard_map/ppermute | solution.py:397
  16.8 10.8 %collective-permute-start.4 = (bf16[528,256]{1,0:T(8,128)(2,1)S(1)}, bf16[528,256]{1,0:T(8,128)(2,1)S(1)}, u32[]{:S(2)}, u32[]{:S(2)}) collective-permute-start(bf16[528,256]{1,0:T(8,128)(2,1)S(1)} %collective-permute-done.refs_3_), channel_id=1, source_target_pairs={{0,1},{1,0},{2,3},{3,2},{4,8},{5,9},{6,10},{7,11},{8,12},{9,13},{1... | collective-permute-start | bytes 811016 | tf_op jit(solution)/shard_map/ppermute | solution.py:397
  18.1 5.8 %collective-permute-start.3 = (bf16[528,256]{1,0:T(8,128)(2,1)S(1)}, bf16[528,256]{1,0:T(8,128)(2,1)S(1)}, u32[]{:S(2)}, u32[]{:S(2)}) collective-permute-start(bf16[528,256]{1,0:T(8,128)(2,1)S(1)} %collective-permute-done.refs_3_), channel_id=1, source_target_pairs={{0,1},{1,0},{2,3},{3,2},{4,5},{5,4},{6,7},{7,6},{8,9},{9,8},{10,11... | collective-permute-start | bytes 811016 | tf_op jit(solution)/shard_map/ppermute | solution.py:388
  19.5 12.1 %collective-permute-start.1 = (bf16[528,256]{1,0:T(8,128)(2,1)S(1)}, bf16[528,256]{1,0:T(8,128)(2,1)S(1)}, u32[]{:S(2)}, u32[]{:S(2)}) collective-permute-start(bf16[528,256]{1,0:T(8,128)(2,1)S(1)} %broadcast_select_fusion), channel_id=1, source_target_pairs={{0,2},{2,0},{4,6},{6,4},{8,10},{10,8},{12,14},{14,12},{1,3},{3,1},... | collective-permute-start | bytes 811016 | tf_op jit(solution)/shard_map/ppermute | solution.py:404
  23.8 11.7 %copy-start = (bf16[256,4096]{1,0:T(8,128)(2,1)S(1)}, bf16[256,4096]{1,0:T(8,128)(2,1)}, u32[]{:S(2)}) copy-start(bf16[256,4096]{1,0:T(8,128)(2,1)} %w_ref.3) | copy-start | bytes 6291460
  25.9 6.2 %collective-permute-start.8 = (bf16[528,256]{1,0:T(8,128)(2,1)S(1)}, bf16[528,256]{1,0:T(8,128)(2,1)S(1)}, u32[]{:S(2)}, u32[]{:S(2)}) collective-permute-start(bf16[528,256]{1,0:T(8,128)(2,1)S(1)} %collective-permute-done.7.refs_2_), channel_id=1, source_target_pairs={{0,1},{1,0},{2,3},{3,2},{4,5},{5,4},{6,7},{7,6},{8,9},{9,8},{10,11... | collective-permute-start | bytes 811016 | tf_op jit(solution)/shard_map/ppermute | solution.py:388
  31.6 1.6 %collective-permute-start.5 = (bf16[528,256]{1,0:T(8,128)(2,1)S(1)}, bf16[528,256]{1,0:T(8,128)(2,1)S(1)}, u32[]{:S(2)}, u32[]{:S(2)}) collective-permute-start(bf16[528,256]{1,0:T(8,128)(2,1)S(1)} %collective-permute-done.1.refs_2_), channel_id=1, source_target_pairs={{0,1},{1,0},{2,3},{3,2},{4,5},{5,4},{6,7},{7,6},{8,9},{9,8},{10,11... | collective-permute-start | bytes 811016 | tf_op jit(solution)/shard_map/ppermute | solution.py:388
  32.0 1.6 %collective-permute-start.6 = (bf16[528,256]{1,0:T(8,128)(2,1)S(1)}, bf16[528,256]{1,0:T(8,128)(2,1)S(1)}, u32[]{:S(2)}, u32[]{:S(2)}) collective-permute-start(bf16[528,256]{1,0:T(8,128)(2,1)S(1)} %collective-permute-done.4.refs_3_), channel_id=1, source_target_pairs={{0,1},{1,0},{2,3},{3,2},{4,5},{5,4},{6,7},{7,6},{8,9},{9,8},{10,11... | collective-permute-start | bytes 811016 | tf_op jit(solution)/shard_map/ppermute | solution.py:388
  35.1 2.4 %collective-permute-start.9 = (bf16[512,256]{1,0:T(8,128)(2,1)S(1)}, bf16[512,256]{1,0:T(8,128)(2,1)S(1)}, u32[]{:S(2)}, u32[]{:S(2)}) collective-permute-start(bf16[512,256]{1,0:T(8,128)(2,1)S(1)} %attend_last.1.a_ref), channel_id=1, source_target_pairs={{0,1},{1,0},{2,3},{3,2},{4,5},{5,4},{6,7},{7,6},{8,9},{9,8},{10,11... | collective-permute-start | bytes 786440 | tf_op jit(solution)/shard_map/ppermute | solution.py:388

commit v13 on v9

--- a/solution.py
+++ b/solution.py
@@ -20,53 +20,57 @@
 
 def norm_kv_kernel(x_ref, gain_hbm, w_ref, seg_hbm, msg_ref, normed_ref, xs, ws, gain_ref, seg_ref, sems):
     rows, width = xs.shape
-    tile, part = rows // 2, rows // 8
-    pieces = 4
-    deep = width // pieces
-
-    def tokens_copy(i):
-        return pltpu.make_async_copy(x_ref.at[pl.ds(i * part, part)], xs.at[pl.ds(i * part, part)], sems.at[i])
-
-    def weights_copy(i):
-        return pltpu.make_async_copy(w_ref.at[pl.ds(i * deep, deep)], ws.at[pl.ds(i * deep, deep)], sems.at[8 + i])
+    steps = 2
+    tile, part = rows // steps, rows // 4
+
+    def tokens_copy(step):
+        span = pl.ds(pl.multiple_of(step * tile, tile), tile)
+        return pltpu.make_async_copy(x_ref.at[span], xs.at[span], sems.at[step])
+
+    def weights_copy():
+        return pltpu.make_async_copy(w_ref, ws, sems.at[2])
 
     def gain_copy():
-        return pltpu.make_async_copy(gain_hbm, gain_ref, sems.at[12])
+        return pltpu.make_async_copy(gain_hbm, gain_ref, sems.at[3])
 
     def segments_copy():
-        return pltpu.make_async_copy(seg_hbm, seg_ref, sems.at[13])
-
-    for i in range(4):
-        tokens_copy(i).start()
+        return pltpu.make_async_copy(seg_hbm, seg_ref, sems.at[4])
+
+    tokens_copy(0).start()
     gain_copy().start()
-    for i in range(pieces):
-        weights_copy(i).start()
-    for i in range(4, 8):
-        tokens_copy(i).start()
+    weights_copy().start()
+    tokens_copy(1).start()
     segments_copy().start()
 
     def wide(first, count, start):
-        return xs[first:first + count, start:start + LANES].astype(jnp.float32)
-
-    for first in range(0, rows, tile):
-        for at in range(first, first + tile, part):
-            tokens_copy(at // part).wait()
-        total = wide(first, tile, 0)
+        return xs[pl.ds(pl.multiple_of(first, part), count), start:start + LANES].astype(jnp.float32)
+
+    def stats(first):
+        total = wide(first, part, 0)
         for start in range(LANES, width, LANES):
-            total = total + wide(first, tile, start)
-        mean = jnp.broadcast_to(jnp.sum(total, axis=1, keepdims=True) * (1.0 / width), (tile, LANES))
-        square = jnp.zeros((tile, LANES), jnp.float32)
+            total = total + wide(first, part, start)
+        mean = jnp.broadcast_to(jnp.sum(total, axis=1, keepdims=True) * (1.0 / width), (part, LANES))
+        square = jnp.zeros((part, LANES), jnp.float32)
         for start in range(0, width, LANES):
-            center = wide(first, tile, start) - mean
+            center = wide(first, part, start) - mean
             square = square + center * center
         spread = jnp.sum(square, axis=1, keepdims=True) * (1.0 / width)
-        scale = jnp.broadcast_to(lax.rsqrt(spread + 1e-05), (tile, LANES))
-        if first == 0:
+        return mean, jnp.broadcast_to(lax.rsqrt(spread + 1e-05), (part, LANES))
+
+    def body(step, carry):
+        first = step * tile
+        tokens_copy(step).wait()
+        halves = [stats(first + at) for at in range(0, tile, part)]
+        mean = jnp.concatenate([h[0] for h in halves], axis=0)
+        scale = jnp.concatenate([h[1] for h in halves], axis=0)
+
+        @pl.when(step == 0)
+        def _():
             gain_copy().wait()
-            for i in range(pieces):
-                weights_copy(i).wait()
+            weights_copy().wait()
+
         kv = jnp.zeros((tile, ws.shape[1]), jnp.float32)
-        span = slice(first, first + tile)
+        span = pl.ds(pl.multiple_of(first, tile), tile)
         for start in range(0, width, HD):
             for at in (start, start + LANES):
                 normed = (wide(first, tile, at) - mean) * scale * gain_ref[:, at:at + LANES]
@@ -75,6 +79,9 @@
                 normed_ref[span, start:start + HD], ws[start:start + HD, :], preferred_element_type=jnp.float32
             )
         msg_ref[span, :] = kv.astype(jnp.bfloat16)
+        return carry
+
+    lax.fori_loop(0, steps, body, 0)
     segments_copy().wait()
     seg = seg_ref[...].astype(jnp.float32)
     low = jnp.broadcast_to(seg[:, :HD], (8, HD))
@@ -104,7 +111,7 @@
             pltpu.VMEM((width, cols), jnp.bfloat16),
             pltpu.VMEM((1, width), jnp.float32),
             pltpu.VMEM((1, rows), jnp.int32),
-            pltpu.SemaphoreType.DMA((14,)),
+            pltpu.SemaphoreType.DMA((5,)),
         ],
         compiler_params=pltpu.CompilerParams(vmem_limit_bytes=24 * MIB),
         cost_estimate=pl.CostEstimate(
@@ -145,7 +152,7 @@
         state_ref, refs = refs[0], refs[1:]
     out_ref, scores = refs
     rows = q_ref.shape[0]
-    tile = rows // 2
+    tile = rows
     part = lax.axis_index("tp")
     place = lax.axis_index("seq")
 
@@ -229,7 +236,7 @@
         in_specs=[vmem] * len(operands),
         out_specs=vmem,
         out_shape=pltpu.VMEM((rows, HD), jnp.bfloat16) if last else pltpu.VMEM((rows, HD + 2 * LANES), jnp.float32),
-        scratch_shapes=[pltpu.VMEM((blocks, rows // 2, rows), jnp.float32)],
+        scratch_shapes=[pltpu.VMEM((blocks, rows, rows), jnp.float32)],
         input_output_aliases={} if first or last else {len(operands) - 1: 0},
         compiler_params=pltpu.CompilerParams(vmem_limit_bytes=12 * MIB),
         cost_estimate=pl.CostEstimate(

time: 41.3 us -> 41.2 us (level)
  transfers between devices with their start and end apart: 11 -> 11, of which waited for: 4 -> 4; matrix products, arithmetic and copies ran while one was open for 0% -> 0% of each run, Pallas kernels for 37% -> 36%
where the time goes in v13:
time: 41.2 us; the launch traced here: 41 us
  Pallas kernels  19.4 us (47%)
  starting transfers between devices  11 us (27%)
  waiting for transfers between devices  10.2 us (25%)
    pallas_call x1, Pallas kernels, norm_kv(): pl.pallas_call(norm_kv_kernel, in_specs=[hbm] * 4, out_specs=[vmem, vmem]...  6.09 us
    ppermute x7, starting transfers between devices, swap_cores(): return lax.ppermute(x, 'tp', [(0, 1), (1, 0)])  5.81 us
    ppermute x3, waiting for transfers between devices, shift(): return lax.ppermute(x, ('seq', 'tp'), pairs)  4.91 us
    pallas_call x1, Pallas kernels, project_out(): pl.pallas_call(output_kernel, in_specs=[vmem] * len(operands), out_specs=...  4.6 us
    ppermute x3, starting transfers between devices, shift(): return lax.ppermute(x, ('seq', 'tp'), pairs)  3.88 us
    ppermute x1, waiting for transfers between devices, on_device(): lax.ppermute(jnp.where(odd, held, message), 'seq', [(i, i ^ 1) for i in r...  3.83 us
    pallas_call x1, Pallas kernels, spread_bounds(): pl.pallas_call(bounds_kernel, in_specs=[vmem, vmem, pl.BlockSpec(memory_s...  3.05 us
    pallas_call x3, Pallas kernels, attend(): pl.pallas_call(functools.partial(attend_kernel, plan, first, last), in_sp...  2.58 us
  transfers between devices with their start and end apart: 11, of which 4 were waited for; matrix products, arithmetic and copies ran while one was open for 0% of the time, Pallas kernels for 36%

profile of v13, /device:TPU:11, one launch (start us, length us, event | category | flops | bytes accessed | tf_op | source)
XLA Modules:
  0.0 41.0 jit_solution(9105110528391664981)
XLA Ops:
  0.0 0.7 %collective-permute-start.10 = (bf16[256,4096]{1,0:T(8,128)(2,1)}, bf16[256,4096]{1,0:T(8,128)(2,1)S(1)}, u32[]{:S(2)}, u32[]{:S(2)}) collective-permute-start(bf16[256,4096]{1,0:T(8,128)(2,1)} %w_ref.5), channel_id=1, source_target_pairs={{0,1},{1,0},{2,3},{3,2},{4,5},{5,4},{6,7},{7,6},{8,9},{9,8},{10,11... | collective-permute-start | bytes 6291464 | tf_op jit(solution)/shard_map/ppermute | solution.py:379
  0.7 6.1 %norm_kv.1 = (bf16[528,256]{1,0:T(8,128)(2,1)S(1)}, bf16[512,4096]{1,0:T(8,128)(2,1)S(1)}) custom-call(bf16[512,4096]{1,0:T(8,128)(2,1)} %x_ref.3, f32[1,4096]{1,0:T(1,128)} %bitcast.10, bf16[4096,256]{1,0:T(8,128)(2,1)} %w_ref.3, s32[1,512]{1,0:T(1,128)} %bitcast.6), custom_call_target="tpu_custom_call" | custom-call | flops 1073741824 | bytes 10485760 | tf_op jit(solution)/shard_map/norm_kv/pallas_call | solution.py:104
  6.8 0.0 copy-start.3
  6.8 1.3 %collective-permute-start = (bf16[528,256]{1,0:T(8,128)(2,1)S(1)}, bf16[528,256]{1,0:T(8,128)(2,1)S(1)}, u32[]{:S(2)}, u32[]{:S(2)}) collective-permute-start(bf16[528,256]{1,0:T(8,128)(2,1)S(1)} %get-tuple-element.21.refs_2_), channel_id=1, source_target_pairs={{0,4},{1,5},{2,6},{3,7},{4,8},{5,9},{6,10},{7,11},{8,12},{9,13},{1... | collective-permute-start | bytes 811016 | tf_op jit(solution)/shard_map/ppermute | solution.py:388
  8.2 0.4 %collective-permute-start.2 = (bf16[528,256]{1,0:T(8,128)(2,1)S(1)}, bf16[528,256]{1,0:T(8,128)(2,1)S(1)}, u32[]{:S(2)}, u32[]{:S(2)}) collective-permute-start(bf16[528,256]{1,0:T(8,128)(2,1)S(1)} %get-tuple-element.21.refs_2_), channel_id=1, source_target_pairs={{0,1},{1,0},{2,3},{3,2},{4,5},{5,4},{6,7},{7,6},{8,9},{9,8},{10,11... | collective-permute-start | bytes 811016 | tf_op jit(solution)/shard_map/ppermute | solution.py:379
  8.6 1.2 %project_query.1.refs_0_ = bf16[512,256]{1,0:T(8,128)(2,1)S(1)} custom-call(bf16[512,4096]{1,0:T(8,128)(2,1)S(1)} %get-tuple-element.22.x_ref, bf16[4096,256]{1,0:T(8,128)(2,1)S(1)} %copy-done), custom_call_target="tpu_custom_call" | custom-call | flops 1073741824 | bytes 6291456 | tf_op jit(solution)/shard_map/project_query/pallas_call | solution.py:132
  9.9 4.9 %collective-permute-done.refs_3_ = bf16[528,256]{1,0:T(8,128)(2,1)S(1)} collective-permute-done((bf16[528,256]{1,0:T(8,128)(2,1)S(1)}, bf16[528,256]{1,0:T(8,128)(2,1)S(1)}, u32[]{:S(2)}, u32[]{:S(2)}) %collective-permute-start) | collective-permute-done | bytes 270368 | tf_op jit(solution)/shard_map/ppermute | solution.py:388
  14.8 1.2 %collective-permute-start.7 = (bf16[528,256]{1,0:T(8,128)(2,1)S(1)}, bf16[528,256]{1,0:T(8,128)(2,1)S(1)}, u32[]{:S(2)}, u32[]{:S(2)}) collective-permute-start(bf16[528,256]{1,0:T(8,128)(2,1)S(1)} %collective-permute-done.refs_3_), channel_id=1, source_target_pairs={{0,1},{1,0},{2,3},{3,2},{4,6},{5,7},{6,8},{7,9},{8,10},{9,11},{10,... | collective-permute-start | bytes 811016 | tf_op jit(solution)/shard_map/ppermute | solution.py:388
  16.0 1.3 %collective-permute-start.4 = (bf16[528,256]{1,0:T(8,128)(2,1)S(1)}, bf16[528,256]{1,0:T(8,128)(2,1)S(1)}, u32[]{:S(2)}, u32[]{:S(2)}) collective-permute-start(bf16[528,256]{1,0:T(8,128)(2,1)S(1)} %collective-permute-done.refs_3_), channel_id=1, source_target_pairs={{0,1},{1,0},{2,3},{3,2},{4,8},{5,9},{6,10},{7,11},{8,12},{9,13},{1... | collective-permute-start | bytes 811016 | tf_op jit(solution)/shard_map/ppermute | solution.py:388
  17.3 1.5 %collective-permute-start.3 = (bf16[528,256]{1,0:T(8,128)(2,1)S(1)}, bf16[528,256]{1,0:T(8,128)(2,1)S(1)}, u32[]{:S(2)}, u32[]{:S(2)}) collective-permute-start(bf16[528,256]{1,0:T(8,128)(2,1)S(1)} %collective-permute-done.refs_3_), channel_id=1, source_target_pairs={{0,1},{1,0},{2,3},{3,2},{4,5},{5,4},{6,7},{7,6},{8,9},{9,8},{10,11... | collective-permute-start | bytes 811016 | tf_op jit(solution)/shard_map/ppermute | solution.py:379
  18.9 1.3 %collective-permute-start.1 = (bf16[528,256]{1,0:T(8,128)(2,1)S(1)}, bf16[528,256]{1,0:T(8,128)(2,1)S(1)}, u32[]{:S(2)}, u32[]{:S(2)}) collective-permute-start(bf16[528,256]{1,0:T(8,128)(2,1)S(1)} %broadcast_select_fusion), channel_id=1, source_target_pairs={{0,2},{2,0},{4,6},{6,4},{8,10},{10,8},{12,14},{14,12},{1,3},{3,1},... | collective-permute-start | bytes 811016 | tf_op jit(solution)/shard_map/ppermute | solution.py:395
  20.2 3.0 %spread_bounds.1 = (bf16[512,4096]{1,0:T(8,128)(2,1)S(1)}, bf16[512,4096]{1,0:T(8,128)(2,1)S(1)}, f32[512,4096]{1,0:T(8,128)S(1)}) custom-call(s32[32,512]{1,0:T(8,128)S(1)} %bitcast.4, s32[32,512]{1,0:T(8,128)S(1)} %bitcast.5, bf16[512,4096]{1,0:T(8,128)(2,1)} %x_ref.3), custom_call_target="tpu_custom_call" | custom-call | flops 16777216 | bytes 131072 | tf_op jit(solution)/shard_map/spread_bounds/pallas_call | solution.py:274
  23.3 0.0 copy-start.1
  23.3 1.5 %attend_first.1.refs_4_ = f32[512,512]{1,0:T(8,128)S(1)} custom-call(bf16[512,256]{1,0:T(8,128)(2,1)S(1)} %project_query.1.refs_0_, s32[1,512]{1,0:T(1,128)S(1)} %bitcast.7, bf16[528,256]{1,0:T(8,128)(2,1)S(1)} %get-tuple-element.21.refs_2_, bf16[528,256]{1,0:T(8,128)(2,1)S(1)} %collective-permute-done.refs_3_, ...), custom_call_target="tpu_custom_call" | custom-call | flops 536870912 | bytes 1048576 | tf_op jit(solution)/shard_map/attend_first/pallas_call | solution.py:234
  24.8 2.2 %collective-permute-start.8 = (bf16[528,256]{1,0:T(8,128)(2,1)S(1)}, bf16[528,256]{1,0:T(8,128)(2,1)S(1)}, u32[]{:S(2)}, u32[]{:S(2)}) collective-permute-start(bf16[528,256]{1,0:T(8,128)(2,1)S(1)} %collective-permute-done.7.refs_2_), channel_id=1, source_target_pairs={{0,1},{1,0},{2,3},{3,2},{4,5},{5,4},{6,7},{7,6},{8,9},{9,8},{10,11... | collective-permute-start | bytes 811016 | tf_op jit(solution)/shard_map/ppermute | solution.py:379
  27.0 3.8 %collective-permute-done.1.refs_2_ = bf16[528,256]{1,0:T(8,128)(2,1)S(1)} collective-permute-done((bf16[528,256]{1,0:T(8,128)(2,1)S(1)}, bf16[528,256]{1,0:T(8,128)(2,1)S(1)}, u32[]{:S(2)}, u32[]{:S(2)}) %collective-permute-start.1) | collective-permute-done | bytes 270368 | tf_op jit(solution)/shard_map/ppermute | solution.py:395
  30.8 0.4 %collective-permute-start.5 = (bf16[528,256]{1,0:T(8,128)(2,1)S(1)}, bf16[528,256]{1,0:T(8,128)(2,1)S(1)}, u32[]{:S(2)}, u32[]{:S(2)}) collective-permute-start(bf16[528,256]{1,0:T(8,128)(2,1)S(1)} %collective-permute-done.1.refs_2_), channel_id=1, source_target_pairs={{0,1},{1,0},{2,3},{3,2},{4,5},{5,4},{6,7},{7,6},{8,9},{9,8},{10,11... | collective-permute-start | bytes 811016 | tf_op jit(solution)/shard_map/ppermute | solution.py:379
  31.3 0.1 collective-permute-start.6
  31.4 1.1 %collective-permute-done.5.refs_4_ = bf16[528,256]{1,0:T(8,128)(2,1)S(1)} collective-permute-done((bf16[528,256]{1,0:T(8,128)(2,1)S(1)}, bf16[528,256]{1,0:T(8,128)(2,1)S(1)}, u32[]{:S(2)}, u32[]{:S(2)}) %collective-permute-start.5) | collective-permute-done | bytes 270368 | tf_op jit(solution)/shard_map/ppermute | solution.py:379
  32.5 0.4 collective-permute-done.6.refs_5_
  32.8 1.1 %attend_last.1.a_ref = bf16[512,256]{1,0:T(8,128)(2,1)S(1)} custom-call(bf16[512,256]{1,0:T(8,128)(2,1)S(1)} %project_query.1.refs_0_, s32[1,512]{1,0:T(1,128)S(1)} %bitcast.9, bf16[528,256]{1,0:T(8,128)(2,1)S(1)} %collective-permute-done.1.refs_2_, bf16[528,256]{1,0:T(8,128)(2,1)S(1)} %collective-permute-done.4.refs_3_, ...), custom_call_target="tpu_custom_call" | custom-call | flops 536870912 | bytes 1048576 | tf_op jit(solution)/shard_map/attend_last/pallas_call | solution.py:234
  33.9 0.4 %collective-permute-start.9 = (bf16[512,256]{1,0:T(8,128)(2,1)S(1)}, bf16[512,256]{1,0:T(8,128)(2,1)S(1)}, u32[]{:S(2)}, u32[]{:S(2)}) collective-permute-start(bf16[512,256]{1,0:T(8,128)(2,1)S(1)} %attend_last.1.a_ref), channel_id=1, source_target_pairs={{0,1},{1,0},{2,3},{3,2},{4,5},{5,4},{6,7},{7,6},{8,9},{9,8},{10,11... | collective-permute-start | bytes 786440 | tf_op jit(solution)/shard_map/ppermute | solution.py:379
  34.4 1.9 %project_own.1.quant_ref = bf16[512,4096]{1,0:T(8,128)(2,1)S(1)} custom-call(bf16[512,256]{1,0:T(8,128)(2,1)S(1)} %attend_last.1.a_ref, bf16[256,4096]{1,0:T(8,128)(2,1)S(1)} %copy-done.1, bf16[512,4096]{1,0:T(8,128)(2,1)S(1)} %get-tuple-element.30.sum_ref), custom_call_target="tpu_custom_call" | custom-call | flops 1073741824 | bytes 10485760 | tf_op jit(solution)/shard_map/project_own/pallas_call | solution.py:312
  36.3 4.6 %project_out.1 = bf16[512,4096]{1,0:T(8,128)(2,1)} custom-call(bf16[512,256]{1,0:T(8,128)(2,1)S(1)} %collective-permute-done.9.b_ref, bf16[256,4096]{1,0:T(8,128)(2,1)S(1)} %collective-permute-done.10.wb_ref, bf16[512,4096]{1,0:T(8,128)(2,1)S(1)} %project_own.1.quant_ref, f32[512,4096]{1,0:T(8,128)S(1)} %get-tuple-element.32.x_ref, ...), custom_call_target="tpu_custom_call" | custom-call | flops 1073741824 | bytes 10485760 | tf_op jit(solution)/shard_map/project_out/pallas_call | solution.py:361
  (17 shorter events, 0.1 us)
Async XLA Ops:
  0.0 8.6 %copy-start = (bf16[4096,256]{1,0:T(8,128)(2,1)S(1)}, bf16[4096,256]{1,0:T(8,128)(2,1)}, u32[]{:S(2)}) copy-start(bf16[4096,256]{1,0:T(8,128)(2,1)} %w_ref.4) | copy-start | bytes 6291460
  0.0 36.2 %collective-permute-start.10 = (bf16[256,4096]{1,0:T(8,128)(2,1)}, bf16[256,4096]{1,0:T(8,128)(2,1)S(1)}, u32[]{:S(2)}, u32[]{:S(2)}) collective-permute-start(bf16[256,4096]{1,0:T(8,128)(2,1)} %w_ref.5), channel_id=1, source_target_pairs={{0,1},{1,0},{2,3},{3,2},{4,5},{5,4},{6,7},{7,6},{8,9},{9,8},{10,11... | collective-permute-start | bytes 6291464 | tf_op jit(solution)/shard_map/ppermute | solution.py:379
  6.8 13.4 %copy-start.2 = (s32[512,32]{0,1:T(8,128)S(1)}, s32[512,32]{0,1:T(8,128)}, u32[]{:S(2)}) copy-start(s32[512,32]{0,1:T(8,128)} %param.14) | copy-start | bytes 196612
  6.8 13.4 %copy-start.3 = (s32[512,32]{0,1:T(8,128)S(1)}, s32[512,32]{0,1:T(8,128)}, u32[]{:S(2)}) copy-start(s32[512,32]{0,1:T(8,128)} %param.15) | copy-start | bytes 196612
  6.8 8.0 %collective-permute-start = (bf16[528,256]{1,0:T(8,128)(2,1)S(1)}, bf16[528,256]{1,0:T(8,128)(2,1)S(1)}, u32[]{:S(2)}, u32[]{:S(2)}) collective-permute-start(bf16[528,256]{1,0:T(8,128)(2,1)S(1)} %get-tuple-element.21.refs_2_), channel_id=1, source_target_pairs={{0,4},{1,5},{2,6},{3,7},{4,8},{5,9},{6,10},{7,11},{8,12},{9,13},{1... | collective-permute-start | bytes 811016 | tf_op jit(solution)/shard_map/ppermute | solution.py:388
  8.2 10.7 %collective-permute-start.2 = (bf16[528,256]{1,0:T(8,128)(2,1)S(1)}, bf16[528,256]{1,0:T(8,128)(2,1)S(1)}, u32[]{:S(2)}, u32[]{:S(2)}) collective-permute-start(bf16[528,256]{1,0:T(8,128)(2,1)S(1)} %get-tuple-element.21.refs_2_), channel_id=1, source_target_pairs={{0,1},{1,0},{2,3},{3,2},{4,5},{5,4},{6,7},{7,6},{8,9},{9,8},{10,11... | collective-permute-start | bytes 811016 | tf_op jit(solution)/shard_map/ppermute | solution.py:379
  9.9 13.4 %copy-start.4 = (s32[512]{0:T(512)S(1)}, s32[512]{0:T(512)}, u32[]{:S(2)}) copy-start(s32[512]{0:T(512)} %param.10) | copy-start | bytes 6148
  14.8 10.0 %collective-permute-start.7 = (bf16[528,256]{1,0:T(8,128)(2,1)S(1)}, bf16[528,256]{1,0:T(8,128)(2,1)S(1)}, u32[]{:S(2)}, u32[]{:S(2)}) collective-permute-start(bf16[528,256]{1,0:T(8,128)(2,1)S(1)} %collective-permute-done.refs_3_), channel_id=1, source_target_pairs={{0,1},{1,0},{2,3},{3,2},{4,6},{5,7},{6,8},{7,9},{8,10},{9,11},{10,... | collective-permute-start | bytes 811016 | tf_op jit(solution)/shard_map/ppermute | solution.py:388
  16.0 11.0 %collective-permute-start.4 = (bf16[528,256]{1,0:T(8,128)(2,1)S(1)}, bf16[528,256]{1,0:T(8,128)(2,1)S(1)}, u32[]{:S(2)}, u32[]{:S(2)}) collective-permute-start(bf16[528,256]{1,0:T(8,128)(2,1)S(1)} %collective-permute-done.refs_3_), channel_id=1, source_target_pairs={{0,1},{1,0},{2,3},{3,2},{4,8},{5,9},{6,10},{7,11},{8,12},{9,13},{1... | collective-permute-start | bytes 811016 | tf_op jit(solution)/shard_map/ppermute | solution.py:388
  17.3 6.0 %collective-permute-start.3 = (bf16[528,256]{1,0:T(8,128)(2,1)S(1)}, bf16[528,256]{1,0:T(8,128)(2,1)S(1)}, u32[]{:S(2)}, u32[]{:S(2)}) collective-permute-start(bf16[528,256]{1,0:T(8,128)(2,1)S(1)} %collective-permute-done.refs_3_), channel_id=1, source_target_pairs={{0,1},{1,0},{2,3},{3,2},{4,5},{5,4},{6,7},{7,6},{8,9},{9,8},{10,11... | collective-permute-start | bytes 811016 | tf_op jit(solution)/shard_map/ppermute | solution.py:379
  18.9 11.9 %collective-permute-start.1 = (bf16[528,256]{1,0:T(8,128)(2,1)S(1)}, bf16[528,256]{1,0:T(8,128)(2,1)S(1)}, u32[]{:S(2)}, u32[]{:S(2)}) collective-permute-start(bf16[528,256]{1,0:T(8,128)(2,1)S(1)} %broadcast_select_fusion), channel_id=1, source_target_pairs={{0,2},{2,0},{4,6},{6,4},{8,10},{10,8},{12,14},{14,12},{1,3},{3,1},... | collective-permute-start | bytes 811016 | tf_op jit(solution)/shard_map/ppermute | solution.py:395
  23.3 11.1 %copy-start.1 = (bf16[256,4096]{1,0:T(8,128)(2,1)S(1)}, bf16[256,4096]{1,0:T(8,128)(2,1)}, u32[]{:S(2)}) copy-start(bf16[256,4096]{1,0:T(8,128)(2,1)} %w_ref.5) | copy-start | bytes 6291460
  24.8 6.5 %collective-permute-start.8 = (bf16[528,256]{1,0:T(8,128)(2,1)S(1)}, bf16[528,256]{1,0:T(8,128)(2,1)S(1)}, u32[]{:S(2)}, u32[]{:S(2)}) collective-permute-start(bf16[528,256]{1,0:T(8,128)(2,1)S(1)} %collective-permute-done.7.refs_2_), channel_id=1, source_target_pairs={{0,1},{1,0},{2,3},{3,2},{4,5},{5,4},{6,7},{7,6},{8,9},{9,8},{10,11... | collective-permute-start | bytes 811016 | tf_op jit(solution)/shard_map/ppermute | solution.py:379
  30.8 1.6 %collective-permute-start.5 = (bf16[528,256]{1,0:T(8,128)(2,1)S(1)}, bf16[528,256]{1,0:T(8,128)(2,1)S(1)}, u32[]{:S(2)}, u32[]{:S(2)}) collective-permute-start(bf16[528,256]{1,0:T(8,128)(2,1)S(1)} %collective-permute-done.1.refs_2_), channel_id=1, source_target_pairs={{0,1},{1,0},{2,3},{3,2},{4,5},{5,4},{6,7},{7,6},{8,9},{9,8},{10,11... | collective-permute-start | bytes 811016 | tf_op jit(solution)/shard_map/ppermute | solution.py:379
  31.3 1.6 %collective-permute-start.6 = (bf16[528,256]{1,0:T(8,128)(2,1)S(1)}, bf16[528,256]{1,0:T(8,128)(2,1)S(1)}, u32[]{:S(2)}, u32[]{:S(2)}) collective-permute-start(bf16[528,256]{1,0:T(8,128)(2,1)S(1)} %collective-permute-done.4.refs_3_), channel_id=1, source_target_pairs={{0,1},{1,0},{2,3},{3,2},{4,5},{5,4},{6,7},{7,6},{8,9},{9,8},{10,11... | collective-permute-start | bytes 811016 | tf_op jit(solution)/shard_map/ppermute | solution.py:379
  33.9 2.3 %collective-permute-start.9 = (bf16[512,256]{1,0:T(8,128)(2,1)S(1)}, bf16[512,256]{1,0:T(8,128)(2,1)S(1)}, u32[]{:S(2)}, u32[]{:S(2)}) collective-permute-start(bf16[512,256]{1,0:T(8,128)(2,1)S(1)} %attend_last.1.a_ref), channel_id=1, source_target_pairs={{0,1},{1,0},{2,3},{3,2},{4,5},{5,4},{6,7},{7,6},{8,9},{9,8},{10,11... | collective-permute-start | bytes 786440 | tf_op jit(solution)/shard_map/ppermute | solution.py:379

commit v14 on v13

--- a/solution.py
+++ b/solution.py
@@ -20,30 +20,37 @@
 
 def norm_kv_kernel(x_ref, gain_hbm, w_ref, seg_hbm, msg_ref, normed_ref, xs, ws, gain_ref, seg_ref, sems):
     rows, width = xs.shape
-    steps = 2
-    tile, part = rows // steps, rows // 4
-
-    def tokens_copy(step):
-        span = pl.ds(pl.multiple_of(step * tile, tile), tile)
-        return pltpu.make_async_copy(x_ref.at[span], xs.at[span], sems.at[step])
-
-    def weights_copy():
-        return pltpu.make_async_copy(w_ref, ws, sems.at[2])
+    tile, part = rows // 2, rows // 4
+
+    def cut(source, target, first, count, pieces, sem):
+        size = count // pieces
+        return [
+            pltpu.make_async_copy(
+                source.at[pl.ds(first + i * size, size)], target.at[pl.ds(first + i * size, size)], sems.at[sem + i]
+            )
+            for i in range(pieces)
+        ]
+
+    def early_tokens(half):
+        return cut(x_ref, xs, half * part, part, 4, 4 * half)
+
+    def late_tokens():
+        return cut(x_ref, xs, tile, tile, 2, 8)
+
+    def weights():
+        return cut(w_ref, ws, 0, width, 4, 10)
 
     def gain_copy():
-        return pltpu.make_async_copy(gain_hbm, gain_ref, sems.at[3])
+        return pltpu.make_async_copy(gain_hbm, gain_ref, sems.at[14])
 
     def segments_copy():
-        return pltpu.make_async_copy(seg_hbm, seg_ref, sems.at[4])
-
-    tokens_copy(0).start()
-    gain_copy().start()
-    weights_copy().start()
-    tokens_copy(1).start()
-    segments_copy().start()
+        return pltpu.make_async_copy(seg_hbm, seg_ref, sems.at[15])
+
+    for copy in early_tokens(0) + early_tokens(1) + [gain_copy()] + weights() + late_tokens() + [segments_copy()]:
+        copy.start()
 
     def wide(first, count, start):
-        return xs[pl.ds(pl.multiple_of(first, part), count), start:start + LANES].astype(jnp.float32)
+        return xs[first:first + count, start:start + LANES].astype(jnp.float32)
 
     def stats(first):
         total = wide(first, part, 0)
@@ -57,20 +64,11 @@
         spread = jnp.sum(square, axis=1, keepdims=True) * (1.0 / width)
         return mean, jnp.broadcast_to(lax.rsqrt(spread + 1e-05), (part, LANES))
 
-    def body(step, carry):
-        first = step * tile
-        tokens_copy(step).wait()
-        halves = [stats(first + at) for at in range(0, tile, part)]
+    def project(first, halves):
         mean = jnp.concatenate([h[0] for h in halves], axis=0)
         scale = jnp.concatenate([h[1] for h in halves], axis=0)
-
-        @pl.when(step == 0)
-        def _():
-            gain_copy().wait()
-            weights_copy().wait()
-
         kv = jnp.zeros((tile, ws.shape[1]), jnp.float32)
-        span = pl.ds(pl.multiple_of(first, tile), tile)
+        span = slice(first, first + tile)
         for start in range(0, width, HD):
             for at in (start, start + LANES):
                 normed = (wide(first, tile, at) - mean) * scale * gain_ref[:, at:at + LANES]
@@ -79,9 +77,18 @@
                 normed_ref[span, start:start + HD], ws[start:start + HD, :], preferred_element_type=jnp.float32
             )
         msg_ref[span, :] = kv.astype(jnp.bfloat16)
-        return carry
-
-    lax.fori_loop(0, steps, body, 0)
+
+    halves = []
+    for half in range(2):
+        for copy in early_tokens(half):
+            copy.wait()
+        halves.append(stats(half * part))
+    for copy in [gain_copy()] + weights():
+        copy.wait()
+    project(0, halves)
+    for copy in late_tokens():
+        copy.wait()
+    project(tile, [stats(tile), stats(tile + part)])
     segments_copy().wait()
     seg = seg_ref[...].astype(jnp.float32)
     low = jnp.broadcast_to(seg[:, :HD], (8, HD))
@@ -111,7 +118,7 @@
             pltpu.VMEM((width, cols), jnp.bfloat16),
             pltpu.VMEM((1, width), jnp.float32),
             pltpu.VMEM((1, rows), jnp.int32),
-            pltpu.SemaphoreType.DMA((5,)),
+            pltpu.SemaphoreType.DMA((16,)),
         ],
         compiler_params=pltpu.CompilerParams(vmem_limit_bytes=24 * MIB),
         cost_estimate=pl.CostEstimate(
@@ -152,31 +159,32 @@
         state_ref, refs = refs[0], refs[1:]
     out_ref, scores = refs
     rows = q_ref.shape[0]
-    tile = rows
+    tile = rows // 2
     part = lax.axis_index("tp")
     place = lax.axis_index("seq")
 
     def finish(span, weighted, total):
         out_ref[span, :] = (weighted / jnp.sum(total, axis=1, keepdims=True)).astype(jnp.bfloat16)
 
-    def update(count, keys, values):
+    def update(slots, keys, values):
         own_seg = jnp.transpose(jnp.broadcast_to(seg_ref[...].astype(jnp.float32), (8, rows)))[:, 0:1]
-        key_segs = []
-        for slot in range(count):
+        key_segs = {}
+        for slot in slots:
             packed = mine[slot][rows:, :].astype(jnp.float32)
-            key_segs.append(jnp.concatenate([packed[0:1, :], packed[8:9, :]], axis=1))
+            key_segs[slot] = jnp.concatenate([packed[0:1, :], packed[8:9, :]], axis=1)
         for start in range(0, rows, tile):
             span = slice(start, start + tile)
             query = q_ref[span, :]
             best = None if first else state_ref[span, HD:HD + LANES]
-            bounds = []
-            for slot, (back, furthest) in enumerate(plan[:count]):
+            bounds = {}
+            for slot in slots:
+                back, furthest = plan[slot]
                 low, high = 0, rows
                 if back == 0:
                     high = start + tile
                 elif furthest:
                     low = start
-                bounds.append((low, high))
+                bounds[slot] = (low, high)
                 raw = lax.dot_general(query, keys[slot][low:high, :], NT, preferred_element_type=jnp.float32)
                 allowed = key_segs[slot][:, low:high] == own_seg[span, :]
                 if back == 0:
@@ -195,7 +203,7 @@
                 shrink = jnp.exp2((state_ref[span, HD:HD + LANES] - top) * FACTOR)
                 total = state_ref[span, HD + LANES:] * shrink
                 weighted = state_ref[span, :HD] * jnp.concatenate([shrink, shrink], axis=1)
-            for slot in range(count):
+            for slot in slots:
                 low, high = bounds[slot]
                 pieces = []
                 for at in range(low, high, LANES):
@@ -211,13 +219,14 @@
                 out_ref[span, HD:HD + LANES] = top
                 out_ref[span, HD + LANES:] = total
 
+    order = sorted(range(blocks), key=lambda slot: plan[slot][0])
     for count in range(1 if first else 0, blocks + 1):
-        reached = place >= (plan[count - 1][0] if count > 0 else 0)
+        reached = place >= (plan[order[count - 1]][0] if count > 0 else 0)
         if count < blocks:
-            reached = reached & (place < plan[count][0])
+            reached = reached & (place < plan[order[count]][0])
         if count > 0:
-            pl.when(reached & (part == 0))(functools.partial(update, count, mine, other))
-            pl.when(reached & (part == 1))(functools.partial(update, count, other, mine))
+            pl.when(reached & (part == 0))(functools.partial(update, order[:count], mine, other))
+            pl.when(reached & (part == 1))(functools.partial(update, order[:count], other, mine))
         elif last:
 
             @pl.when(reached)
@@ -236,7 +245,7 @@
         in_specs=[vmem] * len(operands),
         out_specs=vmem,
         out_shape=pltpu.VMEM((rows, HD), jnp.bfloat16) if last else pltpu.VMEM((rows, HD + 2 * LANES), jnp.float32),
-        scratch_shapes=[pltpu.VMEM((blocks, rows, rows), jnp.float32)],
+        scratch_shapes=[pltpu.VMEM((blocks, rows // 2, rows), jnp.float32)],
         input_output_aliases={} if first or last else {len(operands) - 1: 0},
         compiler_params=pltpu.CompilerParams(vmem_limit_bytes=12 * MIB),
         cost_estimate=pl.CostEstimate(
@@ -398,7 +407,7 @@
         step = shift(held, 1, back)
         held = shift(held, 2, back)
         parts.append([(back + 1, step)] + ([(back + 2, held)] if back + 2 < window else []))
-    parts.append([(1, beside), (window, held)])
+    parts.append([(window, held), (1, beside)])
     exps = lax.optimization_barrier((sum_exps, out_exps, query))[:2]
     bounds = spread_bounds(*exps, tokens)
     state = None

time: 41.2 us -> 41 us (level)
  no operation moved by 1% of the time
where the time goes in v14:
time: 41 us; the launch traced here: 40.9 us
  Pallas kernels  19.4 us (47%)
  starting transfers between devices  10.9 us (27%)
  waiting for transfers between devices  10.2 us (25%)
    pallas_call x1, Pallas kernels, norm_kv(): pl.pallas_call(norm_kv_kernel, in_specs=[hbm] * 4, out_specs=[vmem, vmem]...  5.97 us
    ppermute x7, starting transfers between devices, swap_cores(): return lax.ppermute(x, 'tp', [(0, 1), (1, 0)])  5.72 us
    ppermute x3, waiting for transfers between devices, shift(): return lax.ppermute(x, ('seq', 'tp'), pairs)  4.91 us
    pallas_call x1, Pallas kernels, project_out(): pl.pallas_call(output_kernel, in_specs=[vmem] * len(operands), out_specs=...  4.6 us
    ppermute x3, starting transfers between devices, shift(): return lax.ppermute(x, ('seq', 'tp'), pairs)  3.89 us
    ppermute x1, waiting for transfers between devices, on_device(): lax.ppermute(jnp.where(odd, held, message), 'seq', [(i, i ^ 1) for i in r...  3.83 us
    pallas_call x1, Pallas kernels, spread_bounds(): pl.pallas_call(bounds_kernel, in_specs=[vmem, vmem, pl.BlockSpec(memory_s...  3.05 us
    pallas_call x3, Pallas kernels, attend(): pl.pallas_call(functools.partial(attend_kernel, plan, first, last), in_sp...  2.67 us
  transfers between devices with their start and end apart: 11, of which 4 were waited for; matrix products, arithmetic and copies ran while one was open for 0% of the time, Pallas kernels for 36%

profile of v14, /device:TPU:11, one launch (start us, length us, event | category | flops | bytes accessed | tf_op | source)
XLA Modules:
  0.0 40.9 jit_solution(15726967149069775661)
XLA Ops:
  0.0 0.7 %collective-permute-start.10 = (bf16[256,4096]{1,0:T(8,128)(2,1)}, bf16[256,4096]{1,0:T(8,128)(2,1)S(1)}, u32[]{:S(2)}, u32[]{:S(2)}) collective-permute-start(bf16[256,4096]{1,0:T(8,128)(2,1)} %w_ref.5), channel_id=1, source_target_pairs={{0,1},{1,0},{2,3},{3,2},{4,5},{5,4},{6,7},{7,6},{8,9},{9,8},{10,11... | collective-permute-start | bytes 6291464 | tf_op jit(solution)/shard_map/ppermute | solution.py:388
  0.7 6.0 %norm_kv.1 = (bf16[528,256]{1,0:T(8,128)(2,1)S(1)}, bf16[512,4096]{1,0:T(8,128)(2,1)S(1)}) custom-call(bf16[512,4096]{1,0:T(8,128)(2,1)} %x_ref.3, f32[1,4096]{1,0:T(1,128)} %bitcast.10, bf16[4096,256]{1,0:T(8,128)(2,1)} %w_ref.3, s32[1,512]{1,0:T(1,128)} %bitcast.6), custom_call_target="tpu_custom_call" | custom-call | flops 1073741824 | bytes 10485760 | tf_op jit(solution)/shard_map/norm_kv/pallas_call | solution.py:111
  6.7 0.0 copy-start.2
  6.7 0.0 copy-start.3
  6.7 1.3 %collective-permute-start = (bf16[528,256]{1,0:T(8,128)(2,1)S(1)}, bf16[528,256]{1,0:T(8,128)(2,1)S(1)}, u32[]{:S(2)}, u32[]{:S(2)}) collective-permute-start(bf16[528,256]{1,0:T(8,128)(2,1)S(1)} %get-tuple-element.21.refs_2_), channel_id=1, source_target_pairs={{0,4},{1,5},{2,6},{3,7},{4,8},{5,9},{6,10},{7,11},{8,12},{9,13},{1... | collective-permute-start | bytes 811016 | tf_op jit(solution)/shard_map/ppermute | solution.py:397
  8.0 0.4 %collective-permute-start.2 = (bf16[528,256]{1,0:T(8,128)(2,1)S(1)}, bf16[528,256]{1,0:T(8,128)(2,1)S(1)}, u32[]{:S(2)}, u32[]{:S(2)}) collective-permute-start(bf16[528,256]{1,0:T(8,128)(2,1)S(1)} %get-tuple-element.21.refs_2_), channel_id=1, source_target_pairs={{0,1},{1,0},{2,3},{3,2},{4,5},{5,4},{6,7},{7,6},{8,9},{9,8},{10,11... | collective-permute-start | bytes 811016 | tf_op jit(solution)/shard_map/ppermute | solution.py:388
  8.5 1.2 %project_query.1.refs_0_ = bf16[512,256]{1,0:T(8,128)(2,1)S(1)} custom-call(bf16[512,4096]{1,0:T(8,128)(2,1)S(1)} %get-tuple-element.22.x_ref, bf16[4096,256]{1,0:T(8,128)(2,1)S(1)} %copy-done), custom_call_target="tpu_custom_call" | custom-call | flops 1073741824 | bytes 6291456 | tf_op jit(solution)/shard_map/project_query/pallas_call | solution.py:139
  9.7 4.9 %collective-permute-done.refs_3_ = bf16[528,256]{1,0:T(8,128)(2,1)S(1)} collective-permute-done((bf16[528,256]{1,0:T(8,128)(2,1)S(1)}, bf16[528,256]{1,0:T(8,128)(2,1)S(1)}, u32[]{:S(2)}, u32[]{:S(2)}) %collective-permute-start) | collective-permute-done | bytes 270368 | tf_op jit(solution)/shard_map/ppermute | solution.py:397
  14.7 1.2 %collective-permute-start.7 = (bf16[528,256]{1,0:T(8,128)(2,1)S(1)}, bf16[528,256]{1,0:T(8,128)(2,1)S(1)}, u32[]{:S(2)}, u32[]{:S(2)}) collective-permute-start(bf16[528,256]{1,0:T(8,128)(2,1)S(1)} %collective-permute-done.refs_3_), channel_id=1, source_target_pairs={{0,1},{1,0},{2,3},{3,2},{4,6},{5,7},{6,8},{7,9},{8,10},{9,11},{10,... | collective-permute-start | bytes 811016 | tf_op jit(solution)/shard_map/ppermute | solution.py:397
  15.9 1.3 %collective-permute-start.3 = (bf16[528,256]{1,0:T(8,128)(2,1)S(1)}, bf16[528,256]{1,0:T(8,128)(2,1)S(1)}, u32[]{:S(2)}, u32[]{:S(2)}) collective-permute-start(bf16[528,256]{1,0:T(8,128)(2,1)S(1)} %collective-permute-done.refs_3_), channel_id=1, source_target_pairs={{0,1},{1,0},{2,3},{3,2},{4,5},{5,4},{6,7},{7,6},{8,9},{9,8},{10,11... | collective-permute-start | bytes 811016 | tf_op jit(solution)/shard_map/ppermute | solution.py:388
  17.2 1.3 %collective-permute-start.4 = (bf16[528,256]{1,0:T(8,128)(2,1)S(1)}, bf16[528,256]{1,0:T(8,128)(2,1)S(1)}, u32[]{:S(2)}, u32[]{:S(2)}) collective-permute-start(bf16[528,256]{1,0:T(8,128)(2,1)S(1)} %broadcast_select_fusion), channel_id=1, source_target_pairs={{0,2},{2,0},{4,6},{6,4},{8,10},{10,8},{12,14},{14,12},{1,3},{3,1},... | collective-permute-start | bytes 811016 | tf_op jit(solution)/shard_map/ppermute | solution.py:404
  18.5 1.3 %collective-permute-start.1 = (bf16[528,256]{1,0:T(8,128)(2,1)S(1)}, bf16[528,256]{1,0:T(8,128)(2,1)S(1)}, u32[]{:S(2)}, u32[]{:S(2)}) collective-permute-start(bf16[528,256]{1,0:T(8,128)(2,1)S(1)} %collective-permute-done.refs_3_), channel_id=1, source_target_pairs={{0,1},{1,0},{2,3},{3,2},{4,8},{5,9},{6,10},{7,11},{8,12},{9,13},{1... | collective-permute-start | bytes 811016 | tf_op jit(solution)/shard_map/ppermute | solution.py:397
  19.8 3.0 %spread_bounds.1 = (bf16[512,4096]{1,0:T(8,128)(2,1)S(1)}, bf16[512,4096]{1,0:T(8,128)(2,1)S(1)}, f32[512,4096]{1,0:T(8,128)S(1)}) custom-call(s32[32,512]{1,0:T(8,128)S(1)} %bitcast.4, s32[32,512]{1,0:T(8,128)S(1)} %bitcast.5, bf16[512,4096]{1,0:T(8,128)(2,1)} %x_ref.3), custom_call_target="tpu_custom_call" | custom-call | flops 16777216 | bytes 131072 | tf_op jit(solution)/shard_map/spread_bounds/pallas_call | solution.py:283
  22.9 1.6 %attend_first.1.refs_4_ = f32[512,512]{1,0:T(8,128)S(1)} custom-call(bf16[512,256]{1,0:T(8,128)(2,1)S(1)} %project_query.1.refs_0_, s32[1,512]{1,0:T(1,128)S(1)} %bitcast.7, bf16[528,256]{1,0:T(8,128)(2,1)S(1)} %get-tuple-element.21.refs_2_, bf16[528,256]{1,0:T(8,128)(2,1)S(1)} %collective-permute-done.refs_3_, ...), custom_call_target="tpu_custom_call" | custom-call | flops 536870912 | bytes 1048576 | tf_op jit(solution)/shard_map/attend_first/pallas_call | solution.py:243
  24.5 2.4 %collective-permute-start.8 = (bf16[528,256]{1,0:T(8,128)(2,1)S(1)}, bf16[528,256]{1,0:T(8,128)(2,1)S(1)}, u32[]{:S(2)}, u32[]{:S(2)}) collective-permute-start(bf16[528,256]{1,0:T(8,128)(2,1)S(1)} %collective-permute-done.7.refs_2_), channel_id=1, source_target_pairs={{0,1},{1,0},{2,3},{3,2},{4,5},{5,4},{6,7},{7,6},{8,9},{9,8},{10,11... | collective-permute-start | bytes 811016 | tf_op jit(solution)/shard_map/ppermute | solution.py:388
  26.9 3.8 %collective-permute-done.4.refs_3_ = bf16[528,256]{1,0:T(8,128)(2,1)S(1)} collective-permute-done((bf16[528,256]{1,0:T(8,128)(2,1)S(1)}, bf16[528,256]{1,0:T(8,128)(2,1)S(1)}, u32[]{:S(2)}, u32[]{:S(2)}) %collective-permute-start.4) | collective-permute-done | bytes 270368 | tf_op jit(solution)/shard_map/ppermute | solution.py:404
  30.7 0.4 %collective-permute-start.5 = (bf16[528,256]{1,0:T(8,128)(2,1)S(1)}, bf16[528,256]{1,0:T(8,128)(2,1)S(1)}, u32[]{:S(2)}, u32[]{:S(2)}) collective-permute-start(bf16[528,256]{1,0:T(8,128)(2,1)S(1)} %collective-permute-done.1.refs_2_), channel_id=1, source_target_pairs={{0,1},{1,0},{2,3},{3,2},{4,5},{5,4},{6,7},{7,6},{8,9},{9,8},{10,11... | collective-permute-start | bytes 811016 | tf_op jit(solution)/shard_map/ppermute | solution.py:388
  31.2 0.1 collective-permute-start.6
  31.2 1.1 %collective-permute-done.5.refs_4_ = bf16[528,256]{1,0:T(8,128)(2,1)S(1)} collective-permute-done((bf16[528,256]{1,0:T(8,128)(2,1)S(1)}, bf16[528,256]{1,0:T(8,128)(2,1)S(1)}, u32[]{:S(2)}, u32[]{:S(2)}) %collective-permute-start.5) | collective-permute-done | bytes 270368 | tf_op jit(solution)/shard_map/ppermute | solution.py:388
  32.3 0.4 collective-permute-done.6.refs_5_
  32.7 1.1 %attend_last.1.a_ref = bf16[512,256]{1,0:T(8,128)(2,1)S(1)} custom-call(bf16[512,256]{1,0:T(8,128)(2,1)S(1)} %project_query.1.refs_0_, s32[1,512]{1,0:T(1,128)S(1)} %bitcast.9, bf16[528,256]{1,0:T(8,128)(2,1)S(1)} %collective-permute-done.1.refs_2_, bf16[528,256]{1,0:T(8,128)(2,1)S(1)} %collective-permute-done.4.refs_3_, ...), custom_call_target="tpu_custom_call" | custom-call | flops 536870912 | bytes 1048576 | tf_op jit(solution)/shard_map/attend_last/pallas_call | solution.py:243
  33.8 0.4 %collective-permute-start.9 = (bf16[512,256]{1,0:T(8,128)(2,1)S(1)}, bf16[512,256]{1,0:T(8,128)(2,1)S(1)}, u32[]{:S(2)}, u32[]{:S(2)}) collective-permute-start(bf16[512,256]{1,0:T(8,128)(2,1)S(1)} %attend_last.1.a_ref), channel_id=1, source_target_pairs={{0,1},{1,0},{2,3},{3,2},{4,5},{5,4},{6,7},{7,6},{8,9},{9,8},{10,11... | collective-permute-start | bytes 786440 | tf_op jit(solution)/shard_map/ppermute | solution.py:388
  34.2 1.9 %project_own.1.quant_ref = bf16[512,4096]{1,0:T(8,128)(2,1)S(1)} custom-call(bf16[512,256]{1,0:T(8,128)(2,1)S(1)} %attend_last.1.a_ref, bf16[256,4096]{1,0:T(8,128)(2,1)S(1)} %copy-done.1, bf16[512,4096]{1,0:T(8,128)(2,1)S(1)} %get-tuple-element.30.sum_ref), custom_call_target="tpu_custom_call" | custom-call | flops 1073741824 | bytes 10485760 | tf_op jit(solution)/shard_map/project_own/pallas_call | solution.py:321
  36.1 4.6 %project_out.1 = bf16[512,4096]{1,0:T(8,128)(2,1)} custom-call(bf16[512,256]{1,0:T(8,128)(2,1)S(1)} %collective-permute-done.9.b_ref, bf16[256,4096]{1,0:T(8,128)(2,1)S(1)} %collective-permute-done.10.wb_ref, bf16[512,4096]{1,0:T(8,128)(2,1)S(1)} %project_own.1.quant_ref, f32[512,4096]{1,0:T(8,128)S(1)} %get-tuple-element.32.x_ref, ...), custom_call_target="tpu_custom_call" | custom-call | flops 1073741824 | bytes 10485760 | tf_op jit(solution)/shard_map/project_out/pallas_call | solution.py:370
  (17 shorter events, 0.1 us)
Async XLA Ops:
  0.0 8.5 %copy-start = (bf16[4096,256]{1,0:T(8,128)(2,1)S(1)}, bf16[4096,256]{1,0:T(8,128)(2,1)}, u32[]{:S(2)}) copy-start(bf16[4096,256]{1,0:T(8,128)(2,1)} %w_ref.4) | copy-start | bytes 6291460
  0.0 36.1 %collective-permute-start.10 = (bf16[256,4096]{1,0:T(8,128)(2,1)}, bf16[256,4096]{1,0:T(8,128)(2,1)S(1)}, u32[]{:S(2)}, u32[]{:S(2)}) collective-permute-start(bf16[256,4096]{1,0:T(8,128)(2,1)} %w_ref.5), channel_id=1, source_target_pairs={{0,1},{1,0},{2,3},{3,2},{4,5},{5,4},{6,7},{7,6},{8,9},{9,8},{10,11... | collective-permute-start | bytes 6291464 | tf_op jit(solution)/shard_map/ppermute | solution.py:388
  6.7 13.1 %copy-start.2 = (s32[512,32]{0,1:T(8,128)S(1)}, s32[512,32]{0,1:T(8,128)}, u32[]{:S(2)}) copy-start(s32[512,32]{0,1:T(8,128)} %param.14) | copy-start | bytes 196612
  6.7 13.1 %copy-start.3 = (s32[512,32]{0,1:T(8,128)S(1)}, s32[512,32]{0,1:T(8,128)}, u32[]{:S(2)}) copy-start(s32[512,32]{0,1:T(8,128)} %param.15) | copy-start | bytes 196612
  6.7 8.0 %collective-permute-start = (bf16[528,256]{1,0:T(8,128)(2,1)S(1)}, bf16[528,256]{1,0:T(8,128)(2,1)S(1)}, u32[]{:S(2)}, u32[]{:S(2)}) collective-permute-start(bf16[528,256]{1,0:T(8,128)(2,1)S(1)} %get-tuple-element.21.refs_2_), channel_id=1, source_target_pairs={{0,4},{1,5},{2,6},{3,7},{4,8},{5,9},{6,10},{7,11},{8,12},{9,13},{1... | collective-permute-start | bytes 811016 | tf_op jit(solution)/shard_map/ppermute | solution.py:397
  8.0 10.5 %collective-permute-start.2 = (bf16[528,256]{1,0:T(8,128)(2,1)S(1)}, bf16[528,256]{1,0:T(8,128)(2,1)S(1)}, u32[]{:S(2)}, u32[]{:S(2)}) collective-permute-start(bf16[528,256]{1,0:T(8,128)(2,1)S(1)} %get-tuple-element.21.refs_2_), channel_id=1, source_target_pairs={{0,1},{1,0},{2,3},{3,2},{4,5},{5,4},{6,7},{7,6},{8,9},{9,8},{10,11... | collective-permute-start | bytes 811016 | tf_op jit(solution)/shard_map/ppermute | solution.py:388
  9.7 13.1 %copy-start.4 = (s32[512]{0:T(512)S(1)}, s32[512]{0:T(512)}, u32[]{:S(2)}) copy-start(s32[512]{0:T(512)} %param.10) | copy-start | bytes 6148
  14.7 9.8 %collective-permute-start.7 = (bf16[528,256]{1,0:T(8,128)(2,1)S(1)}, bf16[528,256]{1,0:T(8,128)(2,1)S(1)}, u32[]{:S(2)}, u32[]{:S(2)}) collective-permute-start(bf16[528,256]{1,0:T(8,128)(2,1)S(1)} %collective-permute-done.refs_3_), channel_id=1, source_target_pairs={{0,1},{1,0},{2,3},{3,2},{4,6},{5,7},{6,8},{7,9},{8,10},{9,11},{10,... | collective-permute-start | bytes 811016 | tf_op jit(solution)/shard_map/ppermute | solution.py:397
  15.9 7.0 %collective-permute-start.3 = (bf16[528,256]{1,0:T(8,128)(2,1)S(1)}, bf16[528,256]{1,0:T(8,128)(2,1)S(1)}, u32[]{:S(2)}, u32[]{:S(2)}) collective-permute-start(bf16[528,256]{1,0:T(8,128)(2,1)S(1)} %collective-permute-done.refs_3_), channel_id=1, source_target_pairs={{0,1},{1,0},{2,3},{3,2},{4,5},{5,4},{6,7},{7,6},{8,9},{9,8},{10,11... | collective-permute-start | bytes 811016 | tf_op jit(solution)/shard_map/ppermute | solution.py:388
  17.2 13.5 %collective-permute-start.4 = (bf16[528,256]{1,0:T(8,128)(2,1)S(1)}, bf16[528,256]{1,0:T(8,128)(2,1)S(1)}, u32[]{:S(2)}, u32[]{:S(2)}) collective-permute-start(bf16[528,256]{1,0:T(8,128)(2,1)S(1)} %broadcast_select_fusion), channel_id=1, source_target_pairs={{0,2},{2,0},{4,6},{6,4},{8,10},{10,8},{12,14},{14,12},{1,3},{3,1},... | collective-permute-start | bytes 811016 | tf_op jit(solution)/shard_map/ppermute | solution.py:404
  18.5 12.2 %collective-permute-start.1 = (bf16[528,256]{1,0:T(8,128)(2,1)S(1)}, bf16[528,256]{1,0:T(8,128)(2,1)S(1)}, u32[]{:S(2)}, u32[]{:S(2)}) collective-permute-start(bf16[528,256]{1,0:T(8,128)(2,1)S(1)} %collective-permute-done.refs_3_), channel_id=1, source_target_pairs={{0,1},{1,0},{2,3},{3,2},{4,8},{5,9},{6,10},{7,11},{8,12},{9,13},{1... | collective-permute-start | bytes 811016 | tf_op jit(solution)/shard_map/ppermute | solution.py:397
  22.9 11.4 %copy-start.1 = (bf16[256,4096]{1,0:T(8,128)(2,1)S(1)}, bf16[256,4096]{1,0:T(8,128)(2,1)}, u32[]{:S(2)}) copy-start(bf16[256,4096]{1,0:T(8,128)(2,1)} %w_ref.5) | copy-start | bytes 6291460
  24.5 6.7 %collective-permute-start.8 = (bf16[528,256]{1,0:T(8,128)(2,1)S(1)}, bf16[528,256]{1,0:T(8,128)(2,1)S(1)}, u32[]{:S(2)}, u32[]{:S(2)}) collective-permute-start(bf16[528,256]{1,0:T(8,128)(2,1)S(1)} %collective-permute-done.7.refs_2_), channel_id=1, source_target_pairs={{0,1},{1,0},{2,3},{3,2},{4,5},{5,4},{6,7},{7,6},{8,9},{9,8},{10,11... | collective-permute-start | bytes 811016 | tf_op jit(solution)/shard_map/ppermute | solution.py:388
  30.7 1.6 %collective-permute-start.5 = (bf16[528,256]{1,0:T(8,128)(2,1)S(1)}, bf16[528,256]{1,0:T(8,128)(2,1)S(1)}, u32[]{:S(2)}, u32[]{:S(2)}) collective-permute-start(bf16[528,256]{1,0:T(8,128)(2,1)S(1)} %collective-permute-done.1.refs_2_), channel_id=1, source_target_pairs={{0,1},{1,0},{2,3},{3,2},{4,5},{5,4},{6,7},{7,6},{8,9},{9,8},{10,11... | collective-permute-start | bytes 811016 | tf_op jit(solution)/shard_map/ppermute | solution.py:388
  31.2 1.6 %collective-permute-start.6 = (bf16[528,256]{1,0:T(8,128)(2,1)S(1)}, bf16[528,256]{1,0:T(8,128)(2,1)S(1)}, u32[]{:S(2)}, u32[]{:S(2)}) collective-permute-start(bf16[528,256]{1,0:T(8,128)(2,1)S(1)} %collective-permute-done.4.refs_3_), channel_id=1, source_target_pairs={{0,1},{1,0},{2,3},{3,2},{4,5},{5,4},{6,7},{7,6},{8,9},{9,8},{10,11... | collective-permute-start | bytes 811016 | tf_op jit(solution)/shard_map/ppermute | solution.py:388
  33.8 2.3 %collective-permute-start.9 = (bf16[512,256]{1,0:T(8,128)(2,1)S(1)}, bf16[512,256]{1,0:T(8,128)(2,1)S(1)}, u32[]{:S(2)}, u32[]{:S(2)}) collective-permute-start(bf16[512,256]{1,0:T(8,128)(2,1)S(1)} %attend_last.1.a_ref), channel_id=1, source_target_pairs={{0,1},{1,0},{2,3},{3,2},{4,5},{5,4},{6,7},{7,6},{8,9},{9,8},{10,11... | collective-permute-start | bytes 786440 | tf_op jit(solution)/shard_map/ppermute | solution.py:388

commit v15 on v14

--- a/solution.py
+++ b/solution.py
@@ -32,19 +32,19 @@
         ]
 
     def early_tokens(half):
-        return cut(x_ref, xs, half * part, part, 4, 4 * half)
+        return cut(x_ref, xs, half * part, part, 8 - 4 * half, 8 * half)
 
     def late_tokens():
-        return cut(x_ref, xs, tile, tile, 2, 8)
+        return cut(x_ref, xs, tile, tile, 2, 12)
 
     def weights():
-        return cut(w_ref, ws, 0, width, 4, 10)
+        return cut(w_ref, ws, 0, width, 4, 14)
 
     def gain_copy():
-        return pltpu.make_async_copy(gain_hbm, gain_ref, sems.at[14])
+        return pltpu.make_async_copy(gain_hbm, gain_ref, sems.at[18])
 
     def segments_copy():
-        return pltpu.make_async_copy(seg_hbm, seg_ref, sems.at[15])
+        return pltpu.make_async_copy(seg_hbm, seg_ref, sems.at[19])
 
     for copy in early_tokens(0) + early_tokens(1) + [gain_copy()] + weights() + late_tokens() + [segments_copy()]:
         copy.start()
@@ -53,16 +53,16 @@
         return xs[first:first + count, start:start + LANES].astype(jnp.float32)
 
     def stats(first):
-        total = wide(first, part, 0)
-        for start in range(LANES, width, LANES):
-            total = total + wide(first, part, start)
-        mean = jnp.broadcast_to(jnp.sum(total, axis=1, keepdims=True) * (1.0 / width), (part, LANES))
+        pivot = jnp.broadcast_to(jnp.sum(wide(first, part, 0), axis=1, keepdims=True) * (1.0 / LANES), (part, LANES))
+        total = jnp.zeros((part, LANES), jnp.float32)
         square = jnp.zeros((part, LANES), jnp.float32)
         for start in range(0, width, LANES):
-            center = wide(first, part, start) - mean
-            square = square + center * center
-        spread = jnp.sum(square, axis=1, keepdims=True) * (1.0 / width)
-        return mean, jnp.broadcast_to(lax.rsqrt(spread + 1e-05), (part, LANES))
+            away = wide(first, part, start) - pivot
+            total = total + away
+            square = square + away * away
+        shift = jnp.sum(total, axis=1, keepdims=True) * (1.0 / width)
+        spread = jnp.maximum(jnp.sum(square, axis=1, keepdims=True) * (1.0 / width) - shift * shift, 0.0)
+        return pivot + shift, jnp.broadcast_to(lax.rsqrt(spread + 1e-05), (part, LANES))
 
     def project(first, halves):
         mean = jnp.concatenate([h[0] for h in halves], axis=0)
@@ -118,7 +118,7 @@
             pltpu.VMEM((width, cols), jnp.bfloat16),
             pltpu.VMEM((1, width), jnp.float32),
             pltpu.VMEM((1, rows), jnp.int32),
-            pltpu.SemaphoreType.DMA((16,)),
+            pltpu.SemaphoreType.DMA((20,)),
         ],
         compiler_params=pltpu.CompilerParams(vmem_limit_bytes=24 * MIB),
         cost_estimate=pl.CostEstimate(
@@ -299,19 +299,12 @@
 def own_kernel(a_ref, w_ref, sum_ref, out_ref):
     rows, width = out_ref.shape
     tile = rows // 2
-    chunk = width // 4
-
-    def body(step, carry):
-        for at in range(0, chunk, HD):
-            cols = pl.ds(pl.multiple_of(step * chunk + at, HD), HD)
-            weights = w_ref[:, cols]
-            for start in range(0, rows, tile):
-                span = slice(start, start + tile)
-                term = jnp.dot(a_ref[span, :], weights, preferred_element_type=jnp.float32)
-                out_ref[span, cols] = clip(term, sum_ref[span, cols])
-        return carry
-
-    lax.fori_loop(0, 4, body, 0)
+    for at in range(0, width, HD):
+        cols = slice(at, at + HD)
+        for start in range(0, rows, tile):
+            span = slice(start, start + tile)
+            term = jnp.dot(a_ref[span, :], w_ref[:, cols], preferred_element_type=jnp.float32)
+            out_ref[span, cols] = clip(term, sum_ref[span, cols])
 
 
 def project_own(attended, w_out, sum_bound):
@@ -333,38 +326,28 @@
 
 def output_kernel(b_ref, wb_ref, quant_ref, x_ref, sum_ref, last_ref, out_ref, staged, sems):
     rows, width = x_ref.shape
-    pieces = sems.shape[0]
-    piece = width // pieces
-    chunk = width // 2
     tile = rows // 2
 
     def copy(index):
-        span = pl.ds(pl.multiple_of(index * piece, piece), piece)
+        span = slice(index * HD, (index + 1) * HD)
         return pltpu.make_async_copy(staged.at[:, span], out_ref.at[:, span], sems.at[index])
 
-    def body(step, carry):
-        for at in range(0, chunk, HD):
-            cols = pl.ds(pl.multiple_of(step * chunk + at, HD), HD)
-            weights = wb_ref[:, cols]
-            for start in range(0, rows, tile):
-                span = slice(start, start + tile)
-                term = jnp.dot(b_ref[span, :], weights, preferred_element_type=jnp.float32)
-                other = clip(term, sum_ref[span, cols])
-                quant = other.astype(jnp.float32) + quant_ref[span, cols].astype(jnp.float32)
-                staged[span, cols] = clip(x_ref[span, cols] + quant, last_ref[span, cols])
-            if (at + HD) % piece == 0:
-                copy(step * (chunk // piece) + at // piece).start()
-        return carry
-
-    lax.fori_loop(0, width // chunk, body, 0)
-    for index in range(pieces):
+    for index in range(width // HD):
+        cols = slice(index * HD, (index + 1) * HD)
+        for start in range(0, rows, tile):
+            span = slice(start, start + tile)
+            term = jnp.dot(b_ref[span, :], wb_ref[:, cols], preferred_element_type=jnp.float32)
+            quant = clip(term, sum_ref[span, cols]).astype(jnp.float32) + quant_ref[span, cols].astype(jnp.float32)
+            staged[span, cols] = clip(x_ref[span, cols] + quant, last_ref[span, cols])
+        copy(index).start()
+    for index in range(width // HD):
         copy(index).wait()
 
 
 def project_out(att_other, w_other, quant_own, sum_bound, out_bound, tokens):
     rows, width = tokens.shape
     depth = att_other.shape[1]
-    pieces = 8
+    pieces = width // HD
     vmem = pl.BlockSpec(memory_space=pltpu.VMEM)
     operands = [att_other, w_other, quant_own, tokens, sum_bound, out_bound]
     return pl.pallas_call(

time: 41 us -> 40.5 us (0.988)
  Pallas kernels: 19.4 us -> 18.8 us
where the time goes in v15:
time: 40.5 us; the launch traced here: 40.4 us
  Pallas kernels  18.8 us (46%)
  starting transfers between devices  10.9 us (27%)
  waiting for transfers between devices  10.3 us (25%)
    pallas_call x1, Pallas kernels, norm_kv(): pl.pallas_call(norm_kv_kernel, in_specs=[hbm] * 4, out_specs=[vmem, vmem]...  6.04 us
    ppermute x7, starting transfers between devices, swap_cores(): return lax.ppermute(x, 'tp', [(0, 1), (1, 0)])  5.71 us
    ppermute x3, waiting for transfers between devices, shift(): return lax.ppermute(x, ('seq', 'tp'), pairs)  4.93 us
    pallas_call x1, Pallas kernels, project_out(): pl.pallas_call(output_kernel, in_specs=[vmem] * len(operands), out_specs=...  4.32 us
    ppermute x3, starting transfers between devices, shift(): return lax.ppermute(x, ('seq', 'tp'), pairs)  3.89 us
    ppermute x1, waiting for transfers between devices, on_device(): lax.ppermute(jnp.where(odd, held, message), 'seq', [(i, i ^ 1) for i in r...  3.83 us
    pallas_call x1, Pallas kernels, spread_bounds(): pl.pallas_call(bounds_kernel, in_specs=[vmem, vmem, pl.BlockSpec(memory_s...  3.05 us
    pallas_call x3, Pallas kernels, attend(): pl.pallas_call(functools.partial(attend_kernel, plan, first, last), in_sp...  2.66 us
  transfers between devices with their start and end apart: 11, of which 4 were waited for; matrix products, arithmetic and copies ran while one was open for 0% of the time, Pallas kernels for 36%

profile of v15, /device:TPU:11, one launch (start us, length us, event | category | flops | bytes accessed | tf_op | source)
XLA Modules:
  0.0 40.4 jit_solution(11505686395599930080)
XLA Ops:
  0.0 0.7 %collective-permute-start.10 = (bf16[256,4096]{1,0:T(8,128)(2,1)}, bf16[256,4096]{1,0:T(8,128)(2,1)S(1)}, u32[]{:S(2)}, u32[]{:S(2)}) collective-permute-start(bf16[256,4096]{1,0:T(8,128)(2,1)} %w_ref.5), channel_id=1, source_target_pairs={{0,1},{1,0},{2,3},{3,2},{4,5},{5,4},{6,7},{7,6},{8,9},{9,8},{10,11... | collective-permute-start | bytes 6291464 | tf_op jit(solution)/shard_map/ppermute | solution.py:371
  0.7 6.0 %norm_kv.1 = (bf16[528,256]{1,0:T(8,128)(2,1)S(1)}, bf16[512,4096]{1,0:T(8,128)(2,1)S(1)}) custom-call(bf16[512,4096]{1,0:T(8,128)(2,1)} %x_ref.3, f32[1,4096]{1,0:T(1,128)} %bitcast.10, bf16[4096,256]{1,0:T(8,128)(2,1)} %w_ref.3, s32[1,512]{1,0:T(1,128)} %bitcast.6), custom_call_target="tpu_custom_call" | custom-call | flops 1073741824 | bytes 10485760 | tf_op jit(solution)/shard_map/norm_kv/pallas_call | solution.py:111
  6.7 0.0 copy-start.3
  6.7 1.3 %collective-permute-start = (bf16[528,256]{1,0:T(8,128)(2,1)S(1)}, bf16[528,256]{1,0:T(8,128)(2,1)S(1)}, u32[]{:S(2)}, u32[]{:S(2)}) collective-permute-start(bf16[528,256]{1,0:T(8,128)(2,1)S(1)} %get-tuple-element.21.refs_2_), channel_id=1, source_target_pairs={{0,4},{1,5},{2,6},{3,7},{4,8},{5,9},{6,10},{7,11},{8,12},{9,13},{1... | collective-permute-start | bytes 811016 | tf_op jit(solution)/shard_map/ppermute | solution.py:380
  8.1 0.4 %collective-permute-start.2 = (bf16[528,256]{1,0:T(8,128)(2,1)S(1)}, bf16[528,256]{1,0:T(8,128)(2,1)S(1)}, u32[]{:S(2)}, u32[]{:S(2)}) collective-permute-start(bf16[528,256]{1,0:T(8,128)(2,1)S(1)} %get-tuple-element.21.refs_2_), channel_id=1, source_target_pairs={{0,1},{1,0},{2,3},{3,2},{4,5},{5,4},{6,7},{7,6},{8,9},{9,8},{10,11... | collective-permute-start | bytes 811016 | tf_op jit(solution)/shard_map/ppermute | solution.py:371
  8.5 1.2 %project_query.1.refs_0_ = bf16[512,256]{1,0:T(8,128)(2,1)S(1)} custom-call(bf16[512,4096]{1,0:T(8,128)(2,1)S(1)} %get-tuple-element.22.x_ref, bf16[4096,256]{1,0:T(8,128)(2,1)S(1)} %copy-done), custom_call_target="tpu_custom_call" | custom-call | flops 1073741824 | bytes 6291456 | tf_op jit(solution)/shard_map/project_query/pallas_call | solution.py:139
  9.8 0.0 copy-start.4
  9.8 4.9 %collective-permute-done.refs_3_ = bf16[528,256]{1,0:T(8,128)(2,1)S(1)} collective-permute-done((bf16[528,256]{1,0:T(8,128)(2,1)S(1)}, bf16[528,256]{1,0:T(8,128)(2,1)S(1)}, u32[]{:S(2)}, u32[]{:S(2)}) %collective-permute-start) | collective-permute-done | bytes 270368 | tf_op jit(solution)/shard_map/ppermute | solution.py:380
  14.7 1.2 %collective-permute-start.7 = (bf16[528,256]{1,0:T(8,128)(2,1)S(1)}, bf16[528,256]{1,0:T(8,128)(2,1)S(1)}, u32[]{:S(2)}, u32[]{:S(2)}) collective-permute-start(bf16[528,256]{1,0:T(8,128)(2,1)S(1)} %collective-permute-done.refs_3_), channel_id=1, source_target_pairs={{0,1},{1,0},{2,3},{3,2},{4,6},{5,7},{6,8},{7,9},{8,10},{9,11},{10,... | collective-permute-start | bytes 811016 | tf_op jit(solution)/shard_map/ppermute | solution.py:380
  16.0 1.2 %collective-permute-start.3 = (bf16[528,256]{1,0:T(8,128)(2,1)S(1)}, bf16[528,256]{1,0:T(8,128)(2,1)S(1)}, u32[]{:S(2)}, u32[]{:S(2)}) collective-permute-start(bf16[528,256]{1,0:T(8,128)(2,1)S(1)} %collective-permute-done.refs_3_), channel_id=1, source_target_pairs={{0,1},{1,0},{2,3},{3,2},{4,5},{5,4},{6,7},{7,6},{8,9},{9,8},{10,11... | collective-permute-start | bytes 811016 | tf_op jit(solution)/shard_map/ppermute | solution.py:371
  17.3 1.3 %collective-permute-start.4 = (bf16[528,256]{1,0:T(8,128)(2,1)S(1)}, bf16[528,256]{1,0:T(8,128)(2,1)S(1)}, u32[]{:S(2)}, u32[]{:S(2)}) collective-permute-start(bf16[528,256]{1,0:T(8,128)(2,1)S(1)} %broadcast_select_fusion), channel_id=1, source_target_pairs={{0,2},{2,0},{4,6},{6,4},{8,10},{10,8},{12,14},{14,12},{1,3},{3,1},... | collective-permute-start | bytes 811016 | tf_op jit(solution)/shard_map/ppermute | solution.py:387
  18.6 1.3 %collective-permute-start.1 = (bf16[528,256]{1,0:T(8,128)(2,1)S(1)}, bf16[528,256]{1,0:T(8,128)(2,1)S(1)}, u32[]{:S(2)}, u32[]{:S(2)}) collective-permute-start(bf16[528,256]{1,0:T(8,128)(2,1)S(1)} %collective-permute-done.refs_3_), channel_id=1, source_target_pairs={{0,1},{1,0},{2,3},{3,2},{4,8},{5,9},{6,10},{7,11},{8,12},{9,13},{1... | collective-permute-start | bytes 811016 | tf_op jit(solution)/shard_map/ppermute | solution.py:380
  19.9 3.0 %spread_bounds.1 = (bf16[512,4096]{1,0:T(8,128)(2,1)S(1)}, bf16[512,4096]{1,0:T(8,128)(2,1)S(1)}, f32[512,4096]{1,0:T(8,128)S(1)}) custom-call(s32[32,512]{1,0:T(8,128)S(1)} %bitcast.4, s32[32,512]{1,0:T(8,128)S(1)} %bitcast.5, bf16[512,4096]{1,0:T(8,128)(2,1)} %x_ref.3), custom_call_target="tpu_custom_call" | custom-call | flops 16777216 | bytes 131072 | tf_op jit(solution)/shard_map/spread_bounds/pallas_call | solution.py:283
  23.0 1.6 %attend_first.1.refs_4_ = f32[512,512]{1,0:T(8,128)S(1)} custom-call(bf16[512,256]{1,0:T(8,128)(2,1)S(1)} %project_query.1.refs_0_, s32[1,512]{1,0:T(1,128)S(1)} %bitcast.7, bf16[528,256]{1,0:T(8,128)(2,1)S(1)} %get-tuple-element.21.refs_2_, bf16[528,256]{1,0:T(8,128)(2,1)S(1)} %collective-permute-done.refs_3_, ...), custom_call_target="tpu_custom_call" | custom-call | flops 536870912 | bytes 1048576 | tf_op jit(solution)/shard_map/attend_first/pallas_call | solution.py:243
  24.6 2.4 %collective-permute-start.8 = (bf16[528,256]{1,0:T(8,128)(2,1)S(1)}, bf16[528,256]{1,0:T(8,128)(2,1)S(1)}, u32[]{:S(2)}, u32[]{:S(2)}) collective-permute-start(bf16[528,256]{1,0:T(8,128)(2,1)S(1)} %collective-permute-done.7.refs_2_), channel_id=1, source_target_pairs={{0,1},{1,0},{2,3},{3,2},{4,5},{5,4},{6,7},{7,6},{8,9},{9,8},{10,11... | collective-permute-start | bytes 811016 | tf_op jit(solution)/shard_map/ppermute | solution.py:371
  27.0 3.8 %collective-permute-done.4.refs_3_ = bf16[528,256]{1,0:T(8,128)(2,1)S(1)} collective-permute-done((bf16[528,256]{1,0:T(8,128)(2,1)S(1)}, bf16[528,256]{1,0:T(8,128)(2,1)S(1)}, u32[]{:S(2)}, u32[]{:S(2)}) %collective-permute-start.4) | collective-permute-done | bytes 270368 | tf_op jit(solution)/shard_map/ppermute | solution.py:387
  30.8 0.4 %collective-permute-start.5 = (bf16[528,256]{1,0:T(8,128)(2,1)S(1)}, bf16[528,256]{1,0:T(8,128)(2,1)S(1)}, u32[]{:S(2)}, u32[]{:S(2)}) collective-permute-start(bf16[528,256]{1,0:T(8,128)(2,1)S(1)} %collective-permute-done.1.refs_2_), channel_id=1, source_target_pairs={{0,1},{1,0},{2,3},{3,2},{4,5},{5,4},{6,7},{7,6},{8,9},{9,8},{10,11... | collective-permute-start | bytes 811016 | tf_op jit(solution)/shard_map/ppermute | solution.py:371
  31.2 0.1 collective-permute-start.6
  31.3 1.1 %collective-permute-done.5.refs_4_ = bf16[528,256]{1,0:T(8,128)(2,1)S(1)} collective-permute-done((bf16[528,256]{1,0:T(8,128)(2,1)S(1)}, bf16[528,256]{1,0:T(8,128)(2,1)S(1)}, u32[]{:S(2)}, u32[]{:S(2)}) %collective-permute-start.5) | collective-permute-done | bytes 270368 | tf_op jit(solution)/shard_map/ppermute | solution.py:371
  32.4 0.4 collective-permute-done.6.refs_5_
  32.8 1.1 %attend_last.1.a_ref = bf16[512,256]{1,0:T(8,128)(2,1)S(1)} custom-call(bf16[512,256]{1,0:T(8,128)(2,1)S(1)} %project_query.1.refs_0_, s32[1,512]{1,0:T(1,128)S(1)} %bitcast.9, bf16[528,256]{1,0:T(8,128)(2,1)S(1)} %collective-permute-done.1.refs_2_, bf16[528,256]{1,0:T(8,128)(2,1)S(1)} %collective-permute-done.4.refs_3_, ...), custom_call_target="tpu_custom_call" | custom-call | flops 536870912 | bytes 1048576 | tf_op jit(solution)/shard_map/attend_last/pallas_call | solution.py:243
  33.9 0.4 %collective-permute-start.9 = (bf16[512,256]{1,0:T(8,128)(2,1)S(1)}, bf16[512,256]{1,0:T(8,128)(2,1)S(1)}, u32[]{:S(2)}, u32[]{:S(2)}) collective-permute-start(bf16[512,256]{1,0:T(8,128)(2,1)S(1)} %attend_last.1.a_ref), channel_id=1, source_target_pairs={{0,1},{1,0},{2,3},{3,2},{4,5},{5,4},{6,7},{7,6},{8,9},{9,8},{10,11... | collective-permute-start | bytes 786440 | tf_op jit(solution)/shard_map/ppermute | solution.py:371
  34.3 1.5 %project_own.1.quant_ref = bf16[512,4096]{1,0:T(8,128)(2,1)S(1)} custom-call(bf16[512,256]{1,0:T(8,128)(2,1)S(1)} %attend_last.1.a_ref, bf16[256,4096]{1,0:T(8,128)(2,1)S(1)} %copy-done.1, bf16[512,4096]{1,0:T(8,128)(2,1)S(1)} %get-tuple-element.30.sum_ref), custom_call_target="tpu_custom_call" | custom-call | flops 1073741824 | bytes 10485760 | tf_op jit(solution)/shard_map/project_own/pallas_call | solution.py:314
  35.9 4.3 %project_out.1 = bf16[512,4096]{1,0:T(8,128)(2,1)} custom-call(bf16[512,256]{1,0:T(8,128)(2,1)S(1)} %collective-permute-done.9.b_ref, bf16[256,4096]{1,0:T(8,128)(2,1)S(1)} %collective-permute-done.10.wb_ref, bf16[512,4096]{1,0:T(8,128)(2,1)S(1)} %project_own.1.quant_ref, f32[512,4096]{1,0:T(8,128)S(1)} %get-tuple-element.32.x_ref, ...), custom_call_target="tpu_custom_call" | custom-call | flops 1073741824 | bytes 10485760 | tf_op jit(solution)/shard_map/project_out/pallas_call | solution.py:353
  (17 shorter events, 0.1 us)
Async XLA Ops:
  0.0 8.5 %copy-start = (bf16[4096,256]{1,0:T(8,128)(2,1)S(1)}, bf16[4096,256]{1,0:T(8,128)(2,1)}, u32[]{:S(2)}) copy-start(bf16[4096,256]{1,0:T(8,128)(2,1)} %w_ref.4) | copy-start | bytes 6291460
  0.0 35.9 %collective-permute-start.10 = (bf16[256,4096]{1,0:T(8,128)(2,1)}, bf16[256,4096]{1,0:T(8,128)(2,1)S(1)}, u32[]{:S(2)}, u32[]{:S(2)}) collective-permute-start(bf16[256,4096]{1,0:T(8,128)(2,1)} %w_ref.5), channel_id=1, source_target_pairs={{0,1},{1,0},{2,3},{3,2},{4,5},{5,4},{6,7},{7,6},{8,9},{9,8},{10,11... | collective-permute-start | bytes 6291464 | tf_op jit(solution)/shard_map/ppermute | solution.py:371
  6.7 13.1 %copy-start.2 = (s32[512,32]{0,1:T(8,128)S(1)}, s32[512,32]{0,1:T(8,128)}, u32[]{:S(2)}) copy-start(s32[512,32]{0,1:T(8,128)} %param.14) | copy-start | bytes 196612
  6.7 13.1 %copy-start.3 = (s32[512,32]{0,1:T(8,128)S(1)}, s32[512,32]{0,1:T(8,128)}, u32[]{:S(2)}) copy-start(s32[512,32]{0,1:T(8,128)} %param.15) | copy-start | bytes 196612
  6.7 8.0 %collective-permute-start = (bf16[528,256]{1,0:T(8,128)(2,1)S(1)}, bf16[528,256]{1,0:T(8,128)(2,1)S(1)}, u32[]{:S(2)}, u32[]{:S(2)}) collective-permute-start(bf16[528,256]{1,0:T(8,128)(2,1)S(1)} %get-tuple-element.21.refs_2_), channel_id=1, source_target_pairs={{0,4},{1,5},{2,6},{3,7},{4,8},{5,9},{6,10},{7,11},{8,12},{9,13},{1... | collective-permute-start | bytes 811016 | tf_op jit(solution)/shard_map/ppermute | solution.py:380
  8.1 10.5 %collective-permute-start.2 = (bf16[528,256]{1,0:T(8,128)(2,1)S(1)}, bf16[528,256]{1,0:T(8,128)(2,1)S(1)}, u32[]{:S(2)}, u32[]{:S(2)}) collective-permute-start(bf16[528,256]{1,0:T(8,128)(2,1)S(1)} %get-tuple-element.21.refs_2_), channel_id=1, source_target_pairs={{0,1},{1,0},{2,3},{3,2},{4,5},{5,4},{6,7},{7,6},{8,9},{9,8},{10,11... | collective-permute-start | bytes 811016 | tf_op jit(solution)/shard_map/ppermute | solution.py:371
  9.8 13.2 %copy-start.4 = (s32[512]{0:T(512)S(1)}, s32[512]{0:T(512)}, u32[]{:S(2)}) copy-start(s32[512]{0:T(512)} %param.10) | copy-start | bytes 6148
  14.7 9.8 %collective-permute-start.7 = (bf16[528,256]{1,0:T(8,128)(2,1)S(1)}, bf16[528,256]{1,0:T(8,128)(2,1)S(1)}, u32[]{:S(2)}, u32[]{:S(2)}) collective-permute-start(bf16[528,256]{1,0:T(8,128)(2,1)S(1)} %collective-permute-done.refs_3_), channel_id=1, source_target_pairs={{0,1},{1,0},{2,3},{3,2},{4,6},{5,7},{6,8},{7,9},{8,10},{9,11},{10,... | collective-permute-start | bytes 811016 | tf_op jit(solution)/shard_map/ppermute | solution.py:380
  16.0 7.0 %collective-permute-start.3 = (bf16[528,256]{1,0:T(8,128)(2,1)S(1)}, bf16[528,256]{1,0:T(8,128)(2,1)S(1)}, u32[]{:S(2)}, u32[]{:S(2)}) collective-permute-start(bf16[528,256]{1,0:T(8,128)(2,1)S(1)} %collective-permute-done.refs_3_), channel_id=1, source_target_pairs={{0,1},{1,0},{2,3},{3,2},{4,5},{5,4},{6,7},{7,6},{8,9},{9,8},{10,11... | collective-permute-start | bytes 811016 | tf_op jit(solution)/shard_map/ppermute | solution.py:371
  17.3 13.5 %collective-permute-start.4 = (bf16[528,256]{1,0:T(8,128)(2,1)S(1)}, bf16[528,256]{1,0:T(8,128)(2,1)S(1)}, u32[]{:S(2)}, u32[]{:S(2)}) collective-permute-start(bf16[528,256]{1,0:T(8,128)(2,1)S(1)} %broadcast_select_fusion), channel_id=1, source_target_pairs={{0,2},{2,0},{4,6},{6,4},{8,10},{10,8},{12,14},{14,12},{1,3},{3,1},... | collective-permute-start | bytes 811016 | tf_op jit(solution)/shard_map/ppermute | solution.py:387
  18.6 12.2 %collective-permute-start.1 = (bf16[528,256]{1,0:T(8,128)(2,1)S(1)}, bf16[528,256]{1,0:T(8,128)(2,1)S(1)}, u32[]{:S(2)}, u32[]{:S(2)}) collective-permute-start(bf16[528,256]{1,0:T(8,128)(2,1)S(1)} %collective-permute-done.refs_3_), channel_id=1, source_target_pairs={{0,1},{1,0},{2,3},{3,2},{4,8},{5,9},{6,10},{7,11},{8,12},{9,13},{1... | collective-permute-start | bytes 811016 | tf_op jit(solution)/shard_map/ppermute | solution.py:380
  22.9 11.4 %copy-start.1 = (bf16[256,4096]{1,0:T(8,128)(2,1)S(1)}, bf16[256,4096]{1,0:T(8,128)(2,1)}, u32[]{:S(2)}) copy-start(bf16[256,4096]{1,0:T(8,128)(2,1)} %w_ref.5) | copy-start | bytes 6291460
  24.6 6.7 %collective-permute-start.8 = (bf16[528,256]{1,0:T(8,128)(2,1)S(1)}, bf16[528,256]{1,0:T(8,128)(2,1)S(1)}, u32[]{:S(2)}, u32[]{:S(2)}) collective-permute-start(bf16[528,256]{1,0:T(8,128)(2,1)S(1)} %collective-permute-done.7.refs_2_), channel_id=1, source_target_pairs={{0,1},{1,0},{2,3},{3,2},{4,5},{5,4},{6,7},{7,6},{8,9},{9,8},{10,11... | collective-permute-start | bytes 811016 | tf_op jit(solution)/shard_map/ppermute | solution.py:371
  30.8 1.6 %collective-permute-start.5 = (bf16[528,256]{1,0:T(8,128)(2,1)S(1)}, bf16[528,256]{1,0:T(8,128)(2,1)S(1)}, u32[]{:S(2)}, u32[]{:S(2)}) collective-permute-start(bf16[528,256]{1,0:T(8,128)(2,1)S(1)} %collective-permute-done.1.refs_2_), channel_id=1, source_target_pairs={{0,1},{1,0},{2,3},{3,2},{4,5},{5,4},{6,7},{7,6},{8,9},{9,8},{10,11... | collective-permute-start | bytes 811016 | tf_op jit(solution)/shard_map/ppermute | solution.py:371
  31.2 1.6 %collective-permute-start.6 = (bf16[528,256]{1,0:T(8,128)(2,1)S(1)}, bf16[528,256]{1,0:T(8,128)(2,1)S(1)}, u32[]{:S(2)}, u32[]{:S(2)}) collective-permute-start(bf16[528,256]{1,0:T(8,128)(2,1)S(1)} %collective-permute-done.4.refs_3_), channel_id=1, source_target_pairs={{0,1},{1,0},{2,3},{3,2},{4,5},{5,4},{6,7},{7,6},{8,9},{9,8},{10,11... | collective-permute-start | bytes 811016 | tf_op jit(solution)/shard_map/ppermute | solution.py:371
  33.9 2.0 %collective-permute-start.9 = (bf16[512,256]{1,0:T(8,128)(2,1)S(1)}, bf16[512,256]{1,0:T(8,128)(2,1)S(1)}, u32[]{:S(2)}, u32[]{:S(2)}) collective-permute-start(bf16[512,256]{1,0:T(8,128)(2,1)S(1)} %attend_last.1.a_ref), channel_id=1, source_target_pairs={{0,1},{1,0},{2,3},{3,2},{4,5},{5,4},{6,7},{7,6},{8,9},{9,8},{10,11... | collective-permute-start | bytes 786440 | tf_op jit(solution)/shard_map/ppermute | solution.py:371

commit v16 on v15

--- a/solution.py
+++ b/solution.py
@@ -35,7 +35,7 @@
         return cut(x_ref, xs, half * part, part, 8 - 4 * half, 8 * half)
 
     def late_tokens():
-        return cut(x_ref, xs, tile, tile, 2, 12)
+        return cut(x_ref, xs, tile, tile, 1, 12)
 
     def weights():
         return cut(w_ref, ws, 0, width, 4, 14)
@@ -53,16 +53,16 @@
         return xs[first:first + count, start:start + LANES].astype(jnp.float32)
 
     def stats(first):
-        pivot = jnp.broadcast_to(jnp.sum(wide(first, part, 0), axis=1, keepdims=True) * (1.0 / LANES), (part, LANES))
-        total = jnp.zeros((part, LANES), jnp.float32)
+        total = wide(first, part, 0)
+        for start in range(LANES, width, LANES):
+            total = total + wide(first, part, start)
+        mean = jnp.broadcast_to(jnp.sum(total, axis=1, keepdims=True) * (1.0 / width), (part, LANES))
         square = jnp.zeros((part, LANES), jnp.float32)
         for start in range(0, width, LANES):
-            away = wide(first, part, start) - pivot
-            total = total + away
-            square = square + away * away
-        shift = jnp.sum(total, axis=1, keepdims=True) * (1.0 / width)
-        spread = jnp.maximum(jnp.sum(square, axis=1, keepdims=True) * (1.0 / width) - shift * shift, 0.0)
-        return pivot + shift, jnp.broadcast_to(lax.rsqrt(spread + 1e-05), (part, LANES))
+            center = wide(first, part, start) - mean
+            square = square + center * center
+        spread = jnp.sum(square, axis=1, keepdims=True) * (1.0 / width)
+        return mean, jnp.broadcast_to(lax.rsqrt(spread + 1e-05), (part, LANES))
 
     def project(first, halves):
         mean = jnp.concatenate([h[0] for h in halves], axis=0)
@@ -70,6 +70,8 @@
         kv = jnp.zeros((tile, ws.shape[1]), jnp.float32)
         span = slice(first, first + tile)
         for start in range(0, width, HD):
+            if first == 0 and start % (width // 4) == 0:
+                weights()[4 * start // width].wait()
             for at in (start, start + LANES):
                 normed = (wide(first, tile, at) - mean) * scale * gain_ref[:, at:at + LANES]
                 normed_ref[span, at:at + LANES] = normed.astype(jnp.bfloat16)
@@ -83,8 +85,7 @@
         for copy in early_tokens(half):
             copy.wait()
         halves.append(stats(half * part))
-    for copy in [gain_copy()] + weights():
-        copy.wait()
+    gain_copy().wait()
     project(0, halves)
     for copy in late_tokens():
         copy.wait()
@@ -164,10 +165,14 @@
     place = lax.axis_index("seq")
 
     def finish(span, weighted, total):
-        out_ref[span, :] = (weighted / jnp.sum(total, axis=1, keepdims=True)).astype(jnp.bfloat16)
+        inverse = jnp.broadcast_to(1.0 / jnp.sum(total, axis=1, keepdims=True), total.shape)
+        out_ref[span, :] = (weighted * jnp.concatenate([inverse, inverse], axis=1)).astype(jnp.bfloat16)
 
     def update(slots, keys, values):
-        own_seg = jnp.transpose(jnp.broadcast_to(seg_ref[...].astype(jnp.float32), (8, rows)))[:, 0:1]
+        if first:
+            out_ref[:, HD + 2 * LANES:] = jnp.transpose(
+                jnp.broadcast_to(seg_ref[...].astype(jnp.float32), (LANES, rows))
+            )
         key_segs = {}
         for slot in slots:
             packed = mine[slot][rows:, :].astype(jnp.float32)
@@ -175,7 +180,8 @@
         for start in range(0, rows, tile):
             span = slice(start, start + tile)
             query = q_ref[span, :]
-            best = None if first else state_ref[span, HD:HD + LANES]
+            own_seg = (out_ref if first else state_ref)[span, HD + 2 * LANES:]
+            best = before = None if first else state_ref[span, HD:HD + LANES]
             bounds = {}
             for slot in slots:
                 back, furthest = plan[slot]
@@ -186,22 +192,21 @@
                     low = start
                 bounds[slot] = (low, high)
                 raw = lax.dot_general(query, keys[slot][low:high, :], NT, preferred_element_type=jnp.float32)
-                allowed = key_segs[slot][:, low:high] == own_seg[span, :]
-                if back == 0:
-                    row_pos = start + lax.broadcasted_iota(jnp.int32, raw.shape, 0)
-                    allowed = allowed & (lax.broadcasted_iota(jnp.int32, raw.shape, 1) <= row_pos)
-                masked = jnp.where(allowed, raw, NEG)
-                scores[slot, :, low:high] = masked
-                for at in range(0, high - low, LANES):
-                    piece = masked[:, at:at + LANES]
+                for at in range(low, high, LANES):
+                    allowed = key_segs[slot][:, at:at + LANES] == own_seg
+                    if back == 0:
+                        row_pos = start + lax.broadcasted_iota(jnp.int32, allowed.shape, 0)
+                        allowed = allowed & (at + lax.broadcasted_iota(jnp.int32, allowed.shape, 1) <= row_pos)
+                    piece = jnp.where(allowed, raw[:, at - low:at - low + LANES], NEG)
+                    scores[slot, :, at:at + LANES] = piece
                     best = piece if best is None else jnp.maximum(best, piece)
             top = jnp.broadcast_to(jnp.max(best, axis=1, keepdims=True), (tile, LANES))
             if first:
                 total = jnp.zeros((tile, LANES), jnp.float32)
                 weighted = jnp.zeros((tile, HD), jnp.float32)
             else:
-                shrink = jnp.exp2((state_ref[span, HD:HD + LANES] - top) * FACTOR)
-                total = state_ref[span, HD + LANES:] * shrink
+                shrink = jnp.exp2((before - top) * FACTOR)
+                total = state_ref[span, HD + LANES:HD + 2 * LANES] * shrink
                 weighted = state_ref[span, :HD] * jnp.concatenate([shrink, shrink], axis=1)
             for slot in slots:
                 low, high = bounds[slot]
@@ -217,7 +222,7 @@
             else:
                 out_ref[span, :HD] = weighted
                 out_ref[span, HD:HD + LANES] = top
-                out_ref[span, HD + LANES:] = total
+                out_ref[span, HD + LANES:HD + 2 * LANES] = total
 
     order = sorted(range(blocks), key=lambda slot: plan[slot][0])
     for count in range(1 if first else 0, blocks + 1):
@@ -231,7 +236,7 @@
 
             @pl.when(reached)
             def _():
-                finish(slice(0, rows), state_ref[:, :HD], state_ref[:, HD + LANES:])
+                finish(slice(0, rows), state_ref[:, :HD], state_ref[:, HD + LANES:HD + 2 * LANES])
 
 
 def attend(query, segments, plan, mine, other, state, last):
@@ -244,7 +249,7 @@
         functools.partial(attend_kernel, plan, first, last),
         in_specs=[vmem] * len(operands),
         out_specs=vmem,
-        out_shape=pltpu.VMEM((rows, HD), jnp.bfloat16) if last else pltpu.VMEM((rows, HD + 2 * LANES), jnp.float32),
+        out_shape=pltpu.VMEM((rows, HD), jnp.bfloat16) if last else pltpu.VMEM((rows, HD + 3 * LANES), jnp.float32),
         scratch_shapes=[pltpu.VMEM((blocks, rows // 2, rows), jnp.float32)],
         input_output_aliases={} if first or last else {len(operands) - 1: 0},
         compiler_params=pltpu.CompilerParams(vmem_limit_bytes=12 * MIB),

time: 40.5 us -> 40.4 us (level)
  no operation moved by 1% of the time
where the time goes in v16:
time: 40.4 us; the launch traced here: 40.3 us
  Pallas kernels  18.9 us (47%)
  starting transfers between devices  10.8 us (27%)
  waiting for transfers between devices  10.3 us (25%)
    pallas_call x1, Pallas kernels, norm_kv(): pl.pallas_call(norm_kv_kernel, in_specs=[hbm] * 4, out_specs=[vmem, vmem]...  6.23 us
    ppermute x7, starting transfers between devices, swap_cores(): return lax.ppermute(x, 'tp', [(0, 1), (1, 0)])  5.62 us
    ppermute x3, waiting for transfers between devices, shift(): return lax.ppermute(x, ('seq', 'tp'), pairs)  4.93 us
    pallas_call x1, Pallas kernels, project_out(): pl.pallas_call(output_kernel, in_specs=[vmem] * len(operands), out_specs=...  4.31 us
    ppermute x3, starting transfers between devices, shift(): return lax.ppermute(x, ('seq', 'tp'), pairs)  3.88 us
    ppermute x1, waiting for transfers between devices, on_device(): lax.ppermute(jnp.where(odd, held, message), 'seq', [(i, i ^ 1) for i in r...  3.84 us
    pallas_call x1, Pallas kernels, spread_bounds(): pl.pallas_call(bounds_kernel, in_specs=[vmem, vmem, pl.BlockSpec(memory_s...  3.05 us
    pallas_call x3, Pallas kernels, attend(): pl.pallas_call(functools.partial(attend_kernel, plan, first, last), in_sp...  2.49 us
  transfers between devices with their start and end apart: 11, of which 4 were waited for; matrix products, arithmetic and copies ran while one was open for 0% of the time, Pallas kernels for 36%

profile of v16, /device:TPU:11, one launch (start us, length us, event | category | flops | bytes accessed | tf_op | source)
XLA Modules:
  0.0 40.3 jit_solution(9333507660118005702)
XLA Ops:
  0.0 0.7 %collective-permute-start.10 = (bf16[256,4096]{1,0:T(8,128)(2,1)}, bf16[256,4096]{1,0:T(8,128)(2,1)S(1)}, u32[]{:S(2)}, u32[]{:S(2)}) collective-permute-start(bf16[256,4096]{1,0:T(8,128)(2,1)} %w_ref.5), channel_id=1, source_target_pairs={{0,1},{1,0},{2,3},{3,2},{4,5},{5,4},{6,7},{7,6},{8,9},{9,8},{10,11... | collective-permute-start | bytes 6291464 | tf_op jit(solution)/shard_map/ppermute | solution.py:376
  0.7 6.2 %norm_kv.1 = (bf16[528,256]{1,0:T(8,128)(2,1)S(1)}, bf16[512,4096]{1,0:T(8,128)(2,1)S(1)}) custom-call(bf16[512,4096]{1,0:T(8,128)(2,1)} %x_ref.3, f32[1,4096]{1,0:T(1,128)} %bitcast.10, bf16[4096,256]{1,0:T(8,128)(2,1)} %w_ref.3, s32[1,512]{1,0:T(1,128)} %bitcast.6), custom_call_target="tpu_custom_call" | custom-call | flops 1073741824 | bytes 10485760 | tf_op jit(solution)/shard_map/norm_kv/pallas_call | solution.py:112
  6.9 0.0 copy-start.2
  6.9 0.0 copy-start.3
  6.9 1.3 %collective-permute-start = (bf16[528,256]{1,0:T(8,128)(2,1)S(1)}, bf16[528,256]{1,0:T(8,128)(2,1)S(1)}, u32[]{:S(2)}, u32[]{:S(2)}) collective-permute-start(bf16[528,256]{1,0:T(8,128)(2,1)S(1)} %get-tuple-element.21.refs_2_), channel_id=1, source_target_pairs={{0,4},{1,5},{2,6},{3,7},{4,8},{5,9},{6,10},{7,11},{8,12},{9,13},{1... | collective-permute-start | bytes 811016 | tf_op jit(solution)/shard_map/ppermute | solution.py:385
  8.3 0.4 %collective-permute-start.2 = (bf16[528,256]{1,0:T(8,128)(2,1)S(1)}, bf16[528,256]{1,0:T(8,128)(2,1)S(1)}, u32[]{:S(2)}, u32[]{:S(2)}) collective-permute-start(bf16[528,256]{1,0:T(8,128)(2,1)S(1)} %get-tuple-element.21.refs_2_), channel_id=1, source_target_pairs={{0,1},{1,0},{2,3},{3,2},{4,5},{5,4},{6,7},{7,6},{8,9},{9,8},{10,11... | collective-permute-start | bytes 811016 | tf_op jit(solution)/shard_map/ppermute | solution.py:376
  8.7 1.2 %project_query.1.refs_0_ = bf16[512,256]{1,0:T(8,128)(2,1)S(1)} custom-call(bf16[512,4096]{1,0:T(8,128)(2,1)S(1)} %get-tuple-element.22.x_ref, bf16[4096,256]{1,0:T(8,128)(2,1)S(1)} %copy-done), custom_call_target="tpu_custom_call" | custom-call | flops 1073741824 | bytes 6291456 | tf_op jit(solution)/shard_map/project_query/pallas_call | solution.py:140
  10.0 4.9 %collective-permute-done.refs_3_ = bf16[528,256]{1,0:T(8,128)(2,1)S(1)} collective-permute-done((bf16[528,256]{1,0:T(8,128)(2,1)S(1)}, bf16[528,256]{1,0:T(8,128)(2,1)S(1)}, u32[]{:S(2)}, u32[]{:S(2)}) %collective-permute-start) | collective-permute-done | bytes 270368 | tf_op jit(solution)/shard_map/ppermute | solution.py:385
  14.9 1.2 %collective-permute-start.7 = (bf16[528,256]{1,0:T(8,128)(2,1)S(1)}, bf16[528,256]{1,0:T(8,128)(2,1)S(1)}, u32[]{:S(2)}, u32[]{:S(2)}) collective-permute-start(bf16[528,256]{1,0:T(8,128)(2,1)S(1)} %collective-permute-done.refs_3_), channel_id=1, source_target_pairs={{0,1},{1,0},{2,3},{3,2},{4,6},{5,7},{6,8},{7,9},{8,10},{9,11},{10,... | collective-permute-start | bytes 811016 | tf_op jit(solution)/shard_map/ppermute | solution.py:385
  16.2 1.2 %collective-permute-start.3 = (bf16[528,256]{1,0:T(8,128)(2,1)S(1)}, bf16[528,256]{1,0:T(8,128)(2,1)S(1)}, u32[]{:S(2)}, u32[]{:S(2)}) collective-permute-start(bf16[528,256]{1,0:T(8,128)(2,1)S(1)} %collective-permute-done.refs_3_), channel_id=1, source_target_pairs={{0,1},{1,0},{2,3},{3,2},{4,5},{5,4},{6,7},{7,6},{8,9},{9,8},{10,11... | collective-permute-start | bytes 811016 | tf_op jit(solution)/shard_map/ppermute | solution.py:376
  17.4 1.3 %collective-permute-start.4 = (bf16[528,256]{1,0:T(8,128)(2,1)S(1)}, bf16[528,256]{1,0:T(8,128)(2,1)S(1)}, u32[]{:S(2)}, u32[]{:S(2)}) collective-permute-start(bf16[528,256]{1,0:T(8,128)(2,1)S(1)} %broadcast_select_fusion), channel_id=1, source_target_pairs={{0,2},{2,0},{4,6},{6,4},{8,10},{10,8},{12,14},{14,12},{1,3},{3,1},... | collective-permute-start | bytes 811016 | tf_op jit(solution)/shard_map/ppermute | solution.py:392
  18.8 1.3 %collective-permute-start.1 = (bf16[528,256]{1,0:T(8,128)(2,1)S(1)}, bf16[528,256]{1,0:T(8,128)(2,1)S(1)}, u32[]{:S(2)}, u32[]{:S(2)}) collective-permute-start(bf16[528,256]{1,0:T(8,128)(2,1)S(1)} %collective-permute-done.refs_3_), channel_id=1, source_target_pairs={{0,1},{1,0},{2,3},{3,2},{4,8},{5,9},{6,10},{7,11},{8,12},{9,13},{1... | collective-permute-start | bytes 811016 | tf_op jit(solution)/shard_map/ppermute | solution.py:385
  20.1 3.0 %spread_bounds.1 = (bf16[512,4096]{1,0:T(8,128)(2,1)S(1)}, bf16[512,4096]{1,0:T(8,128)(2,1)S(1)}, f32[512,4096]{1,0:T(8,128)S(1)}) custom-call(s32[32,512]{1,0:T(8,128)S(1)} %bitcast.4, s32[32,512]{1,0:T(8,128)S(1)} %bitcast.5, bf16[512,4096]{1,0:T(8,128)(2,1)} %x_ref.3), custom_call_target="tpu_custom_call" | custom-call | flops 16777216 | bytes 131072 | tf_op jit(solution)/shard_map/spread_bounds/pallas_call | solution.py:288
  23.1 1.7 %attend_first.1.refs_4_ = f32[512,640]{1,0:T(8,128)S(1)} custom-call(bf16[512,256]{1,0:T(8,128)(2,1)S(1)} %project_query.1.refs_0_, s32[1,512]{1,0:T(1,128)S(1)} %bitcast.7, bf16[528,256]{1,0:T(8,128)(2,1)S(1)} %get-tuple-element.21.refs_2_, bf16[528,256]{1,0:T(8,128)(2,1)S(1)} %collective-permute-done.refs_3_, ...), custom_call_target="tpu_custom_call" | custom-call | flops 536870912 | bytes 1048576 | tf_op jit(solution)/shard_map/attend_first/pallas_call | solution.py:248
  24.8 2.3 %collective-permute-start.8 = (bf16[528,256]{1,0:T(8,128)(2,1)S(1)}, bf16[528,256]{1,0:T(8,128)(2,1)S(1)}, u32[]{:S(2)}, u32[]{:S(2)}) collective-permute-start(bf16[528,256]{1,0:T(8,128)(2,1)S(1)} %collective-permute-done.7.refs_2_), channel_id=1, source_target_pairs={{0,1},{1,0},{2,3},{3,2},{4,5},{5,4},{6,7},{7,6},{8,9},{9,8},{10,11... | collective-permute-start | bytes 811016 | tf_op jit(solution)/shard_map/ppermute | solution.py:376
  27.1 3.8 %collective-permute-done.4.refs_3_ = bf16[528,256]{1,0:T(8,128)(2,1)S(1)} collective-permute-done((bf16[528,256]{1,0:T(8,128)(2,1)S(1)}, bf16[528,256]{1,0:T(8,128)(2,1)S(1)}, u32[]{:S(2)}, u32[]{:S(2)}) %collective-permute-start.4) | collective-permute-done | bytes 270368 | tf_op jit(solution)/shard_map/ppermute | solution.py:392
  31.0 0.4 %collective-permute-start.5 = (bf16[528,256]{1,0:T(8,128)(2,1)S(1)}, bf16[528,256]{1,0:T(8,128)(2,1)S(1)}, u32[]{:S(2)}, u32[]{:S(2)}) collective-permute-start(bf16[528,256]{1,0:T(8,128)(2,1)S(1)} %collective-permute-done.1.refs_2_), channel_id=1, source_target_pairs={{0,1},{1,0},{2,3},{3,2},{4,5},{5,4},{6,7},{7,6},{8,9},{9,8},{10,11... | collective-permute-start | bytes 811016 | tf_op jit(solution)/shard_map/ppermute | solution.py:376
  31.4 0.1 collective-permute-start.6
  31.5 1.1 %collective-permute-done.5.refs_4_ = bf16[528,256]{1,0:T(8,128)(2,1)S(1)} collective-permute-done((bf16[528,256]{1,0:T(8,128)(2,1)S(1)}, bf16[528,256]{1,0:T(8,128)(2,1)S(1)}, u32[]{:S(2)}, u32[]{:S(2)}) %collective-permute-start.5) | collective-permute-done | bytes 270368 | tf_op jit(solution)/shard_map/ppermute | solution.py:376
  32.6 0.4 collective-permute-done.6.refs_5_
  33.0 0.8 %attend_last.1.a_ref = bf16[512,256]{1,0:T(8,128)(2,1)S(1)} custom-call(bf16[512,256]{1,0:T(8,128)(2,1)S(1)} %project_query.1.refs_0_, s32[1,512]{1,0:T(1,128)S(1)} %bitcast.9, bf16[528,256]{1,0:T(8,128)(2,1)S(1)} %collective-permute-done.1.refs_2_, bf16[528,256]{1,0:T(8,128)(2,1)S(1)} %collective-permute-done.4.refs_3_, ...), custom_call_target="tpu_custom_call" | custom-call | flops 536870912 | bytes 1048576 | tf_op jit(solution)/shard_map/attend_last/pallas_call | solution.py:248
  33.8 0.4 %collective-permute-start.9 = (bf16[512,256]{1,0:T(8,128)(2,1)S(1)}, bf16[512,256]{1,0:T(8,128)(2,1)S(1)}, u32[]{:S(2)}, u32[]{:S(2)}) collective-permute-start(bf16[512,256]{1,0:T(8,128)(2,1)S(1)} %attend_last.1.a_ref), channel_id=1, source_target_pairs={{0,1},{1,0},{2,3},{3,2},{4,5},{5,4},{6,7},{7,6},{8,9},{9,8},{10,11... | collective-permute-start | bytes 786440 | tf_op jit(solution)/shard_map/ppermute | solution.py:376
  34.3 1.5 %project_own.1.quant_ref = bf16[512,4096]{1,0:T(8,128)(2,1)S(1)} custom-call(bf16[512,256]{1,0:T(8,128)(2,1)S(1)} %attend_last.1.a_ref, bf16[256,4096]{1,0:T(8,128)(2,1)S(1)} %copy-done.1, bf16[512,4096]{1,0:T(8,128)(2,1)S(1)} %get-tuple-element.30.sum_ref), custom_call_target="tpu_custom_call" | custom-call | flops 1073741824 | bytes 10485760 | tf_op jit(solution)/shard_map/project_own/pallas_call | solution.py:319
  35.8 4.3 %project_out.1 = bf16[512,4096]{1,0:T(8,128)(2,1)} custom-call(bf16[512,256]{1,0:T(8,128)(2,1)S(1)} %collective-permute-done.9.b_ref, bf16[256,4096]{1,0:T(8,128)(2,1)S(1)} %collective-permute-done.10.wb_ref, bf16[512,4096]{1,0:T(8,128)(2,1)S(1)} %project_own.1.quant_ref, f32[512,4096]{1,0:T(8,128)S(1)} %get-tuple-element.32.x_ref, ...), custom_call_target="tpu_custom_call" | custom-call | flops 1073741824 | bytes 10485760 | tf_op jit(solution)/shard_map/project_out/pallas_call | solution.py:358
  (17 shorter events, 0.1 us)
Async XLA Ops:
  0.0 8.7 %copy-start = (bf16[4096,256]{1,0:T(8,128)(2,1)S(1)}, bf16[4096,256]{1,0:T(8,128)(2,1)}, u32[]{:S(2)}) copy-start(bf16[4096,256]{1,0:T(8,128)(2,1)} %w_ref.4) | copy-start | bytes 6291460
  0.0 35.8 %collective-permute-start.10 = (bf16[256,4096]{1,0:T(8,128)(2,1)}, bf16[256,4096]{1,0:T(8,128)(2,1)S(1)}, u32[]{:S(2)}, u32[]{:S(2)}) collective-permute-start(bf16[256,4096]{1,0:T(8,128)(2,1)} %w_ref.5), channel_id=1, source_target_pairs={{0,1},{1,0},{2,3},{3,2},{4,5},{5,4},{6,7},{7,6},{8,9},{9,8},{10,11... | collective-permute-start | bytes 6291464 | tf_op jit(solution)/shard_map/ppermute | solution.py:376
  6.9 13.1 %copy-start.2 = (s32[512,32]{0,1:T(8,128)S(1)}, s32[512,32]{0,1:T(8,128)}, u32[]{:S(2)}) copy-start(s32[512,32]{0,1:T(8,128)} %param.14) | copy-start | bytes 196612
  6.9 13.1 %copy-start.3 = (s32[512,32]{0,1:T(8,128)S(1)}, s32[512,32]{0,1:T(8,128)}, u32[]{:S(2)}) copy-start(s32[512,32]{0,1:T(8,128)} %param.15) | copy-start | bytes 196612
  6.9 8.0 %collective-permute-start = (bf16[528,256]{1,0:T(8,128)(2,1)S(1)}, bf16[528,256]{1,0:T(8,128)(2,1)S(1)}, u32[]{:S(2)}, u32[]{:S(2)}) collective-permute-start(bf16[528,256]{1,0:T(8,128)(2,1)S(1)} %get-tuple-element.21.refs_2_), channel_id=1, source_target_pairs={{0,4},{1,5},{2,6},{3,7},{4,8},{5,9},{6,10},{7,11},{8,12},{9,13},{1... | collective-permute-start | bytes 811016 | tf_op jit(solution)/shard_map/ppermute | solution.py:385
  8.3 10.5 %collective-permute-start.2 = (bf16[528,256]{1,0:T(8,128)(2,1)S(1)}, bf16[528,256]{1,0:T(8,128)(2,1)S(1)}, u32[]{:S(2)}, u32[]{:S(2)}) collective-permute-start(bf16[528,256]{1,0:T(8,128)(2,1)S(1)} %get-tuple-element.21.refs_2_), channel_id=1, source_target_pairs={{0,1},{1,0},{2,3},{3,2},{4,5},{5,4},{6,7},{7,6},{8,9},{9,8},{10,11... | collective-permute-start | bytes 811016 | tf_op jit(solution)/shard_map/ppermute | solution.py:376
  10.0 13.2 %copy-start.4 = (s32[512]{0:T(512)S(1)}, s32[512]{0:T(512)}, u32[]{:S(2)}) copy-start(s32[512]{0:T(512)} %param.10) | copy-start | bytes 6148
  14.9 9.9 %collective-permute-start.7 = (bf16[528,256]{1,0:T(8,128)(2,1)S(1)}, bf16[528,256]{1,0:T(8,128)(2,1)S(1)}, u32[]{:S(2)}, u32[]{:S(2)}) collective-permute-start(bf16[528,256]{1,0:T(8,128)(2,1)S(1)} %collective-permute-done.refs_3_), channel_id=1, source_target_pairs={{0,1},{1,0},{2,3},{3,2},{4,6},{5,7},{6,8},{7,9},{8,10},{9,11},{10,... | collective-permute-start | bytes 811016 | tf_op jit(solution)/shard_map/ppermute | solution.py:385
  16.2 7.0 %collective-permute-start.3 = (bf16[528,256]{1,0:T(8,128)(2,1)S(1)}, bf16[528,256]{1,0:T(8,128)(2,1)S(1)}, u32[]{:S(2)}, u32[]{:S(2)}) collective-permute-start(bf16[528,256]{1,0:T(8,128)(2,1)S(1)} %collective-permute-done.refs_3_), channel_id=1, source_target_pairs={{0,1},{1,0},{2,3},{3,2},{4,5},{5,4},{6,7},{7,6},{8,9},{9,8},{10,11... | collective-permute-start | bytes 811016 | tf_op jit(solution)/shard_map/ppermute | solution.py:376
  17.4 13.5 %collective-permute-start.4 = (bf16[528,256]{1,0:T(8,128)(2,1)S(1)}, bf16[528,256]{1,0:T(8,128)(2,1)S(1)}, u32[]{:S(2)}, u32[]{:S(2)}) collective-permute-start(bf16[528,256]{1,0:T(8,128)(2,1)S(1)} %broadcast_select_fusion), channel_id=1, source_target_pairs={{0,2},{2,0},{4,6},{6,4},{8,10},{10,8},{12,14},{14,12},{1,3},{3,1},... | collective-permute-start | bytes 811016 | tf_op jit(solution)/shard_map/ppermute | solution.py:392
  18.8 12.2 %collective-permute-start.1 = (bf16[528,256]{1,0:T(8,128)(2,1)S(1)}, bf16[528,256]{1,0:T(8,128)(2,1)S(1)}, u32[]{:S(2)}, u32[]{:S(2)}) collective-permute-start(bf16[528,256]{1,0:T(8,128)(2,1)S(1)} %collective-permute-done.refs_3_), channel_id=1, source_target_pairs={{0,1},{1,0},{2,3},{3,2},{4,8},{5,9},{6,10},{7,11},{8,12},{9,13},{1... | collective-permute-start | bytes 811016 | tf_op jit(solution)/shard_map/ppermute | solution.py:385
  23.1 11.1 %copy-start.1 = (bf16[256,4096]{1,0:T(8,128)(2,1)S(1)}, bf16[256,4096]{1,0:T(8,128)(2,1)}, u32[]{:S(2)}) copy-start(bf16[256,4096]{1,0:T(8,128)(2,1)} %w_ref.5) | copy-start | bytes 6291460
  24.8 6.7 %collective-permute-start.8 = (bf16[528,256]{1,0:T(8,128)(2,1)S(1)}, bf16[528,256]{1,0:T(8,128)(2,1)S(1)}, u32[]{:S(2)}, u32[]{:S(2)}) collective-permute-start(bf16[528,256]{1,0:T(8,128)(2,1)S(1)} %collective-permute-done.7.refs_2_), channel_id=1, source_target_pairs={{0,1},{1,0},{2,3},{3,2},{4,5},{5,4},{6,7},{7,6},{8,9},{9,8},{10,11... | collective-permute-start | bytes 811016 | tf_op jit(solution)/shard_map/ppermute | solution.py:376
  31.0 1.6 %collective-permute-start.5 = (bf16[528,256]{1,0:T(8,128)(2,1)S(1)}, bf16[528,256]{1,0:T(8,128)(2,1)S(1)}, u32[]{:S(2)}, u32[]{:S(2)}) collective-permute-start(bf16[528,256]{1,0:T(8,128)(2,1)S(1)} %collective-permute-done.1.refs_2_), channel_id=1, source_target_pairs={{0,1},{1,0},{2,3},{3,2},{4,5},{5,4},{6,7},{7,6},{8,9},{9,8},{10,11... | collective-permute-start | bytes 811016 | tf_op jit(solution)/shard_map/ppermute | solution.py:376
  31.4 1.6 %collective-permute-start.6 = (bf16[528,256]{1,0:T(8,128)(2,1)S(1)}, bf16[528,256]{1,0:T(8,128)(2,1)S(1)}, u32[]{:S(2)}, u32[]{:S(2)}) collective-permute-start(bf16[528,256]{1,0:T(8,128)(2,1)S(1)} %collective-permute-done.4.refs_3_), channel_id=1, source_target_pairs={{0,1},{1,0},{2,3},{3,2},{4,5},{5,4},{6,7},{7,6},{8,9},{9,8},{10,11... | collective-permute-start | bytes 811016 | tf_op jit(solution)/shard_map/ppermute | solution.py:376
  33.8 2.0 %collective-permute-start.9 = (bf16[512,256]{1,0:T(8,128)(2,1)S(1)}, bf16[512,256]{1,0:T(8,128)(2,1)S(1)}, u32[]{:S(2)}, u32[]{:S(2)}) collective-permute-start(bf16[512,256]{1,0:T(8,128)(2,1)S(1)} %attend_last.1.a_ref), channel_id=1, source_target_pairs={{0,1},{1,0},{2,3},{3,2},{4,5},{5,4},{6,7},{7,6},{8,9},{9,8},{10,11... | collective-permute-start | bytes 786440 | tf_op jit(solution)/shard_map/ppermute | solution.py:376

commit v17 on v16

--- a/solution.py
+++ b/solution.py
@@ -32,19 +32,19 @@
         ]
 
     def early_tokens(half):
-        return cut(x_ref, xs, half * part, part, 8 - 4 * half, 8 * half)
+        return cut(x_ref, xs, half * part, part, 4, 4 * half)
 
     def late_tokens():
-        return cut(x_ref, xs, tile, tile, 1, 12)
+        return cut(x_ref, xs, tile, tile, 2, 8)
 
     def weights():
-        return cut(w_ref, ws, 0, width, 4, 14)
+        return cut(w_ref, ws, 0, width, 4, 10)
 
     def gain_copy():
-        return pltpu.make_async_copy(gain_hbm, gain_ref, sems.at[18])
+        return pltpu.make_async_copy(gain_hbm, gain_ref, sems.at[14])
 
     def segments_copy():
-        return pltpu.make_async_copy(seg_hbm, seg_ref, sems.at[19])
+        return pltpu.make_async_copy(seg_hbm, seg_ref, sems.at[15])
 
     for copy in early_tokens(0) + early_tokens(1) + [gain_copy()] + weights() + late_tokens() + [segments_copy()]:
         copy.start()
@@ -64,32 +64,26 @@
         spread = jnp.sum(square, axis=1, keepdims=True) * (1.0 / width)
         return mean, jnp.broadcast_to(lax.rsqrt(spread + 1e-05), (part, LANES))
 
-    def project(first, halves):
-        mean = jnp.concatenate([h[0] for h in halves], axis=0)
-        scale = jnp.concatenate([h[1] for h in halves], axis=0)
-        kv = jnp.zeros((tile, ws.shape[1]), jnp.float32)
-        span = slice(first, first + tile)
-        for start in range(0, width, HD):
-            if first == 0 and start % (width // 4) == 0:
-                weights()[4 * start // width].wait()
-            for at in (start, start + LANES):
-                normed = (wide(first, tile, at) - mean) * scale * gain_ref[:, at:at + LANES]
-                normed_ref[span, at:at + LANES] = normed.astype(jnp.bfloat16)
-            kv = kv + jnp.dot(
-                normed_ref[span, start:start + HD], ws[start:start + HD, :], preferred_element_type=jnp.float32
-            )
-        msg_ref[span, :] = kv.astype(jnp.bfloat16)
-
-    halves = []
+    pieces = []
     for half in range(2):
         for copy in early_tokens(half):
             copy.wait()
-        halves.append(stats(half * part))
-    gain_copy().wait()
-    project(0, halves)
+        pieces.append(stats(half * part))
     for copy in late_tokens():
         copy.wait()
-    project(tile, [stats(tile), stats(tile + part)])
+    pieces += [stats(tile), stats(tile + part)]
+    mean = [jnp.concatenate([p[0] for p in pieces[i:i + 2]], axis=0) for i in (0, 2)]
+    scale = [jnp.concatenate([p[1] for p in pieces[i:i + 2]], axis=0) for i in (0, 2)]
+    for copy in [gain_copy()] + weights():
+        copy.wait()
+    kv = jnp.zeros((rows, ws.shape[1]), jnp.float32)
+    for start in range(0, width, HD):
+        for half in range(2):
+            for at in (start, start + LANES):
+                normed = (wide(half * tile, tile, at) - mean[half]) * scale[half] * gain_ref[:, at:at + LANES]
+                normed_ref[half * tile:(half + 1) * tile, at:at + LANES] = normed.astype(jnp.bfloat16)
+        kv = kv + jnp.dot(normed_ref[:, start:start + HD], ws[start:start + HD, :], preferred_element_type=jnp.float32)
+    msg_ref[:rows, :] = kv.astype(jnp.bfloat16)
     segments_copy().wait()
     seg = seg_ref[...].astype(jnp.float32)
     low = jnp.broadcast_to(seg[:, :HD], (8, HD))
@@ -119,7 +113,7 @@
             pltpu.VMEM((width, cols), jnp.bfloat16),
             pltpu.VMEM((1, width), jnp.float32),
             pltpu.VMEM((1, rows), jnp.int32),
-            pltpu.SemaphoreType.DMA((20,)),
+            pltpu.SemaphoreType.DMA((16,)),
         ],
         compiler_params=pltpu.CompilerParams(vmem_limit_bytes=24 * MIB),
         cost_estimate=pl.CostEstimate(
@@ -301,15 +295,25 @@
     return jnp.minimum(jnp.maximum(value.astype(jnp.bfloat16), -bound), bound)
 
 
+def in_tiles(a_ref, w_ref, finish):
+    rows = a_ref.shape[0]
+    tile = rows // 2
+    waiting = None
+    for at in range(0, w_ref.shape[1], HD):
+        for start in range(0, rows, tile):
+            span, cols = slice(start, start + tile), slice(at, at + HD)
+            term = jnp.dot(a_ref[span, :], w_ref[:, cols], preferred_element_type=jnp.float32)
+            if waiting is not None:
+                finish(*waiting)
+            waiting = (span, cols, term)
+    finish(*waiting)
+
+
 def own_kernel(a_ref, w_ref, sum_ref, out_ref):
-    rows, width = out_ref.shape
-    tile = rows // 2
-    for at in range(0, width, HD):
-        cols = slice(at, at + HD)
-        for start in range(0, rows, tile):
-            span = slice(start, start + tile)
-            term = jnp.dot(a_ref[span, :], w_ref[:, cols], preferred_element_type=jnp.float32)
-            out_ref[span, cols] = clip(term, sum_ref[span, cols])
+    def finish(span, cols, term):
+        out_ref[span, cols] = clip(term, sum_ref[span, cols])
+
+    in_tiles(a_ref, w_ref, finish)
 
 
 def project_own(attended, w_out, sum_bound):
@@ -331,20 +335,18 @@
 
 def output_kernel(b_ref, wb_ref, quant_ref, x_ref, sum_ref, last_ref, out_ref, staged, sems):
     rows, width = x_ref.shape
-    tile = rows // 2
 
     def copy(index):
         span = slice(index * HD, (index + 1) * HD)
         return pltpu.make_async_copy(staged.at[:, span], out_ref.at[:, span], sems.at[index])
 
-    for index in range(width // HD):
-        cols = slice(index * HD, (index + 1) * HD)
-        for start in range(0, rows, tile):
-            span = slice(start, start + tile)
-            term = jnp.dot(b_ref[span, :], wb_ref[:, cols], preferred_element_type=jnp.float32)
-            quant = clip(term, sum_ref[span, cols]).astype(jnp.float32) + quant_ref[span, cols].astype(jnp.float32)
-            staged[span, cols] = clip(x_ref[span, cols] + quant, last_ref[span, cols])
-        copy(index).start()
+    def finish(span, cols, term):
+        quant = clip(term, sum_ref[span, cols]).astype(jnp.float32) + quant_ref[span, cols].astype(jnp.float32)
+        staged[span, cols] = clip(x_ref[span, cols] + quant, last_ref[span, cols])
+        if span.stop == rows:
+            copy(cols.start // HD).start()
+
+    in_tiles(b_ref, wb_ref, finish)
     for index in range(width // HD):
         copy(index).wait()
 

time: 40.4 us -> 40.7 us (level)
  no operation moved by 1% of the time
where the time goes in v17:
time: 40.7 us; the launch traced here: 40.5 us
  Pallas kernels  18.9 us (46%)
  starting transfers between devices  11 us (27%)
  waiting for transfers between devices  10.3 us (25%)
    pallas_call x1, Pallas kernels, norm_kv(): pl.pallas_call(norm_kv_kernel, in_specs=[hbm] * 4, out_specs=[vmem, vmem]...  6.44 us
    ppermute x7, starting transfers between devices, swap_cores(): return lax.ppermute(x, 'tp', [(0, 1), (1, 0)])  5.79 us
    ppermute x3, waiting for transfers between devices, shift(): return lax.ppermute(x, ('seq', 'tp'), pairs)  4.94 us
    pallas_call x1, Pallas kernels, project_out(): pl.pallas_call(output_kernel, in_specs=[vmem] * len(operands), out_specs=...  4.32 us
    ppermute x3, starting transfers between devices, shift(): return lax.ppermute(x, ('seq', 'tp'), pairs)  3.88 us
    ppermute x1, waiting for transfers between devices, on_device(): lax.ppermute(jnp.where(odd, held, message), 'seq', [(i, i ^ 1) for i in r...  3.84 us
    pallas_call x1, Pallas kernels, spread_bounds(): pl.pallas_call(bounds_kernel, in_specs=[vmem, vmem, pl.BlockSpec(memory_s...  3.05 us
    pallas_call x3, Pallas kernels, attend(): pl.pallas_call(functools.partial(attend_kernel, plan, first, last), in_sp...  2.31 us
  transfers between devices with their start and end apart: 11, of which 4 were waited for; matrix products, arithmetic and copies ran while one was open for 0% of the time, Pallas kernels for 36%

profile of v17, /device:TPU:11, one launch (start us, length us, event | category | flops | bytes accessed | tf_op | source)
XLA Modules:
  0.0 40.5 jit_solution(15893193714486465602)
XLA Ops:
  0.0 0.7 %collective-permute-start.10 = (bf16[256,4096]{1,0:T(8,128)(2,1)}, bf16[256,4096]{1,0:T(8,128)(2,1)S(1)}, u32[]{:S(2)}, u32[]{:S(2)}) collective-permute-start(bf16[256,4096]{1,0:T(8,128)(2,1)} %w_ref.5), channel_id=1, source_target_pairs={{0,1},{1,0},{2,3},{3,2},{4,5},{5,4},{6,7},{7,6},{8,9},{9,8},{10,11... | collective-permute-start | bytes 6291464 | tf_op jit(solution)/shard_map/ppermute | solution.py:378
  0.7 6.4 %norm_kv.1 = (bf16[528,256]{1,0:T(8,128)(2,1)S(1)}, bf16[512,4096]{1,0:T(8,128)(2,1)S(1)}) custom-call(bf16[512,4096]{1,0:T(8,128)(2,1)} %x_ref.3, f32[1,4096]{1,0:T(1,128)} %bitcast.10, bf16[4096,256]{1,0:T(8,128)(2,1)} %w_ref.3, s32[1,512]{1,0:T(1,128)} %bitcast.6), custom_call_target="tpu_custom_call" | custom-call | flops 1073741824 | bytes 10485760 | tf_op jit(solution)/shard_map/norm_kv/pallas_call | solution.py:106
  7.1 0.0 copy-start.2
  7.1 0.0 copy-start.3
  7.2 1.3 %collective-permute-start = (bf16[528,256]{1,0:T(8,128)(2,1)S(1)}, bf16[528,256]{1,0:T(8,128)(2,1)S(1)}, u32[]{:S(2)}, u32[]{:S(2)}) collective-permute-start(bf16[528,256]{1,0:T(8,128)(2,1)S(1)} %get-tuple-element.21.refs_2_), channel_id=1, source_target_pairs={{0,4},{1,5},{2,6},{3,7},{4,8},{5,9},{6,10},{7,11},{8,12},{9,13},{1... | collective-permute-start | bytes 811016 | tf_op jit(solution)/shard_map/ppermute | solution.py:387
  8.5 0.4 %collective-permute-start.2 = (bf16[528,256]{1,0:T(8,128)(2,1)S(1)}, bf16[528,256]{1,0:T(8,128)(2,1)S(1)}, u32[]{:S(2)}, u32[]{:S(2)}) collective-permute-start(bf16[528,256]{1,0:T(8,128)(2,1)S(1)} %get-tuple-element.21.refs_2_), channel_id=1, source_target_pairs={{0,1},{1,0},{2,3},{3,2},{4,5},{5,4},{6,7},{7,6},{8,9},{9,8},{10,11... | collective-permute-start | bytes 811016 | tf_op jit(solution)/shard_map/ppermute | solution.py:378
  8.9 1.2 %project_query.1.refs_0_ = bf16[512,256]{1,0:T(8,128)(2,1)S(1)} custom-call(bf16[512,4096]{1,0:T(8,128)(2,1)S(1)} %get-tuple-element.22.x_ref, bf16[4096,256]{1,0:T(8,128)(2,1)S(1)} %copy-done), custom_call_target="tpu_custom_call" | custom-call | flops 1073741824 | bytes 6291456 | tf_op jit(solution)/shard_map/project_query/pallas_call | solution.py:134
  10.2 4.9 %collective-permute-done.refs_3_ = bf16[528,256]{1,0:T(8,128)(2,1)S(1)} collective-permute-done((bf16[528,256]{1,0:T(8,128)(2,1)S(1)}, bf16[528,256]{1,0:T(8,128)(2,1)S(1)}, u32[]{:S(2)}, u32[]{:S(2)}) %collective-permute-start) | collective-permute-done | bytes 270368 | tf_op jit(solution)/shard_map/ppermute | solution.py:387
  15.2 1.2 %collective-permute-start.7 = (bf16[528,256]{1,0:T(8,128)(2,1)S(1)}, bf16[528,256]{1,0:T(8,128)(2,1)S(1)}, u32[]{:S(2)}, u32[]{:S(2)}) collective-permute-start(bf16[528,256]{1,0:T(8,128)(2,1)S(1)} %collective-permute-done.refs_3_), channel_id=1, source_target_pairs={{0,1},{1,0},{2,3},{3,2},{4,6},{5,7},{6,8},{7,9},{8,10},{9,11},{10,... | collective-permute-start | bytes 811016 | tf_op jit(solution)/shard_map/ppermute | solution.py:387
  16.4 1.2 %collective-permute-start.3 = (bf16[528,256]{1,0:T(8,128)(2,1)S(1)}, bf16[528,256]{1,0:T(8,128)(2,1)S(1)}, u32[]{:S(2)}, u32[]{:S(2)}) collective-permute-start(bf16[528,256]{1,0:T(8,128)(2,1)S(1)} %collective-permute-done.refs_3_), channel_id=1, source_target_pairs={{0,1},{1,0},{2,3},{3,2},{4,5},{5,4},{6,7},{7,6},{8,9},{9,8},{10,11... | collective-permute-start | bytes 811016 | tf_op jit(solution)/shard_map/ppermute | solution.py:378
  17.7 1.3 %collective-permute-start.4 = (bf16[528,256]{1,0:T(8,128)(2,1)S(1)}, bf16[528,256]{1,0:T(8,128)(2,1)S(1)}, u32[]{:S(2)}, u32[]{:S(2)}) collective-permute-start(bf16[528,256]{1,0:T(8,128)(2,1)S(1)} %broadcast_select_fusion), channel_id=1, source_target_pairs={{0,2},{2,0},{4,6},{6,4},{8,10},{10,8},{12,14},{14,12},{1,3},{3,1},... | collective-permute-start | bytes 811016 | tf_op jit(solution)/shard_map/ppermute | solution.py:394
  19.0 1.3 %collective-permute-start.1 = (bf16[528,256]{1,0:T(8,128)(2,1)S(1)}, bf16[528,256]{1,0:T(8,128)(2,1)S(1)}, u32[]{:S(2)}, u32[]{:S(2)}) collective-permute-start(bf16[528,256]{1,0:T(8,128)(2,1)S(1)} %collective-permute-done.refs_3_), channel_id=1, source_target_pairs={{0,1},{1,0},{2,3},{3,2},{4,8},{5,9},{6,10},{7,11},{8,12},{9,13},{1... | collective-permute-start | bytes 811016 | tf_op jit(solution)/shard_map/ppermute | solution.py:387
  20.3 3.0 %spread_bounds.1 = (bf16[512,4096]{1,0:T(8,128)(2,1)S(1)}, bf16[512,4096]{1,0:T(8,128)(2,1)S(1)}, f32[512,4096]{1,0:T(8,128)S(1)}) custom-call(s32[32,512]{1,0:T(8,128)S(1)} %bitcast.4, s32[32,512]{1,0:T(8,128)S(1)} %bitcast.5, bf16[512,4096]{1,0:T(8,128)(2,1)} %x_ref.3), custom_call_target="tpu_custom_call" | custom-call | flops 16777216 | bytes 131072 | tf_op jit(solution)/shard_map/spread_bounds/pallas_call | solution.py:282
  23.4 1.5 %attend_first.1.refs_4_ = f32[512,640]{1,0:T(8,128)S(1)} custom-call(bf16[512,256]{1,0:T(8,128)(2,1)S(1)} %project_query.1.refs_0_, s32[1,512]{1,0:T(1,128)S(1)} %bitcast.7, bf16[528,256]{1,0:T(8,128)(2,1)S(1)} %get-tuple-element.21.refs_2_, bf16[528,256]{1,0:T(8,128)(2,1)S(1)} %collective-permute-done.refs_3_, ...), custom_call_target="tpu_custom_call" | custom-call | flops 536870912 | bytes 1048576 | tf_op jit(solution)/shard_map/attend_first/pallas_call | solution.py:242
  24.9 2.5 %collective-permute-start.8 = (bf16[528,256]{1,0:T(8,128)(2,1)S(1)}, bf16[528,256]{1,0:T(8,128)(2,1)S(1)}, u32[]{:S(2)}, u32[]{:S(2)}) collective-permute-start(bf16[528,256]{1,0:T(8,128)(2,1)S(1)} %collective-permute-done.7.refs_2_), channel_id=1, source_target_pairs={{0,1},{1,0},{2,3},{3,2},{4,5},{5,4},{6,7},{7,6},{8,9},{9,8},{10,11... | collective-permute-start | bytes 811016 | tf_op jit(solution)/shard_map/ppermute | solution.py:378
  27.4 3.8 %collective-permute-done.4.refs_3_ = bf16[528,256]{1,0:T(8,128)(2,1)S(1)} collective-permute-done((bf16[528,256]{1,0:T(8,128)(2,1)S(1)}, bf16[528,256]{1,0:T(8,128)(2,1)S(1)}, u32[]{:S(2)}, u32[]{:S(2)}) %collective-permute-start.4) | collective-permute-done | bytes 270368 | tf_op jit(solution)/shard_map/ppermute | solution.py:394
  31.2 0.4 %collective-permute-start.5 = (bf16[528,256]{1,0:T(8,128)(2,1)S(1)}, bf16[528,256]{1,0:T(8,128)(2,1)S(1)}, u32[]{:S(2)}, u32[]{:S(2)}) collective-permute-start(bf16[528,256]{1,0:T(8,128)(2,1)S(1)} %collective-permute-done.1.refs_2_), channel_id=1, source_target_pairs={{0,1},{1,0},{2,3},{3,2},{4,5},{5,4},{6,7},{7,6},{8,9},{9,8},{10,11... | collective-permute-start | bytes 811016 | tf_op jit(solution)/shard_map/ppermute | solution.py:378
  31.6 0.1 collective-permute-start.6
  31.7 1.1 %collective-permute-done.5.refs_4_ = bf16[528,256]{1,0:T(8,128)(2,1)S(1)} collective-permute-done((bf16[528,256]{1,0:T(8,128)(2,1)S(1)}, bf16[528,256]{1,0:T(8,128)(2,1)S(1)}, u32[]{:S(2)}, u32[]{:S(2)}) %collective-permute-start.5) | collective-permute-done | bytes 270368 | tf_op jit(solution)/shard_map/ppermute | solution.py:378
  32.8 0.4 collective-permute-done.6.refs_5_
  33.2 0.8 %attend_last.1.a_ref = bf16[512,256]{1,0:T(8,128)(2,1)S(1)} custom-call(bf16[512,256]{1,0:T(8,128)(2,1)S(1)} %project_query.1.refs_0_, s32[1,512]{1,0:T(1,128)S(1)} %bitcast.9, bf16[528,256]{1,0:T(8,128)(2,1)S(1)} %collective-permute-done.1.refs_2_, bf16[528,256]{1,0:T(8,128)(2,1)S(1)} %collective-permute-done.4.refs_3_, ...), custom_call_target="tpu_custom_call" | custom-call | flops 536870912 | bytes 1048576 | tf_op jit(solution)/shard_map/attend_last/pallas_call | solution.py:242
  34.0 0.4 %collective-permute-start.9 = (bf16[512,256]{1,0:T(8,128)(2,1)S(1)}, bf16[512,256]{1,0:T(8,128)(2,1)S(1)}, u32[]{:S(2)}, u32[]{:S(2)}) collective-permute-start(bf16[512,256]{1,0:T(8,128)(2,1)S(1)} %attend_last.1.a_ref), channel_id=1, source_target_pairs={{0,1},{1,0},{2,3},{3,2},{4,5},{5,4},{6,7},{7,6},{8,9},{9,8},{10,11... | collective-permute-start | bytes 786440 | tf_op jit(solution)/shard_map/ppermute | solution.py:378
  34.5 1.5 %project_own.1.quant_ref = bf16[512,4096]{1,0:T(8,128)(2,1)S(1)} custom-call(bf16[512,256]{1,0:T(8,128)(2,1)S(1)} %attend_last.1.a_ref, bf16[256,4096]{1,0:T(8,128)(2,1)S(1)} %copy-done.1, bf16[512,4096]{1,0:T(8,128)(2,1)S(1)} %get-tuple-element.30.sum_ref), custom_call_target="tpu_custom_call" | custom-call | flops 1073741824 | bytes 10485760 | tf_op jit(solution)/shard_map/project_own/pallas_call | solution.py:323
  36.0 4.3 %project_out.1 = bf16[512,4096]{1,0:T(8,128)(2,1)} custom-call(bf16[512,256]{1,0:T(8,128)(2,1)S(1)} %collective-permute-done.9.b_ref, bf16[256,4096]{1,0:T(8,128)(2,1)S(1)} %collective-permute-done.10.wb_ref, bf16[512,4096]{1,0:T(8,128)(2,1)S(1)} %project_own.1.quant_ref, f32[512,4096]{1,0:T(8,128)S(1)} %get-tuple-element.32.x_ref, ...), custom_call_target="tpu_custom_call" | custom-call | flops 1073741824 | bytes 10485760 | tf_op jit(solution)/shard_map/project_out/pallas_call | solution.py:360
  (17 shorter events, 0.1 us)
Async XLA Ops:
  0.0 8.9 %copy-start = (bf16[4096,256]{1,0:T(8,128)(2,1)S(1)}, bf16[4096,256]{1,0:T(8,128)(2,1)}, u32[]{:S(2)}) copy-start(bf16[4096,256]{1,0:T(8,128)(2,1)} %w_ref.4) | copy-start | bytes 6291460
  0.0 36.0 %collective-permute-start.10 = (bf16[256,4096]{1,0:T(8,128)(2,1)}, bf16[256,4096]{1,0:T(8,128)(2,1)S(1)}, u32[]{:S(2)}, u32[]{:S(2)}) collective-permute-start(bf16[256,4096]{1,0:T(8,128)(2,1)} %w_ref.5), channel_id=1, source_target_pairs={{0,1},{1,0},{2,3},{3,2},{4,5},{5,4},{6,7},{7,6},{8,9},{9,8},{10,11... | collective-permute-start | bytes 6291464 | tf_op jit(solution)/shard_map/ppermute | solution.py:378
  7.1 13.1 %copy-start.2 = (s32[512,32]{0,1:T(8,128)S(1)}, s32[512,32]{0,1:T(8,128)}, u32[]{:S(2)}) copy-start(s32[512,32]{0,1:T(8,128)} %param.14) | copy-start | bytes 196612
  7.1 13.1 %copy-start.3 = (s32[512,32]{0,1:T(8,128)S(1)}, s32[512,32]{0,1:T(8,128)}, u32[]{:S(2)}) copy-start(s32[512,32]{0,1:T(8,128)} %param.15) | copy-start | bytes 196612
  7.2 8.0 %collective-permute-start = (bf16[528,256]{1,0:T(8,128)(2,1)S(1)}, bf16[528,256]{1,0:T(8,128)(2,1)S(1)}, u32[]{:S(2)}, u32[]{:S(2)}) collective-permute-start(bf16[528,256]{1,0:T(8,128)(2,1)S(1)} %get-tuple-element.21.refs_2_), channel_id=1, source_target_pairs={{0,4},{1,5},{2,6},{3,7},{4,8},{5,9},{6,10},{7,11},{8,12},{9,13},{1... | collective-permute-start | bytes 811016 | tf_op jit(solution)/shard_map/ppermute | solution.py:387
  8.5 10.5 %collective-permute-start.2 = (bf16[528,256]{1,0:T(8,128)(2,1)S(1)}, bf16[528,256]{1,0:T(8,128)(2,1)S(1)}, u32[]{:S(2)}, u32[]{:S(2)}) collective-permute-start(bf16[528,256]{1,0:T(8,128)(2,1)S(1)} %get-tuple-element.21.refs_2_), channel_id=1, source_target_pairs={{0,1},{1,0},{2,3},{3,2},{4,5},{5,4},{6,7},{7,6},{8,9},{9,8},{10,11... | collective-permute-start | bytes 811016 | tf_op jit(solution)/shard_map/ppermute | solution.py:378
  10.2 13.2 %copy-start.4 = (s32[512]{0:T(512)S(1)}, s32[512]{0:T(512)}, u32[]{:S(2)}) copy-start(s32[512]{0:T(512)} %param.10) | copy-start | bytes 6148
  15.2 9.7 %collective-permute-start.7 = (bf16[528,256]{1,0:T(8,128)(2,1)S(1)}, bf16[528,256]{1,0:T(8,128)(2,1)S(1)}, u32[]{:S(2)}, u32[]{:S(2)}) collective-permute-start(bf16[528,256]{1,0:T(8,128)(2,1)S(1)} %collective-permute-done.refs_3_), channel_id=1, source_target_pairs={{0,1},{1,0},{2,3},{3,2},{4,6},{5,7},{6,8},{7,9},{8,10},{9,11},{10,... | collective-permute-start | bytes 811016 | tf_op jit(solution)/shard_map/ppermute | solution.py:387
  16.4 7.0 %collective-permute-start.3 = (bf16[528,256]{1,0:T(8,128)(2,1)S(1)}, bf16[528,256]{1,0:T(8,128)(2,1)S(1)}, u32[]{:S(2)}, u32[]{:S(2)}) collective-permute-start(bf16[528,256]{1,0:T(8,128)(2,1)S(1)} %collective-permute-done.refs_3_), channel_id=1, source_target_pairs={{0,1},{1,0},{2,3},{3,2},{4,5},{5,4},{6,7},{7,6},{8,9},{9,8},{10,11... | collective-permute-start | bytes 811016 | tf_op jit(solution)/shard_map/ppermute | solution.py:378
  17.7 13.5 %collective-permute-start.4 = (bf16[528,256]{1,0:T(8,128)(2,1)S(1)}, bf16[528,256]{1,0:T(8,128)(2,1)S(1)}, u32[]{:S(2)}, u32[]{:S(2)}) collective-permute-start(bf16[528,256]{1,0:T(8,128)(2,1)S(1)} %broadcast_select_fusion), channel_id=1, source_target_pairs={{0,2},{2,0},{4,6},{6,4},{8,10},{10,8},{12,14},{14,12},{1,3},{3,1},... | collective-permute-start | bytes 811016 | tf_op jit(solution)/shard_map/ppermute | solution.py:394
  19.0 12.2 %collective-permute-start.1 = (bf16[528,256]{1,0:T(8,128)(2,1)S(1)}, bf16[528,256]{1,0:T(8,128)(2,1)S(1)}, u32[]{:S(2)}, u32[]{:S(2)}) collective-permute-start(bf16[528,256]{1,0:T(8,128)(2,1)S(1)} %collective-permute-done.refs_3_), channel_id=1, source_target_pairs={{0,1},{1,0},{2,3},{3,2},{4,8},{5,9},{6,10},{7,11},{8,12},{9,13},{1... | collective-permute-start | bytes 811016 | tf_op jit(solution)/shard_map/ppermute | solution.py:387
  23.3 11.2 %copy-start.1 = (bf16[256,4096]{1,0:T(8,128)(2,1)S(1)}, bf16[256,4096]{1,0:T(8,128)(2,1)}, u32[]{:S(2)}) copy-start(bf16[256,4096]{1,0:T(8,128)(2,1)} %w_ref.5) | copy-start | bytes 6291460
  24.9 6.9 %collective-permute-start.8 = (bf16[528,256]{1,0:T(8,128)(2,1)S(1)}, bf16[528,256]{1,0:T(8,128)(2,1)S(1)}, u32[]{:S(2)}, u32[]{:S(2)}) collective-permute-start(bf16[528,256]{1,0:T(8,128)(2,1)S(1)} %collective-permute-done.7.refs_2_), channel_id=1, source_target_pairs={{0,1},{1,0},{2,3},{3,2},{4,5},{5,4},{6,7},{7,6},{8,9},{9,8},{10,11... | collective-permute-start | bytes 811016 | tf_op jit(solution)/shard_map/ppermute | solution.py:378
  31.2 1.6 %collective-permute-start.5 = (bf16[528,256]{1,0:T(8,128)(2,1)S(1)}, bf16[528,256]{1,0:T(8,128)(2,1)S(1)}, u32[]{:S(2)}, u32[]{:S(2)}) collective-permute-start(bf16[528,256]{1,0:T(8,128)(2,1)S(1)} %collective-permute-done.1.refs_2_), channel_id=1, source_target_pairs={{0,1},{1,0},{2,3},{3,2},{4,5},{5,4},{6,7},{7,6},{8,9},{9,8},{10,11... | collective-permute-start | bytes 811016 | tf_op jit(solution)/shard_map/ppermute | solution.py:378
  31.6 1.6 %collective-permute-start.6 = (bf16[528,256]{1,0:T(8,128)(2,1)S(1)}, bf16[528,256]{1,0:T(8,128)(2,1)S(1)}, u32[]{:S(2)}, u32[]{:S(2)}) collective-permute-start(bf16[528,256]{1,0:T(8,128)(2,1)S(1)} %collective-permute-done.4.refs_3_), channel_id=1, source_target_pairs={{0,1},{1,0},{2,3},{3,2},{4,5},{5,4},{6,7},{7,6},{8,9},{9,8},{10,11... | collective-permute-start | bytes 811016 | tf_op jit(solution)/shard_map/ppermute | solution.py:378
  34.0 2.0 %collective-permute-start.9 = (bf16[512,256]{1,0:T(8,128)(2,1)S(1)}, bf16[512,256]{1,0:T(8,128)(2,1)S(1)}, u32[]{:S(2)}, u32[]{:S(2)}) collective-permute-start(bf16[512,256]{1,0:T(8,128)(2,1)S(1)} %attend_last.1.a_ref), channel_id=1, source_target_pairs={{0,1},{1,0},{2,3},{3,2},{4,5},{5,4},{6,7},{7,6},{8,9},{9,8},{10,11... | collective-permute-start | bytes 786440 | tf_op jit(solution)/shard_map/ppermute | solution.py:378

commit v18 on v16

--- a/solution.py
+++ b/solution.py
@@ -18,7 +18,7 @@
 FACTOR = HD ** (-0.5) * 1.4426950408889634
 
 
-def norm_kv_kernel(x_ref, gain_hbm, w_ref, seg_hbm, msg_ref, normed_ref, xs, ws, gain_ref, seg_ref, sems):
+def norm_kv_kernel(x_ref, gain_hbm, w_ref, seg_hbm, next_ref, msg_ref, normed_ref, near_ref, xs, ws, gain_ref, seg_ref, sems):
     rows, width = xs.shape
     tile, part = rows // 2, rows // 4
 
@@ -32,19 +32,22 @@
         ]
 
     def early_tokens(half):
-        return cut(x_ref, xs, half * part, part, 8 - 4 * half, 8 * half)
+        return cut(x_ref, xs, half * part, part, 4, 4 * half)
 
     def late_tokens():
-        return cut(x_ref, xs, tile, tile, 1, 12)
+        return cut(x_ref, xs, tile, tile, 2, 8)
 
     def weights():
-        return cut(w_ref, ws, 0, width, 4, 14)
+        return cut(w_ref, ws, 0, width, 4, 10)
 
     def gain_copy():
-        return pltpu.make_async_copy(gain_hbm, gain_ref, sems.at[18])
+        return pltpu.make_async_copy(gain_hbm, gain_ref, sems.at[14])
 
     def segments_copy():
-        return pltpu.make_async_copy(seg_hbm, seg_ref, sems.at[19])
+        return pltpu.make_async_copy(seg_hbm, seg_ref, sems.at[15])
+
+    def next_copy():
+        return pltpu.make_async_copy(next_ref, near_ref, sems.at[16])
 
     for copy in early_tokens(0) + early_tokens(1) + [gain_copy()] + weights() + late_tokens() + [segments_copy()]:
         copy.start()
@@ -70,8 +73,6 @@
         kv = jnp.zeros((tile, ws.shape[1]), jnp.float32)
         span = slice(first, first + tile)
         for start in range(0, width, HD):
-            if first == 0 and start % (width // 4) == 0:
-                weights()[4 * start // width].wait()
             for at in (start, start + LANES):
                 normed = (wide(first, tile, at) - mean) * scale * gain_ref[:, at:at + LANES]
                 normed_ref[span, at:at + LANES] = normed.astype(jnp.bfloat16)
@@ -85,7 +86,9 @@
         for copy in early_tokens(half):
             copy.wait()
         halves.append(stats(half * part))
-    gain_copy().wait()
+    for copy in [gain_copy()] + weights():
+        copy.wait()
+    next_copy().start()
     project(0, halves)
     for copy in late_tokens():
         copy.wait()
@@ -95,6 +98,7 @@
     low = jnp.broadcast_to(seg[:, :HD], (8, HD))
     high = jnp.broadcast_to(seg[:, HD:], (8, HD))
     msg_ref[rows:, :] = jnp.concatenate([low, high], axis=0).astype(jnp.bfloat16)
+    next_copy().wait()
 
 
 def in_hbm(x):
@@ -105,28 +109,32 @@
     return pltpu.with_memory_space_constraint(x, pltpu.VMEM)
 
 
-def norm_kv(tokens, gain, w_keyval, segments):
+def norm_kv(tokens, gain, w_keyval, segments, w_next):
     rows, width = tokens.shape
     cols = w_keyval.shape[1]
     vmem, hbm = pl.BlockSpec(memory_space=pltpu.VMEM), pl.BlockSpec(memory_space=pltpu.HBM)
     return pl.pallas_call(
         norm_kv_kernel,
-        in_specs=[hbm] * 4,
-        out_specs=[vmem, vmem],
-        out_shape=[pltpu.VMEM((rows + SEG_ROWS, cols), jnp.bfloat16), pltpu.VMEM((rows, width), jnp.bfloat16)],
+        in_specs=[hbm] * 5,
+        out_specs=[vmem] * 3,
+        out_shape=[
+            pltpu.VMEM((rows + SEG_ROWS, cols), jnp.bfloat16),
+            pltpu.VMEM((rows, width), jnp.bfloat16),
+            pltpu.VMEM(w_next.shape, w_next.dtype),
+        ],
         scratch_shapes=[
             pltpu.VMEM((rows, width), jnp.bfloat16),
             pltpu.VMEM((width, cols), jnp.bfloat16),
             pltpu.VMEM((1, width), jnp.float32),
             pltpu.VMEM((1, rows), jnp.int32),
-            pltpu.SemaphoreType.DMA((20,)),
+            pltpu.SemaphoreType.DMA((17,)),
         ],
         compiler_params=pltpu.CompilerParams(vmem_limit_bytes=24 * MIB),
         cost_estimate=pl.CostEstimate(
             flops=2 * rows * width * cols, bytes_accessed=4 * rows * width + 2 * width * cols, transcendentals=0
         ),
         name="norm_kv",
-    )(in_hbm(tokens), in_hbm(gain.reshape(1, width)), in_hbm(w_keyval), in_hbm(segments.reshape(1, rows)))
+    )(*[in_hbm(x) for x in (tokens, gain.reshape(1, width), w_keyval, segments.reshape(1, rows), w_next)])
 
 
 def query_kernel(x_ref, w_ref, out_ref):
@@ -260,17 +268,18 @@
     )(*[in_vmem(operand) for operand in operands])
 
 
-def bounds_kernel(sum_ref, out_exp_ref, x_ref, sum_bound_ref, out_bound_ref, wide_ref, near, sem):
+def bounds_kernel(sum_ref, out_exp_ref, x_ref, sum_bound_ref, sum_low_ref, out_bound_ref, out_low_ref, wide_ref, near, sem):
     groups, rows = sum_ref.shape
     fetch = pltpu.make_async_copy(x_ref, near, sem)
     fetch.start()
     per = sum_bound_ref.shape[1] // groups
-    for exps, bound_ref in ((sum_ref, sum_bound_ref), (out_exp_ref, out_bound_ref)):
+    for exps, bound_ref, low_ref in ((sum_ref, sum_bound_ref, sum_low_ref), (out_exp_ref, out_bound_ref, out_low_ref)):
         power = jnp.left_shift(jnp.int32(1), exps[...] - MIN_EXP).astype(jnp.float32)
         bound = jnp.transpose(power * (LIMIT * 2.0 ** MIN_EXP))
         for group in range(groups):
             wide = jnp.broadcast_to(bound[:, group:group + 1], (rows, per)).astype(jnp.bfloat16)
             bound_ref[:, group * per:(group + 1) * per] = wide
+            low_ref[:, group * per:(group + 1) * per] = -wide
     fetch.wait()
 
     def widen(step, carry):
@@ -288,8 +297,8 @@
     return pl.pallas_call(
         bounds_kernel,
         in_specs=[vmem, vmem, pl.BlockSpec(memory_space=pltpu.HBM)],
-        out_specs=[vmem] * 3,
-        out_shape=[pltpu.VMEM((rows, width), jnp.bfloat16)] * 2 + [pltpu.VMEM((rows, width), jnp.float32)],
+        out_specs=[vmem] * 5,
+        out_shape=[pltpu.VMEM((rows, width), jnp.bfloat16)] * 4 + [pltpu.VMEM((rows, width), jnp.float32)],
         scratch_shapes=[pltpu.VMEM((rows, width), jnp.bfloat16), pltpu.SemaphoreType.DMA(())],
         compiler_params=pltpu.CompilerParams(vmem_limit_bytes=10 * MIB),
         cost_estimate=pl.CostEstimate(flops=8 * rows * width, bytes_accessed=8 * rows * groups, transcendentals=0),
@@ -297,11 +306,11 @@
     )(in_vmem(sum_exps.T), in_vmem(out_exps.T), in_hbm(tokens))
 
 
-def clip(value, bound):
-    return jnp.minimum(jnp.maximum(value.astype(jnp.bfloat16), -bound), bound)
-
-
-def own_kernel(a_ref, w_ref, sum_ref, out_ref):
+def clip(value, bound, low):
+    return jnp.minimum(jnp.maximum(value.astype(jnp.bfloat16), low), bound)
+
+
+def own_kernel(a_ref, w_ref, sum_ref, low_ref, out_ref):
     rows, width = out_ref.shape
     tile = rows // 2
     for at in range(0, width, HD):
@@ -309,16 +318,16 @@
         for start in range(0, rows, tile):
             span = slice(start, start + tile)
             term = jnp.dot(a_ref[span, :], w_ref[:, cols], preferred_element_type=jnp.float32)
-            out_ref[span, cols] = clip(term, sum_ref[span, cols])
-
-
-def project_own(attended, w_out, sum_bound):
+            out_ref[span, cols] = clip(term, sum_ref[span, cols], low_ref[span, cols])
+
+
+def project_own(attended, w_out, sum_bound, sum_low):
     rows, depth = attended.shape
     width = w_out.shape[1]
     vmem = pl.BlockSpec(memory_space=pltpu.VMEM)
     return pl.pallas_call(
         own_kernel,
-        in_specs=[vmem] * 3,
+        in_specs=[vmem] * 4,
         out_specs=vmem,
         out_shape=pltpu.VMEM((rows, width), jnp.bfloat16),
         compiler_params=pltpu.CompilerParams(vmem_limit_bytes=8 * MIB),
@@ -326,10 +335,10 @@
             flops=2 * rows * width * depth, bytes_accessed=4 * rows * width + 2 * width * depth, transcendentals=0
         ),
         name="project_own",
-    )(in_vmem(attended), in_vmem(w_out), in_vmem(sum_bound))
-
-
-def output_kernel(b_ref, wb_ref, quant_ref, x_ref, sum_ref, last_ref, out_ref, staged, sems):
+    )(in_vmem(attended), in_vmem(w_out), in_vmem(sum_bound), in_vmem(sum_low))
+
+
+def output_kernel(b_ref, wb_ref, quant_ref, x_ref, sum_ref, sum_low_ref, last_ref, last_low_ref, out_ref, staged, sems):
     rows, width = x_ref.shape
     tile = rows // 2
 
@@ -342,19 +351,20 @@
         for start in range(0, rows, tile):
             span = slice(start, start + tile)
             term = jnp.dot(b_ref[span, :], wb_ref[:, cols], preferred_element_type=jnp.float32)
-            quant = clip(term, sum_ref[span, cols]).astype(jnp.float32) + quant_ref[span, cols].astype(jnp.float32)
-            staged[span, cols] = clip(x_ref[span, cols] + quant, last_ref[span, cols])
+            other = clip(term, sum_ref[span, cols], sum_low_ref[span, cols])
+            quant = other.astype(jnp.float32) + quant_ref[span, cols].astype(jnp.float32)
+            staged[span, cols] = clip(x_ref[span, cols] + quant, last_ref[span, cols], last_low_ref[span, cols])
         copy(index).start()
     for index in range(width // HD):
         copy(index).wait()
 
 
-def project_out(att_other, w_other, quant_own, sum_bound, out_bound, tokens):
+def project_out(att_other, w_other, quant_own, sum_bound, sum_low, out_bound, out_low, tokens):
     rows, width = tokens.shape
     depth = att_other.shape[1]
     pieces = width // HD
     vmem = pl.BlockSpec(memory_space=pltpu.VMEM)
-    operands = [att_other, w_other, quant_own, tokens, sum_bound, out_bound]
+    operands = [att_other, w_other, quant_own, tokens, sum_bound, sum_low, out_bound, out_low]
     return pl.pallas_call(
         output_kernel,
         in_specs=[vmem] * len(operands),
@@ -385,8 +395,8 @@
         return lax.ppermute(x, ("seq", "tp"), pairs)
 
     w_other = swap_cores(w_out)
-    message, normed = norm_kv(tokens, gain, w_keyval, segments)
-    query = project_query(normed, w_query)
+    message, normed, w_near = norm_kv(tokens, gain, w_keyval, segments, w_query)
+    query = project_query(normed, w_near)
     held, query = lax.optimization_barrier((shift(message, 2, 0), query))
     odd = lax.rem(lax.axis_index("seq"), 2) == 1
     beside = lax.ppermute(jnp.where(odd, held, message), "seq", [(i, i ^ 1) for i in range(seq_size)])
@@ -408,7 +418,7 @@
             mine = [lax.optimization_barrier((block, early))[0] for block in mine]
         other = [swap_cores(m) for m in mine]
         state = attend(query, segments, plan, mine, other, state, number == len(parts) - 1)
-    quant_own = project_own(state, w_out, bounds[0])
+    quant_own = project_own(state, w_out, *bounds[:2])
     return project_out(swap_cores(state), w_other, quant_own, *bounds)
 
 

time: 40.4 us -> 41.3 us (1.022)
  Pallas kernels: 18.9 us -> 22.1 us
  starting transfers between devices: 10.8 us -> 8.77 us
    pallas_call x1, Pallas kernels: 3.05 us -> 5.55 us  [spread_bounds(): pl.pallas_call(bounds_kernel, in_specs=[vmem, vmem, pl.BlockSpec(memory_s...]
    ppermute x7, starting transfers between devices: 5.62 us -> 3.58 us  [swap_cores(): return lax.ppermute(x, 'tp', [(0, 1), (1, 0)])]
    pallas_call x1, Pallas kernels: 4.31 us -> 5.05 us  [project_out(): pl.pallas_call(output_kernel, in_specs=[vmem] * len(operands), out_specs=...]
    ppermute x1, waiting for transfers between devices: 3.84 us -> 3.22 us  [on_device(): lax.ppermute(jnp.where(odd, held, message), 'seq', [(i, i ^ 1) for i in r...]
  transfers between devices with their start and end apart: 11 -> 11, of which waited for: 4 -> 4; matrix products, arithmetic and copies ran while one was open for 0% -> 0% of each run, Pallas kernels for 36% -> 41%
where the time goes in v18:
time: 41.3 us; the launch traced here: 41.2 us
  Pallas kernels  22.1 us (54%)
  waiting for transfers between devices  9.98 us (24%)
  starting transfers between devices  8.77 us (21%)
    pallas_call x1, Pallas kernels, norm_kv(): pl.pallas_call(norm_kv_kernel, in_specs=[hbm] * 5, out_specs=[vmem] * 3,...  5.98 us
    pallas_call x1, Pallas kernels, spread_bounds(): pl.pallas_call(bounds_kernel, in_specs=[vmem, vmem, pl.BlockSpec(memory_s...  5.55 us
    ppermute x3, waiting for transfers between devices, shift(): return lax.ppermute(x, ('seq', 'tp'), pairs)  5.27 us
    pallas_call x1, Pallas kernels, project_out(): pl.pallas_call(output_kernel, in_specs=[vmem] * len(operands), out_specs=...  5.05 us
    ppermute x3, starting transfers between devices, shift(): return lax.ppermute(x, ('seq', 'tp'), pairs)  3.89 us
    ppermute x7, starting transfers between devices, swap_cores(): return lax.ppermute(x, 'tp', [(0, 1), (1, 0)])  3.58 us
    ppermute x1, waiting for transfers between devices, on_device(): lax.ppermute(jnp.where(odd, held, message), 'seq', [(i, i ^ 1) for i in r...  3.22 us
    pallas_call x3, Pallas kernels, attend(): pl.pallas_call(functools.partial(attend_kernel, plan, first, last), in_sp...  2.49 us
  transfers between devices with their start and end apart: 11, of which 4 were waited for; matrix products, arithmetic and copies ran while one was open for 0% of the time, Pallas kernels for 41%

profile of v18, /device:TPU:11, one launch (start us, length us, event | category | flops | bytes accessed | tf_op | source)
XLA Modules:
  0.0 41.2 jit_solution(16596787844065582203)
XLA Ops:
  0.0 0.7 %collective-permute-start.10 = (bf16[256,4096]{1,0:T(8,128)(2,1)}, bf16[256,4096]{1,0:T(8,128)(2,1)S(1)}, u32[]{:S(2)}, u32[]{:S(2)}) collective-permute-start(bf16[256,4096]{1,0:T(8,128)(2,1)} %w_ref.3), channel_id=1, source_target_pairs={{0,1},{1,0},{2,3},{3,2},{4,5},{5,4},{6,7},{7,6},{8,9},{9,8},{10,11... | collective-permute-start | bytes 6291464 | tf_op jit(solution)/shard_map/ppermute | solution.py:386
  0.7 6.0 %norm_kv.1 = (bf16[528,256]{1,0:T(8,128)(2,1)S(1)}, bf16[512,4096]{1,0:T(8,128)(2,1)S(1)}, bf16[4096,256]{1,0:T(8,128)(2,1)S(1)}) custom-call(bf16[512,4096]{1,0:T(8,128)(2,1)} %x_ref.3, f32[1,4096]{1,0:T(1,128)} %bitcast.10, bf16[4096,256]{1,0:T(8,128)(2,1)} %w_ref.2, s32[1,512]{1,0:T(1,128)} %bitcast.6, bf16[4096,256]{1,0:T(8,128)(2,1)} %next_ref.1), custom_call_target="tpu_custom_call" | custom-call | flops 1073741824 | bytes 10485760 | tf_op jit(solution)/shard_map/norm_kv/pallas_call | solution.py:116
  6.7 0.0 copy-start.1
  6.7 0.0 copy-start.2
  6.7 1.3 %collective-permute-start = (bf16[528,256]{1,0:T(8,128)(2,1)S(1)}, bf16[528,256]{1,0:T(8,128)(2,1)S(1)}, u32[]{:S(2)}, u32[]{:S(2)}) collective-permute-start(bf16[528,256]{1,0:T(8,128)(2,1)S(1)} %get-tuple-element.26.refs_2_), channel_id=1, source_target_pairs={{0,4},{1,5},{2,6},{3,7},{4,8},{5,9},{6,10},{7,11},{8,12},{9,13},{1... | collective-permute-start | bytes 811016 | tf_op jit(solution)/shard_map/ppermute | solution.py:395
  8.0 0.3 collective-permute-start.2
  8.3 1.2 %project_query.1.refs_0_ = bf16[512,256]{1,0:T(8,128)(2,1)S(1)} custom-call(bf16[512,4096]{1,0:T(8,128)(2,1)S(1)} %get-tuple-element.27.x_ref, bf16[4096,256]{1,0:T(8,128)(2,1)S(1)} %get-tuple-element.28.w_ref), custom_call_target="tpu_custom_call" | custom-call | flops 1073741824 | bytes 6291456 | tf_op jit(solution)/shard_map/project_query/pallas_call | solution.py:148
  9.6 5.3 %collective-permute-done.refs_3_ = bf16[528,256]{1,0:T(8,128)(2,1)S(1)} collective-permute-done((bf16[528,256]{1,0:T(8,128)(2,1)S(1)}, bf16[528,256]{1,0:T(8,128)(2,1)S(1)}, u32[]{:S(2)}, u32[]{:S(2)}) %collective-permute-start) | collective-permute-done | bytes 270368 | tf_op jit(solution)/shard_map/ppermute | solution.py:395
  14.9 1.2 %collective-permute-start.7 = (bf16[528,256]{1,0:T(8,128)(2,1)S(1)}, bf16[528,256]{1,0:T(8,128)(2,1)S(1)}, u32[]{:S(2)}, u32[]{:S(2)}) collective-permute-start(bf16[528,256]{1,0:T(8,128)(2,1)S(1)} %collective-permute-done.refs_3_), channel_id=1, source_target_pairs={{0,1},{1,0},{2,3},{3,2},{4,6},{5,7},{6,8},{7,9},{8,10},{9,11},{10,... | collective-permute-start | bytes 811016 | tf_op jit(solution)/shard_map/ppermute | solution.py:395
  16.1 1.1 %collective-permute-start.3 = (bf16[528,256]{1,0:T(8,128)(2,1)S(1)}, bf16[528,256]{1,0:T(8,128)(2,1)S(1)}, u32[]{:S(2)}, u32[]{:S(2)}) collective-permute-start(bf16[528,256]{1,0:T(8,128)(2,1)S(1)} %collective-permute-done.refs_3_), channel_id=1, source_target_pairs={{0,1},{1,0},{2,3},{3,2},{4,5},{5,4},{6,7},{7,6},{8,9},{9,8},{10,11... | collective-permute-start | bytes 811016 | tf_op jit(solution)/shard_map/ppermute | solution.py:386
  17.2 1.3 %collective-permute-start.4 = (bf16[528,256]{1,0:T(8,128)(2,1)S(1)}, bf16[528,256]{1,0:T(8,128)(2,1)S(1)}, u32[]{:S(2)}, u32[]{:S(2)}) collective-permute-start(bf16[528,256]{1,0:T(8,128)(2,1)S(1)} %broadcast_select_fusion), channel_id=1, source_target_pairs={{0,2},{2,0},{4,6},{6,4},{8,10},{10,8},{12,14},{14,12},{1,3},{3,1},... | collective-permute-start | bytes 811016 | tf_op jit(solution)/shard_map/ppermute | solution.py:402
  18.5 1.3 %collective-permute-start.1 = (bf16[528,256]{1,0:T(8,128)(2,1)S(1)}, bf16[528,256]{1,0:T(8,128)(2,1)S(1)}, u32[]{:S(2)}, u32[]{:S(2)}) collective-permute-start(bf16[528,256]{1,0:T(8,128)(2,1)S(1)} %collective-permute-done.refs_3_), channel_id=1, source_target_pairs={{0,1},{1,0},{2,3},{3,2},{4,8},{5,9},{6,10},{7,11},{8,12},{9,13},{1... | collective-permute-start | bytes 811016 | tf_op jit(solution)/shard_map/ppermute | solution.py:395
  19.8 5.6 %spread_bounds.1 = (bf16[512,4096]{1,0:T(8,128)(2,1)S(1)}, bf16[512,4096]{1,0:T(8,128)(2,1)S(1)}, bf16[512,4096]{1,0:T(8,128)(2,1)S(1)}, bf16[512,4096]{1,0:T(8,128)(2,1)S(1)}, f32[512,4096]{1,0:T(8,128)S(1)}) custom-call(s32[32,512]{1,0:T(8,128)S(1)} %bitcast.4, s32[32,512]{1,0:T(8,128)S(1)} %bitcast.5, bf16[512,4096]{1,0:T(8,128)(2,1)} %x_ref.3), custom_call_target="tpu_custom_call" | custom-call | flops 16777216 | bytes 131072 | tf_op jit(solution)/shard_map/spread_bounds/pallas_call | solution.py:297
  25.4 1.7 %attend_first.1.refs_4_ = f32[512,640]{1,0:T(8,128)S(1)} custom-call(bf16[512,256]{1,0:T(8,128)(2,1)S(1)} %project_query.1.refs_0_, s32[1,512]{1,0:T(1,128)S(1)} %bitcast.7, bf16[528,256]{1,0:T(8,128)(2,1)S(1)} %get-tuple-element.26.refs_2_, bf16[528,256]{1,0:T(8,128)(2,1)S(1)} %collective-permute-done.refs_3_, ...), custom_call_target="tpu_custom_call" | custom-call | flops 536870912 | bytes 1048576 | tf_op jit(solution)/shard_map/attend_first/pallas_call | solution.py:256
  27.1 0.6 %collective-permute-start.8 = (bf16[528,256]{1,0:T(8,128)(2,1)S(1)}, bf16[528,256]{1,0:T(8,128)(2,1)S(1)}, u32[]{:S(2)}, u32[]{:S(2)}) collective-permute-start(bf16[528,256]{1,0:T(8,128)(2,1)S(1)} %collective-permute-done.7.refs_2_), channel_id=1, source_target_pairs={{0,1},{1,0},{2,3},{3,2},{4,5},{5,4},{6,7},{7,6},{8,9},{9,8},{10,11... | collective-permute-start | bytes 811016 | tf_op jit(solution)/shard_map/ppermute | solution.py:386
  27.7 3.2 %collective-permute-done.4.refs_3_ = bf16[528,256]{1,0:T(8,128)(2,1)S(1)} collective-permute-done((bf16[528,256]{1,0:T(8,128)(2,1)S(1)}, bf16[528,256]{1,0:T(8,128)(2,1)S(1)}, u32[]{:S(2)}, u32[]{:S(2)}) %collective-permute-start.4) | collective-permute-done | bytes 270368 | tf_op jit(solution)/shard_map/ppermute | solution.py:402
  30.9 0.4 %collective-permute-start.5 = (bf16[528,256]{1,0:T(8,128)(2,1)S(1)}, bf16[528,256]{1,0:T(8,128)(2,1)S(1)}, u32[]{:S(2)}, u32[]{:S(2)}) collective-permute-start(bf16[528,256]{1,0:T(8,128)(2,1)S(1)} %collective-permute-done.1.refs_2_), channel_id=1, source_target_pairs={{0,1},{1,0},{2,3},{3,2},{4,5},{5,4},{6,7},{7,6},{8,9},{9,8},{10,11... | collective-permute-start | bytes 811016 | tf_op jit(solution)/shard_map/ppermute | solution.py:386
  31.3 0.1 collective-permute-start.6
  31.4 1.1 %collective-permute-done.5.refs_4_ = bf16[528,256]{1,0:T(8,128)(2,1)S(1)} collective-permute-done((bf16[528,256]{1,0:T(8,128)(2,1)S(1)}, bf16[528,256]{1,0:T(8,128)(2,1)S(1)}, u32[]{:S(2)}, u32[]{:S(2)}) %collective-permute-start.5) | collective-permute-done | bytes 270368 | tf_op jit(solution)/shard_map/ppermute | solution.py:386
  32.5 0.4 collective-permute-done.6.refs_5_
  32.9 0.8 %attend_last.1.a_ref = bf16[512,256]{1,0:T(8,128)(2,1)S(1)} custom-call(bf16[512,256]{1,0:T(8,128)(2,1)S(1)} %project_query.1.refs_0_, s32[1,512]{1,0:T(1,128)S(1)} %bitcast.9, bf16[528,256]{1,0:T(8,128)(2,1)S(1)} %collective-permute-done.1.refs_2_, bf16[528,256]{1,0:T(8,128)(2,1)S(1)} %collective-permute-done.4.refs_3_, ...), custom_call_target="tpu_custom_call" | custom-call | flops 536870912 | bytes 1048576 | tf_op jit(solution)/shard_map/attend_last/pallas_call | solution.py:256
  33.7 0.4 %collective-permute-start.9 = (bf16[512,256]{1,0:T(8,128)(2,1)S(1)}, bf16[512,256]{1,0:T(8,128)(2,1)S(1)}, u32[]{:S(2)}, u32[]{:S(2)}) collective-permute-start(bf16[512,256]{1,0:T(8,128)(2,1)S(1)} %attend_last.1.a_ref), channel_id=1, source_target_pairs={{0,1},{1,0},{2,3},{3,2},{4,5},{5,4},{6,7},{7,6},{8,9},{9,8},{10,11... | collective-permute-start | bytes 786440 | tf_op jit(solution)/shard_map/ppermute | solution.py:386
  34.2 1.8 %project_own.1.quant_ref = bf16[512,4096]{1,0:T(8,128)(2,1)S(1)} custom-call(bf16[512,256]{1,0:T(8,128)(2,1)S(1)} %attend_last.1.a_ref, bf16[256,4096]{1,0:T(8,128)(2,1)S(1)} %copy-done, bf16[512,4096]{1,0:T(8,128)(2,1)S(1)} %get-tuple-element.38.sum_ref, bf16[512,4096]{1,0:T(8,128)(2,1)S(1)} %get-tuple-element.39.low_ref.sum_low_ref), custom_call_target="tpu_custom_call" | custom-call | flops 1073741824 | bytes 10485760 | tf_op jit(solution)/shard_map/project_own/pallas_call | solution.py:328
  36.0 5.0 %project_out.1 = bf16[512,4096]{1,0:T(8,128)(2,1)} custom-call(bf16[512,256]{1,0:T(8,128)(2,1)S(1)} %collective-permute-done.9.b_ref, bf16[256,4096]{1,0:T(8,128)(2,1)S(1)} %collective-permute-done.10.wb_ref, bf16[512,4096]{1,0:T(8,128)(2,1)S(1)} %project_own.1.quant_ref, f32[512,4096]{1,0:T(8,128)S(1)} %get-tuple-element.42.x_ref, ...), custom_call_target="tpu_custom_call" | custom-call | flops 1073741824 | bytes 10485760 | tf_op jit(solution)/shard_map/project_out/pallas_call | solution.py:368
  (15 shorter events, 0.1 us)
Async XLA Ops:
  0.0 36.0 %collective-permute-start.10 = (bf16[256,4096]{1,0:T(8,128)(2,1)}, bf16[256,4096]{1,0:T(8,128)(2,1)S(1)}, u32[]{:S(2)}, u32[]{:S(2)}) collective-permute-start(bf16[256,4096]{1,0:T(8,128)(2,1)} %w_ref.3), channel_id=1, source_target_pairs={{0,1},{1,0},{2,3},{3,2},{4,5},{5,4},{6,7},{7,6},{8,9},{9,8},{10,11... | collective-permute-start | bytes 6291464 | tf_op jit(solution)/shard_map/ppermute | solution.py:386
  6.7 13.1 %copy-start.1 = (s32[512,32]{0,1:T(8,128)S(1)}, s32[512,32]{0,1:T(8,128)}, u32[]{:S(2)}) copy-start(s32[512,32]{0,1:T(8,128)} %param.14) | copy-start | bytes 196612
  6.7 13.1 %copy-start.2 = (s32[512,32]{0,1:T(8,128)S(1)}, s32[512,32]{0,1:T(8,128)}, u32[]{:S(2)}) copy-start(s32[512,32]{0,1:T(8,128)} %param.15) | copy-start | bytes 196612
  6.7 8.2 %collective-permute-start = (bf16[528,256]{1,0:T(8,128)(2,1)S(1)}, bf16[528,256]{1,0:T(8,128)(2,1)S(1)}, u32[]{:S(2)}, u32[]{:S(2)}) collective-permute-start(bf16[528,256]{1,0:T(8,128)(2,1)S(1)} %get-tuple-element.26.refs_2_), channel_id=1, source_target_pairs={{0,4},{1,5},{2,6},{3,7},{4,8},{5,9},{6,10},{7,11},{8,12},{9,13},{1... | collective-permute-start | bytes 811016 | tf_op jit(solution)/shard_map/ppermute | solution.py:395
  8.0 10.5 %collective-permute-start.2 = (bf16[528,256]{1,0:T(8,128)(2,1)S(1)}, bf16[528,256]{1,0:T(8,128)(2,1)S(1)}, u32[]{:S(2)}, u32[]{:S(2)}) collective-permute-start(bf16[528,256]{1,0:T(8,128)(2,1)S(1)} %get-tuple-element.26.refs_2_), channel_id=1, source_target_pairs={{0,1},{1,0},{2,3},{3,2},{4,5},{5,4},{6,7},{7,6},{8,9},{9,8},{10,11... | collective-permute-start | bytes 811016 | tf_op jit(solution)/shard_map/ppermute | solution.py:386
  9.6 15.8 %copy-start.3 = (s32[512]{0:T(512)S(1)}, s32[512]{0:T(512)}, u32[]{:S(2)}) copy-start(s32[512]{0:T(512)} %param.10) | copy-start | bytes 6148
  14.9 12.2 %collective-permute-start.7 = (bf16[528,256]{1,0:T(8,128)(2,1)S(1)}, bf16[528,256]{1,0:T(8,128)(2,1)S(1)}, u32[]{:S(2)}, u32[]{:S(2)}) collective-permute-start(bf16[528,256]{1,0:T(8,128)(2,1)S(1)} %collective-permute-done.refs_3_), channel_id=1, source_target_pairs={{0,1},{1,0},{2,3},{3,2},{4,6},{5,7},{6,8},{7,9},{8,10},{9,11},{10,... | collective-permute-start | bytes 811016 | tf_op jit(solution)/shard_map/ppermute | solution.py:395
  16.1 9.3 %collective-permute-start.3 = (bf16[528,256]{1,0:T(8,128)(2,1)S(1)}, bf16[528,256]{1,0:T(8,128)(2,1)S(1)}, u32[]{:S(2)}, u32[]{:S(2)}) collective-permute-start(bf16[528,256]{1,0:T(8,128)(2,1)S(1)} %collective-permute-done.refs_3_), channel_id=1, source_target_pairs={{0,1},{1,0},{2,3},{3,2},{4,5},{5,4},{6,7},{7,6},{8,9},{9,8},{10,11... | collective-permute-start | bytes 811016 | tf_op jit(solution)/shard_map/ppermute | solution.py:386
  17.2 13.7 %collective-permute-start.4 = (bf16[528,256]{1,0:T(8,128)(2,1)S(1)}, bf16[528,256]{1,0:T(8,128)(2,1)S(1)}, u32[]{:S(2)}, u32[]{:S(2)}) collective-permute-start(bf16[528,256]{1,0:T(8,128)(2,1)S(1)} %broadcast_select_fusion), channel_id=1, source_target_pairs={{0,2},{2,0},{4,6},{6,4},{8,10},{10,8},{12,14},{14,12},{1,3},{3,1},... | collective-permute-start | bytes 811016 | tf_op jit(solution)/shard_map/ppermute | solution.py:402
  18.5 12.4 %collective-permute-start.1 = (bf16[528,256]{1,0:T(8,128)(2,1)S(1)}, bf16[528,256]{1,0:T(8,128)(2,1)S(1)}, u32[]{:S(2)}, u32[]{:S(2)}) collective-permute-start(bf16[528,256]{1,0:T(8,128)(2,1)S(1)} %collective-permute-done.refs_3_), channel_id=1, source_target_pairs={{0,1},{1,0},{2,3},{3,2},{4,8},{5,9},{6,10},{7,11},{8,12},{9,13},{1... | collective-permute-start | bytes 811016 | tf_op jit(solution)/shard_map/ppermute | solution.py:395
  25.4 8.8 %copy-start = (bf16[256,4096]{1,0:T(8,128)(2,1)S(1)}, bf16[256,4096]{1,0:T(8,128)(2,1)}, u32[]{:S(2)}) copy-start(bf16[256,4096]{1,0:T(8,128)(2,1)} %w_ref.3) | copy-start | bytes 6291460
  27.1 4.3 %collective-permute-start.8 = (bf16[528,256]{1,0:T(8,128)(2,1)S(1)}, bf16[528,256]{1,0:T(8,128)(2,1)S(1)}, u32[]{:S(2)}, u32[]{:S(2)}) collective-permute-start(bf16[528,256]{1,0:T(8,128)(2,1)S(1)} %collective-permute-done.7.refs_2_), channel_id=1, source_target_pairs={{0,1},{1,0},{2,3},{3,2},{4,5},{5,4},{6,7},{7,6},{8,9},{9,8},{10,11... | collective-permute-start | bytes 811016 | tf_op jit(solution)/shard_map/ppermute | solution.py:386
  30.9 1.6 %collective-permute-start.5 = (bf16[528,256]{1,0:T(8,128)(2,1)S(1)}, bf16[528,256]{1,0:T(8,128)(2,1)S(1)}, u32[]{:S(2)}, u32[]{:S(2)}) collective-permute-start(bf16[528,256]{1,0:T(8,128)(2,1)S(1)} %collective-permute-done.1.refs_2_), channel_id=1, source_target_pairs={{0,1},{1,0},{2,3},{3,2},{4,5},{5,4},{6,7},{7,6},{8,9},{9,8},{10,11... | collective-permute-start | bytes 811016 | tf_op jit(solution)/shard_map/ppermute | solution.py:386
  31.3 1.6 %collective-permute-start.6 = (bf16[528,256]{1,0:T(8,128)(2,1)S(1)}, bf16[528,256]{1,0:T(8,128)(2,1)S(1)}, u32[]{:S(2)}, u32[]{:S(2)}) collective-permute-start(bf16[528,256]{1,0:T(8,128)(2,1)S(1)} %collective-permute-done.4.refs_3_), channel_id=1, source_target_pairs={{0,1},{1,0},{2,3},{3,2},{4,5},{5,4},{6,7},{7,6},{8,9},{9,8},{10,11... | collective-permute-start | bytes 811016 | tf_op jit(solution)/shard_map/ppermute | solution.py:386
  33.7 2.2 %collective-permute-start.9 = (bf16[512,256]{1,0:T(8,128)(2,1)S(1)}, bf16[512,256]{1,0:T(8,128)(2,1)S(1)}, u32[]{:S(2)}, u32[]{:S(2)}) collective-permute-start(bf16[512,256]{1,0:T(8,128)(2,1)S(1)} %attend_last.1.a_ref), channel_id=1, source_target_pairs={{0,1},{1,0},{2,3},{3,2},{4,5},{5,4},{6,7},{7,6},{8,9},{9,8},{10,11... | collective-permute-start | bytes 786440 | tf_op jit(solution)/shard_map/ppermute | solution.py:386

commit v19 on v18

--- a/solution.py
+++ b/solution.py
@@ -268,26 +268,18 @@
     )(*[in_vmem(operand) for operand in operands])
 
 
-def bounds_kernel(sum_ref, out_exp_ref, x_ref, sum_bound_ref, sum_low_ref, out_bound_ref, out_low_ref, wide_ref, near, sem):
+def bounds_kernel(sum_ref, out_exp_ref, x_ref, sum_bound_ref, out_bound_ref, near_ref, sem):
     groups, rows = sum_ref.shape
-    fetch = pltpu.make_async_copy(x_ref, near, sem)
+    fetch = pltpu.make_async_copy(x_ref, near_ref, sem)
     fetch.start()
     per = sum_bound_ref.shape[1] // groups
-    for exps, bound_ref, low_ref in ((sum_ref, sum_bound_ref, sum_low_ref), (out_exp_ref, out_bound_ref, out_low_ref)):
+    for exps, bound_ref in ((sum_ref, sum_bound_ref), (out_exp_ref, out_bound_ref)):
         power = jnp.left_shift(jnp.int32(1), exps[...] - MIN_EXP).astype(jnp.float32)
         bound = jnp.transpose(power * (LIMIT * 2.0 ** MIN_EXP))
         for group in range(groups):
             wide = jnp.broadcast_to(bound[:, group:group + 1], (rows, per)).astype(jnp.bfloat16)
             bound_ref[:, group * per:(group + 1) * per] = wide
-            low_ref[:, group * per:(group + 1) * per] = -wide
     fetch.wait()
-
-    def widen(step, carry):
-        span = pl.ds(pl.multiple_of(step * 64, 64), 64)
-        wide_ref[span, :] = near[span, :].astype(jnp.float32)
-        return carry
-
-    lax.fori_loop(0, rows // 64, widen, 0)
 
 
 def spread_bounds(sum_exps, out_exps, tokens):
@@ -297,20 +289,20 @@
     return pl.pallas_call(
         bounds_kernel,
         in_specs=[vmem, vmem, pl.BlockSpec(memory_space=pltpu.HBM)],
-        out_specs=[vmem] * 5,
-        out_shape=[pltpu.VMEM((rows, width), jnp.bfloat16)] * 4 + [pltpu.VMEM((rows, width), jnp.float32)],
-        scratch_shapes=[pltpu.VMEM((rows, width), jnp.bfloat16), pltpu.SemaphoreType.DMA(())],
+        out_specs=[vmem] * 3,
+        out_shape=[pltpu.VMEM((rows, width), jnp.bfloat16)] * 3,
+        scratch_shapes=[pltpu.SemaphoreType.DMA(())],
         compiler_params=pltpu.CompilerParams(vmem_limit_bytes=10 * MIB),
         cost_estimate=pl.CostEstimate(flops=8 * rows * width, bytes_accessed=8 * rows * groups, transcendentals=0),
         name="spread_bounds",
     )(in_vmem(sum_exps.T), in_vmem(out_exps.T), in_hbm(tokens))
 
 
-def clip(value, bound, low):
-    return jnp.minimum(jnp.maximum(value.astype(jnp.bfloat16), low), bound)
-
-
-def own_kernel(a_ref, w_ref, sum_ref, low_ref, out_ref):
+def clip(value, bound):
+    return jnp.minimum(jnp.maximum(value.astype(jnp.bfloat16), -bound), bound)
+
+
+def own_kernel(a_ref, w_ref, sum_ref, out_ref):
     rows, width = out_ref.shape
     tile = rows // 2
     for at in range(0, width, HD):
@@ -318,16 +310,16 @@
         for start in range(0, rows, tile):
             span = slice(start, start + tile)
             term = jnp.dot(a_ref[span, :], w_ref[:, cols], preferred_element_type=jnp.float32)
-            out_ref[span, cols] = clip(term, sum_ref[span, cols], low_ref[span, cols])
-
-
-def project_own(attended, w_out, sum_bound, sum_low):
+            out_ref[span, cols] = clip(term, sum_ref[span, cols])
+
+
+def project_own(attended, w_out, sum_bound):
     rows, depth = attended.shape
     width = w_out.shape[1]
     vmem = pl.BlockSpec(memory_space=pltpu.VMEM)
     return pl.pallas_call(
         own_kernel,
-        in_specs=[vmem] * 4,
+        in_specs=[vmem] * 3,
         out_specs=vmem,
         out_shape=pltpu.VMEM((rows, width), jnp.bfloat16),
         compiler_params=pltpu.CompilerParams(vmem_limit_bytes=8 * MIB),
@@ -335,10 +327,10 @@
             flops=2 * rows * width * depth, bytes_accessed=4 * rows * width + 2 * width * depth, transcendentals=0
         ),
         name="project_own",
-    )(in_vmem(attended), in_vmem(w_out), in_vmem(sum_bound), in_vmem(sum_low))
-
-
-def output_kernel(b_ref, wb_ref, quant_ref, x_ref, sum_ref, sum_low_ref, last_ref, last_low_ref, out_ref, staged, sems):
+    )(in_vmem(attended), in_vmem(w_out), in_vmem(sum_bound))
+
+
+def output_kernel(b_ref, wb_ref, quant_ref, x_ref, sum_ref, last_ref, out_ref, staged, sems):
     rows, width = x_ref.shape
     tile = rows // 2
 
@@ -351,20 +343,19 @@
         for start in range(0, rows, tile):
             span = slice(start, start + tile)
             term = jnp.dot(b_ref[span, :], wb_ref[:, cols], preferred_element_type=jnp.float32)
-            other = clip(term, sum_ref[span, cols], sum_low_ref[span, cols])
-            quant = other.astype(jnp.float32) + quant_ref[span, cols].astype(jnp.float32)
-            staged[span, cols] = clip(x_ref[span, cols] + quant, last_ref[span, cols], last_low_ref[span, cols])
+            quant = clip(term, sum_ref[span, cols]).astype(jnp.float32) + quant_ref[span, cols].astype(jnp.float32)
+            staged[span, cols] = clip(x_ref[span, cols].astype(jnp.float32) + quant, last_ref[span, cols])
         copy(index).start()
     for index in range(width // HD):
         copy(index).wait()
 
 
-def project_out(att_other, w_other, quant_own, sum_bound, sum_low, out_bound, out_low, tokens):
+def project_out(att_other, w_other, quant_own, sum_bound, out_bound, tokens):
     rows, width = tokens.shape
     depth = att_other.shape[1]
     pieces = width // HD
     vmem = pl.BlockSpec(memory_space=pltpu.VMEM)
-    operands = [att_other, w_other, quant_own, tokens, sum_bound, sum_low, out_bound, out_low]
+    operands = [att_other, w_other, quant_own, tokens, sum_bound, out_bound]
     return pl.pallas_call(
         output_kernel,
         in_specs=[vmem] * len(operands),
@@ -418,7 +409,7 @@
             mine = [lax.optimization_barrier((block, early))[0] for block in mine]
         other = [swap_cores(m) for m in mine]
         state = attend(query, segments, plan, mine, other, state, number == len(parts) - 1)
-    quant_own = project_own(state, w_out, *bounds[:2])
+    quant_own = project_own(state, w_out, bounds[0])
     return project_out(swap_cores(state), w_other, quant_own, *bounds)
 
 

time: 41.3 us -> 40.7 us (0.985)
  Pallas kernels: 22.1 us -> 18.4 us
  starting transfers between devices: 8.77 us -> 11 us
  waiting for transfers between devices: 9.98 us -> 10.8 us
    pallas_call x1, Pallas kernels: 5.55 us -> 2.49 us  [spread_bounds(): pl.pallas_call(bounds_kernel, in_specs=[vmem, vmem, pl.BlockSpec(memory_s...]
    ppermute x7, starting transfers between devices: 3.58 us -> 5.82 us  [swap_cores(): return lax.ppermute(x, 'tp', [(0, 1), (1, 0)])]
    ppermute x1, waiting for transfers between devices: 3.22 us -> 4.04 us  [on_device(): lax.ppermute(jnp.where(odd, held, message), 'seq', [(i, i ^ 1) for i in r...]
  transfers between devices with their start and end apart: 11 -> 11, of which waited for: 4 -> 4; matrix products, arithmetic and copies ran while one was open for 0% -> 0% of each run, Pallas kernels for 41% -> 34%
where the time goes in v19:
time: 40.7 us; the launch traced here: 40.6 us
  Pallas kernels  18.4 us (45%)
  starting transfers between devices  11 us (27%)
  waiting for transfers between devices  10.8 us (27%)
    pallas_call x1, Pallas kernels, norm_kv(): pl.pallas_call(norm_kv_kernel, in_specs=[hbm] * 5, out_specs=[vmem] * 3,...  5.98 us
    ppermute x7, starting transfers between devices, swap_cores(): return lax.ppermute(x, 'tp', [(0, 1), (1, 0)])  5.82 us
    ppermute x3, waiting for transfers between devices, shift(): return lax.ppermute(x, ('seq', 'tp'), pairs)  5.27 us
    pallas_call x1, Pallas kernels, project_out(): pl.pallas_call(output_kernel, in_specs=[vmem] * len(operands), out_specs=...  4.7 us
    ppermute x1, waiting for transfers between devices, on_device(): lax.ppermute(jnp.where(odd, held, message), 'seq', [(i, i ^ 1) for i in r...  4.04 us
    ppermute x3, starting transfers between devices, shift(): return lax.ppermute(x, ('seq', 'tp'), pairs)  3.89 us
    pallas_call x1, Pallas kernels, spread_bounds(): pl.pallas_call(bounds_kernel, in_specs=[vmem, vmem, pl.BlockSpec(memory_s...  2.49 us
    pallas_call x3, Pallas kernels, attend(): pl.pallas_call(functools.partial(attend_kernel, plan, first, last), in_sp...  2.49 us
  transfers between devices with their start and end apart: 11, of which 4 were waited for; matrix products, arithmetic and copies ran while one was open for 0% of the time, Pallas kernels for 34%

profile of v19, /device:TPU:11, one launch (start us, length us, event | category | flops | bytes accessed | tf_op | source)
XLA Modules:
  0.0 40.6 jit_solution(9449264994743415641)
XLA Ops:
  0.0 0.7 %collective-permute-start.10 = (bf16[256,4096]{1,0:T(8,128)(2,1)}, bf16[256,4096]{1,0:T(8,128)(2,1)S(1)}, u32[]{:S(2)}, u32[]{:S(2)}) collective-permute-start(bf16[256,4096]{1,0:T(8,128)(2,1)} %w_ref.3), channel_id=1, source_target_pairs={{0,1},{1,0},{2,3},{3,2},{4,5},{5,4},{6,7},{7,6},{8,9},{9,8},{10,11... | collective-permute-start | bytes 6291464 | tf_op jit(solution)/shard_map/ppermute | solution.py:377
  0.7 6.0 %norm_kv.1 = (bf16[528,256]{1,0:T(8,128)(2,1)S(1)}, bf16[512,4096]{1,0:T(8,128)(2,1)S(1)}, bf16[4096,256]{1,0:T(8,128)(2,1)S(1)}) custom-call(bf16[512,4096]{1,0:T(8,128)(2,1)} %x_ref.3, f32[1,4096]{1,0:T(1,128)} %bitcast.10, bf16[4096,256]{1,0:T(8,128)(2,1)} %w_ref.2, s32[1,512]{1,0:T(1,128)} %bitcast.6, bf16[4096,256]{1,0:T(8,128)(2,1)} %next_ref.1), custom_call_target="tpu_custom_call" | custom-call | flops 1073741824 | bytes 10485760 | tf_op jit(solution)/shard_map/norm_kv/pallas_call | solution.py:116
  6.7 0.0 copy-start.1
  6.7 0.0 copy-start.2
  6.7 1.3 %collective-permute-start = (bf16[528,256]{1,0:T(8,128)(2,1)S(1)}, bf16[528,256]{1,0:T(8,128)(2,1)S(1)}, u32[]{:S(2)}, u32[]{:S(2)}) collective-permute-start(bf16[528,256]{1,0:T(8,128)(2,1)S(1)} %get-tuple-element.22.refs_2_), channel_id=1, source_target_pairs={{0,4},{1,5},{2,6},{3,7},{4,8},{5,9},{6,10},{7,11},{8,12},{9,13},{1... | collective-permute-start | bytes 811016 | tf_op jit(solution)/shard_map/ppermute | solution.py:386
  8.0 0.3 collective-permute-start.2
  8.3 1.2 %project_query.1.refs_0_ = bf16[512,256]{1,0:T(8,128)(2,1)S(1)} custom-call(bf16[512,4096]{1,0:T(8,128)(2,1)S(1)} %get-tuple-element.23.x_ref, bf16[4096,256]{1,0:T(8,128)(2,1)S(1)} %get-tuple-element.24.w_ref), custom_call_target="tpu_custom_call" | custom-call | flops 1073741824 | bytes 6291456 | tf_op jit(solution)/shard_map/project_query/pallas_call | solution.py:148
  9.6 5.3 %collective-permute-done.refs_3_ = bf16[528,256]{1,0:T(8,128)(2,1)S(1)} collective-permute-done((bf16[528,256]{1,0:T(8,128)(2,1)S(1)}, bf16[528,256]{1,0:T(8,128)(2,1)S(1)}, u32[]{:S(2)}, u32[]{:S(2)}) %collective-permute-start) | collective-permute-done | bytes 270368 | tf_op jit(solution)/shard_map/ppermute | solution.py:386
  14.9 1.2 %collective-permute-start.7 = (bf16[528,256]{1,0:T(8,128)(2,1)S(1)}, bf16[528,256]{1,0:T(8,128)(2,1)S(1)}, u32[]{:S(2)}, u32[]{:S(2)}) collective-permute-start(bf16[528,256]{1,0:T(8,128)(2,1)S(1)} %collective-permute-done.refs_3_), channel_id=1, source_target_pairs={{0,1},{1,0},{2,3},{3,2},{4,6},{5,7},{6,8},{7,9},{8,10},{9,11},{10,... | collective-permute-start | bytes 811016 | tf_op jit(solution)/shard_map/ppermute | solution.py:386
  16.1 1.1 %collective-permute-start.3 = (bf16[528,256]{1,0:T(8,128)(2,1)S(1)}, bf16[528,256]{1,0:T(8,128)(2,1)S(1)}, u32[]{:S(2)}, u32[]{:S(2)}) collective-permute-start(bf16[528,256]{1,0:T(8,128)(2,1)S(1)} %collective-permute-done.refs_3_), channel_id=1, source_target_pairs={{0,1},{1,0},{2,3},{3,2},{4,5},{5,4},{6,7},{7,6},{8,9},{9,8},{10,11... | collective-permute-start | bytes 811016 | tf_op jit(solution)/shard_map/ppermute | solution.py:377
  17.2 1.3 %collective-permute-start.4 = (bf16[528,256]{1,0:T(8,128)(2,1)S(1)}, bf16[528,256]{1,0:T(8,128)(2,1)S(1)}, u32[]{:S(2)}, u32[]{:S(2)}) collective-permute-start(bf16[528,256]{1,0:T(8,128)(2,1)S(1)} %broadcast_select_fusion), channel_id=1, source_target_pairs={{0,2},{2,0},{4,6},{6,4},{8,10},{10,8},{12,14},{14,12},{1,3},{3,1},... | collective-permute-start | bytes 811016 | tf_op jit(solution)/shard_map/ppermute | solution.py:393
  18.5 1.3 %collective-permute-start.1 = (bf16[528,256]{1,0:T(8,128)(2,1)S(1)}, bf16[528,256]{1,0:T(8,128)(2,1)S(1)}, u32[]{:S(2)}, u32[]{:S(2)}) collective-permute-start(bf16[528,256]{1,0:T(8,128)(2,1)S(1)} %collective-permute-done.refs_3_), channel_id=1, source_target_pairs={{0,1},{1,0},{2,3},{3,2},{4,8},{5,9},{6,10},{7,11},{8,12},{9,13},{1... | collective-permute-start | bytes 811016 | tf_op jit(solution)/shard_map/ppermute | solution.py:386
  19.8 2.5 %spread_bounds.1 = (bf16[512,4096]{1,0:T(8,128)(2,1)S(1)}, bf16[512,4096]{1,0:T(8,128)(2,1)S(1)}, bf16[512,4096]{1,0:T(8,128)(2,1)S(1)}) custom-call(s32[32,512]{1,0:T(8,128)S(1)} %bitcast.4, s32[32,512]{1,0:T(8,128)S(1)} %bitcast.5, bf16[512,4096]{1,0:T(8,128)(2,1)} %x_ref.3), custom_call_target="tpu_custom_call" | custom-call | flops 16777216 | bytes 131072 | tf_op jit(solution)/shard_map/spread_bounds/pallas_call | solution.py:289
  22.3 1.7 %attend_first.1.refs_4_ = f32[512,640]{1,0:T(8,128)S(1)} custom-call(bf16[512,256]{1,0:T(8,128)(2,1)S(1)} %project_query.1.refs_0_, s32[1,512]{1,0:T(1,128)S(1)} %bitcast.7, bf16[528,256]{1,0:T(8,128)(2,1)S(1)} %get-tuple-element.22.refs_2_, bf16[528,256]{1,0:T(8,128)(2,1)S(1)} %collective-permute-done.refs_3_, ...), custom_call_target="tpu_custom_call" | custom-call | flops 536870912 | bytes 1048576 | tf_op jit(solution)/shard_map/attend_first/pallas_call | solution.py:256
  24.0 2.8 %collective-permute-start.8 = (bf16[528,256]{1,0:T(8,128)(2,1)S(1)}, bf16[528,256]{1,0:T(8,128)(2,1)S(1)}, u32[]{:S(2)}, u32[]{:S(2)}) collective-permute-start(bf16[528,256]{1,0:T(8,128)(2,1)S(1)} %collective-permute-done.7.refs_2_), channel_id=1, source_target_pairs={{0,1},{1,0},{2,3},{3,2},{4,5},{5,4},{6,7},{7,6},{8,9},{9,8},{10,11... | collective-permute-start | bytes 811016 | tf_op jit(solution)/shard_map/ppermute | solution.py:377
  26.9 4.0 %collective-permute-done.4.refs_3_ = bf16[528,256]{1,0:T(8,128)(2,1)S(1)} collective-permute-done((bf16[528,256]{1,0:T(8,128)(2,1)S(1)}, bf16[528,256]{1,0:T(8,128)(2,1)S(1)}, u32[]{:S(2)}, u32[]{:S(2)}) %collective-permute-start.4) | collective-permute-done | bytes 270368 | tf_op jit(solution)/shard_map/ppermute | solution.py:393
  30.9 0.4 %collective-permute-start.5 = (bf16[528,256]{1,0:T(8,128)(2,1)S(1)}, bf16[528,256]{1,0:T(8,128)(2,1)S(1)}, u32[]{:S(2)}, u32[]{:S(2)}) collective-permute-start(bf16[528,256]{1,0:T(8,128)(2,1)S(1)} %collective-permute-done.1.refs_2_), channel_id=1, source_target_pairs={{0,1},{1,0},{2,3},{3,2},{4,5},{5,4},{6,7},{7,6},{8,9},{9,8},{10,11... | collective-permute-start | bytes 811016 | tf_op jit(solution)/shard_map/ppermute | solution.py:377
  31.3 0.1 collective-permute-start.6
  31.4 1.1 %collective-permute-done.5.refs_4_ = bf16[528,256]{1,0:T(8,128)(2,1)S(1)} collective-permute-done((bf16[528,256]{1,0:T(8,128)(2,1)S(1)}, bf16[528,256]{1,0:T(8,128)(2,1)S(1)}, u32[]{:S(2)}, u32[]{:S(2)}) %collective-permute-start.5) | collective-permute-done | bytes 270368 | tf_op jit(solution)/shard_map/ppermute | solution.py:377
  32.5 0.4 collective-permute-done.6.refs_5_
  32.9 0.8 %attend_last.1.a_ref = bf16[512,256]{1,0:T(8,128)(2,1)S(1)} custom-call(bf16[512,256]{1,0:T(8,128)(2,1)S(1)} %project_query.1.refs_0_, s32[1,512]{1,0:T(1,128)S(1)} %bitcast.9, bf16[528,256]{1,0:T(8,128)(2,1)S(1)} %collective-permute-done.1.refs_2_, bf16[528,256]{1,0:T(8,128)(2,1)S(1)} %collective-permute-done.4.refs_3_, ...), custom_call_target="tpu_custom_call" | custom-call | flops 536870912 | bytes 1048576 | tf_op jit(solution)/shard_map/attend_last/pallas_call | solution.py:256
  33.7 0.4 %collective-permute-start.9 = (bf16[512,256]{1,0:T(8,128)(2,1)S(1)}, bf16[512,256]{1,0:T(8,128)(2,1)S(1)}, u32[]{:S(2)}, u32[]{:S(2)}) collective-permute-start(bf16[512,256]{1,0:T(8,128)(2,1)S(1)} %attend_last.1.a_ref), channel_id=1, source_target_pairs={{0,1},{1,0},{2,3},{3,2},{4,5},{5,4},{6,7},{7,6},{8,9},{9,8},{10,11... | collective-permute-start | bytes 786440 | tf_op jit(solution)/shard_map/ppermute | solution.py:377
  34.2 1.5 %project_own.1.quant_ref = bf16[512,4096]{1,0:T(8,128)(2,1)S(1)} custom-call(bf16[512,256]{1,0:T(8,128)(2,1)S(1)} %attend_last.1.a_ref, bf16[256,4096]{1,0:T(8,128)(2,1)S(1)} %copy-done, bf16[512,4096]{1,0:T(8,128)(2,1)S(1)} %get-tuple-element.32.sum_ref), custom_call_target="tpu_custom_call" | custom-call | flops 1073741824 | bytes 10485760 | tf_op jit(solution)/shard_map/project_own/pallas_call | solution.py:320
  35.7 4.7 %project_out.1 = bf16[512,4096]{1,0:T(8,128)(2,1)} custom-call(bf16[512,256]{1,0:T(8,128)(2,1)S(1)} %collective-permute-done.9.b_ref, bf16[256,4096]{1,0:T(8,128)(2,1)S(1)} %collective-permute-done.10.wb_ref, bf16[512,4096]{1,0:T(8,128)(2,1)S(1)} %project_own.1.quant_ref, bf16[512,4096]{1,0:T(8,128)(2,1)S(1)} %get-tuple-element.34.x_ref, ...), custom_call_target="tpu_custom_call" | custom-call | flops 1073741824 | bytes 10485760 | tf_op jit(solution)/shard_map/project_out/pallas_call | solution.py:359
  (15 shorter events, 0.1 us)
Async XLA Ops:
  0.0 35.7 %collective-permute-start.10 = (bf16[256,4096]{1,0:T(8,128)(2,1)}, bf16[256,4096]{1,0:T(8,128)(2,1)S(1)}, u32[]{:S(2)}, u32[]{:S(2)}) collective-permute-start(bf16[256,4096]{1,0:T(8,128)(2,1)} %w_ref.3), channel_id=1, source_target_pairs={{0,1},{1,0},{2,3},{3,2},{4,5},{5,4},{6,7},{7,6},{8,9},{9,8},{10,11... | collective-permute-start | bytes 6291464 | tf_op jit(solution)/shard_map/ppermute | solution.py:377
  6.7 13.1 %copy-start.1 = (s32[512,32]{0,1:T(8,128)S(1)}, s32[512,32]{0,1:T(8,128)}, u32[]{:S(2)}) copy-start(s32[512,32]{0,1:T(8,128)} %param.14) | copy-start | bytes 196612
  6.7 13.1 %copy-start.2 = (s32[512,32]{0,1:T(8,128)S(1)}, s32[512,32]{0,1:T(8,128)}, u32[]{:S(2)}) copy-start(s32[512,32]{0,1:T(8,128)} %param.15) | copy-start | bytes 196612
  6.7 8.2 %collective-permute-start = (bf16[528,256]{1,0:T(8,128)(2,1)S(1)}, bf16[528,256]{1,0:T(8,128)(2,1)S(1)}, u32[]{:S(2)}, u32[]{:S(2)}) collective-permute-start(bf16[528,256]{1,0:T(8,128)(2,1)S(1)} %get-tuple-element.22.refs_2_), channel_id=1, source_target_pairs={{0,4},{1,5},{2,6},{3,7},{4,8},{5,9},{6,10},{7,11},{8,12},{9,13},{1... | collective-permute-start | bytes 811016 | tf_op jit(solution)/shard_map/ppermute | solution.py:386
  8.0 10.5 %collective-permute-start.2 = (bf16[528,256]{1,0:T(8,128)(2,1)S(1)}, bf16[528,256]{1,0:T(8,128)(2,1)S(1)}, u32[]{:S(2)}, u32[]{:S(2)}) collective-permute-start(bf16[528,256]{1,0:T(8,128)(2,1)S(1)} %get-tuple-element.22.refs_2_), channel_id=1, source_target_pairs={{0,1},{1,0},{2,3},{3,2},{4,5},{5,4},{6,7},{7,6},{8,9},{9,8},{10,11... | collective-permute-start | bytes 811016 | tf_op jit(solution)/shard_map/ppermute | solution.py:377
  9.6 12.8 %copy-start.3 = (s32[512]{0:T(512)S(1)}, s32[512]{0:T(512)}, u32[]{:S(2)}) copy-start(s32[512]{0:T(512)} %param.10) | copy-start | bytes 6148
  14.9 9.2 %collective-permute-start.7 = (bf16[528,256]{1,0:T(8,128)(2,1)S(1)}, bf16[528,256]{1,0:T(8,128)(2,1)S(1)}, u32[]{:S(2)}, u32[]{:S(2)}) collective-permute-start(bf16[528,256]{1,0:T(8,128)(2,1)S(1)} %collective-permute-done.refs_3_), channel_id=1, source_target_pairs={{0,1},{1,0},{2,3},{3,2},{4,6},{5,7},{6,8},{7,9},{8,10},{9,11},{10,... | collective-permute-start | bytes 811016 | tf_op jit(solution)/shard_map/ppermute | solution.py:386
  16.1 6.2 %collective-permute-start.3 = (bf16[528,256]{1,0:T(8,128)(2,1)S(1)}, bf16[528,256]{1,0:T(8,128)(2,1)S(1)}, u32[]{:S(2)}, u32[]{:S(2)}) collective-permute-start(bf16[528,256]{1,0:T(8,128)(2,1)S(1)} %collective-permute-done.refs_3_), channel_id=1, source_target_pairs={{0,1},{1,0},{2,3},{3,2},{4,5},{5,4},{6,7},{7,6},{8,9},{9,8},{10,11... | collective-permute-start | bytes 811016 | tf_op jit(solution)/shard_map/ppermute | solution.py:377
  17.2 13.7 %collective-permute-start.4 = (bf16[528,256]{1,0:T(8,128)(2,1)S(1)}, bf16[528,256]{1,0:T(8,128)(2,1)S(1)}, u32[]{:S(2)}, u32[]{:S(2)}) collective-permute-start(bf16[528,256]{1,0:T(8,128)(2,1)S(1)} %broadcast_select_fusion), channel_id=1, source_target_pairs={{0,2},{2,0},{4,6},{6,4},{8,10},{10,8},{12,14},{14,12},{1,3},{3,1},... | collective-permute-start | bytes 811016 | tf_op jit(solution)/shard_map/ppermute | solution.py:393
  18.5 12.4 %collective-permute-start.1 = (bf16[528,256]{1,0:T(8,128)(2,1)S(1)}, bf16[528,256]{1,0:T(8,128)(2,1)S(1)}, u32[]{:S(2)}, u32[]{:S(2)}) collective-permute-start(bf16[528,256]{1,0:T(8,128)(2,1)S(1)} %collective-permute-done.refs_3_), channel_id=1, source_target_pairs={{0,1},{1,0},{2,3},{3,2},{4,8},{5,9},{6,10},{7,11},{8,12},{9,13},{1... | collective-permute-start | bytes 811016 | tf_op jit(solution)/shard_map/ppermute | solution.py:386
  22.3 11.9 %copy-start = (bf16[256,4096]{1,0:T(8,128)(2,1)S(1)}, bf16[256,4096]{1,0:T(8,128)(2,1)}, u32[]{:S(2)}) copy-start(bf16[256,4096]{1,0:T(8,128)(2,1)} %w_ref.3) | copy-start | bytes 6291460
  24.0 7.4 %collective-permute-start.8 = (bf16[528,256]{1,0:T(8,128)(2,1)S(1)}, bf16[528,256]{1,0:T(8,128)(2,1)S(1)}, u32[]{:S(2)}, u32[]{:S(2)}) collective-permute-start(bf16[528,256]{1,0:T(8,128)(2,1)S(1)} %collective-permute-done.7.refs_2_), channel_id=1, source_target_pairs={{0,1},{1,0},{2,3},{3,2},{4,5},{5,4},{6,7},{7,6},{8,9},{9,8},{10,11... | collective-permute-start | bytes 811016 | tf_op jit(solution)/shard_map/ppermute | solution.py:377
  30.9 1.6 %collective-permute-start.5 = (bf16[528,256]{1,0:T(8,128)(2,1)S(1)}, bf16[528,256]{1,0:T(8,128)(2,1)S(1)}, u32[]{:S(2)}, u32[]{:S(2)}) collective-permute-start(bf16[528,256]{1,0:T(8,128)(2,1)S(1)} %collective-permute-done.1.refs_2_), channel_id=1, source_target_pairs={{0,1},{1,0},{2,3},{3,2},{4,5},{5,4},{6,7},{7,6},{8,9},{9,8},{10,11... | collective-permute-start | bytes 811016 | tf_op jit(solution)/shard_map/ppermute | solution.py:377
  31.3 1.6 %collective-permute-start.6 = (bf16[528,256]{1,0:T(8,128)(2,1)S(1)}, bf16[528,256]{1,0:T(8,128)(2,1)S(1)}, u32[]{:S(2)}, u32[]{:S(2)}) collective-permute-start(bf16[528,256]{1,0:T(8,128)(2,1)S(1)} %collective-permute-done.4.refs_3_), channel_id=1, source_target_pairs={{0,1},{1,0},{2,3},{3,2},{4,5},{5,4},{6,7},{7,6},{8,9},{9,8},{10,11... | collective-permute-start | bytes 811016 | tf_op jit(solution)/shard_map/ppermute | solution.py:377
  33.7 2.0 %collective-permute-start.9 = (bf16[512,256]{1,0:T(8,128)(2,1)S(1)}, bf16[512,256]{1,0:T(8,128)(2,1)S(1)}, u32[]{:S(2)}, u32[]{:S(2)}) collective-permute-start(bf16[512,256]{1,0:T(8,128)(2,1)S(1)} %attend_last.1.a_ref), channel_id=1, source_target_pairs={{0,1},{1,0},{2,3},{3,2},{4,5},{5,4},{6,7},{7,6},{8,9},{9,8},{10,11... | collective-permute-start | bytes 786440 | tf_op jit(solution)/shard_map/ppermute | solution.py:377

commit v20 on v19

--- a/solution.py
+++ b/solution.py
@@ -268,9 +268,9 @@
     )(*[in_vmem(operand) for operand in operands])
 
 
-def bounds_kernel(sum_ref, out_exp_ref, x_ref, sum_bound_ref, out_bound_ref, near_ref, sem):
+def bounds_kernel(sum_ref, out_exp_ref, x_ref, sum_bound_ref, out_bound_ref, wide_ref, near, sem):
     groups, rows = sum_ref.shape
-    fetch = pltpu.make_async_copy(x_ref, near_ref, sem)
+    fetch = pltpu.make_async_copy(x_ref, near, sem)
     fetch.start()
     per = sum_bound_ref.shape[1] // groups
     for exps, bound_ref in ((sum_ref, sum_bound_ref), (out_exp_ref, out_bound_ref)):
@@ -281,6 +281,13 @@
             bound_ref[:, group * per:(group + 1) * per] = wide
     fetch.wait()
 
+    def widen(step, carry):
+        span = pl.ds(pl.multiple_of(step * 64, 64), 64)
+        wide_ref[span, :] = near[span, :].astype(jnp.float32)
+        return carry
+
+    lax.fori_loop(0, rows // 64, widen, 0)
+
 
 def spread_bounds(sum_exps, out_exps, tokens):
     rows, width = tokens.shape
@@ -290,8 +297,8 @@
         bounds_kernel,
         in_specs=[vmem, vmem, pl.BlockSpec(memory_space=pltpu.HBM)],
         out_specs=[vmem] * 3,
-        out_shape=[pltpu.VMEM((rows, width), jnp.bfloat16)] * 3,
-        scratch_shapes=[pltpu.SemaphoreType.DMA(())],
+        out_shape=[pltpu.VMEM((rows, width), jnp.bfloat16)] * 2 + [pltpu.VMEM((rows, width), jnp.float32)],
+        scratch_shapes=[pltpu.VMEM((rows, width), jnp.bfloat16), pltpu.SemaphoreType.DMA(())],
         compiler_params=pltpu.CompilerParams(vmem_limit_bytes=10 * MIB),
         cost_estimate=pl.CostEstimate(flops=8 * rows * width, bytes_accessed=8 * rows * groups, transcendentals=0),
         name="spread_bounds",
@@ -344,7 +351,7 @@
             span = slice(start, start + tile)
             term = jnp.dot(b_ref[span, :], wb_ref[:, cols], preferred_element_type=jnp.float32)
             quant = clip(term, sum_ref[span, cols]).astype(jnp.float32) + quant_ref[span, cols].astype(jnp.float32)
-            staged[span, cols] = clip(x_ref[span, cols].astype(jnp.float32) + quant, last_ref[span, cols])
+            staged[span, cols] = clip(x_ref[span, cols] + quant, last_ref[span, cols])
         copy(index).start()
     for index in range(width // HD):
         copy(index).wait()

time: 40.7 us -> 40.4 us (level)
  starting transfers between devices: 11 us -> 10.5 us
    ppermute x7, starting transfers between devices: 5.82 us -> 5.26 us  [swap_cores(): return lax.ppermute(x, 'tp', [(0, 1), (1, 0)])]
    pallas_call x1, Pallas kernels: 2.49 us -> 3.05 us  [spread_bounds(): pl.pallas_call(bounds_kernel, in_specs=[vmem, vmem, pl.BlockSpec(memory_s...]
  transfers between devices with their start and end apart: 11 -> 11, of which waited for: 4 -> 4; matrix products, arithmetic and copies ran while one was open for 0% -> 0% of each run, Pallas kernels for 34% -> 36%
where the time goes in v20:
time: 40.4 us; the launch traced here: 40.2 us
  Pallas kernels  18.6 us (46%)
  waiting for transfers between devices  10.8 us (27%)
  starting transfers between devices  10.5 us (26%)
    pallas_call x1, Pallas kernels, norm_kv(): pl.pallas_call(norm_kv_kernel, in_specs=[hbm] * 5, out_specs=[vmem] * 3,...  5.98 us
    ppermute x3, waiting for transfers between devices, shift(): return lax.ppermute(x, ('seq', 'tp'), pairs)  5.27 us
    ppermute x7, starting transfers between devices, swap_cores(): return lax.ppermute(x, 'tp', [(0, 1), (1, 0)])  5.26 us
    pallas_call x1, Pallas kernels, project_out(): pl.pallas_call(output_kernel, in_specs=[vmem] * len(operands), out_specs=...  4.33 us
    ppermute x1, waiting for transfers between devices, on_device(): lax.ppermute(jnp.where(odd, held, message), 'seq', [(i, i ^ 1) for i in r...  4.04 us
    ppermute x3, starting transfers between devices, shift(): return lax.ppermute(x, ('seq', 'tp'), pairs)  3.89 us
    pallas_call x1, Pallas kernels, spread_bounds(): pl.pallas_call(bounds_kernel, in_specs=[vmem, vmem, pl.BlockSpec(memory_s...  3.05 us
    pallas_call x3, Pallas kernels, attend(): pl.pallas_call(functools.partial(attend_kernel, plan, first, last), in_sp...  2.49 us
  transfers between devices with their start and end apart: 11, of which 4 were waited for; matrix products, arithmetic and copies ran while one was open for 0% of the time, Pallas kernels for 36%

profile of v20, /device:TPU:11, one launch (start us, length us, event | category | flops | bytes accessed | tf_op | source)
XLA Modules:
  0.0 40.2 jit_solution(9640405335617342135)
XLA Ops:
  0.0 0.7 %collective-permute-start.10 = (bf16[256,4096]{1,0:T(8,128)(2,1)}, bf16[256,4096]{1,0:T(8,128)(2,1)S(1)}, u32[]{:S(2)}, u32[]{:S(2)}) collective-permute-start(bf16[256,4096]{1,0:T(8,128)(2,1)} %w_ref.3), channel_id=1, source_target_pairs={{0,1},{1,0},{2,3},{3,2},{4,5},{5,4},{6,7},{7,6},{8,9},{9,8},{10,11... | collective-permute-start | bytes 6291464 | tf_op jit(solution)/shard_map/ppermute | solution.py:384
  0.7 6.0 %norm_kv.1 = (bf16[528,256]{1,0:T(8,128)(2,1)S(1)}, bf16[512,4096]{1,0:T(8,128)(2,1)S(1)}, bf16[4096,256]{1,0:T(8,128)(2,1)S(1)}) custom-call(bf16[512,4096]{1,0:T(8,128)(2,1)} %x_ref.3, f32[1,4096]{1,0:T(1,128)} %bitcast.10, bf16[4096,256]{1,0:T(8,128)(2,1)} %w_ref.2, s32[1,512]{1,0:T(1,128)} %bitcast.6, bf16[4096,256]{1,0:T(8,128)(2,1)} %next_ref.1), custom_call_target="tpu_custom_call" | custom-call | flops 1073741824 | bytes 10485760 | tf_op jit(solution)/shard_map/norm_kv/pallas_call | solution.py:116
  6.7 0.0 copy-start.1
  6.7 0.0 copy-start.2
  6.7 1.3 %collective-permute-start = (bf16[528,256]{1,0:T(8,128)(2,1)S(1)}, bf16[528,256]{1,0:T(8,128)(2,1)S(1)}, u32[]{:S(2)}, u32[]{:S(2)}) collective-permute-start(bf16[528,256]{1,0:T(8,128)(2,1)S(1)} %get-tuple-element.22.refs_2_), channel_id=1, source_target_pairs={{0,4},{1,5},{2,6},{3,7},{4,8},{5,9},{6,10},{7,11},{8,12},{9,13},{1... | collective-permute-start | bytes 811016 | tf_op jit(solution)/shard_map/ppermute | solution.py:393
  8.0 0.3 collective-permute-start.2
  8.3 1.2 %project_query.1.refs_0_ = bf16[512,256]{1,0:T(8,128)(2,1)S(1)} custom-call(bf16[512,4096]{1,0:T(8,128)(2,1)S(1)} %get-tuple-element.23.x_ref, bf16[4096,256]{1,0:T(8,128)(2,1)S(1)} %get-tuple-element.24.w_ref), custom_call_target="tpu_custom_call" | custom-call | flops 1073741824 | bytes 6291456 | tf_op jit(solution)/shard_map/project_query/pallas_call | solution.py:148
  9.6 5.3 %collective-permute-done.refs_3_ = bf16[528,256]{1,0:T(8,128)(2,1)S(1)} collective-permute-done((bf16[528,256]{1,0:T(8,128)(2,1)S(1)}, bf16[528,256]{1,0:T(8,128)(2,1)S(1)}, u32[]{:S(2)}, u32[]{:S(2)}) %collective-permute-start) | collective-permute-done | bytes 270368 | tf_op jit(solution)/shard_map/ppermute | solution.py:393
  14.9 1.2 %collective-permute-start.7 = (bf16[528,256]{1,0:T(8,128)(2,1)S(1)}, bf16[528,256]{1,0:T(8,128)(2,1)S(1)}, u32[]{:S(2)}, u32[]{:S(2)}) collective-permute-start(bf16[528,256]{1,0:T(8,128)(2,1)S(1)} %collective-permute-done.refs_3_), channel_id=1, source_target_pairs={{0,1},{1,0},{2,3},{3,2},{4,6},{5,7},{6,8},{7,9},{8,10},{9,11},{10,... | collective-permute-start | bytes 811016 | tf_op jit(solution)/shard_map/ppermute | solution.py:393
  16.1 1.1 %collective-permute-start.3 = (bf16[528,256]{1,0:T(8,128)(2,1)S(1)}, bf16[528,256]{1,0:T(8,128)(2,1)S(1)}, u32[]{:S(2)}, u32[]{:S(2)}) collective-permute-start(bf16[528,256]{1,0:T(8,128)(2,1)S(1)} %collective-permute-done.refs_3_), channel_id=1, source_target_pairs={{0,1},{1,0},{2,3},{3,2},{4,5},{5,4},{6,7},{7,6},{8,9},{9,8},{10,11... | collective-permute-start | bytes 811016 | tf_op jit(solution)/shard_map/ppermute | solution.py:384
  17.2 1.3 %collective-permute-start.4 = (bf16[528,256]{1,0:T(8,128)(2,1)S(1)}, bf16[528,256]{1,0:T(8,128)(2,1)S(1)}, u32[]{:S(2)}, u32[]{:S(2)}) collective-permute-start(bf16[528,256]{1,0:T(8,128)(2,1)S(1)} %broadcast_select_fusion), channel_id=1, source_target_pairs={{0,2},{2,0},{4,6},{6,4},{8,10},{10,8},{12,14},{14,12},{1,3},{3,1},... | collective-permute-start | bytes 811016 | tf_op jit(solution)/shard_map/ppermute | solution.py:400
  18.5 1.3 %collective-permute-start.1 = (bf16[528,256]{1,0:T(8,128)(2,1)S(1)}, bf16[528,256]{1,0:T(8,128)(2,1)S(1)}, u32[]{:S(2)}, u32[]{:S(2)}) collective-permute-start(bf16[528,256]{1,0:T(8,128)(2,1)S(1)} %collective-permute-done.refs_3_), channel_id=1, source_target_pairs={{0,1},{1,0},{2,3},{3,2},{4,8},{5,9},{6,10},{7,11},{8,12},{9,13},{1... | collective-permute-start | bytes 811016 | tf_op jit(solution)/shard_map/ppermute | solution.py:393
  19.8 3.0 %spread_bounds.1 = (bf16[512,4096]{1,0:T(8,128)(2,1)S(1)}, bf16[512,4096]{1,0:T(8,128)(2,1)S(1)}, f32[512,4096]{1,0:T(8,128)S(1)}) custom-call(s32[32,512]{1,0:T(8,128)S(1)} %bitcast.4, s32[32,512]{1,0:T(8,128)S(1)} %bitcast.5, bf16[512,4096]{1,0:T(8,128)(2,1)} %x_ref.3), custom_call_target="tpu_custom_call" | custom-call | flops 16777216 | bytes 131072 | tf_op jit(solution)/shard_map/spread_bounds/pallas_call | solution.py:296
  22.9 1.7 %attend_first.1.refs_4_ = f32[512,640]{1,0:T(8,128)S(1)} custom-call(bf16[512,256]{1,0:T(8,128)(2,1)S(1)} %project_query.1.refs_0_, s32[1,512]{1,0:T(1,128)S(1)} %bitcast.7, bf16[528,256]{1,0:T(8,128)(2,1)S(1)} %get-tuple-element.22.refs_2_, bf16[528,256]{1,0:T(8,128)(2,1)S(1)} %collective-permute-done.refs_3_, ...), custom_call_target="tpu_custom_call" | custom-call | flops 536870912 | bytes 1048576 | tf_op jit(solution)/shard_map/attend_first/pallas_call | solution.py:256
  24.6 2.3 %collective-permute-start.8 = (bf16[528,256]{1,0:T(8,128)(2,1)S(1)}, bf16[528,256]{1,0:T(8,128)(2,1)S(1)}, u32[]{:S(2)}, u32[]{:S(2)}) collective-permute-start(bf16[528,256]{1,0:T(8,128)(2,1)S(1)} %collective-permute-done.7.refs_2_), channel_id=1, source_target_pairs={{0,1},{1,0},{2,3},{3,2},{4,5},{5,4},{6,7},{7,6},{8,9},{9,8},{10,11... | collective-permute-start | bytes 811016 | tf_op jit(solution)/shard_map/ppermute | solution.py:384
  26.9 4.0 %collective-permute-done.4.refs_3_ = bf16[528,256]{1,0:T(8,128)(2,1)S(1)} collective-permute-done((bf16[528,256]{1,0:T(8,128)(2,1)S(1)}, bf16[528,256]{1,0:T(8,128)(2,1)S(1)}, u32[]{:S(2)}, u32[]{:S(2)}) %collective-permute-start.4) | collective-permute-done | bytes 270368 | tf_op jit(solution)/shard_map/ppermute | solution.py:400
  30.9 0.4 %collective-permute-start.5 = (bf16[528,256]{1,0:T(8,128)(2,1)S(1)}, bf16[528,256]{1,0:T(8,128)(2,1)S(1)}, u32[]{:S(2)}, u32[]{:S(2)}) collective-permute-start(bf16[528,256]{1,0:T(8,128)(2,1)S(1)} %collective-permute-done.1.refs_2_), channel_id=1, source_target_pairs={{0,1},{1,0},{2,3},{3,2},{4,5},{5,4},{6,7},{7,6},{8,9},{9,8},{10,11... | collective-permute-start | bytes 811016 | tf_op jit(solution)/shard_map/ppermute | solution.py:384
  31.3 0.1 collective-permute-start.6
  31.4 1.1 %collective-permute-done.5.refs_4_ = bf16[528,256]{1,0:T(8,128)(2,1)S(1)} collective-permute-done((bf16[528,256]{1,0:T(8,128)(2,1)S(1)}, bf16[528,256]{1,0:T(8,128)(2,1)S(1)}, u32[]{:S(2)}, u32[]{:S(2)}) %collective-permute-start.5) | collective-permute-done | bytes 270368 | tf_op jit(solution)/shard_map/ppermute | solution.py:384
  32.5 0.4 collective-permute-done.6.refs_5_
  32.9 0.8 %attend_last.1.a_ref = bf16[512,256]{1,0:T(8,128)(2,1)S(1)} custom-call(bf16[512,256]{1,0:T(8,128)(2,1)S(1)} %project_query.1.refs_0_, s32[1,512]{1,0:T(1,128)S(1)} %bitcast.9, bf16[528,256]{1,0:T(8,128)(2,1)S(1)} %collective-permute-done.1.refs_2_, bf16[528,256]{1,0:T(8,128)(2,1)S(1)} %collective-permute-done.4.refs_3_, ...), custom_call_target="tpu_custom_call" | custom-call | flops 536870912 | bytes 1048576 | tf_op jit(solution)/shard_map/attend_last/pallas_call | solution.py:256
  33.7 0.4 %collective-permute-start.9 = (bf16[512,256]{1,0:T(8,128)(2,1)S(1)}, bf16[512,256]{1,0:T(8,128)(2,1)S(1)}, u32[]{:S(2)}, u32[]{:S(2)}) collective-permute-start(bf16[512,256]{1,0:T(8,128)(2,1)S(1)} %attend_last.1.a_ref), channel_id=1, source_target_pairs={{0,1},{1,0},{2,3},{3,2},{4,5},{5,4},{6,7},{7,6},{8,9},{9,8},{10,11... | collective-permute-start | bytes 786440 | tf_op jit(solution)/shard_map/ppermute | solution.py:384
  34.2 1.5 %project_own.1.quant_ref = bf16[512,4096]{1,0:T(8,128)(2,1)S(1)} custom-call(bf16[512,256]{1,0:T(8,128)(2,1)S(1)} %attend_last.1.a_ref, bf16[256,4096]{1,0:T(8,128)(2,1)S(1)} %copy-done, bf16[512,4096]{1,0:T(8,128)(2,1)S(1)} %get-tuple-element.32.sum_ref), custom_call_target="tpu_custom_call" | custom-call | flops 1073741824 | bytes 10485760 | tf_op jit(solution)/shard_map/project_own/pallas_call | solution.py:327
  35.7 4.3 %project_out.1 = bf16[512,4096]{1,0:T(8,128)(2,1)} custom-call(bf16[512,256]{1,0:T(8,128)(2,1)S(1)} %collective-permute-done.9.b_ref, bf16[256,4096]{1,0:T(8,128)(2,1)S(1)} %collective-permute-done.10.wb_ref, bf16[512,4096]{1,0:T(8,128)(2,1)S(1)} %project_own.1.quant_ref, f32[512,4096]{1,0:T(8,128)S(1)} %get-tuple-element.34.x_ref, ...), custom_call_target="tpu_custom_call" | custom-call | flops 1073741824 | bytes 10485760 | tf_op jit(solution)/shard_map/project_out/pallas_call | solution.py:366
  (15 shorter events, 0.1 us)
Async XLA Ops:
  0.0 35.7 %collective-permute-start.10 = (bf16[256,4096]{1,0:T(8,128)(2,1)}, bf16[256,4096]{1,0:T(8,128)(2,1)S(1)}, u32[]{:S(2)}, u32[]{:S(2)}) collective-permute-start(bf16[256,4096]{1,0:T(8,128)(2,1)} %w_ref.3), channel_id=1, source_target_pairs={{0,1},{1,0},{2,3},{3,2},{4,5},{5,4},{6,7},{7,6},{8,9},{9,8},{10,11... | collective-permute-start | bytes 6291464 | tf_op jit(solution)/shard_map/ppermute | solution.py:384
  6.7 13.1 %copy-start.1 = (s32[512,32]{0,1:T(8,128)S(1)}, s32[512,32]{0,1:T(8,128)}, u32[]{:S(2)}) copy-start(s32[512,32]{0,1:T(8,128)} %param.14) | copy-start | bytes 196612
  6.7 13.1 %copy-start.2 = (s32[512,32]{0,1:T(8,128)S(1)}, s32[512,32]{0,1:T(8,128)}, u32[]{:S(2)}) copy-start(s32[512,32]{0,1:T(8,128)} %param.15) | copy-start | bytes 196612
  6.7 8.2 %collective-permute-start = (bf16[528,256]{1,0:T(8,128)(2,1)S(1)}, bf16[528,256]{1,0:T(8,128)(2,1)S(1)}, u32[]{:S(2)}, u32[]{:S(2)}) collective-permute-start(bf16[528,256]{1,0:T(8,128)(2,1)S(1)} %get-tuple-element.22.refs_2_), channel_id=1, source_target_pairs={{0,4},{1,5},{2,6},{3,7},{4,8},{5,9},{6,10},{7,11},{8,12},{9,13},{1... | collective-permute-start | bytes 811016 | tf_op jit(solution)/shard_map/ppermute | solution.py:393
  8.0 10.5 %collective-permute-start.2 = (bf16[528,256]{1,0:T(8,128)(2,1)S(1)}, bf16[528,256]{1,0:T(8,128)(2,1)S(1)}, u32[]{:S(2)}, u32[]{:S(2)}) collective-permute-start(bf16[528,256]{1,0:T(8,128)(2,1)S(1)} %get-tuple-element.22.refs_2_), channel_id=1, source_target_pairs={{0,1},{1,0},{2,3},{3,2},{4,5},{5,4},{6,7},{7,6},{8,9},{9,8},{10,11... | collective-permute-start | bytes 811016 | tf_op jit(solution)/shard_map/ppermute | solution.py:384
  9.6 13.3 %copy-start.3 = (s32[512]{0:T(512)S(1)}, s32[512]{0:T(512)}, u32[]{:S(2)}) copy-start(s32[512]{0:T(512)} %param.10) | copy-start | bytes 6148
  14.9 9.7 %collective-permute-start.7 = (bf16[528,256]{1,0:T(8,128)(2,1)S(1)}, bf16[528,256]{1,0:T(8,128)(2,1)S(1)}, u32[]{:S(2)}, u32[]{:S(2)}) collective-permute-start(bf16[528,256]{1,0:T(8,128)(2,1)S(1)} %collective-permute-done.refs_3_), channel_id=1, source_target_pairs={{0,1},{1,0},{2,3},{3,2},{4,6},{5,7},{6,8},{7,9},{8,10},{9,11},{10,... | collective-permute-start | bytes 811016 | tf_op jit(solution)/shard_map/ppermute | solution.py:393
  16.1 6.8 %collective-permute-start.3 = (bf16[528,256]{1,0:T(8,128)(2,1)S(1)}, bf16[528,256]{1,0:T(8,128)(2,1)S(1)}, u32[]{:S(2)}, u32[]{:S(2)}) collective-permute-start(bf16[528,256]{1,0:T(8,128)(2,1)S(1)} %collective-permute-done.refs_3_), channel_id=1, source_target_pairs={{0,1},{1,0},{2,3},{3,2},{4,5},{5,4},{6,7},{7,6},{8,9},{9,8},{10,11... | collective-permute-start | bytes 811016 | tf_op jit(solution)/shard_map/ppermute | solution.py:384
  17.2 13.7 %collective-permute-start.4 = (bf16[528,256]{1,0:T(8,128)(2,1)S(1)}, bf16[528,256]{1,0:T(8,128)(2,1)S(1)}, u32[]{:S(2)}, u32[]{:S(2)}) collective-permute-start(bf16[528,256]{1,0:T(8,128)(2,1)S(1)} %broadcast_select_fusion), channel_id=1, source_target_pairs={{0,2},{2,0},{4,6},{6,4},{8,10},{10,8},{12,14},{14,12},{1,3},{3,1},... | collective-permute-start | bytes 811016 | tf_op jit(solution)/shard_map/ppermute | solution.py:400
  18.5 12.4 %collective-permute-start.1 = (bf16[528,256]{1,0:T(8,128)(2,1)S(1)}, bf16[528,256]{1,0:T(8,128)(2,1)S(1)}, u32[]{:S(2)}, u32[]{:S(2)}) collective-permute-start(bf16[528,256]{1,0:T(8,128)(2,1)S(1)} %collective-permute-done.refs_3_), channel_id=1, source_target_pairs={{0,1},{1,0},{2,3},{3,2},{4,8},{5,9},{6,10},{7,11},{8,12},{9,13},{1... | collective-permute-start | bytes 811016 | tf_op jit(solution)/shard_map/ppermute | solution.py:393
  22.9 11.3 %copy-start = (bf16[256,4096]{1,0:T(8,128)(2,1)S(1)}, bf16[256,4096]{1,0:T(8,128)(2,1)}, u32[]{:S(2)}) copy-start(bf16[256,4096]{1,0:T(8,128)(2,1)} %w_ref.3) | copy-start | bytes 6291460
  24.6 6.8 %collective-permute-start.8 = (bf16[528,256]{1,0:T(8,128)(2,1)S(1)}, bf16[528,256]{1,0:T(8,128)(2,1)S(1)}, u32[]{:S(2)}, u32[]{:S(2)}) collective-permute-start(bf16[528,256]{1,0:T(8,128)(2,1)S(1)} %collective-permute-done.7.refs_2_), channel_id=1, source_target_pairs={{0,1},{1,0},{2,3},{3,2},{4,5},{5,4},{6,7},{7,6},{8,9},{9,8},{10,11... | collective-permute-start | bytes 811016 | tf_op jit(solution)/shard_map/ppermute | solution.py:384
  30.9 1.6 %collective-permute-start.5 = (bf16[528,256]{1,0:T(8,128)(2,1)S(1)}, bf16[528,256]{1,0:T(8,128)(2,1)S(1)}, u32[]{:S(2)}, u32[]{:S(2)}) collective-permute-start(bf16[528,256]{1,0:T(8,128)(2,1)S(1)} %collective-permute-done.1.refs_2_), channel_id=1, source_target_pairs={{0,1},{1,0},{2,3},{3,2},{4,5},{5,4},{6,7},{7,6},{8,9},{9,8},{10,11... | collective-permute-start | bytes 811016 | tf_op jit(solution)/shard_map/ppermute | solution.py:384
  31.3 1.6 %collective-permute-start.6 = (bf16[528,256]{1,0:T(8,128)(2,1)S(1)}, bf16[528,256]{1,0:T(8,128)(2,1)S(1)}, u32[]{:S(2)}, u32[]{:S(2)}) collective-permute-start(bf16[528,256]{1,0:T(8,128)(2,1)S(1)} %collective-permute-done.4.refs_3_), channel_id=1, source_target_pairs={{0,1},{1,0},{2,3},{3,2},{4,5},{5,4},{6,7},{7,6},{8,9},{9,8},{10,11... | collective-permute-start | bytes 811016 | tf_op jit(solution)/shard_map/ppermute | solution.py:384
  33.7 2.0 %collective-permute-start.9 = (bf16[512,256]{1,0:T(8,128)(2,1)S(1)}, bf16[512,256]{1,0:T(8,128)(2,1)S(1)}, u32[]{:S(2)}, u32[]{:S(2)}) collective-permute-start(bf16[512,256]{1,0:T(8,128)(2,1)S(1)} %attend_last.1.a_ref), channel_id=1, source_target_pairs={{0,1},{1,0},{2,3},{3,2},{4,5},{5,4},{6,7},{7,6},{8,9},{9,8},{10,11... | collective-permute-start | bytes 786440 | tf_op jit(solution)/shard_map/ppermute | solution.py:384

commit v21 on v20

--- a/solution.py
+++ b/solution.py
@@ -414,7 +414,11 @@
             bounds, state = early = lax.optimization_barrier((bounds, state))
         if number > 0:
             mine = [lax.optimization_barrier((block, early))[0] for block in mine]
-        other = [swap_cores(m) for m in mine]
+        other = []
+        for block in mine:
+            if number == len(parts) - 1 and other:
+                block = lax.optimization_barrier((block, other[-1]))[0]
+            other.append(swap_cores(block))
         state = attend(query, segments, plan, mine, other, state, number == len(parts) - 1)
     quant_own = project_own(state, w_out, bounds[0])
     return project_out(swap_cores(state), w_other, quant_own, *bounds)

time: 40.4 us -> 41.4 us (1.025); the launches traced: 40.2 us -> 40.6 us
  starting transfers between devices: 10.5 us -> 9.11 us
  waiting for transfers between devices: 10.8 us -> 11.8 us
  local copies, waits for them, and re-layouts: 0.03 us -> 0.86 us
    ppermute x7, starting transfers between devices: 5.26 us -> 3.92 us  [swap_cores(): return lax.ppermute(x, 'tp', [(0, 1), (1, 0)])]
    unnamed x8, local copies, waits for them, and re-layouts: 0.03 us -> 0.86 us
    ppermute x1, waiting for transfers between devices: 4.04 us -> 4.83 us  [on_device(): lax.ppermute(jnp.where(odd, held, message), 'seq', [(i, i ^ 1) for i in r...]
    ppermute x3, waiting for transfers between devices: 5.27 us -> 5.74 us  [shift(): return lax.ppermute(x, ('seq', 'tp'), pairs)]
  transfers between devices with their start and end apart: 11 -> 11, of which waited for: 4 -> 4; matrix products, arithmetic and copies ran while one was open for 0% -> 0% of each run, Pallas kernels for 36% -> 35%
where the time goes in v21:
time: 41.4 us; the launch traced here: 40.6 us
  Pallas kernels  18.6 us (45%)
  waiting for transfers between devices  11.8 us (29%)
  starting transfers between devices  9.11 us (22%)
  local copies, waits for them, and re-layouts  0.86 us (2%)
    pallas_call x1, Pallas kernels, norm_kv(): pl.pallas_call(norm_kv_kernel, in_specs=[hbm] * 5, out_specs=[vmem] * 3,...  5.98 us
    ppermute x3, waiting for transfers between devices, shift(): return lax.ppermute(x, ('seq', 'tp'), pairs)  5.74 us
    ppermute x1, waiting for transfers between devices, on_device(): lax.ppermute(jnp.where(odd, held, message), 'seq', [(i, i ^ 1) for i in r...  4.83 us
    pallas_call x1, Pallas kernels, project_out(): pl.pallas_call(output_kernel, in_specs=[vmem] * len(operands), out_specs=...  4.33 us
    ppermute x7, starting transfers between devices, swap_cores(): return lax.ppermute(x, 'tp', [(0, 1), (1, 0)])  3.92 us
    ppermute x3, starting transfers between devices, shift(): return lax.ppermute(x, ('seq', 'tp'), pairs)  3.88 us
    pallas_call x1, Pallas kernels, spread_bounds(): pl.pallas_call(bounds_kernel, in_specs=[vmem, vmem, pl.BlockSpec(memory_s...  3.05 us
    pallas_call x3, Pallas kernels, attend(): pl.pallas_call(functools.partial(attend_kernel, plan, first, last), in_sp...  2.46 us
  transfers between devices with their start and end apart: 11, of which 4 were waited for; matrix products, arithmetic and copies ran while one was open for 0% of the time, Pallas kernels for 35%

profile of v21, /device:TPU:11, one launch (start us, length us, event | category | flops | bytes accessed | tf_op | source)
XLA Modules:
  0.0 40.6 jit_solution(9598847958409006031)
XLA Ops:
  0.0 0.7 %collective-permute-start.10 = (bf16[256,4096]{1,0:T(8,128)(2,1)}, bf16[256,4096]{1,0:T(8,128)(2,1)S(1)}, u32[]{:S(2)}, u32[]{:S(2)}) collective-permute-start(bf16[256,4096]{1,0:T(8,128)(2,1)} %w_ref.3), channel_id=1, source_target_pairs={{0,1},{1,0},{2,3},{3,2},{4,5},{5,4},{6,7},{7,6},{8,9},{9,8},{10,11... | collective-permute-start | bytes 6291464 | tf_op jit(solution)/shard_map/ppermute | solution.py:384
  0.7 6.0 %norm_kv.1 = (bf16[528,256]{1,0:T(8,128)(2,1)S(1)}, bf16[512,4096]{1,0:T(8,128)(2,1)S(1)}, bf16[4096,256]{1,0:T(8,128)(2,1)S(1)}) custom-call(bf16[512,4096]{1,0:T(8,128)(2,1)} %x_ref.3, f32[1,4096]{1,0:T(1,128)} %bitcast.10, bf16[4096,256]{1,0:T(8,128)(2,1)} %w_ref.2, s32[1,512]{1,0:T(1,128)} %bitcast.6, bf16[4096,256]{1,0:T(8,128)(2,1)} %next_ref.1), custom_call_target="tpu_custom_call" | custom-call | flops 1073741824 | bytes 10485760 | tf_op jit(solution)/shard_map/norm_kv/pallas_call | solution.py:116
  6.7 0.0 copy-start.1
  6.7 1.3 %collective-permute-start = (bf16[528,256]{1,0:T(8,128)(2,1)S(1)}, bf16[528,256]{1,0:T(8,128)(2,1)S(1)}, u32[]{:S(2)}, u32[]{:S(2)}) collective-permute-start(bf16[528,256]{1,0:T(8,128)(2,1)S(1)} %get-tuple-element.23.refs_2_), channel_id=1, source_target_pairs={{0,4},{1,5},{2,6},{3,7},{4,8},{5,9},{6,10},{7,11},{8,12},{9,13},{1... | collective-permute-start | bytes 811016 | tf_op jit(solution)/shard_map/ppermute | solution.py:393
  8.0 0.3 collective-permute-start.2
  8.3 1.2 %project_query.1.refs_0_ = bf16[512,256]{1,0:T(8,128)(2,1)S(1)} custom-call(bf16[512,4096]{1,0:T(8,128)(2,1)S(1)} %get-tuple-element.24.x_ref, bf16[4096,256]{1,0:T(8,128)(2,1)S(1)} %get-tuple-element.25.w_ref), custom_call_target="tpu_custom_call" | custom-call | flops 1073741824 | bytes 6291456 | tf_op jit(solution)/shard_map/project_query/pallas_call | solution.py:148
  9.6 5.3 %collective-permute-done.refs_3_ = bf16[528,256]{1,0:T(8,128)(2,1)S(1)} collective-permute-done((bf16[528,256]{1,0:T(8,128)(2,1)S(1)}, bf16[528,256]{1,0:T(8,128)(2,1)S(1)}, u32[]{:S(2)}, u32[]{:S(2)}) %collective-permute-start) | collective-permute-done | bytes 270368 | tf_op jit(solution)/shard_map/ppermute | solution.py:393
  14.8 0.8 %collective-permute-start.3 = (bf16[528,256]{1,0:T(8,128)(2,1)S(1)}, bf16[528,256]{1,0:T(8,128)(2,1)S(1)}, u32[]{:S(2)}, u32[]{:S(2)}) collective-permute-start(bf16[528,256]{1,0:T(8,128)(2,1)S(1)} %collective-permute-done.refs_3_), channel_id=1, source_target_pairs={{0,1},{1,0},{2,3},{3,2},{4,5},{5,4},{6,7},{7,6},{8,9},{9,8},{10,11... | collective-permute-start | bytes 811016 | tf_op jit(solution)/shard_map/ppermute | solution.py:384
  15.6 1.2 %collective-permute-start.7 = (bf16[528,256]{1,0:T(8,128)(2,1)S(1)}, bf16[528,256]{1,0:T(8,128)(2,1)S(1)}, u32[]{:S(2)}, u32[]{:S(2)}) collective-permute-start(bf16[528,256]{1,0:T(8,128)(2,1)S(1)} %collective-permute-done.refs_3_), channel_id=1, source_target_pairs={{0,1},{1,0},{2,3},{3,2},{4,6},{5,7},{6,8},{7,9},{8,10},{9,11},{10,... | collective-permute-start | bytes 811016 | tf_op jit(solution)/shard_map/ppermute | solution.py:393
  16.9 1.3 %collective-permute-start.1 = (bf16[528,256]{1,0:T(8,128)(2,1)S(1)}, bf16[528,256]{1,0:T(8,128)(2,1)S(1)}, u32[]{:S(2)}, u32[]{:S(2)}) collective-permute-start(bf16[528,256]{1,0:T(8,128)(2,1)S(1)} %collective-permute-done.refs_3_), channel_id=1, source_target_pairs={{0,1},{1,0},{2,3},{3,2},{4,8},{5,9},{6,10},{7,11},{8,12},{9,13},{1... | collective-permute-start | bytes 811016 | tf_op jit(solution)/shard_map/ppermute | solution.py:393
  18.2 0.8 %copy-done.2 = s32[512,32]{0,1:T(8,128)S(1)} copy-done((s32[512,32]{0,1:T(8,128)S(1)}, s32[512,32]{0,1:T(8,128)}, u32[]{:S(2)}) %copy-start.2) | copy-done | bytes 65560
  19.0 3.0 %spread_bounds.1 = (bf16[512,4096]{1,0:T(8,128)(2,1)S(1)}, bf16[512,4096]{1,0:T(8,128)(2,1)S(1)}, f32[512,4096]{1,0:T(8,128)S(1)}) custom-call(s32[32,512]{1,0:T(8,128)S(1)} %bitcast.4, s32[32,512]{1,0:T(8,128)S(1)} %bitcast.5, bf16[512,4096]{1,0:T(8,128)(2,1)} %x_ref.3), custom_call_target="tpu_custom_call" | custom-call | flops 16777216 | bytes 131072 | tf_op jit(solution)/shard_map/spread_bounds/pallas_call | solution.py:296
  22.1 1.3 %collective-permute-start.4 = (bf16[528,256]{1,0:T(8,128)(2,1)S(1)}, bf16[528,256]{1,0:T(8,128)(2,1)S(1)}, u32[]{:S(2)}, u32[]{:S(2)}) collective-permute-start(bf16[528,256]{1,0:T(8,128)(2,1)S(1)} %broadcast_select_fusion), channel_id=1, source_target_pairs={{0,2},{2,0},{4,6},{6,4},{8,10},{10,8},{12,14},{14,12},{1,3},{3,1},... | collective-permute-start | bytes 811016 | tf_op jit(solution)/shard_map/ppermute | solution.py:400
  23.4 1.6 %attend_first.1.refs_4_ = f32[512,640]{1,0:T(8,128)S(1)} custom-call(bf16[512,256]{1,0:T(8,128)(2,1)S(1)} %project_query.1.refs_0_, s32[1,512]{1,0:T(1,128)S(1)} %bitcast.7, bf16[528,256]{1,0:T(8,128)(2,1)S(1)} %get-tuple-element.23.refs_2_, bf16[528,256]{1,0:T(8,128)(2,1)S(1)} %collective-permute-done.refs_3_, ...), custom_call_target="tpu_custom_call" | custom-call | flops 536870912 | bytes 1048576 | tf_op jit(solution)/shard_map/attend_first/pallas_call | solution.py:256
  25.1 0.5 %collective-permute-done.1.refs_2_ = bf16[528,256]{1,0:T(8,128)(2,1)S(1)} collective-permute-done((bf16[528,256]{1,0:T(8,128)(2,1)S(1)}, bf16[528,256]{1,0:T(8,128)(2,1)S(1)}, u32[]{:S(2)}, u32[]{:S(2)}) %collective-permute-start.1) | collective-permute-done | bytes 270368 | tf_op jit(solution)/shard_map/ppermute | solution.py:393
  25.6 1.1 %collective-permute-start.5 = (bf16[528,256]{1,0:T(8,128)(2,1)S(1)}, bf16[528,256]{1,0:T(8,128)(2,1)S(1)}, u32[]{:S(2)}, u32[]{:S(2)}) collective-permute-start(bf16[528,256]{1,0:T(8,128)(2,1)S(1)} %collective-permute-done.1.refs_2_), channel_id=1, source_target_pairs={{0,1},{1,0},{2,3},{3,2},{4,5},{5,4},{6,7},{7,6},{8,9},{9,8},{10,11... | collective-permute-start | bytes 811016 | tf_op jit(solution)/shard_map/ppermute | solution.py:384
  26.7 0.0 collective-permute-start.8
  26.7 4.8 %collective-permute-done.4.refs_3_ = bf16[528,256]{1,0:T(8,128)(2,1)S(1)} collective-permute-done((bf16[528,256]{1,0:T(8,128)(2,1)S(1)}, bf16[528,256]{1,0:T(8,128)(2,1)S(1)}, u32[]{:S(2)}, u32[]{:S(2)}) %collective-permute-start.4) | collective-permute-done | bytes 270368 | tf_op jit(solution)/shard_map/ppermute | solution.py:400
  31.5 0.6 %collective-permute-start.6 = (bf16[528,256]{1,0:T(8,128)(2,1)S(1)}, bf16[528,256]{1,0:T(8,128)(2,1)S(1)}, u32[]{:S(2)}, u32[]{:S(2)}) collective-permute-start(bf16[528,256]{1,0:T(8,128)(2,1)S(1)} %collective-permute-done.4.refs_3_), channel_id=1, source_target_pairs={{0,1},{1,0},{2,3},{3,2},{4,5},{5,4},{6,7},{7,6},{8,9},{9,8},{10,11... | collective-permute-start | bytes 811016 | tf_op jit(solution)/shard_map/ppermute | solution.py:384
  32.1 1.2 %collective-permute-done.6.refs_5_ = bf16[528,256]{1,0:T(8,128)(2,1)S(1)} collective-permute-done((bf16[528,256]{1,0:T(8,128)(2,1)S(1)}, bf16[528,256]{1,0:T(8,128)(2,1)S(1)}, u32[]{:S(2)}, u32[]{:S(2)}) %collective-permute-start.6) | collective-permute-done | bytes 270368 | tf_op jit(solution)/shard_map/ppermute | solution.py:384
  33.3 0.8 %attend_last.1.a_ref = bf16[512,256]{1,0:T(8,128)(2,1)S(1)} custom-call(bf16[512,256]{1,0:T(8,128)(2,1)S(1)} %project_query.1.refs_0_, s32[1,512]{1,0:T(1,128)S(1)} %bitcast.9, bf16[528,256]{1,0:T(8,128)(2,1)S(1)} %collective-permute-done.1.refs_2_, bf16[528,256]{1,0:T(8,128)(2,1)S(1)} %collective-permute-done.4.refs_3_, ...), custom_call_target="tpu_custom_call" | custom-call | flops 536870912 | bytes 1048576 | tf_op jit(solution)/shard_map/attend_last/pallas_call | solution.py:256
  34.1 0.5 %collective-permute-start.9 = (bf16[512,256]{1,0:T(8,128)(2,1)S(1)}, bf16[512,256]{1,0:T(8,128)(2,1)S(1)}, u32[]{:S(2)}, u32[]{:S(2)}) collective-permute-start(bf16[512,256]{1,0:T(8,128)(2,1)S(1)} %attend_last.1.a_ref), channel_id=1, source_target_pairs={{0,1},{1,0},{2,3},{3,2},{4,5},{5,4},{6,7},{7,6},{8,9},{9,8},{10,11... | collective-permute-start | bytes 786440 | tf_op jit(solution)/shard_map/ppermute | solution.py:384
  34.6 1.5 %project_own.1.quant_ref = bf16[512,4096]{1,0:T(8,128)(2,1)S(1)} custom-call(bf16[512,256]{1,0:T(8,128)(2,1)S(1)} %attend_last.1.a_ref, bf16[256,4096]{1,0:T(8,128)(2,1)S(1)} %copy-done, bf16[512,4096]{1,0:T(8,128)(2,1)S(1)} %get-tuple-element.33.sum_ref), custom_call_target="tpu_custom_call" | custom-call | flops 1073741824 | bytes 10485760 | tf_op jit(solution)/shard_map/project_own/pallas_call | solution.py:327
  36.1 4.3 %project_out.1 = bf16[512,4096]{1,0:T(8,128)(2,1)} custom-call(bf16[512,256]{1,0:T(8,128)(2,1)S(1)} %collective-permute-done.9.b_ref, bf16[256,4096]{1,0:T(8,128)(2,1)S(1)} %collective-permute-done.10.wb_ref, bf16[512,4096]{1,0:T(8,128)(2,1)S(1)} %project_own.1.quant_ref, f32[512,4096]{1,0:T(8,128)S(1)} %get-tuple-element.35.x_ref, ...), custom_call_target="tpu_custom_call" | custom-call | flops 1073741824 | bytes 10485760 | tf_op jit(solution)/shard_map/project_out/pallas_call | solution.py:366
  (15 shorter events, 0.1 us)
Async XLA Ops:
  0.0 36.1 %collective-permute-start.10 = (bf16[256,4096]{1,0:T(8,128)(2,1)}, bf16[256,4096]{1,0:T(8,128)(2,1)S(1)}, u32[]{:S(2)}, u32[]{:S(2)}) collective-permute-start(bf16[256,4096]{1,0:T(8,128)(2,1)} %w_ref.3), channel_id=1, source_target_pairs={{0,1},{1,0},{2,3},{3,2},{4,5},{5,4},{6,7},{7,6},{8,9},{9,8},{10,11... | collective-permute-start | bytes 6291464 | tf_op jit(solution)/shard_map/ppermute | solution.py:384
  6.7 11.5 %copy-start.1 = (s32[512,32]{0,1:T(8,128)S(1)}, s32[512,32]{0,1:T(8,128)}, u32[]{:S(2)}) copy-start(s32[512,32]{0,1:T(8,128)} %param.14) | copy-start | bytes 196612
  6.7 8.2 %collective-permute-start = (bf16[528,256]{1,0:T(8,128)(2,1)S(1)}, bf16[528,256]{1,0:T(8,128)(2,1)S(1)}, u32[]{:S(2)}, u32[]{:S(2)}) collective-permute-start(bf16[528,256]{1,0:T(8,128)(2,1)S(1)} %get-tuple-element.23.refs_2_), channel_id=1, source_target_pairs={{0,4},{1,5},{2,6},{3,7},{4,8},{5,9},{6,10},{7,11},{8,12},{9,13},{1... | collective-permute-start | bytes 811016 | tf_op jit(solution)/shard_map/ppermute | solution.py:393
  8.0 14.1 %collective-permute-start.2 = (bf16[528,256]{1,0:T(8,128)(2,1)S(1)}, bf16[528,256]{1,0:T(8,128)(2,1)S(1)}, u32[]{:S(2)}, u32[]{:S(2)}) collective-permute-start(bf16[528,256]{1,0:T(8,128)(2,1)S(1)} %get-tuple-element.23.refs_2_), channel_id=1, source_target_pairs={{0,1},{1,0},{2,3},{3,2},{4,5},{5,4},{6,7},{7,6},{8,9},{9,8},{10,11... | collective-permute-start | bytes 811016 | tf_op jit(solution)/shard_map/ppermute | solution.py:384
  9.6 13.9 %copy-start.3 = (s32[512]{0:T(512)S(1)}, s32[512]{0:T(512)}, u32[]{:S(2)}) copy-start(s32[512]{0:T(512)} %param.10) | copy-start | bytes 6148
  14.8 8.6 %collective-permute-start.3 = (bf16[528,256]{1,0:T(8,128)(2,1)S(1)}, bf16[528,256]{1,0:T(8,128)(2,1)S(1)}, u32[]{:S(2)}, u32[]{:S(2)}) collective-permute-start(bf16[528,256]{1,0:T(8,128)(2,1)S(1)} %collective-permute-done.refs_3_), channel_id=1, source_target_pairs={{0,1},{1,0},{2,3},{3,2},{4,5},{5,4},{6,7},{7,6},{8,9},{9,8},{10,11... | collective-permute-start | bytes 811016 | tf_op jit(solution)/shard_map/ppermute | solution.py:384
  15.6 11.0 %collective-permute-start.7 = (bf16[528,256]{1,0:T(8,128)(2,1)S(1)}, bf16[528,256]{1,0:T(8,128)(2,1)S(1)}, u32[]{:S(2)}, u32[]{:S(2)}) collective-permute-start(bf16[528,256]{1,0:T(8,128)(2,1)S(1)} %collective-permute-done.refs_3_), channel_id=1, source_target_pairs={{0,1},{1,0},{2,3},{3,2},{4,6},{5,7},{6,8},{7,9},{8,10},{9,11},{10,... | collective-permute-start | bytes 811016 | tf_op jit(solution)/shard_map/ppermute | solution.py:393
  16.9 8.7 %collective-permute-start.1 = (bf16[528,256]{1,0:T(8,128)(2,1)S(1)}, bf16[528,256]{1,0:T(8,128)(2,1)S(1)}, u32[]{:S(2)}, u32[]{:S(2)}) collective-permute-start(bf16[528,256]{1,0:T(8,128)(2,1)S(1)} %collective-permute-done.refs_3_), channel_id=1, source_target_pairs={{0,1},{1,0},{2,3},{3,2},{4,8},{5,9},{6,10},{7,11},{8,12},{9,13},{1... | collective-permute-start | bytes 811016 | tf_op jit(solution)/shard_map/ppermute | solution.py:393
  18.2 0.8 %copy-start.2 = (s32[512,32]{0,1:T(8,128)S(1)}, s32[512,32]{0,1:T(8,128)}, u32[]{:S(2)}) copy-start(s32[512,32]{0,1:T(8,128)} %param.15) | copy-start | bytes 196612
  22.1 12.5 %copy-start = (bf16[256,4096]{1,0:T(8,128)(2,1)S(1)}, bf16[256,4096]{1,0:T(8,128)(2,1)}, u32[]{:S(2)}) copy-start(bf16[256,4096]{1,0:T(8,128)(2,1)} %w_ref.3) | copy-start | bytes 6291460
  22.1 9.4 %collective-permute-start.4 = (bf16[528,256]{1,0:T(8,128)(2,1)S(1)}, bf16[528,256]{1,0:T(8,128)(2,1)S(1)}, u32[]{:S(2)}, u32[]{:S(2)}) collective-permute-start(bf16[528,256]{1,0:T(8,128)(2,1)S(1)} %broadcast_select_fusion), channel_id=1, source_target_pairs={{0,2},{2,0},{4,6},{6,4},{8,10},{10,8},{12,14},{14,12},{1,3},{3,1},... | collective-permute-start | bytes 811016 | tf_op jit(solution)/shard_map/ppermute | solution.py:400
  25.6 6.0 %collective-permute-start.5 = (bf16[528,256]{1,0:T(8,128)(2,1)S(1)}, bf16[528,256]{1,0:T(8,128)(2,1)S(1)}, u32[]{:S(2)}, u32[]{:S(2)}) collective-permute-start(bf16[528,256]{1,0:T(8,128)(2,1)S(1)} %collective-permute-done.1.refs_2_), channel_id=1, source_target_pairs={{0,1},{1,0},{2,3},{3,2},{4,5},{5,4},{6,7},{7,6},{8,9},{9,8},{10,11... | collective-permute-start | bytes 811016 | tf_op jit(solution)/shard_map/ppermute | solution.py:384
  26.7 5.5 %collective-permute-start.8 = (bf16[528,256]{1,0:T(8,128)(2,1)S(1)}, bf16[528,256]{1,0:T(8,128)(2,1)S(1)}, u32[]{:S(2)}, u32[]{:S(2)}) collective-permute-start(bf16[528,256]{1,0:T(8,128)(2,1)S(1)} %collective-permute-done.7.refs_2_), channel_id=1, source_target_pairs={{0,1},{1,0},{2,3},{3,2},{4,5},{5,4},{6,7},{7,6},{8,9},{9,8},{10,11... | collective-permute-start | bytes 811016 | tf_op jit(solution)/shard_map/ppermute | solution.py:384
  31.5 1.8 %collective-permute-start.6 = (bf16[528,256]{1,0:T(8,128)(2,1)S(1)}, bf16[528,256]{1,0:T(8,128)(2,1)S(1)}, u32[]{:S(2)}, u32[]{:S(2)}) collective-permute-start(bf16[528,256]{1,0:T(8,128)(2,1)S(1)} %collective-permute-done.4.refs_3_), channel_id=1, source_target_pairs={{0,1},{1,0},{2,3},{3,2},{4,5},{5,4},{6,7},{7,6},{8,9},{9,8},{10,11... | collective-permute-start | bytes 811016 | tf_op jit(solution)/shard_map/ppermute | solution.py:384
  34.1 2.0 %collective-permute-start.9 = (bf16[512,256]{1,0:T(8,128)(2,1)S(1)}, bf16[512,256]{1,0:T(8,128)(2,1)S(1)}, u32[]{:S(2)}, u32[]{:S(2)}) collective-permute-start(bf16[512,256]{1,0:T(8,128)(2,1)S(1)} %attend_last.1.a_ref), channel_id=1, source_target_pairs={{0,1},{1,0},{2,3},{3,2},{4,5},{5,4},{6,7},{7,6},{8,9},{9,8},{10,11... | collective-permute-start | bytes 786440 | tf_op jit(solution)/shard_map/ppermute | solution.py:384

commit v22 on v20

--- a/solution.py
+++ b/solution.py
@@ -400,7 +400,7 @@
     beside = lax.ppermute(jnp.where(odd, held, message), "seq", [(i, i ^ 1) for i in range(seq_size)])
     parts = [[(0, message), (2, held)]]
     for back in range(2, window, 2):
-        step = shift(held, 1, back)
+        step = shift(held, 1, 0)
         held = shift(held, 2, back)
         parts.append([(back + 1, step)] + ([(back + 2, held)] if back + 2 < window else []))
     parts.append([(window, held), (1, beside)])

time: 40.4 us -> 43.1 us (1.067)
  the two profiles are of different devices: /device:TPU:11 before, /device:TPU:0 now
where the time goes in v22:
time: 43.1 us; the launch traced here: 42.9 us
  waiting for transfers between devices  19 us (44%)
  Pallas kernels  17.4 us (40%)
  starting transfers between devices  6.17 us (14%)
    ppermute x3, waiting for transfers between devices, shift(): return lax.ppermute(x, ('seq', 'tp'), pairs)  13.3 us
    pallas_call x1, Pallas kernels, norm_kv(): pl.pallas_call(norm_kv_kernel, in_specs=[hbm] * 5, out_specs=[vmem] * 3,...  5.98 us
    ppermute x3, starting transfers between devices, shift(): return lax.ppermute(x, ('seq', 'tp'), pairs)  4.7 us
    pallas_call x1, Pallas kernels, project_out(): pl.pallas_call(output_kernel, in_specs=[vmem] * len(operands), out_specs=...  4.33 us
    ppermute x1, waiting for transfers between devices, on_device(): lax.ppermute(jnp.where(odd, held, message), 'seq', [(i, i ^ 1) for i in r...  4.25 us
    pallas_call x1, Pallas kernels, spread_bounds(): pl.pallas_call(bounds_kernel, in_specs=[vmem, vmem, pl.BlockSpec(memory_s...  3.05 us
    pallas_call x1, Pallas kernels, project_own(): pl.pallas_call(own_kernel, in_specs=[vmem] * 3, out_specs=vmem, out_shape...  1.52 us
    ppermute x7, waiting for transfers between devices, swap_cores(): return lax.ppermute(x, 'tp', [(0, 1), (1, 0)])  1.43 us
  transfers between devices with their start and end apart: 11, of which 5 were waited for; matrix products, arithmetic and copies ran while one was open for 0% of the time, Pallas kernels for 31%

profile of v22, /device:TPU:0, one launch (start us, length us, event | category | flops | bytes accessed | tf_op | source)
XLA Modules:
  0.0 42.9 jit_solution(11750998586708443822)
XLA Ops:
  0.0 0.5 %collective-permute-start.10 = (bf16[256,4096]{1,0:T(8,128)(2,1)}, bf16[256,4096]{1,0:T(8,128)(2,1)S(1)}, u32[]{:S(2)}, u32[]{:S(2)}) collective-permute-start(bf16[256,4096]{1,0:T(8,128)(2,1)} %w_ref.3), channel_id=1, source_target_pairs={{0,1},{1,0},{2,3},{3,2},{4,5},{5,4},{6,7},{7,6},{8,9},{9,8},{10,11... | collective-permute-start | bytes 6291464 | tf_op jit(solution)/shard_map/ppermute | solution.py:384
  0.5 6.0 %norm_kv.1 = (bf16[528,256]{1,0:T(8,128)(2,1)S(1)}, bf16[512,4096]{1,0:T(8,128)(2,1)S(1)}, bf16[4096,256]{1,0:T(8,128)(2,1)S(1)}) custom-call(bf16[512,4096]{1,0:T(8,128)(2,1)} %x_ref.3, f32[1,4096]{1,0:T(1,128)} %bitcast.10, bf16[4096,256]{1,0:T(8,128)(2,1)} %w_ref.2, s32[1,512]{1,0:T(1,128)} %bitcast.6, bf16[4096,256]{1,0:T(8,128)(2,1)} %next_ref.1), custom_call_target="tpu_custom_call" | custom-call | flops 1073741824 | bytes 10485760 | tf_op jit(solution)/shard_map/norm_kv/pallas_call | solution.py:116
  6.4 0.0 copy-start.1
  6.5 0.0 copy-start.2
  6.5 2.6 %collective-permute-start = (bf16[528,256]{1,0:T(8,128)(2,1)S(1)}, bf16[528,256]{1,0:T(8,128)(2,1)S(1)}, u32[]{:S(2)}, u32[]{:S(2)}) collective-permute-start(bf16[528,256]{1,0:T(8,128)(2,1)S(1)} %get-tuple-element.22.refs_2_), channel_id=1, source_target_pairs={{0,4},{1,5},{2,6},{3,7},{4,8},{5,9},{6,10},{7,11},{8,12},{9,13},{1... | collective-permute-start | bytes 811016 | tf_op jit(solution)/shard_map/ppermute | solution.py:393
  9.1 0.2 collective-permute-start.2
  9.3 1.2 %project_query.1.refs_0_ = bf16[512,256]{1,0:T(8,128)(2,1)S(1)} custom-call(bf16[512,4096]{1,0:T(8,128)(2,1)S(1)} %get-tuple-element.23.x_ref, bf16[4096,256]{1,0:T(8,128)(2,1)S(1)} %get-tuple-element.24.w_ref), custom_call_target="tpu_custom_call" | custom-call | flops 1073741824 | bytes 6291456 | tf_op jit(solution)/shard_map/project_query/pallas_call | solution.py:148
  10.6 0.0 copy-start.3
  10.6 7.7 %collective-permute-done.refs_3_ = bf16[528,256]{1,0:T(8,128)(2,1)S(1)} collective-permute-done((bf16[528,256]{1,0:T(8,128)(2,1)S(1)}, bf16[528,256]{1,0:T(8,128)(2,1)S(1)}, u32[]{:S(2)}, u32[]{:S(2)}) %collective-permute-start) | collective-permute-done | bytes 270368 | tf_op jit(solution)/shard_map/ppermute | solution.py:393
  18.3 1.5 %collective-permute-start.7 = (bf16[528,256]{1,0:T(8,128)(2,1)S(1)}, bf16[528,256]{1,0:T(8,128)(2,1)S(1)}, u32[]{:S(2)}, u32[]{:S(2)}) collective-permute-start(bf16[528,256]{1,0:T(8,128)(2,1)S(1)} %collective-permute-done.refs_3_), channel_id=1, source_target_pairs={{0,2},{1,3},{2,4},{3,5},{4,6},{5,7},{6,8},{7,9},{8,10},{9,11},{10,... | collective-permute-start | bytes 811016 | tf_op jit(solution)/shard_map/ppermute | solution.py:393
  19.8 0.1 collective-permute-start.4
  19.9 0.6 %collective-permute-start.1 = (bf16[528,256]{1,0:T(8,128)(2,1)S(1)}, bf16[528,256]{1,0:T(8,128)(2,1)S(1)}, u32[]{:S(2)}, u32[]{:S(2)}) collective-permute-start(bf16[528,256]{1,0:T(8,128)(2,1)S(1)} %collective-permute-done.refs_3_), channel_id=1, source_target_pairs={{0,1},{1,0},{2,3},{3,2},{4,8},{5,9},{6,10},{7,11},{8,12},{9,13},{1... | collective-permute-start | bytes 811016 | tf_op jit(solution)/shard_map/ppermute | solution.py:393
  20.5 3.0 %spread_bounds.1 = (bf16[512,4096]{1,0:T(8,128)(2,1)S(1)}, bf16[512,4096]{1,0:T(8,128)(2,1)S(1)}, f32[512,4096]{1,0:T(8,128)S(1)}) custom-call(s32[32,512]{1,0:T(8,128)S(1)} %bitcast.4, s32[32,512]{1,0:T(8,128)S(1)} %bitcast.5, bf16[512,4096]{1,0:T(8,128)(2,1)} %x_ref.3), custom_call_target="tpu_custom_call" | custom-call | flops 16777216 | bytes 131072 | tf_op jit(solution)/shard_map/spread_bounds/pallas_call | solution.py:296
  23.5 0.0 copy-start
  23.6 1.1 %attend_first.1.refs_4_ = f32[512,640]{1,0:T(8,128)S(1)} custom-call(bf16[512,256]{1,0:T(8,128)(2,1)S(1)} %project_query.1.refs_0_, s32[1,512]{1,0:T(1,128)S(1)} %bitcast.7, bf16[528,256]{1,0:T(8,128)(2,1)S(1)} %get-tuple-element.22.refs_2_, bf16[528,256]{1,0:T(8,128)(2,1)S(1)} %collective-permute-done.refs_3_, ...), custom_call_target="tpu_custom_call" | custom-call | flops 536870912 | bytes 1048576 | tf_op jit(solution)/shard_map/attend_first/pallas_call | solution.py:256
  24.7 5.6 %collective-permute-done.7.refs_2_ = bf16[528,256]{1,0:T(8,128)(2,1)S(1)} collective-permute-done((bf16[528,256]{1,0:T(8,128)(2,1)S(1)}, bf16[528,256]{1,0:T(8,128)(2,1)S(1)}, u32[]{:S(2)}, u32[]{:S(2)}) %collective-permute-start.7) | collective-permute-done | bytes 270368 | tf_op jit(solution)/shard_map/ppermute | solution.py:393
  30.3 4.3 %collective-permute-done.4.refs_3_ = bf16[528,256]{1,0:T(8,128)(2,1)S(1)} collective-permute-done((bf16[528,256]{1,0:T(8,128)(2,1)S(1)}, bf16[528,256]{1,0:T(8,128)(2,1)S(1)}, u32[]{:S(2)}, u32[]{:S(2)}) %collective-permute-start.4) | collective-permute-done | bytes 270368 | tf_op jit(solution)/shard_map/ppermute | solution.py:400
  34.6 0.5 %collective-permute-start.6 = (bf16[528,256]{1,0:T(8,128)(2,1)S(1)}, bf16[528,256]{1,0:T(8,128)(2,1)S(1)}, u32[]{:S(2)}, u32[]{:S(2)}) collective-permute-start(bf16[528,256]{1,0:T(8,128)(2,1)S(1)} %collective-permute-done.4.refs_3_), channel_id=1, source_target_pairs={{0,1},{1,0},{2,3},{3,2},{4,5},{5,4},{6,7},{7,6},{8,9},{9,8},{10,11... | collective-permute-start | bytes 811016 | tf_op jit(solution)/shard_map/ppermute | solution.py:384
  35.1 1.0 %collective-permute-done.5.refs_4_ = bf16[528,256]{1,0:T(8,128)(2,1)S(1)} collective-permute-done((bf16[528,256]{1,0:T(8,128)(2,1)S(1)}, bf16[528,256]{1,0:T(8,128)(2,1)S(1)}, u32[]{:S(2)}, u32[]{:S(2)}) %collective-permute-start.5) | collective-permute-done | bytes 270368 | tf_op jit(solution)/shard_map/ppermute | solution.py:384
  36.1 0.4 collective-permute-done.6.refs_5_
  36.5 0.2 attend_last.1.a_ref
  36.7 0.2 collective-permute-start.9
  36.9 1.5 %project_own.1.quant_ref = bf16[512,4096]{1,0:T(8,128)(2,1)S(1)} custom-call(bf16[512,256]{1,0:T(8,128)(2,1)S(1)} %attend_last.1.a_ref, bf16[256,4096]{1,0:T(8,128)(2,1)S(1)} %copy-done, bf16[512,4096]{1,0:T(8,128)(2,1)S(1)} %get-tuple-element.32.sum_ref), custom_call_target="tpu_custom_call" | custom-call | flops 1073741824 | bytes 10485760 | tf_op jit(solution)/shard_map/project_own/pallas_call | solution.py:327
  38.5 4.3 %project_out.1 = bf16[512,4096]{1,0:T(8,128)(2,1)} custom-call(bf16[512,256]{1,0:T(8,128)(2,1)S(1)} %collective-permute-done.9.b_ref, bf16[256,4096]{1,0:T(8,128)(2,1)S(1)} %collective-permute-done.10.wb_ref, bf16[512,4096]{1,0:T(8,128)(2,1)S(1)} %project_own.1.quant_ref, f32[512,4096]{1,0:T(8,128)S(1)} %get-tuple-element.34.x_ref, ...), custom_call_target="tpu_custom_call" | custom-call | flops 1073741824 | bytes 10485760 | tf_op jit(solution)/shard_map/project_out/pallas_call | solution.py:366
  (15 shorter events, 0.1 us)
Async XLA Ops:
  0.0 38.4 %collective-permute-start.10 = (bf16[256,4096]{1,0:T(8,128)(2,1)}, bf16[256,4096]{1,0:T(8,128)(2,1)S(1)}, u32[]{:S(2)}, u32[]{:S(2)}) collective-permute-start(bf16[256,4096]{1,0:T(8,128)(2,1)} %w_ref.3), channel_id=1, source_target_pairs={{0,1},{1,0},{2,3},{3,2},{4,5},{5,4},{6,7},{7,6},{8,9},{9,8},{10,11... | collective-permute-start | bytes 6291464 | tf_op jit(solution)/shard_map/ppermute | solution.py:384
  6.4 14.0 %copy-start.1 = (s32[512,32]{0,1:T(8,128)S(1)}, s32[512,32]{0,1:T(8,128)}, u32[]{:S(2)}) copy-start(s32[512,32]{0,1:T(8,128)} %param.14) | copy-start | bytes 196612
  6.5 14.0 %copy-start.2 = (s32[512,32]{0,1:T(8,128)S(1)}, s32[512,32]{0,1:T(8,128)}, u32[]{:S(2)}) copy-start(s32[512,32]{0,1:T(8,128)} %param.15) | copy-start | bytes 196612
  6.5 11.8 %collective-permute-start = (bf16[528,256]{1,0:T(8,128)(2,1)S(1)}, bf16[528,256]{1,0:T(8,128)(2,1)S(1)}, u32[]{:S(2)}, u32[]{:S(2)}) collective-permute-start(bf16[528,256]{1,0:T(8,128)(2,1)S(1)} %get-tuple-element.22.refs_2_), channel_id=1, source_target_pairs={{0,4},{1,5},{2,6},{3,7},{4,8},{5,9},{6,10},{7,11},{8,12},{9,13},{1... | collective-permute-start | bytes 811016 | tf_op jit(solution)/shard_map/ppermute | solution.py:393
  9.1 10.8 %collective-permute-start.2 = (bf16[528,256]{1,0:T(8,128)(2,1)S(1)}, bf16[528,256]{1,0:T(8,128)(2,1)S(1)}, u32[]{:S(2)}, u32[]{:S(2)}) collective-permute-start(bf16[528,256]{1,0:T(8,128)(2,1)S(1)} %get-tuple-element.22.refs_2_), channel_id=1, source_target_pairs={{0,1},{1,0},{2,3},{3,2},{4,5},{5,4},{6,7},{7,6},{8,9},{9,8},{10,11... | collective-permute-start | bytes 811016 | tf_op jit(solution)/shard_map/ppermute | solution.py:384
  10.6 13.0 %copy-start.3 = (s32[512]{0:T(512)S(1)}, s32[512]{0:T(512)}, u32[]{:S(2)}) copy-start(s32[512]{0:T(512)} %param.10) | copy-start | bytes 6148
  18.3 12.1 %collective-permute-start.7 = (bf16[528,256]{1,0:T(8,128)(2,1)S(1)}, bf16[528,256]{1,0:T(8,128)(2,1)S(1)}, u32[]{:S(2)}, u32[]{:S(2)}) collective-permute-start(bf16[528,256]{1,0:T(8,128)(2,1)S(1)} %collective-permute-done.refs_3_), channel_id=1, source_target_pairs={{0,2},{1,3},{2,4},{3,5},{4,6},{5,7},{6,8},{7,9},{8,10},{9,11},{10,... | collective-permute-start | bytes 811016 | tf_op jit(solution)/shard_map/ppermute | solution.py:393
  19.8 3.8 %collective-permute-start.3 = (bf16[528,256]{1,0:T(8,128)(2,1)S(1)}, bf16[528,256]{1,0:T(8,128)(2,1)S(1)}, u32[]{:S(2)}, u32[]{:S(2)}) collective-permute-start(bf16[528,256]{1,0:T(8,128)(2,1)S(1)} %collective-permute-done.refs_3_), channel_id=1, source_target_pairs={{0,1},{1,0},{2,3},{3,2},{4,5},{5,4},{6,7},{7,6},{8,9},{9,8},{10,11... | collective-permute-start | bytes 811016 | tf_op jit(solution)/shard_map/ppermute | solution.py:384
  19.8 14.8 %collective-permute-start.4 = (bf16[528,256]{1,0:T(8,128)(2,1)S(1)}, bf16[528,256]{1,0:T(8,128)(2,1)S(1)}, u32[]{:S(2)}, u32[]{:S(2)}) collective-permute-start(bf16[528,256]{1,0:T(8,128)(2,1)S(1)} %broadcast_select_fusion), channel_id=1, source_target_pairs={{0,2},{2,0},{4,6},{6,4},{8,10},{10,8},{12,14},{14,12},{1,3},{3,1},... | collective-permute-start | bytes 811016 | tf_op jit(solution)/shard_map/ppermute | solution.py:400
  19.9 14.7 %collective-permute-start.1 = (bf16[528,256]{1,0:T(8,128)(2,1)S(1)}, bf16[528,256]{1,0:T(8,128)(2,1)S(1)}, u32[]{:S(2)}, u32[]{:S(2)}) collective-permute-start(bf16[528,256]{1,0:T(8,128)(2,1)S(1)} %collective-permute-done.refs_3_), channel_id=1, source_target_pairs={{0,1},{1,0},{2,3},{3,2},{4,8},{5,9},{6,10},{7,11},{8,12},{9,13},{1... | collective-permute-start | bytes 811016 | tf_op jit(solution)/shard_map/ppermute | solution.py:393
  23.5 13.4 %copy-start = (bf16[256,4096]{1,0:T(8,128)(2,1)S(1)}, bf16[256,4096]{1,0:T(8,128)(2,1)}, u32[]{:S(2)}) copy-start(bf16[256,4096]{1,0:T(8,128)(2,1)} %w_ref.3) | copy-start | bytes 6291460
  30.3 4.8 %collective-permute-start.8 = (bf16[528,256]{1,0:T(8,128)(2,1)S(1)}, bf16[528,256]{1,0:T(8,128)(2,1)S(1)}, u32[]{:S(2)}, u32[]{:S(2)}) collective-permute-start(bf16[528,256]{1,0:T(8,128)(2,1)S(1)} %collective-permute-done.7.refs_2_), channel_id=1, source_target_pairs={{0,1},{1,0},{2,3},{3,2},{4,5},{5,4},{6,7},{7,6},{8,9},{9,8},{10,11... | collective-permute-start | bytes 811016 | tf_op jit(solution)/shard_map/ppermute | solution.py:384
  34.6 1.5 %collective-permute-start.5 = (bf16[528,256]{1,0:T(8,128)(2,1)S(1)}, bf16[528,256]{1,0:T(8,128)(2,1)S(1)}, u32[]{:S(2)}, u32[]{:S(2)}) collective-permute-start(bf16[528,256]{1,0:T(8,128)(2,1)S(1)} %collective-permute-done.1.refs_2_), channel_id=1, source_target_pairs={{0,1},{1,0},{2,3},{3,2},{4,5},{5,4},{6,7},{7,6},{8,9},{9,8},{10,11... | collective-permute-start | bytes 811016 | tf_op jit(solution)/shard_map/ppermute | solution.py:384
  34.6 1.9 %collective-permute-start.6 = (bf16[528,256]{1,0:T(8,128)(2,1)S(1)}, bf16[528,256]{1,0:T(8,128)(2,1)S(1)}, u32[]{:S(2)}, u32[]{:S(2)}) collective-permute-start(bf16[528,256]{1,0:T(8,128)(2,1)S(1)} %collective-permute-done.4.refs_3_), channel_id=1, source_target_pairs={{0,1},{1,0},{2,3},{3,2},{4,5},{5,4},{6,7},{7,6},{8,9},{9,8},{10,11... | collective-permute-start | bytes 811016 | tf_op jit(solution)/shard_map/ppermute | solution.py:384
  36.7 1.7 %collective-permute-start.9 = (bf16[512,256]{1,0:T(8,128)(2,1)S(1)}, bf16[512,256]{1,0:T(8,128)(2,1)S(1)}, u32[]{:S(2)}, u32[]{:S(2)}) collective-permute-start(bf16[512,256]{1,0:T(8,128)(2,1)S(1)} %attend_last.1.a_ref), channel_id=1, source_target_pairs={{0,1},{1,0},{2,3},{3,2},{4,5},{5,4},{6,7},{7,6},{8,9},{9,8},{10,11... | collective-permute-start | bytes 786440 | tf_op jit(solution)/shard_map/ppermute | solution.py:384
